TPU v7x, 512 devices: a whole 4x4x16 slice. The times are simulated.
512 devices in a mesh: dp: 8 (over y, core), expert: 64 (over x, z).
Axes of the slice: x: 4, y: 4, z: 16, core: 2. Of those that a mesh axis runs over, the one named last changes fastest.
Arguments:
- tokens: bfloat16 [32768, 4096], P(('dp', 'expert')), parts along dimension 0, may hold values from -6 to 6
- routes: int32 [32768, 2], P(('dp', 'expert')), parts along dimension 0, may hold values from 0 to 7, all different within a row; in each aligned block of 64 rows (0 to 63, 64 to 127, ...) at most 20 rows name the same one
- numerators: int32 [32768, 2], P(('dp', 'expert')), parts along dimension 0, may hold values from 1 to 256
- counts: int32 [512], P(('dp', 'expert')), parts along dimension 0, may hold values from 32 to 64, as said below
- w_gate: bfloat16 [32768, 1024], P('expert'), may hold values from -0.09375 to 0.09375
- w_up: bfloat16 [32768, 1024], P('expert'), may hold values from -0.09375 to 0.09375
- w_down: bfloat16 [1024, 32768], P(None, 'expert'), may hold values from -0.1875 to 0.1875
Outputs:
- mixed: bfloat16 [32768, 4096], P(('dp', 'expert')), parts along dimension 0
There are 8 independent parts, one for each index of `dp`. A program takes and returns all parts, laid end to end along the dimension named above; an argument that names none is the same for every part. Nothing has to cross between parts.
Inputs may be any that keep to these rules, and one draw needn't show every extreme that they name: `routes`: each row names 2 different experts. Among the 64 rows of one device no expert is named more than 20 times, and in every draw some device has an expert named exactly 20 times. Rows 0 to counts - 1 of a device are live, the others are ignored; some device is full in every draw.
All inputs are finite; a program needn't handle non-finite values.
Results may differ from a plain program's by a relative error of at most 0.027.
Values may be sent and summed in bfloat16 or wider, within the bound.
No kernel may reach another device: no remote copies, remote signals or barrier semaphores. Data moves between devices by JAX's collectives and lax.ppermute only.
A program may use at most 128 MiB of HBM per device.

v0:
```python
import jax
import jax.numpy as jnp
from jax import lax
from jax.sharding import PartitionSpec as P

BLOCK = 128
GROUP = 8


def partner(block, axis, stride):
    count = lax.axis_size(axis)
    route = []
    for low in range(count):
        high = low | 1 << stride
        if high != low and high < count:
            route += [(low, high), (high, low)]
    return lax.ppermute(block, axis, route)


def snap_scaled(scaled):
    magnitude = jnp.abs(scaled)
    spacing = jnp.full_like(magnitude, 2.0 ** (-9))
    for exponent in range(-5, 9):
        spacing = jnp.where(magnitude >= 2.0**exponent, 2.0 ** (exponent - 3), spacing)
    snapped = jnp.floor(magnitude / spacing + 0.5) * spacing
    return jnp.where(scaled < 0.0, -snapped, snapped)


def pick_half(array_in, own_side, half_width):
    kept_part = lax.dynamic_slice_in_dim(array_in, own_side * half_width, half_width, 1)
    given_part = lax.dynamic_slice_in_dim(array_in, (1 - own_side) * half_width, half_width, 1)
    return (kept_part, given_part)


def join_sides(own_part, partner_part, own_side, axis_dim):
    lower_first = jnp.concatenate([own_part, partner_part], axis=axis_dim)
    upper_first = jnp.concatenate([partner_part, own_part], axis=axis_dim)
    return jnp.where(own_side == 0, lower_first, upper_first)


def local(tokens, routes, numerators, counts, w_gate, w_up, w_down):
    tok_rows, feature_width = tokens.shape
    top_count = routes.shape[1]
    devices = lax.axis_size("expert")
    group_size = GROUP
    levels = group_size.bit_length() - 1
    experts = devices // group_size
    slot_cap = min(tok_rows, 5 * tok_rows * top_count // (4 * experts))
    blocks = feature_width // BLOCK
    dev_index = lax.axis_index("expert")
    recv_count = devices * slot_cap
    values = tokens.astype(jnp.float32).reshape(tok_rows, blocks, BLOCK)
    block_amax = jnp.max(jnp.abs(values), axis=2)
    block_scale = (block_amax + 1e-06) / 448.0
    coded_rows = (
        snap_scaled(values / block_scale[:, :, None])
        .astype(jnp.bfloat16)
        .reshape(tok_rows, feature_width)
    )
    live_rows = jnp.arange(tok_rows) < counts[0]
    live_slots = jnp.repeat(live_rows, top_count)
    onehot = (
        (routes.reshape(-1)[:, None] == jnp.arange(experts)[None, :]) & live_slots[:, None]
    ).astype(jnp.int32)
    slot_index = jnp.sum((jnp.cumsum(onehot, axis=0) - onehot) * onehot, axis=1)
    placed = (
        onehot[:, None, :] * (slot_index[:, None, None] == jnp.arange(slot_cap)[None, :, None])
    ).astype(jnp.float32)
    placed = placed.reshape(tok_rows * top_count, slot_cap * experts)
    assign = jnp.sum(placed.reshape(tok_rows, top_count, slot_cap * experts), axis=1)
    assign_half = assign.astype(jnp.bfloat16)
    slot_share = numerators.reshape(-1).astype(jnp.float32) / 256.0
    rows_out = jnp.einsum(
        "tp,td->pd", assign_half, coded_rows, preferred_element_type=jnp.float32
    ).astype(jnp.bfloat16)
    scales_out = jnp.einsum("tp,tb->pb", assign, block_scale, precision=lax.Precision.HIGHEST)
    shares_out = jnp.dot(slot_share, placed, precision=lax.Precision.HIGHEST).reshape(
        slot_cap, experts
    )
    send_share = jnp.repeat(shares_out, group_size, axis=1)
    send_coded = rows_out.reshape(slot_cap, experts * feature_width)
    send_scale = scales_out.reshape(slot_cap, experts * blocks)
    got_rows, got_scale, got_share = (
        lax.all_to_all(send_coded, "expert", split_axis=1, concat_axis=0, tiled=True),
        lax.all_to_all(
            send_scale.astype(jnp.bfloat16), "expert", split_axis=1, concat_axis=0, tiled=True
        ).astype(send_scale.dtype),
        lax.all_to_all(
            send_share.astype(jnp.bfloat16), "expert", split_axis=1, concat_axis=0, tiled=True
        ).astype(send_share.dtype),
    )
    member_blocks = got_scale.shape[1]
    restored = (
        got_rows.astype(jnp.float32).reshape(recv_count, member_blocks, BLOCK)
        * got_scale[:, :, None]
    )
    restored = restored.reshape(recv_count, member_blocks * BLOCK).astype(jnp.bfloat16)
    gate_sum = jnp.dot(restored, w_gate, preferred_element_type=jnp.float32)
    up_sum = jnp.dot(restored, w_up, preferred_element_type=jnp.float32)
    for bit_level in range(levels - 1, -1, -1):
        half_width = gate_sum.shape[1] // 2
        own_side = dev_index >> bit_level & 1
        kept_gate, given_gate = pick_half(gate_sum, own_side, half_width)
        kept_up, given_up = pick_half(up_sum, own_side, half_width)
        recv_gate, recv_up = (
            partner(given_gate.astype(jnp.bfloat16), "expert", bit_level).astype(given_gate.dtype),
            partner(given_up.astype(jnp.bfloat16), "expert", bit_level).astype(given_up.dtype),
        )
        gate_sum = kept_gate + recv_gate
        up_sum = kept_up + recv_up
    hidden = (jax.nn.silu(gate_sum) * up_sum).astype(jnp.bfloat16)
    for bit_level in range(levels):
        own_side = dev_index >> bit_level & 1
        partner_part = partner(hidden, "expert", bit_level)
        hidden = join_sides(hidden, partner_part, own_side, 1)
    result = jnp.dot(hidden, w_down, preferred_element_type=jnp.float32)
    weighted = (result * got_share).astype(jnp.bfloat16)
    returned = lax.all_to_all(weighted, "expert", split_axis=0, concat_axis=1, tiled=True)
    returned = returned.reshape(slot_cap * experts, feature_width)
    mixed = jnp.einsum("tp,pd->td", assign_half, returned, preferred_element_type=jnp.float32)
    return mixed.astype(jnp.bfloat16)


def solution(mesh):
    placed = (
        P(("dp", "expert"), None),
        P(("dp", "expert"), None),
        P(("dp", "expert"), None),
        P(("dp", "expert")),
        P("expert", None),
        P("expert", None),
        P(None, "expert"),
    )
    return jax.shard_map(
        local, mesh=mesh, in_specs=placed, out_specs=P(("dp", "expert"), None), check_vma=False
    )
```

profile of v0, /device:TPU:1, one launch (start us, length us, event | category | flops | bytes accessed | tf_op | source)
XLA Modules:
  0.0 698.9 jit_solution(7914277211073332730)
XLA Ops:
  0.8 0.2 and.27
  1.0 0.8 copy.19
  2.1 0.2 reduce_window_sum.11
  2.2 0.2 select_reduce_fusion
  2.4 1.1 fusion.8
  3.6 1.2 copy.31
  4.7 0.5 copy.21
  5.3 0.6 convert_element_type.153
  5.9 1.6 reduce_max.9
  7.5 0.2 reduce_sum.19
  7.7 0.2 convolution_convert_fusion.2
  8.0 0.3 convert_element_type.162
  8.3 1.2 copy.24
  9.5 19.1 %all-to-all-start.1 = ((bf16[20,64,4]{0,2,1:T(4,128)(2,1)}), bf16[20,64,4]{0,2,1:T(4,128)(2,1)S(1)}, u32[]{:S(2)}, u32[]{:S(2)}) async-start(bf16[20,64,4]{0,2,1:T(4,128)(2,1)} %copy.24), calls=%async_computation.1 | async-start | bytes 131072 | tf_op jit(solution)/shard_map/all_to_all | solution.py:85
  28.6 0.3 div.35
  29.0 3.0 convolution_convert_fusion
  32.0 2.4 all_to_all.18
  34.4 1.9 copy.22
  36.3 5.8 all-to-all-done.1
  42.1 8.9 %all-to-all-start = ((bf16[20,64,512]{2,0,1:T(8,128)(2,1)}), bf16[20,64,512]{2,0,1:T(8,128)(2,1)S(1)}, u32[]{:S(2)}, u32[]{:S(2)}) async-start(bf16[20,64,512]{2,0,1:T(8,128)(2,1)} %copy.22), calls=%async_computation | async-start | bytes 3145728 | tf_op jit(solution)/shard_map/all_to_all | solution.py:84
  51.2 0.3 copy.26
  51.5 69.9 %all-to-all-done = bf16[20,64,512]{2,0,1:T(8,128)(2,1)S(1)} async-done(((bf16[20,64,512]{2,0,1:T(8,128)(2,1)}), bf16[20,64,512]{2,0,1:T(8,128)(2,1)S(1)}, u32[]{:S(2)}, u32[]{:S(2)}) %all-to-all-start) | async-done | bytes 1310752 | tf_op jit(solution)/shard_map/all_to_all | solution.py:84
  121.4 2.1 convert_bitcast_fusion
  123.5 4.1 reshape.141
  127.6 2.9 mul.79
  130.5 0.7 fusion.1
  131.2 1.7 fusion.39
  132.9 1.2 dynamic-slice_convert_fusion
  134.1 1.5 copy-done.5
  135.6 5.7 collective-permute-start.3
  141.2 1.7 fusion.38
  142.9 2.3 copy-done.3
  145.4 3.5 collective-permute-start
  148.9 188.6 %collective-permute-done.3 = bf16[1280,512]{0,1:T(8,128)(2,1)} collective-permute-done((bf16[1280,512]{0,1:T(8,128)(2,1)}, bf16[1280,512]{0,1:T(8,128)(2,1)}, u32[]{:S(2)}, u32[]{:S(2)}) %collective-permute-start.3) | collective-permute-done | bytes 1310752 | tf_op jit(solution)/shard_map/ppermute | solution.py:17
  337.5 2.5 convert_add_fusion
  340.1 2.1 collective-permute-start.4
  342.2 23.5 %collective-permute-done = bf16[1280,512]{0,1:T(8,128)(2,1)} collective-permute-done((bf16[1280,512]{0,1:T(8,128)(2,1)S(1)}, bf16[1280,512]{0,1:T(8,128)(2,1)}, u32[]{:S(2)}, u32[]{:S(2)}) %collective-permute-start) | collective-permute-done | bytes 1310752 | tf_op jit(solution)/shard_map/ppermute | solution.py:17
  365.7 1.6 convert_add_fusion.1
  367.4 1.9 collective-permute-start.1
  369.3 41.7 %collective-permute-done.4 = bf16[1280,256]{0,1:T(8,128)(2,1)S(1)} collective-permute-done((bf16[1280,256]{0,1:T(8,128)(2,1)S(1)}, bf16[1280,256]{0,1:T(8,128)(2,1)S(1)}, u32[]{:S(2)}, u32[]{:S(2)}) %collective-permute-start.4) | collective-permute-done | bytes 655392 | tf_op jit(solution)/shard_map/ppermute | solution.py:17
  411.2 1.9 collective-permute-start.5
  413.1 12.0 %collective-permute-done.1 = bf16[1280,256]{0,1:T(8,128)(2,1)S(1)} collective-permute-done((bf16[1280,256]{0,1:T(8,128)(2,1)S(1)}, bf16[1280,256]{0,1:T(8,128)(2,1)S(1)}, u32[]{:S(2)}, u32[]{:S(2)}) %collective-permute-start.1) | collective-permute-done | bytes 655392 | tf_op jit(solution)/shard_map/ppermute | solution.py:17
  425.2 1.1 copy-done.2
  426.3 0.8 dynamic-slice_convert_fusion.5
  427.1 1.9 collective-permute-start.2
  429.0 3.1 collective-permute-done.5
  432.1 6.5 collective-permute-done.2
  438.6 1.4 multiply_convert_fusion
  440.0 1.9 collective-permute-start.6
  441.9 8.0 %collective-permute-done.6 = bf16[1280,128]{0,1:T(8,128)(2,1)S(1)} collective-permute-done((bf16[1280,128]{0,1:T(8,128)(2,1)S(1)}, bf16[1280,128]{0,1:T(8,128)(2,1)S(1)}, u32[]{:S(2)}, u32[]{:S(2)}) %collective-permute-start.6) | collective-permute-done | bytes 327712 | tf_op jit(solution)/shard_map/ppermute | solution.py:17
  450.1 1.9 collective-permute-start.7
  452.0 31.6 %collective-permute-done.7 = bf16[1280,256]{0,1:T(8,128)(2,1)} collective-permute-done((bf16[1280,256]{0,1:T(8,128)(2,1)S(1)}, bf16[1280,256]{0,1:T(8,128)(2,1)}, u32[]{:S(2)}, u32[]{:S(2)}) %collective-permute-start.7) | collective-permute-done | bytes 655392 | tf_op jit(solution)/shard_map/ppermute | solution.py:17
  483.6 1.6 maximum_select_fusion.2
  485.3 4.5 collective-permute-start.8
  490.0 1.2 fusion.11
  491.3 0.7 copy.28
  492.0 9.3 %all-to-all-start.2 = ((bf16[20,64,1]{0,2,1:T(2,128)(2,1)}), bf16[20,64,1]{0,2,1:T(2,128)(2,1)S(1)}, u32[]{:S(2)}, u32[]{:S(2)}) async-start(bf16[20,64,1]{0,2,1:T(2,128)(2,1)} %copy.28), calls=%async_computation.2 | async-start | bytes 65536 | tf_op jit(solution)/shard_map/all_to_all | solution.py:88
  501.3 106.7 %all-to-all-done.2 = bf16[20,64,1]{0,2,1:T(2,128)(2,1)S(1)} async-done(((bf16[20,64,1]{0,2,1:T(2,128)(2,1)}), bf16[20,64,1]{0,2,1:T(2,128)(2,1)S(1)}, u32[]{:S(2)}, u32[]{:S(2)}) %all-to-all-start.2) | async-done | bytes 2592 | tf_op jit(solution)/shard_map/all_to_all | solution.py:88
  608.3 4.7 fusion
  613.0 2.2 all_to_all.42
  615.2 78.7 %all_to_all.49 = bf16[64,20,512]{2,1,0:T(8,128)(2,1)S(1)} all-to-all(bf16[64,20,512]{2,1,0:T(8,128)(2,1)S(1)} %all_to_all.42), channel_id=1, replica_groups=mesh['dp'=8,'expert'=64] {'expert'}, dimensions={0} | all-to-all | bytes 2621440 | tf_op jit(solution)/shard_map/all_to_all | solution.py:118
  693.9 1.5 copy.29
  695.4 2.4 reshape.140
  697.8 1.1 convolution_convert_fusion.1
  (42 shorter events, 1.9 us)
Async XLA Ops:
  0.0 131.2 %copy-start = (bf16[512,1024]{1,0:T(8,128)(2,1)S(1)}, bf16[512,1024]{1,0:T(8,128)(2,1)}, u32[]{:S(2)}) copy-start(bf16[512,1024]{1,0:T(8,128)(2,1)} %param.12) | copy-start | bytes 3145732
  5.9 23.1 %copy-start.6 = (bf16[64,4096]{1,0:T(8,128)(2,1)S(1)}, bf16[64,4096]{1,0:T(8,128)(2,1)}, u32[]{:S(2)}) copy-start(bf16[64,4096]{1,0:T(8,128)(2,1)} %param.7) | copy-start | bytes 1572868
  9.5 32.6 %all-to-all-start.1 = ((bf16[20,64,4]{0,2,1:T(4,128)(2,1)}), bf16[20,64,4]{0,2,1:T(4,128)(2,1)S(1)}, u32[]{:S(2)}, u32[]{:S(2)}) async-start(bf16[20,64,4]{0,2,1:T(4,128)(2,1)} %copy.24), calls=%async_computation.1 | async-start | bytes 131072 | tf_op jit(solution)/shard_map/all_to_all | solution.py:85
  42.1 79.3 %all-to-all-start = ((bf16[20,64,512]{2,0,1:T(8,128)(2,1)}), bf16[20,64,512]{2,0,1:T(8,128)(2,1)S(1)}, u32[]{:S(2)}, u32[]{:S(2)}) async-start(bf16[20,64,512]{2,0,1:T(8,128)(2,1)} %copy.22), calls=%async_computation | async-start | bytes 3145728 | tf_op jit(solution)/shard_map/all_to_all | solution.py:84
  127.6 2.9 copy-start.1
  132.9 2.7 copy-start.5
  132.9 8.3 %copy-start.8 = (bf16[512,1024]{1,0:T(8,128)(2,1)S(1)}, bf16[512,1024]{1,0:T(8,128)(2,1)}, u32[]{:S(2)}) copy-start(bf16[512,1024]{1,0:T(8,128)(2,1)} %param.11) | copy-start | bytes 3145732
  135.6 201.9 %collective-permute-start.3 = (bf16[1280,512]{0,1:T(8,128)(2,1)}, bf16[1280,512]{0,1:T(8,128)(2,1)}, u32[]{:S(2)}, u32[]{:S(2)}) collective-permute-start(bf16[1280,512]{0,1:T(8,128)(2,1)} %dynamic-slice_convert_fusion), channel_id=1, source_target_pairs={{0,4},{4,0},{1,5},{5,1},{2,6},{6,2},{3,7},{7,3},{8,12},{12,8},{9,1... | collective-permute-start | bytes 3932168 | tf_op jit(solution)/shard_map/ppermute | solution.py:17
  142.9 2.3 copy-start.3
  145.4 220.3 %collective-permute-start = (bf16[1280,512]{0,1:T(8,128)(2,1)S(1)}, bf16[1280,512]{0,1:T(8,128)(2,1)}, u32[]{:S(2)}, u32[]{:S(2)}) collective-permute-start(bf16[1280,512]{0,1:T(8,128)(2,1)S(1)} %dynamic-slice_convert_fusion.1), channel_id=1, source_target_pairs={{0,4},{4,0},{1,5},{5,1},{2,6},{6,2},{3,7},{7,3},{8,12},{12,8},{9,1... | collective-permute-start | bytes 3932168 | tf_op jit(solution)/shard_map/ppermute | solution.py:17
  337.5 28.2 %copy-start.4 = (f32[1280,1024]{0,1:T(8,128)S(1)}, f32[1280,1024]{0,1:T(8,128)}, u32[]{:S(2)}) copy-start(f32[1280,1024]{0,1:T(8,128)} %copy-done.3) | copy-start | bytes 15728644
  340.1 70.9 %collective-permute-start.4 = (bf16[1280,256]{0,1:T(8,128)(2,1)S(1)}, bf16[1280,256]{0,1:T(8,128)(2,1)S(1)}, u32[]{:S(2)}, u32[]{:S(2)}) collective-permute-start(bf16[1280,256]{0,1:T(8,128)(2,1)S(1)} %dynamic-slice_convert_fusion.2), channel_id=1, source_target_pairs={{0,2},{2,0},{1,3},{3,1},{4,6},{6,4},{5,7},{7,5},{8,10},{10,8},{9,1... | collective-permute-start | bytes 1966088 | tf_op jit(solution)/shard_map/ppermute | solution.py:17
  367.4 57.7 %collective-permute-start.1 = (bf16[1280,256]{0,1:T(8,128)(2,1)S(1)}, bf16[1280,256]{0,1:T(8,128)(2,1)S(1)}, u32[]{:S(2)}, u32[]{:S(2)}) collective-permute-start(bf16[1280,256]{0,1:T(8,128)(2,1)S(1)} %dynamic-slice_convert_fusion.3), channel_id=1, source_target_pairs={{0,2},{2,0},{1,3},{3,1},{4,6},{6,4},{5,7},{7,5},{8,10},{10,8},{9,1... | collective-permute-start | bytes 1966088 | tf_op jit(solution)/shard_map/ppermute | solution.py:17
  411.2 20.9 %collective-permute-start.5 = (bf16[1280,128]{0,1:T(8,128)(2,1)S(1)}, bf16[1280,128]{0,1:T(8,128)(2,1)S(1)}, u32[]{:S(2)}, u32[]{:S(2)}) collective-permute-start(bf16[1280,128]{0,1:T(8,128)(2,1)S(1)} %dynamic-slice_convert_fusion.4), channel_id=1, source_target_pairs={{0,1},{1,0},{2,3},{3,2},{4,5},{5,4},{6,7},{7,6},{8,9},{9,8},{10,11... | collective-permute-start | bytes 983048 | tf_op jit(solution)/shard_map/ppermute | solution.py:17
  425.2 1.1 copy-start.2
  427.1 11.5 %collective-permute-start.2 = (bf16[1280,128]{0,1:T(8,128)(2,1)}, bf16[1280,128]{0,1:T(8,128)(2,1)}, u32[]{:S(2)}, u32[]{:S(2)}) collective-permute-start(bf16[1280,128]{0,1:T(8,128)(2,1)} %dynamic-slice_convert_fusion.5), channel_id=1, source_target_pairs={{0,1},{1,0},{2,3},{3,2},{4,5},{5,4},{6,7},{7,6},{8,9},{9,8},{10,11... | collective-permute-start | bytes 983048 | tf_op jit(solution)/shard_map/ppermute | solution.py:17
  440.0 9.9 %collective-permute-start.6 = (bf16[1280,128]{0,1:T(8,128)(2,1)S(1)}, bf16[1280,128]{0,1:T(8,128)(2,1)S(1)}, u32[]{:S(2)}, u32[]{:S(2)}) collective-permute-start(bf16[1280,128]{0,1:T(8,128)(2,1)S(1)} %multiply_convert_fusion), channel_id=1, source_target_pairs={{0,1},{1,0},{2,3},{3,2},{4,5},{5,4},{6,7},{7,6},{8,9},{9,8},{10,11... | collective-permute-start | bytes 983048 | tf_op jit(solution)/shard_map/ppermute | solution.py:17
  450.0 39.7 %copy-start.7 = (s32[64,2]{0,1:T(2,128)S(1)}, s32[64,2]{0,1:T(2,128)}, u32[]{:S(2)}) copy-start(s32[64,2]{0,1:T(2,128)} %param.9) | copy-start | bytes 1540
  450.1 33.6 %collective-permute-start.7 = (bf16[1280,256]{0,1:T(8,128)(2,1)S(1)}, bf16[1280,256]{0,1:T(8,128)(2,1)}, u32[]{:S(2)}, u32[]{:S(2)}) collective-permute-start(bf16[1280,256]{0,1:T(8,128)(2,1)S(1)} %maximum_select_fusion.3), channel_id=1, source_target_pairs={{0,2},{2,0},{1,3},{3,1},{4,6},{6,4},{5,7},{7,5},{8,10},{10,8},{9,1... | collective-permute-start | bytes 1966088 | tf_op jit(solution)/shard_map/ppermute | solution.py:17
  485.3 123.0 %collective-permute-start.8 = (bf16[1280,512]{0,1:T(8,128)(2,1)S(1)}, bf16[1280,512]{0,1:T(8,128)(2,1)}, u32[]{:S(2)}, u32[]{:S(2)}) collective-permute-start(bf16[1280,512]{0,1:T(8,128)(2,1)S(1)} %maximum_select_fusion.2), channel_id=1, source_target_pairs={{0,4},{4,0},{1,5},{5,1},{2,6},{6,2},{3,7},{7,3},{8,12},{12,8},{9,1... | collective-permute-start | bytes 3932168 | tf_op jit(solution)/shard_map/ppermute | solution.py:17
  492.0 116.1 %all-to-all-start.2 = ((bf16[20,64,1]{0,2,1:T(2,128)(2,1)}), bf16[20,64,1]{0,2,1:T(2,128)(2,1)S(1)}, u32[]{:S(2)}, u32[]{:S(2)}) async-start(bf16[20,64,1]{0,2,1:T(2,128)(2,1)} %copy.28), calls=%async_computation.2 | async-start | bytes 65536 | tf_op jit(solution)/shard_map/all_to_all | solution.py:88
where the time goes:
time: 705 us; the launch traced here: 699 us
  waiting for transfers between devices  497 us (70%)
  blocking collectives  78.7 us (11%)
  starting transfers between devices  62.7 us (9%)
  local copies, waits for them, and re-layouts  31.4 us (4%)
  other arithmetic  13.8 us (2%)
  matrix products  13.7 us (2%)
    ppermute x9, waiting for transfers between devices, partner(): return lax.ppermute(block, axis, route)  315 us
    all_to_all x1, waiting for transfers between devices, local(): lax.all_to_all(send_share.astype(jnp.bfloat16), 'expert', split_axis=1, c...  107 us
    all_to_all x1, blocking collectives, local(): lax.all_to_all(weighted, 'expert', split_axis=0, concat_axis=1, tiled=True)  78.7 us
    all_to_all x1, waiting for transfers between devices, local(): lax.all_to_all(send_coded, 'expert', split_axis=1, concat_axis=0, tiled=T...  69.9 us
    ppermute x9, starting transfers between devices, partner(): return lax.ppermute(block, axis, route)  25.3 us
    all_to_all x1, starting transfers between devices, local(): lax.all_to_all(send_scale.astype(jnp.bfloat16), 'expert', split_axis=1, c...  19.1 us
  transfers between devices with their start and end apart: 12, of which 11 were waited for; matrix products, arithmetic and copies ran while one was open for 2% of the time, Pallas kernels for 0%

commit v1 on v0

v1 whole, which is shorter than its diff:
```python
import functools

import jax
import jax.numpy as jnp
from jax import lax
from jax.experimental import pallas as pl
from jax.experimental.pallas import tpu as pltpu
from jax.sharding import Mesh
from jax.sharding import PartitionSpec as P

Y, C, X, Z = 4, 2, 4, 16
D, F, TOK = 4096, 1024, 64
SHARD = 512
MEMBERS = 8
CAP = 20
SLOTS = 2 * CAP
MAIN = 16
REST = SLOTS - 2 * MAIN
SRC = Y * X
ROWS = SRC * SLOTS
ALL_SLOTS = X * SLOTS
FQ = F // Y
HALF = SHARD // 2
VMEM = 100 * 1024 * 1024 // 2


def slot_layout(place):
    column = (place * 1639) >> 16
    at = place - column * SLOTS
    second = ((at >= MAIN) & (at < 2 * MAIN)) | (at >= 2 * MAIN + REST // 2)
    slot = jnp.where(at < MAIN, at, jnp.where(at < 2 * MAIN + REST // 2, at - MAIN, at - MAIN - REST // 2))
    return 2 * column + second.astype(jnp.int32), slot


def encode_kernel(core_ref, count_ref, routes_ref, tokens_ref, out_ref):
    core = core_ref[0]
    place = lax.broadcasted_iota(jnp.int32, (ALL_SLOTS, TOK), 0)
    row = lax.broadcasted_iota(jnp.int32, (ALL_SLOTS, TOK), 1)
    expert, slot = slot_layout(place)
    named = (routes_ref[0:1, :] == expert) | (routes_ref[1:2, :] == expert)
    named = named & (row < count_ref[0])
    earlier = lax.broadcasted_iota(jnp.int32, (TOK, TOK), 0) < lax.broadcasted_iota(jnp.int32, (TOK, TOK), 1)
    rank = jnp.dot(
        named.astype(jnp.float32).astype(jnp.bfloat16),
        earlier.astype(jnp.float32).astype(jnp.bfloat16),
        preferred_element_type=jnp.float32,
    )
    chosen = named & (rank.astype(jnp.int32) == slot)
    chosen = chosen.astype(jnp.float32).astype(jnp.bfloat16)

    def step(i, carry):
        half = i // MEMBERS
        member = i - half * MEMBERS
        side = jnp.where(half == 0, core, 1 - core)
        start = pl.multiple_of(member * SHARD + side * HALF, HALF)
        parts = []
        values = tokens_ref[:, pl.ds(start, HALF)].astype(jnp.float32)
        for block in range(HALF // 128):
            v = values[:, block * 128 : (block + 1) * 128]
            size = jnp.abs(v)
            scale = (jnp.max(size, axis=1, keepdims=True) + 1e-06) / 448.0
            scaled = v / scale
            x = jnp.abs(scaled)
            spacing = jnp.full_like(x, 2.0**-9)
            for shift, least in ((8, 2.0**2), (4, 2.0**-2), (2, 2.0**-4), (1, 2.0**-5)):
                big = x >= least
                x = jnp.where(big, x * 2.0**-shift, x)
                spacing = jnp.where(big, spacing * 2.0**shift, spacing)
            snapped = jnp.floor(x * 512.0 + 0.5) * spacing
            coded = jnp.where(scaled < 0.0, -snapped, snapped)
            parts.append((coded * scale).astype(jnp.bfloat16))
        restored = jnp.concatenate(parts, axis=1)
        rows = jnp.dot(chosen, restored, preferred_element_type=jnp.float32)
        out_ref[:, pl.ds(pl.multiple_of(i * HALF, HALF), HALF)] = rows.astype(jnp.bfloat16)
        return carry

    lax.fori_loop(0, 2 * MEMBERS, step, 0)


def shares_kernel(count_ref, routes_ref, numerators_ref, out_ref):
    place = lax.broadcasted_iota(jnp.int32, (TOK, ALL_SLOTS), 1)
    row = lax.broadcasted_iota(jnp.int32, (TOK, ALL_SLOTS), 0)
    expert, slot = slot_layout(place)
    live = row < count_ref[0]
    first = (routes_ref[:, 0:1] == expert) & live
    second = (routes_ref[:, 1:2] == expert) & live
    earlier = lax.broadcasted_iota(jnp.int32, (TOK, TOK), 1) < lax.broadcasted_iota(jnp.int32, (TOK, TOK), 0)
    rank = jnp.dot(
        earlier.astype(jnp.float32).astype(jnp.bfloat16),
        (first | second).astype(jnp.float32).astype(jnp.bfloat16),
        preferred_element_type=jnp.float32,
    )
    here = rank.astype(jnp.int32) == slot
    share = numerators_ref[...].astype(jnp.float32) / 256.0
    out = jnp.where(first & here, share[:, 0:1], 0.0) + jnp.where(second & here, share[:, 1:2], 0.0)
    out_ref[...] = out.astype(jnp.bfloat16)


def split_rows(block):
    wide = block.astype(jnp.float32)
    n = wide.shape[-1]
    mixed = wide[:, 2 * MAIN :].reshape(SRC * REST, n)
    return [
        jnp.concatenate([wide[:, e * MAIN : (e + 1) * MAIN].reshape(SRC * MAIN, n), mixed], axis=0).astype(jnp.bfloat16)
        for e in range(2)
    ]


def join_rows(first, second):
    n = first.shape[-1]
    main = SRC * MAIN
    place = lax.broadcasted_iota(jnp.int32, (SRC * REST, n), 0)
    mixed = jnp.where((place & (REST - 1)) < REST // 2, first[main:], second[main:])
    return jnp.concatenate(
        [first[:main].reshape(SRC, MAIN, n), second[:main].reshape(SRC, MAIN, n), mixed.reshape(SRC, REST, n)], axis=1
    )


def hidden_kernel(rows_ref, own_ref, other_ref, out_ref, first_sum, second_sum):
    step = pl.program_id(0)

    @pl.when(step == 0)
    def _():
        first_sum[...] = jnp.zeros_like(first_sum)
        second_sum[...] = jnp.zeros_like(second_sum)

    first, second = split_rows(rows_ref[...])

    def add(weights_ref):
        first_sum[...] += jnp.dot(first, weights_ref[0, 0], preferred_element_type=jnp.float32)
        second_sum[...] += jnp.dot(second, weights_ref[1, 0], preferred_element_type=jnp.float32)

    @pl.when(step < MEMBERS)
    def _():
        add(own_ref)

    @pl.when(step >= MEMBERS)
    def _():
        add(other_ref)

    @pl.when(step == 2 * MEMBERS - 1)
    def _():
        def hidden(total):
            gate = total[:, :FQ]
            return gate / (1.0 + jnp.exp(-gate)) * total[:, FQ:]

        out_ref[...] = join_rows(hidden(first_sum[...]), hidden(second_sum[...])).astype(jnp.bfloat16)


def down_kernel(core_ref, hidden_ref, own_ref, other_ref, out_ref, first_rows, second_rows):
    @pl.when(pl.program_id(0) == 0)
    def _():
        core = core_ref[0]
        for half in range(2):
            side = core if half == 0 else 1 - core
            for quarter in range(Y):
                first, second = split_rows(hidden_ref[quarter, :, :, pl.ds(pl.multiple_of(side * 128, 128), 128)])
                at = (half * Y + quarter) * 128
                first_rows[:, at : at + 128] = first
                second_rows[:, at : at + 128] = second

    def result(expert, rows):
        weights = jnp.concatenate(
            [
                jnp.concatenate([ref[expert, 0], ref[expert, 1]], axis=1)
                for ref in (own_ref, other_ref)
            ],
            axis=0,
        )
        return jnp.dot(rows[...], weights, preferred_element_type=jnp.float32)

    out_ref[...] = join_rows(result(0, first_rows), result(1, second_rows)).astype(jnp.bfloat16)


def mix_kernel(shares_ref, rows_ref, out_ref):
    for quarter in range(Y):
        rows = rows_ref[quarter * X : (quarter + 1) * X].reshape(ALL_SLOTS, MEMBERS * 128)
        mixed = jnp.dot(shares_ref[...], rows, preferred_element_type=jnp.float32).astype(jnp.bfloat16)
        for member in range(MEMBERS):
            at = member * SHARD + quarter * 128
            out_ref[:, at : at + 128] = mixed[:, member * 128 : (member + 1) * 128]


SCALAR = pl.BlockSpec(memory_space=pltpu.SMEM)
WHOLE = pl.BlockSpec(memory_space=pltpu.VMEM)


def shape(dims):
    return jax.ShapeDtypeStruct(dims, jnp.bfloat16)


def params(**extra):
    return pltpu.CompilerParams(vmem_limit_bytes=VMEM, **extra)


def encode(core, counts, routes, tokens):
    return pl.pallas_call(
        encode_kernel,
        out_shape=shape((ALL_SLOTS, D)),
        in_specs=[SCALAR, SCALAR, WHOLE, WHOLE],
        out_specs=WHOLE,
        compiler_params=params(),
        cost_estimate=pl.CostEstimate(flops=2 * ALL_SLOTS * TOK * D, bytes_accessed=2 * (TOK + ALL_SLOTS) * D, transcendentals=0),
    )(core, counts, routes.T, tokens)


def share_table(counts, routes, numerators):
    return pl.pallas_call(
        shares_kernel,
        out_shape=shape((TOK, ALL_SLOTS)),
        in_specs=[SCALAR, WHOLE, WHOLE],
        out_specs=WHOLE,
    )(counts, routes, numerators)


def hidden_rows(rows, own, other):
    last = MEMBERS - 1
    return pl.pallas_call(
        hidden_kernel,
        grid=(2 * MEMBERS,),
        out_shape=shape((SRC, SLOTS, FQ)),
        in_specs=[
            pl.BlockSpec((SRC, SLOTS, HALF), lambda k: (0, 0, k)),
            pl.BlockSpec((2, 1, HALF, 2 * FQ), lambda k: (0, jnp.minimum(k, last), 0, 0)),
            pl.BlockSpec((2, 1, HALF, 2 * FQ), lambda k: (0, jnp.maximum(k - MEMBERS, 0), 0, 0)),
        ],
        out_specs=pl.BlockSpec((SRC, SLOTS, FQ), lambda k: (0, 0, 0)),
        scratch_shapes=[pltpu.VMEM((SRC * (MAIN + REST), 2 * FQ), jnp.float32)] * 2,
        compiler_params=params(),
        cost_estimate=pl.CostEstimate(flops=2 * ROWS * D * 2 * FQ, bytes_accessed=2 * ROWS * D + 8 * D * FQ, transcendentals=0),
    )(rows, own, other)


def down_rows(core, hidden, own, other):
    weights = pl.BlockSpec((2, 2, F // 2, 128), lambda n: (0, n, 0, 0))
    return pl.pallas_call(
        down_kernel,
        grid=(MEMBERS // 2,),
        out_shape=shape((SRC, SLOTS, MEMBERS * 128)),
        in_specs=[
            SCALAR,
            pl.BlockSpec((Y, SRC, SLOTS, FQ), lambda n: (0, 0, 0, 0)),
            weights,
            weights,
        ],
        out_specs=pl.BlockSpec((SRC, SLOTS, 256), lambda n: (0, 0, n)),
        scratch_shapes=[pltpu.VMEM((SRC * (MAIN + REST), F), jnp.bfloat16)] * 2,
        compiler_params=params(),
        cost_estimate=pl.CostEstimate(flops=2 * ROWS * F * F, bytes_accessed=2 * ROWS * F * 2 + 4 * F * F, transcendentals=0),
    )(core, hidden, own, other)


def mix(shares, rows):
    return pl.pallas_call(
        mix_kernel,
        out_shape=shape((TOK, D)),
        in_specs=[WHOLE, WHOLE],
        out_specs=WHOLE,
        compiler_params=params(),
    )(shares, rows)


def swap_cores(block):
    return lax.ppermute(block, "c", [(0, 1), (1, 0)])


def local(tokens, routes, numerators, counts, w_gate, w_up, w_down):
    y, c = lax.axis_index("y"), lax.axis_index("c")
    core = c.astype(jnp.int32).reshape(1)
    gate = lax.dynamic_slice(w_gate, (c * HALF, y * FQ), (HALF, FQ))
    up = lax.dynamic_slice(w_up, (c * HALF, y * FQ), (HALF, FQ))
    down = lax.dynamic_slice(w_down.reshape(Y, 2, 128, SHARD), (0, c, 0, y * 128), (Y, 1, 128, 128))
    own_in = lax.all_gather(jnp.concatenate([gate, up], axis=1), "z").reshape(2, MEMBERS, HALF, 2 * FQ)
    other_in = swap_cores(own_in)
    own_out = lax.all_gather(down.reshape(F // 2, 128), "z").reshape(2, MEMBERS, F // 2, 128)
    other_out = swap_cores(own_out)
    shares = share_table(counts, routes, numerators)
    rows = encode(core, counts, routes, tokens).reshape(X, SLOTS, D)
    rows = lax.all_to_all(rows, "x", 0, 0, tiled=True)
    rows = lax.all_gather(rows, "y").reshape(SRC, SLOTS, D)
    hidden = hidden_rows(rows, own_in, other_in)
    hidden = lax.all_gather(hidden, "y")
    result = down_rows(core, hidden, own_out, other_out)
    result = lax.all_to_all(result, ("y", "x"), 0, 0, tiled=True)
    return mix(shares, result)


def solution(mesh):
    grid = Mesh(mesh.devices.reshape(Y, C, X, Z), ("y", "c", "x", "z"))
    tokens = ("y", "c", "x", "z")
    group = ("x", "z")
    placed = (
        P(tokens, None),
        P(tokens, None),
        P(tokens, None),
        P(tokens),
        P(group, None),
        P(group, None),
        P(None, group),
    )
    return jax.shard_map(local, mesh=grid, in_specs=placed, out_specs=P(tokens, None), check_vma=False)
```

time: 705 us -> 318 us (0.45)
  waiting for transfers between devices: 497 us -> 219 us
  blocking collectives: 78.7 us -> 17.4 us
  starting transfers between devices: 62.7 us -> 29.2 us
  Pallas kernels: 0 us -> 27.1 us
  local copies, waits for them, and re-layouts: 31.4 us -> 7.89 us
  matrix products: 13.7 us -> 0 us
  other arithmetic: 13.8 us -> 0.72 us
  between operations: 1.22 us -> 13.9 us
    ppermute x9 -> x2, waiting for transfers between devices: 315 us -> 0.01 us  [swap_cores(): return lax.ppermute(block, 'c', [(0, 1), (1, 0)])]
    all_gather x0 -> x4, waiting for transfers between devices: none -> 204 us  [the longest x1 61.2 us: local(): rows = lax.all_gather(rows, 'y').reshape(SRC, SLOTS, D)]
    all_to_all x3 -> x1, waiting for transfers between devices: 182 us -> 14.8 us  [local(): result = lax.all_to_all(result, ('y', 'x'), 0, 0, tiled=True)]
    all_to_all x1, blocking collectives: 78.7 us -> 17.4 us  [local(): rows = lax.all_to_all(rows, 'x', 0, 0, tiled=True)]
    all_to_all x3 -> x1, starting transfers between devices: 37.4 us -> 6.22 us  [local(): result = lax.all_to_all(result, ('y', 'x'), 0, 0, tiled=True)]
    pallas_call x0 -> x5, Pallas kernels: none -> 27.1 us  [the longest x1 14.5 us: hidden_rows(): pl.pallas_call(hidden_kernel, grid=(2 * MEMBERS,), out_shape=shape((SRC,...]
    dot_general x7 -> x0, matrix products: 13.7 us -> none  [the longest x1 4.72 us: local(): result = jnp.dot(hidden, w_down, preferred_element_type=jnp.float32)]
    convert_element_type x19 -> x0, local copies, waits for them, and re-layouts: 10.3 us -> none  [the longest x1 4.11 us: local(): got_rows.astype(jnp.float32).reshape(recv_count, member_blocks, BLOCK)]
  transfers between devices with their start and end apart: 12 -> 7, of which waited for: 11 -> 5; matrix products, arithmetic and copies ran while one was open for 2% -> 1% of each run, Pallas kernels for 0% -> 7%
where the time goes in v1:
time: 318 us; the launch traced here: 315 us
  waiting for transfers between devices  219 us (69%)
  starting transfers between devices  29.2 us (9%)
  Pallas kernels  27.1 us (9%)
  blocking collectives  17.4 us (5%)
  between operations  13.9 us (4%)
  local copies, waits for them, and re-layouts  7.89 us (2%)
    all_gather x1, waiting for transfers between devices, local(): rows = lax.all_gather(rows, 'y').reshape(SRC, SLOTS, D)  61.2 us
    all_gather x1, waiting for transfers between devices, local(): lax.all_gather(down.reshape(F // 2, 128), 'z')  60.1 us
    all_gather x1, waiting for transfers between devices, local(): lax.all_gather(jnp.concatenate([gate, up], axis=1), 'z')  50.9 us
    all_gather x1, waiting for transfers between devices, local(): hidden = lax.all_gather(hidden, 'y')  32.1 us
    ppermute x2, starting transfers between devices, swap_cores(): return lax.ppermute(block, 'c', [(0, 1), (1, 0)])  22.9 us
    all_to_all x1, blocking collectives, local(): rows = lax.all_to_all(rows, 'x', 0, 0, tiled=True)  17.4 us
    all_to_all x1, waiting for transfers between devices, local(): result = lax.all_to_all(result, ('y', 'x'), 0, 0, tiled=True)  14.8 us
    pallas_call x1, Pallas kernels, hidden_rows(): pl.pallas_call(hidden_kernel, grid=(2 * MEMBERS,), out_shape=shape((SRC,...  14.5 us
  transfers between devices with their start and end apart: 7, of which 5 were waited for; matrix products, arithmetic and copies ran while one was open for 1% of the time, Pallas kernels for 7%

profile of v1, /device:TPU:1, one launch (start us, length us, event | category | flops | bytes accessed | tf_op | source)
XLA Modules:
  0.0 315.4 jit_solution(6013460108828771218)
XLA Ops:
  6.5 0.0 copy-start
  6.5 0.0 copy-start.3
  6.5 0.0 all-gather.12.cloned.1.call-start
  6.5 1.0 dynamic_slice.10
  7.6 0.9 dynamic_slice.9
  8.5 0.7 pad_maximum_fusion
  9.2 0.0 all-gather.12.cloned.1.call-update
  9.2 0.0 all-gather.8.cloned.1.call-start
  9.3 0.0 copy-done
  9.3 0.7 constant_dynamic-slice_fusion
  10.0 0.0 all-gather.8.cloned.1.call-update
  10.0 0.0 all-gather.10.cloned.1.call-start
  10.7 0.0 copy-done.3
  10.7 0.0 copy-start.5
  10.7 0.7 copy-done.5
  11.4 5.0 %shard_map.74 = bf16[160,4096]{1,0:T(8,128)(2,1)S(1)} custom-call(s32[1]{0:T(128)} %bitcast.core_ref, s32[1]{0:T(128)S(6)} %copy.14.count_ref, s32[2,64]{1,0:T(2,128)S(1)} %bitcast.13, bf16[64,4096]{1,0:T(8,128)(2,1)S(1)} %copy-done.3), custom_call_target="tpu_custom_call" | custom-call | flops 83886080 | bytes 1835008 | tf_op jit(solution)/shard_map/pallas_call | solution.py:197
  16.4 17.4 %all_to_all.10 = bf16[4,40,4096]{2,1,0:T(8,128)(2,1)} all-to-all(bf16[4,40,4096]{2,1,0:T(8,128)(2,1)S(1)} %bitcast.11), channel_id=1, replica_groups=mesh['y'=4,'c'=2,'x'=4,'z'=16] {'x'}, dimensions={0} | all-to-all | bytes 2621440 | tf_op jit(solution)/shard_map/all_to_all | solution.py:279
  33.8 0.0 all-gather.10.cloned.1.call-update
  33.8 0.0 all-gather.14.cloned.1.call-start
  33.9 50.9 %all-gather.12.cloned.1.call-done = bf16[4096,512]{1,0:T(8,128)(2,1)} async-done(((bf16[256,512]{1,0:T(8,128)(2,1)}), bf16[4096,512]{1,0:T(8,128)(2,1)}) %all-gather.12.cloned.1.call-update) | async-done | bytes 4194320 | tf_op jit(solution)/shard_map/all_gather | solution.py:273
  84.8 11.2 %collective-permute-start = (bf16[2,8,256,512]{3,2,1,0:T(8,128)(2,1)}, bf16[2,8,256,512]{3,2,1,0:T(8,128)(2,1)}, u32[]{:S(2)}, u32[]{:S(2)}) collective-permute-start(bf16[2,8,256,512]{3,2,1,0:T(8,128)(2,1)} %bitcast.14), channel_id=1, source_target_pairs={{0,64},{64,0},{1,65},{65,1},{2,66},{66,2},{3,67},{67,3},{4,68},{68... | collective-permute-start | bytes 12582920 | tf_op jit(solution)/shard_map/ppermute | solution.py:264
  96.1 60.1 %all-gather.8.cloned.1.call-done = bf16[16,512,128]{2,1,0:T(8,128)(2,1)} async-done(((bf16[1,512,128]{2,1,0:T(8,128)(2,1)}), bf16[16,512,128]{2,1,0:T(8,128)(2,1)}) %all-gather.8.cloned.1.call-update) | async-done | bytes 2097168 | tf_op jit(solution)/shard_map/all_gather | solution.py:275
  156.2 11.6 %collective-permute-start.1 = (bf16[2,8,512,128]{3,2,1,0:T(8,128)(2,1)}, bf16[2,8,512,128]{3,2,1,0:T(8,128)(2,1)S(1)}, u32[]{:S(2)}, u32[]{:S(2)}) collective-permute-start(bf16[2,8,512,128]{3,2,1,0:T(8,128)(2,1)} %bitcast.16), channel_id=1, source_target_pairs={{0,64},{64,0},{1,65},{65,1},{2,66},{66,2},{3,67},{67,3},{4,68},{68... | collective-permute-start | bytes 6291464 | tf_op jit(solution)/shard_map/ppermute | solution.py:264
  167.8 61.2 %all-gather.10.cloned.1.call-done.rows_ref = bf16[16,40,4096]{2,1,0:T(8,128)(2,1)} async-done(((bf16[4,40,4096]{2,1,0:T(8,128)(2,1)}), bf16[16,40,4096]{2,1,0:T(8,128)(2,1)}) %all-gather.10.cloned.1.call-update) | async-done | bytes 5242896 | tf_op jit(solution)/shard_map/all_gather | solution.py:280
  229.0 0.0 collective-permute-done.other_ref
  229.0 14.5 %shard_map.75 = bf16[16,40,256]{2,1,0:T(8,128)(2,1)} custom-call(bf16[16,40,4096]{2,1,0:T(8,128)(2,1)} %all-gather.10.cloned.1.call-done.rows_ref, bf16[2,8,256,512]{3,2,1,0:T(8,128)(2,1)} %bitcast.15, bf16[2,8,256,512]{3,2,1,0:T(8,128)(2,1)} %collective-permute-done.other_ref), custom_call_target="tpu_custom_call" | custom-call | flops 2684354560 | bytes 13631488 | tf_op jit(solution)/shard_map/pallas_call | solution.py:218
  243.6 0.0 all-gather.14.cloned.1.call-update
  243.6 0.0 collective-permute-done.1.other_ref
  243.6 0.0 copy-start.7
  243.6 32.1 %all-gather.14.cloned.1.call-done = bf16[64,40,256]{2,1,0:T(8,128)(2,1)} async-done(((bf16[16,40,256]{2,1,0:T(8,128)(2,1)}), bf16[64,40,256]{2,1,0:T(8,128)(2,1)}) %all-gather.14.cloned.1.call-update) | async-done | bytes 1310736 | tf_op jit(solution)/shard_map/all_gather | solution.py:282
  275.8 0.0 copy-done.7
  275.8 0.0 copy-start.2
  275.8 1.3 copy-done.2
  277.1 4.7 %shard_map.76 = bf16[16,40,1024]{2,1,0:T(8,128)(2,1)S(1)} custom-call(s32[1]{0:T(128)} %bitcast.core_ref, bf16[4,16,40,256]{3,2,1,0:T(8,128)(2,1)S(1)} %bitcast.12, bf16[2,8,512,128]{3,2,1,0:T(8,128)(2,1)} %bitcast.17, bf16[2,8,512,128]{3,2,1,0:T(8,128)(2,1)} %copy-done.7), custom_call_target="tpu_custom_call" | custom-call | flops 1342177280 | bytes 6815744 | tf_op jit(solution)/shard_map/pallas_call | solution.py:236
  281.8 0.0 copy-start.1
  281.9 1.1 copy-done.1
  282.9 0.0 copy-start.6
  282.9 0.0 copy-start.8
  282.9 6.2 %all-to-all-start.1 = ((bf16[16,40,1024]{2,1,0:T(8,128)(2,1)}), bf16[16,40,1024]{2,1,0:T(8,128)(2,1)S(1)}, u32[]{:S(2)}, u32[]{:S(2)}) async-start(bf16[16,40,1024]{2,1,0:T(8,128)(2,1)} %copy-done.1), calls=%async_computation.1 | async-start | bytes 2621440 | tf_op jit(solution)/shard_map/all_to_all | solution.py:284
  289.1 0.0 copy-done.6
  289.1 0.7 copy.10.routes_ref
  289.9 0.0 copy-done.8
  289.9 0.7 copy.11.numerators_ref
  290.6 1.6 shard_map.73.shares_ref
  292.2 14.8 %all-to-all-done.1.rows_ref = bf16[16,40,1024]{2,1,0:T(8,128)(2,1)S(1)} async-done(((bf16[16,40,1024]{2,1,0:T(8,128)(2,1)}), bf16[16,40,1024]{2,1,0:T(8,128)(2,1)S(1)}, u32[]{:S(2)}, u32[]{:S(2)}) %all-to-all-start.1) | async-done | bytes 1310752 | tf_op jit(solution)/shard_map/all_to_all | solution.py:284
  307.0 0.0 copy-start.4
  307.0 0.8 copy-done.4
  307.8 1.1 shard_map.77
Async XLA Ops:
  6.5 2.8 copy-start
  6.5 4.2 %copy-start.3 = (bf16[64,4096]{1,0:T(8,128)(2,1)S(1)}, bf16[64,4096]{1,0:T(8,128)(2,1)}, u32[]{:S(2)}) copy-start(bf16[64,4096]{1,0:T(8,128)(2,1)} %tokens_ref.1) | copy-start | bytes 1572868
  6.5 78.3 %all-gather.12.cloned.1.call-start = ((), (), s32[]{:S(2)}) async-start(), calls=%async_computation.4 | async-start | bytes 4456448 | tf_op jit(solution)/shard_map/all_gather | solution.py:273
  9.2 147.0 %all-gather.8.cloned.1.call-start = ((), (), s32[]{:S(2)}) async-start(), calls=%async_computation.2 | async-start | bytes 2228224 | tf_op jit(solution)/shard_map/all_gather | solution.py:275
  10.0 219.0 %all-gather.10.cloned.1.call-start = ((), (), s32[]{:S(2)}) async-start(), calls=%async_computation.3 | async-start | bytes 6553600 | tf_op jit(solution)/shard_map/all_gather | solution.py:280
  10.7 0.7 copy-start.5
  33.8 241.9 %all-gather.14.cloned.1.call-start = ((), (), s32[]{:S(2)}) async-start(), calls=%async_computation.5 | async-start | bytes 1638400 | tf_op jit(solution)/shard_map/all_gather | solution.py:282
  84.8 144.2 %collective-permute-start = (bf16[2,8,256,512]{3,2,1,0:T(8,128)(2,1)}, bf16[2,8,256,512]{3,2,1,0:T(8,128)(2,1)}, u32[]{:S(2)}, u32[]{:S(2)}) collective-permute-start(bf16[2,8,256,512]{3,2,1,0:T(8,128)(2,1)} %bitcast.14), channel_id=1, source_target_pairs={{0,64},{64,0},{1,65},{65,1},{2,66},{66,2},{3,67},{67,3},{4,68},{68... | collective-permute-start | bytes 12582920 | tf_op jit(solution)/shard_map/ppermute | solution.py:264
  156.2 87.4 %collective-permute-start.1 = (bf16[2,8,512,128]{3,2,1,0:T(8,128)(2,1)}, bf16[2,8,512,128]{3,2,1,0:T(8,128)(2,1)S(1)}, u32[]{:S(2)}, u32[]{:S(2)}) collective-permute-start(bf16[2,8,512,128]{3,2,1,0:T(8,128)(2,1)} %bitcast.16), channel_id=1, source_target_pairs={{0,64},{64,0},{1,65},{65,1},{2,66},{66,2},{3,67},{67,3},{4,68},{68... | collective-permute-start | bytes 6291464 | tf_op jit(solution)/shard_map/ppermute | solution.py:264
  243.6 32.2 %copy-start.7 = (bf16[2,8,512,128]{3,2,1,0:T(8,128)(2,1)}, bf16[2,8,512,128]{3,2,1,0:T(8,128)(2,1)S(1)}, u32[]{:S(2)}) copy-start(bf16[2,8,512,128]{3,2,1,0:T(8,128)(2,1)S(1)} %collective-permute-done.1.other_ref) | copy-start | bytes 6291460
  275.8 1.3 copy-start.2
  281.8 1.1 copy-start.1
  282.9 6.2 %copy-start.6 = (s32[64,2]{0,1:T(2,128)S(1)}, s32[64,2]{0,1:T(2,128)}, u32[]{:S(2)}) copy-start(s32[64,2]{0,1:T(2,128)} %param.8) | copy-start | bytes 1540
  282.9 7.0 %copy-start.8 = (s32[64,2]{0,1:T(2,128)S(1)}, s32[64,2]{0,1:T(2,128)}, u32[]{:S(2)}) copy-start(s32[64,2]{0,1:T(2,128)} %param.9) | copy-start | bytes 1540
  282.9 24.1 %all-to-all-start.1 = ((bf16[16,40,1024]{2,1,0:T(8,128)(2,1)}), bf16[16,40,1024]{2,1,0:T(8,128)(2,1)S(1)}, u32[]{:S(2)}, u32[]{:S(2)}) async-start(bf16[16,40,1024]{2,1,0:T(8,128)(2,1)} %copy-done.1), calls=%async_computation.1 | async-start | bytes 2621440 | tf_op jit(solution)/shard_map/all_to_all | solution.py:284
  307.0 0.8 copy-start.4
Sparse Core Ops, SparseCore 0:
  9.4 75.3 all-gather.11
  86.9 69.2 all-gather.7
  158.3 70.6 all-gather.9
  243.7 32.0 all-gather.13

commit v2 on v1

v2 whole, which is shorter than its diff:
```python
import functools

import jax
import jax.numpy as jnp
from jax import lax
from jax.experimental import pallas as pl
from jax.experimental.pallas import tpu as pltpu
from jax.sharding import Mesh
from jax.sharding import PartitionSpec as P

Y, C, X, Z = 4, 2, 4, 16
D, F, TOK = 4096, 1024, 64
SHARD = 512
MEMBERS = 8
CAP = 20
SLOTS = 2 * CAP
MAIN = 16
REST = SLOTS - 2 * MAIN
SRC = Y * X
ROWS = SRC * SLOTS
ALL_SLOTS = X * SLOTS
FQ = F // Y
HALF = SHARD // 2
DEEP = 2
OFFSETS = (0, 1, 2, 3)
VMEM = 100 * 1024 * 1024 // 2


def slot_layout(place):
    column = (place * 1639) >> 16
    at = place - column * SLOTS
    second = ((at >= MAIN) & (at < 2 * MAIN)) | (at >= 2 * MAIN + REST // 2)
    slot = jnp.where(at < MAIN, at, jnp.where(at < 2 * MAIN + REST // 2, at - MAIN, at - MAIN - REST // 2))
    return 2 * column + second.astype(jnp.int32), slot


def restore(v):
    scale = (jnp.max(jnp.abs(v), axis=1, keepdims=True) + 1e-06) / 448.0
    scaled = v / scale
    x = jnp.abs(scaled)
    spacing = jnp.full_like(x, 2.0**-9)
    for shift, least in ((8, 2.0**2), (4, 2.0**-2), (2, 2.0**-4), (1, 2.0**-5)):
        big = x >= least
        x = jnp.where(big, x * 2.0**-shift, x)
        spacing = jnp.where(big, spacing * 2.0**shift, spacing)
    snapped = jnp.floor(x * 512.0 + 0.5) * spacing
    coded = jnp.where(scaled < 0.0, -snapped, snapped)
    return (coded * scale).astype(jnp.bfloat16)


def encode_kernel(count_ref, routes_ref, tokens_ref, first_ref, second_ref):
    place = lax.broadcasted_iota(jnp.int32, (ALL_SLOTS, TOK), 0)
    row = lax.broadcasted_iota(jnp.int32, (ALL_SLOTS, TOK), 1)
    expert, slot = slot_layout(place)
    named = (routes_ref[0:1, :] == expert) | (routes_ref[1:2, :] == expert)
    named = named & (row < count_ref[0])
    earlier = lax.broadcasted_iota(jnp.int32, (TOK, TOK), 0) < lax.broadcasted_iota(jnp.int32, (TOK, TOK), 1)
    rank = jnp.dot(
        named.astype(jnp.float32).astype(jnp.bfloat16),
        earlier.astype(jnp.float32).astype(jnp.bfloat16),
        preferred_element_type=jnp.float32,
    )
    chosen = named & (rank.astype(jnp.int32) == slot)
    chosen = chosen.astype(jnp.float32).astype(jnp.bfloat16)

    def step(member, carry):
        for half, out_ref in enumerate((first_ref, second_ref)):
            start = pl.multiple_of(member * SHARD + half * HALF, HALF)
            values = tokens_ref[:, pl.ds(start, HALF)].astype(jnp.float32)
            restored = jnp.concatenate([restore(values[:, b * 128 : (b + 1) * 128]) for b in range(HALF // 128)], axis=1)
            rows = jnp.dot(chosen, restored, preferred_element_type=jnp.float32)
            out_ref[:, pl.ds(pl.multiple_of(member * HALF, HALF), HALF)] = rows.astype(jnp.bfloat16)
        return carry

    lax.fori_loop(0, MEMBERS, step, 0)


def shares_kernel(count_ref, routes_ref, numerators_ref, out_ref):
    place = lax.broadcasted_iota(jnp.int32, (TOK, ALL_SLOTS), 1)
    row = lax.broadcasted_iota(jnp.int32, (TOK, ALL_SLOTS), 0)
    expert, slot = slot_layout(place)
    live = row < count_ref[0]
    first = (routes_ref[:, 0:1] == expert) & live
    second = (routes_ref[:, 1:2] == expert) & live
    earlier = lax.broadcasted_iota(jnp.int32, (TOK, TOK), 1) < lax.broadcasted_iota(jnp.int32, (TOK, TOK), 0)
    rank = jnp.dot(
        earlier.astype(jnp.float32).astype(jnp.bfloat16),
        (first | second).astype(jnp.float32).astype(jnp.bfloat16),
        preferred_element_type=jnp.float32,
    )
    here = rank.astype(jnp.int32) == slot
    share = numerators_ref[...].astype(jnp.float32) / 256.0
    out = jnp.where(first & here, share[:, 0:1], 0.0) + jnp.where(second & here, share[:, 1:2], 0.0)
    out_ref[...] = out.astype(jnp.bfloat16)


def split_rows(block):
    wide = block.astype(jnp.float32)
    n = wide.shape[-1]
    mixed = wide[:, 2 * MAIN :].reshape(SRC * REST, n)
    return [
        jnp.concatenate([wide[:, e * MAIN : (e + 1) * MAIN].reshape(SRC * MAIN, n), mixed], axis=0).astype(jnp.bfloat16)
        for e in range(2)
    ]


def join_rows(first, second):
    n = first.shape[-1]
    main = SRC * MAIN
    place = lax.broadcasted_iota(jnp.int32, (SRC * REST, n), 0)
    mixed = jnp.where((place & (REST - 1)) < REST // 2, first[main:], second[main:])
    return jnp.concatenate(
        [first[:main].reshape(SRC, MAIN, n), second[:main].reshape(SRC, MAIN, n), mixed.reshape(SRC, REST, n)], axis=1
    )


def hidden_kernel(place_ref, *refs):
    rows, weights_ref, out_ref, first_sum, second_sum = refs[:8], refs[8], refs[9], refs[10], refs[11]
    step = pl.program_id(0)

    @pl.when(step == 0)
    def _():
        first_sum[...] = jnp.zeros_like(first_sum)
        second_sum[...] = jnp.zeros_like(second_sum)

    def add(parts):
        first, second = split_rows(jnp.concatenate([ref[...] for ref in parts], axis=0))
        for expert, (block, total) in enumerate(((first, first_sum), (second, second_sum))):
            weights = jnp.concatenate([weights_ref[expert, m, 0] for m in range(DEEP)], axis=0)
            total[...] += jnp.dot(block, weights, preferred_element_type=jnp.float32)

    @pl.when(step < MEMBERS // DEEP)
    def _():
        add(rows[0::2])

    @pl.when(step >= MEMBERS // DEEP)
    def _():
        add(rows[1::2])

    @pl.when(step == 2 * MEMBERS // DEEP - 1)
    def _():
        def hidden(total):
            gate = total[:, :FQ]
            return gate / (1.0 + jnp.exp(-gate)) * total[:, FQ:]

        joined = join_rows(hidden(first_sum[...]), hidden(second_sum[...])).astype(jnp.bfloat16)
        for i, offset in enumerate(OFFSETS):
            source = lax.rem(place_ref[0] + offset, Y)
            block = joined[i * X : (i + 1) * X]
            for copy in range(Y):
                out_ref[copy, pl.ds(source * X, X)] = block


def down_kernel(hidden_ref, weights_ref, out_ref, first_rows, second_rows):
    @pl.when(pl.program_id(0) == 0)
    def _():
        for quarter in range(Y):
            first, second = split_rows(hidden_ref[quarter])
            first_rows[:, quarter * FQ : (quarter + 1) * FQ] = first
            second_rows[:, quarter * FQ : (quarter + 1) * FQ] = second

    def result(expert, rows):
        weights = jnp.concatenate(
            [
                jnp.concatenate([weights_ref[expert, m, half, :, q * 128 : (q + 1) * 128] for m in range(2)], axis=1)
                for q in range(Y)
                for half in range(C)
            ],
            axis=0,
        )
        return jnp.dot(rows[...], weights, preferred_element_type=jnp.float32)

    out_ref[...] = join_rows(result(0, first_rows), result(1, second_rows)).astype(jnp.bfloat16)


def mix_kernel(shares_ref, rows_ref, out_ref):
    for quarter in range(Y):
        rows = rows_ref[quarter * X : (quarter + 1) * X].reshape(ALL_SLOTS, MEMBERS * 128)
        mixed = jnp.dot(shares_ref[...], rows, preferred_element_type=jnp.float32).astype(jnp.bfloat16)
        for member in range(MEMBERS):
            at = member * SHARD + quarter * 128
            out_ref[:, at : at + 128] = mixed[:, member * 128 : (member + 1) * 128]


SCALAR = pl.BlockSpec(memory_space=pltpu.SMEM)
WHOLE = pl.BlockSpec(memory_space=pltpu.VMEM)


def shape(dims):
    return jax.ShapeDtypeStruct(dims, jnp.bfloat16)


def params(**extra):
    return pltpu.CompilerParams(vmem_limit_bytes=VMEM, **extra)


def encode(counts, routes, tokens):
    return pl.pallas_call(
        encode_kernel,
        out_shape=[shape((ALL_SLOTS, D // 2))] * 2,
        in_specs=[SCALAR, WHOLE, WHOLE],
        out_specs=[WHOLE] * 2,
        compiler_params=params(),
        cost_estimate=pl.CostEstimate(flops=2 * ALL_SLOTS * TOK * D, bytes_accessed=2 * (TOK + ALL_SLOTS) * D, transcendentals=0),
    )(counts, routes.T, tokens)


def share_table(counts, routes, numerators):
    return pl.pallas_call(
        shares_kernel,
        out_shape=shape((TOK, ALL_SLOTS)),
        in_specs=[SCALAR, WHOLE, WHOLE],
        out_specs=WHOLE,
    )(counts, routes, numerators)


def hidden_rows(place, rows, weights):
    steps = MEMBERS // DEEP
    first = pl.BlockSpec((X, SLOTS, DEEP * HALF), lambda k: (0, 0, jnp.minimum(k, steps - 1)))
    second = pl.BlockSpec((X, SLOTS, DEEP * HALF), lambda k: (0, 0, jnp.maximum(k - steps, 0)))
    return pl.pallas_call(
        hidden_kernel,
        grid=(2 * steps,),
        out_shape=shape((Y, SRC, SLOTS, FQ)),
        in_specs=[
            SCALAR,
            *[first, second] * Y,
            pl.BlockSpec((2, DEEP, 1, HALF, 2 * FQ), lambda k: (0, lax.rem(k, steps), k // steps, 0, 0)),
        ],
        out_specs=pl.BlockSpec((Y, SRC, SLOTS, FQ), lambda k: (0, 0, 0, 0)),
        scratch_shapes=[pltpu.VMEM((SRC * (MAIN + REST), 2 * FQ), jnp.float32)] * 2,
        compiler_params=params(),
        cost_estimate=pl.CostEstimate(flops=2 * ROWS * D * 2 * FQ, bytes_accessed=2 * ROWS * D + 8 * D * FQ, transcendentals=0),
    )(place, *rows, weights)


def down_rows(hidden, weights):
    return pl.pallas_call(
        down_kernel,
        grid=(MEMBERS // 2,),
        out_shape=shape((SRC, SLOTS, MEMBERS * 128)),
        in_specs=[
            pl.BlockSpec((Y, SRC, SLOTS, FQ), lambda n: (0, 0, 0, 0)),
            pl.BlockSpec((2, 2, C, 128, SHARD), lambda n: (0, n, 0, HALF // 128, 0)),
        ],
        out_specs=pl.BlockSpec((SRC, SLOTS, 256), lambda n: (0, 0, n)),
        scratch_shapes=[pltpu.VMEM((SRC * (MAIN + REST), F), jnp.bfloat16)] * 2,
        compiler_params=params(),
        cost_estimate=pl.CostEstimate(flops=2 * ROWS * F * F, bytes_accessed=2 * ROWS * F * 2 + 4 * F * F, transcendentals=0),
    )(hidden, weights)


def mix(shares, rows):
    return pl.pallas_call(
        mix_kernel,
        out_shape=shape((TOK, D)),
        in_specs=[WHOLE, WHOLE],
        out_specs=WHOLE,
        compiler_params=params(),
    )(shares, rows)


def shift(block, by):
    return lax.ppermute(block, "y", [(i, (i + by) % Y) for i in range(Y)])


def local(tokens, routes, numerators, counts, w_gate, w_up, w_down):
    y, c = lax.axis_index("y"), lax.axis_index("c")
    gate = lax.dynamic_slice(w_gate, (c * HALF, y * FQ), (HALF, FQ))
    up = lax.dynamic_slice(w_up, (c * HALF, y * FQ), (HALF, FQ))
    down = lax.dynamic_slice(w_down.reshape(Y, C, 128, SHARD), (0, c, 0, y * 128), (Y, 1, 128, 128))
    down = jnp.concatenate([down[q, 0] for q in range(Y)], axis=1)
    weights = jnp.concatenate([jnp.concatenate([gate, up], axis=1), down], axis=0)
    weights = lax.all_gather(weights, ("z", "c")).reshape(2, MEMBERS, C, HALF + 128, SHARD)
    shares = share_table(counts, routes, numerators)
    first, second = encode(counts, routes, tokens)
    first = lax.all_to_all(first.reshape(X, SLOTS, D // 2), "x", 0, 0, tiled=True)
    second = lax.all_to_all(second.reshape(X, SLOTS, D // 2), "x", 0, 0, tiled=True)
    first_3, second_1 = shift(first, 1), shift(second, -1)
    second_3, first_1 = shift(second, 1), shift(first, -1)
    first_2, second_2 = shift(first_3, 1), shift(second_1, -1)
    rows = (first, second, first_1, second_1, first_2, second_2, first_3, second_3)
    place = y.astype(jnp.int32).reshape(1)
    hidden = hidden_rows(place, rows, weights)
    hidden = lax.all_to_all(hidden, "y", 0, 0, tiled=True)
    result = down_rows(hidden, weights)
    result = lax.all_to_all(result, ("y", "x"), 0, 0, tiled=True)
    return mix(shares, result)


def solution(mesh):
    grid = Mesh(mesh.devices.reshape(Y, C, X, Z), ("y", "c", "x", "z"))
    tokens = ("y", "c", "x", "z")
    group = ("x", "z")
    placed = (
        P(tokens, None),
        P(tokens, None),
        P(tokens, None),
        P(tokens),
        P(group, None),
        P(group, None),
        P(None, group),
    )
    return jax.shard_map(local, mesh=grid, in_specs=placed, out_specs=P(tokens, None), check_vma=False)
```

time: 318 us -> 175 us (0.55)
  waiting for transfers between devices: 219 us -> 60 us
  blocking collectives: 17.4 us -> 33.6 us
  starting transfers between devices: 29.2 us -> 34.6 us
  Pallas kernels: 27.1 us -> 22.8 us
    all_gather x4 -> x1, waiting for transfers between devices: 204 us -> 16.6 us  [local(): lax.all_gather(weights, ('z', 'c'))]
    ppermute x2 -> x6, waiting for transfers between devices: 0.01 us -> 26.4 us  [shift(): return lax.ppermute(block, 'y', [(i, (i + by) % Y) for i in range(Y)])]
    all_to_all x1 -> x2, blocking collectives: 17.4 us -> 33.6 us  [the longest x1 21.3 us: local(): hidden = lax.all_to_all(hidden, 'y', 0, 0, tiled=True)]
    pallas_call x2, Pallas kernels: 19.6 us -> 14.7 us  [the longest x1 10.4 us: hidden_rows(): pl.pallas_call(hidden_kernel, grid=(2 * steps,), out_shape=shape((Y, SRC,...]
    all_to_all x0 -> x1, starting transfers between devices: none -> 3.48 us  [local(): lax.all_to_all(second.reshape(X, SLOTS, D // 2), 'x', 0, 0, tiled=True)]
    ppermute x2 -> x6, starting transfers between devices: 22.9 us -> 26.3 us  [shift(): return lax.ppermute(block, 'y', [(i, (i + by) % Y) for i in range(Y)])]
  transfers between devices with their start and end apart: 7 -> 9, of which waited for: 5 -> 7; matrix products, arithmetic and copies ran while one was open for 1% -> 1% of each run, Pallas kernels for 7% -> 3%
where the time goes in v2:
time: 175 us; the launch traced here: 173 us
  waiting for transfers between devices  60 us (34%)
  starting transfers between devices  34.6 us (20%)
  blocking collectives  33.6 us (19%)
  Pallas kernels  22.8 us (13%)
  between operations  14.1 us (8%)
  local copies, waits for them, and re-layouts  6.9 us (4%)
    ppermute x6, waiting for transfers between devices, shift(): return lax.ppermute(block, 'y', [(i, (i + by) % Y) for i in range(Y)])  26.4 us
    ppermute x6, starting transfers between devices, shift(): return lax.ppermute(block, 'y', [(i, (i + by) % Y) for i in range(Y)])  26.3 us
    all_to_all x1, blocking collectives, local(): hidden = lax.all_to_all(hidden, 'y', 0, 0, tiled=True)  21.3 us
    all_gather x1, waiting for transfers between devices, local(): lax.all_gather(weights, ('z', 'c'))  16.6 us
    all_to_all x1, waiting for transfers between devices, local(): result = lax.all_to_all(result, ('y', 'x'), 0, 0, tiled=True)  15 us
    all_to_all x1, blocking collectives, local(): lax.all_to_all(first.reshape(X, SLOTS, D // 2), 'x', 0, 0, tiled=True)  12.3 us
    pallas_call x1, Pallas kernels, hidden_rows(): pl.pallas_call(hidden_kernel, grid=(2 * steps,), out_shape=shape((Y, SRC,...  10.4 us
    pallas_call x1, Pallas kernels, down_rows(): pl.pallas_call(down_kernel, grid=(MEMBERS // 2,), out_shape=shape((SRC, S...  5.38 us
  transfers between devices with their start and end apart: 9, of which 7 were waited for; matrix products, arithmetic and copies ran while one was open for 1% of the time, Pallas kernels for 3%

profile of v2, /device:TPU:1, one launch (start us, length us, event | category | flops | bytes accessed | tf_op | source)
XLA Modules:
  0.0 172.8 jit_solution(12996489346560669159)
XLA Ops:
  6.5 0.0 copy-start.4
  6.5 0.0 copy-start.2
  6.5 0.0 all-gather.3.cloned.1.call-start
  6.5 1.0 dynamic_slice.10
  7.5 0.9 dynamic_slice.9
  8.4 0.8 dynamic-slice_bitcast_fusion.3
  9.3 0.8 maximum_maximum_fusion
  10.1 0.0 all-gather.3.cloned.1.call-update
  10.7 0.0 copy-done.4
  10.7 0.0 copy-done.2
  10.8 4.3 %shard_map.74 = (bf16[160,2048]{1,0:T(8,128)(2,1)S(1)}, bf16[160,2048]{1,0:T(8,128)(2,1)}) custom-call(s32[1]{0:T(128)S(6)} %copy.10.count_ref, s32[2,64]{1,0:T(2,128)S(1)} %bitcast.15, bf16[64,4096]{1,0:T(8,128)(2,1)S(1)} %copy-done.2), custom_call_target="tpu_custom_call" | custom-call | flops 83886080 | bytes 1835008 | tf_op jit(solution)/shard_map/pallas_call | solution.py:198
  15.1 12.3 %all_to_all.20.refs_0_ = bf16[4,40,2048]{2,1,0:T(8,128)(2,1)S(1)} all-to-all(bf16[4,40,2048]{2,1,0:T(8,128)(2,1)S(1)} %bitcast.14), channel_id=1, replica_groups=mesh['y'=4,'c'=2,'x'=4,'z'=16] {'x'}, dimensions={0} | all-to-all | bytes 1310720 | tf_op jit(solution)/shard_map/all_to_all | solution.py:277
  27.3 3.5 %all-to-all-start.1 = ((bf16[4,40,2048]{2,1,0:T(8,128)(2,1)}), bf16[4,40,2048]{2,1,0:T(8,128)(2,1)S(1)}, u32[]{:S(2)}, u32[]{:S(2)}) async-start(bf16[4,40,2048]{2,1,0:T(8,128)(2,1)} %bitcast.3), calls=%async_computation.1 | async-start | bytes 1310720 | tf_op jit(solution)/shard_map/all_to_all | solution.py:278
  30.8 5.6 %collective-permute-start.2 = (bf16[4,40,2048]{2,1,0:T(8,128)(2,1)S(1)}, bf16[4,40,2048]{2,1,0:T(8,128)(2,1)}, u32[]{:S(2)}, u32[]{:S(2)}) collective-permute-start(bf16[4,40,2048]{2,1,0:T(8,128)(2,1)S(1)} %all_to_all.20.refs_0_), channel_id=1, source_target_pairs={{0,128},{128,256},{256,384},{384,0},{1,129},{129,257},{257,385},{3... | collective-permute-start | bytes 1966088 | tf_op jit(solution)/shard_map/ppermute | solution.py:264
  36.4 2.0 %all-to-all-done.1.refs_1_ = bf16[4,40,2048]{2,1,0:T(8,128)(2,1)S(1)} async-done(((bf16[4,40,2048]{2,1,0:T(8,128)(2,1)}), bf16[4,40,2048]{2,1,0:T(8,128)(2,1)S(1)}, u32[]{:S(2)}, u32[]{:S(2)}) %all-to-all-start.1) | async-done | bytes 655392 | tf_op jit(solution)/shard_map/all_to_all | solution.py:278
  38.5 8.1 %collective-permute-start.1 = (bf16[4,40,2048]{2,1,0:T(8,128)(2,1)S(1)}, bf16[4,40,2048]{2,1,0:T(8,128)(2,1)S(1)}, u32[]{:S(2)}, u32[]{:S(2)}) collective-permute-start(bf16[4,40,2048]{2,1,0:T(8,128)(2,1)S(1)} %all-to-all-done.1.refs_1_), channel_id=1, source_target_pairs={{0,384},{128,0},{256,128},{384,256},{1,385},{129,1},{257,129},{385... | collective-permute-start | bytes 1966088 | tf_op jit(solution)/shard_map/ppermute | solution.py:264
  46.5 2.4 %collective-permute-start = (bf16[4,40,2048]{2,1,0:T(8,128)(2,1)S(1)}, bf16[4,40,2048]{2,1,0:T(8,128)(2,1)S(1)}, u32[]{:S(2)}, u32[]{:S(2)}) collective-permute-start(bf16[4,40,2048]{2,1,0:T(8,128)(2,1)S(1)} %all_to_all.20.refs_0_), channel_id=1, source_target_pairs={{0,384},{128,0},{256,128},{384,256},{1,385},{129,1},{257,129},{385... | collective-permute-start | bytes 1966088 | tf_op jit(solution)/shard_map/ppermute | solution.py:264
  48.9 2.9 %collective-permute-start.5 = (bf16[4,40,2048]{2,1,0:T(8,128)(2,1)S(1)}, bf16[4,40,2048]{2,1,0:T(8,128)(2,1)S(1)}, u32[]{:S(2)}, u32[]{:S(2)}) collective-permute-start(bf16[4,40,2048]{2,1,0:T(8,128)(2,1)S(1)} %all-to-all-done.1.refs_1_), channel_id=1, source_target_pairs={{0,128},{128,256},{256,384},{384,0},{1,129},{129,257},{257,385},{3... | collective-permute-start | bytes 1966088 | tf_op jit(solution)/shard_map/ppermute | solution.py:264
  51.8 0.0 collective-permute-done.2.refs_6_
  51.9 1.9 %collective-permute-start.3 = (bf16[4,40,2048]{2,1,0:T(8,128)(2,1)}, bf16[4,40,2048]{2,1,0:T(8,128)(2,1)S(1)}, u32[]{:S(2)}, u32[]{:S(2)}) collective-permute-start(bf16[4,40,2048]{2,1,0:T(8,128)(2,1)} %collective-permute-done.2.refs_6_), channel_id=1, source_target_pairs={{0,128},{128,256},{256,384},{384,0},{1,129},{129,257},{257,385},{3... | collective-permute-start | bytes 1966088 | tf_op jit(solution)/shard_map/ppermute | solution.py:264
  53.8 3.7 %collective-permute-done.1.refs_3_ = bf16[4,40,2048]{2,1,0:T(8,128)(2,1)S(1)} collective-permute-done((bf16[4,40,2048]{2,1,0:T(8,128)(2,1)S(1)}, bf16[4,40,2048]{2,1,0:T(8,128)(2,1)S(1)}, u32[]{:S(2)}, u32[]{:S(2)}) %collective-permute-start.1) | collective-permute-done | bytes 655392 | tf_op jit(solution)/shard_map/ppermute | solution.py:264
  57.5 5.4 %collective-permute-start.4 = (bf16[4,40,2048]{2,1,0:T(8,128)(2,1)S(1)}, bf16[4,40,2048]{2,1,0:T(8,128)(2,1)S(1)}, u32[]{:S(2)}, u32[]{:S(2)}) collective-permute-start(bf16[4,40,2048]{2,1,0:T(8,128)(2,1)S(1)} %collective-permute-done.1.refs_3_), channel_id=1, source_target_pairs={{0,384},{128,0},{256,128},{384,256},{1,385},{129,1},{257,129},{385... | collective-permute-start | bytes 1966088 | tf_op jit(solution)/shard_map/ppermute | solution.py:264
  62.9 8.6 %collective-permute-done.refs_2_ = bf16[4,40,2048]{2,1,0:T(8,128)(2,1)S(1)} collective-permute-done((bf16[4,40,2048]{2,1,0:T(8,128)(2,1)S(1)}, bf16[4,40,2048]{2,1,0:T(8,128)(2,1)S(1)}, u32[]{:S(2)}, u32[]{:S(2)}) %collective-permute-start) | collective-permute-done | bytes 655392 | tf_op jit(solution)/shard_map/ppermute | solution.py:264
  71.5 0.0 collective-permute-done.5.refs_7_
  71.5 0.0 copy-start.5
  71.5 7.3 %collective-permute-done.3.refs_4_ = bf16[4,40,2048]{2,1,0:T(8,128)(2,1)S(1)} collective-permute-done((bf16[4,40,2048]{2,1,0:T(8,128)(2,1)}, bf16[4,40,2048]{2,1,0:T(8,128)(2,1)S(1)}, u32[]{:S(2)}, u32[]{:S(2)}) %collective-permute-start.3) | collective-permute-done | bytes 655392 | tf_op jit(solution)/shard_map/ppermute | solution.py:264
  78.8 0.0 copy-done.5
  78.8 6.8 %collective-permute-done.4.refs_5_ = bf16[4,40,2048]{2,1,0:T(8,128)(2,1)S(1)} collective-permute-done((bf16[4,40,2048]{2,1,0:T(8,128)(2,1)S(1)}, bf16[4,40,2048]{2,1,0:T(8,128)(2,1)S(1)}, u32[]{:S(2)}, u32[]{:S(2)}) %collective-permute-start.4) | collective-permute-done | bytes 655392 | tf_op jit(solution)/shard_map/ppermute | solution.py:264
  85.6 0.0 copy-start
  85.6 0.9 copy-done
  86.5 16.6 %all-gather.3.cloned.1.call-done = bf16[12288,512]{1,0:T(8,128)(2,1)} async-done(((bf16[384,512]{1,0:T(8,128)(2,1)}), bf16[12288,512]{1,0:T(8,128)(2,1)}) %all-gather.3.cloned.1.call-update) | async-done | bytes 12582928 | tf_op jit(solution)/shard_map/all_gather | solution.py:274
  103.0 0.0 copy-start.1
  103.0 1.1 copy-done.1
  104.1 10.4 %shard_map.75 = bf16[4,16,40,256]{3,2,1,0:T(8,128)(2,1)} custom-call(s32[1]{0:T(128)} %bitcast.place_ref, bf16[4,40,2048]{2,1,0:T(8,128)(2,1)S(1)} %all_to_all.20.refs_0_, bf16[4,40,2048]{2,1,0:T(8,128)(2,1)S(1)} %all-to-all-done.1.refs_1_, bf16[4,40,2048]{2,1,0:T(8,128)(2,1)S(1)} %collective-permute-done.refs_2_, ...), custom_call_target="tpu_custom_call" | custom-call | flops 2684354560 | bytes 13631488 | tf_op jit(solution)/shard_map/pallas_call | solution.py:221
  114.5 21.3 %all_to_all.21.hidden_ref = bf16[4,16,40,256]{3,2,1,0:T(8,128)(2,1)S(1)} all-to-all(bf16[4,16,40,256]{3,2,1,0:T(8,128)(2,1)} %shard_map.75), channel_id=1, replica_groups=mesh['y'=4,'c'=2,'x'=4,'z'=16] {'y'}, dimensions={0} | all-to-all | bytes 2621440 | tf_op jit(solution)/shard_map/all_to_all | solution.py:285
  135.8 5.4 %shard_map.76 = bf16[16,40,1024]{2,1,0:T(8,128)(2,1)} custom-call(bf16[4,16,40,256]{3,2,1,0:T(8,128)(2,1)S(1)} %all_to_all.21.hidden_ref, bf16[2,8,2,384,512]{4,3,2,1,0:T(8,128)(2,1)} %bitcast.17), custom_call_target="tpu_custom_call" | custom-call | flops 1342177280 | bytes 6815744 | tf_op jit(solution)/shard_map/pallas_call | solution.py:238
  141.2 0.0 copy-start.6
  141.2 4.8 %all-to-all-start.3 = ((bf16[16,40,1024]{2,1,0:T(8,128)(2,1)}), bf16[16,40,1024]{2,1,0:T(8,128)(2,1)S(1)}, u32[]{:S(2)}, u32[]{:S(2)}) async-start(bf16[16,40,1024]{2,1,0:T(8,128)(2,1)} %shard_map.76), calls=%async_computation.3 | async-start | bytes 2621440 | tf_op jit(solution)/shard_map/all_to_all | solution.py:287
  146.0 0.7 copy.8.routes_ref
  146.7 0.0 copy-done.6
  146.7 0.7 copy.9.numerators_ref
  147.4 1.6 shard_map.73.shares_ref
  149.0 15.0 %all-to-all-done.3.rows_ref = bf16[16,40,1024]{2,1,0:T(8,128)(2,1)S(1)} async-done(((bf16[16,40,1024]{2,1,0:T(8,128)(2,1)}), bf16[16,40,1024]{2,1,0:T(8,128)(2,1)S(1)}, u32[]{:S(2)}, u32[]{:S(2)}) %all-to-all-start.3) | async-done | bytes 1310752 | tf_op jit(solution)/shard_map/all_to_all | solution.py:287
  164.1 0.0 copy-start.3
  164.1 0.8 copy-done.3
  164.8 1.1 shard_map.77
Async XLA Ops:
  6.5 4.2 %copy-start.4 = (s32[64,2]{0,1:T(2,128)S(1)}, s32[64,2]{0,1:T(2,128)}, u32[]{:S(2)}) copy-start(s32[64,2]{0,1:T(2,128)} %param.8) | copy-start | bytes 1540
  6.5 4.2 %copy-start.2 = (bf16[64,4096]{1,0:T(8,128)(2,1)S(1)}, bf16[64,4096]{1,0:T(8,128)(2,1)}, u32[]{:S(2)}) copy-start(bf16[64,4096]{1,0:T(8,128)(2,1)} %tokens_ref.1) | copy-start | bytes 1572868
  6.5 96.5 %all-gather.3.cloned.1.call-start = ((), (), s32[]{:S(2)}) async-start(), calls=%async_computation.4 | async-start | bytes 12976128 | tf_op jit(solution)/shard_map/all_gather | solution.py:274
  27.3 11.1 %all-to-all-start.1 = ((bf16[4,40,2048]{2,1,0:T(8,128)(2,1)}), bf16[4,40,2048]{2,1,0:T(8,128)(2,1)S(1)}, u32[]{:S(2)}, u32[]{:S(2)}) async-start(bf16[4,40,2048]{2,1,0:T(8,128)(2,1)} %bitcast.3), calls=%async_computation.1 | async-start | bytes 1310720 | tf_op jit(solution)/shard_map/all_to_all | solution.py:278
  30.8 21.0 %collective-permute-start.2 = (bf16[4,40,2048]{2,1,0:T(8,128)(2,1)S(1)}, bf16[4,40,2048]{2,1,0:T(8,128)(2,1)}, u32[]{:S(2)}, u32[]{:S(2)}) collective-permute-start(bf16[4,40,2048]{2,1,0:T(8,128)(2,1)S(1)} %all_to_all.20.refs_0_), channel_id=1, source_target_pairs={{0,128},{128,256},{256,384},{384,0},{1,129},{129,257},{257,385},{3... | collective-permute-start | bytes 1966088 | tf_op jit(solution)/shard_map/ppermute | solution.py:264
  38.5 19.0 %collective-permute-start.1 = (bf16[4,40,2048]{2,1,0:T(8,128)(2,1)S(1)}, bf16[4,40,2048]{2,1,0:T(8,128)(2,1)S(1)}, u32[]{:S(2)}, u32[]{:S(2)}) collective-permute-start(bf16[4,40,2048]{2,1,0:T(8,128)(2,1)S(1)} %all-to-all-done.1.refs_1_), channel_id=1, source_target_pairs={{0,384},{128,0},{256,128},{384,256},{1,385},{129,1},{257,129},{385... | collective-permute-start | bytes 1966088 | tf_op jit(solution)/shard_map/ppermute | solution.py:264
  46.5 25.0 %collective-permute-start = (bf16[4,40,2048]{2,1,0:T(8,128)(2,1)S(1)}, bf16[4,40,2048]{2,1,0:T(8,128)(2,1)S(1)}, u32[]{:S(2)}, u32[]{:S(2)}) collective-permute-start(bf16[4,40,2048]{2,1,0:T(8,128)(2,1)S(1)} %all_to_all.20.refs_0_), channel_id=1, source_target_pairs={{0,384},{128,0},{256,128},{384,256},{1,385},{129,1},{257,129},{385... | collective-permute-start | bytes 1966088 | tf_op jit(solution)/shard_map/ppermute | solution.py:264
  48.9 22.6 %collective-permute-start.5 = (bf16[4,40,2048]{2,1,0:T(8,128)(2,1)S(1)}, bf16[4,40,2048]{2,1,0:T(8,128)(2,1)S(1)}, u32[]{:S(2)}, u32[]{:S(2)}) collective-permute-start(bf16[4,40,2048]{2,1,0:T(8,128)(2,1)S(1)} %all-to-all-done.1.refs_1_), channel_id=1, source_target_pairs={{0,128},{128,256},{256,384},{384,0},{1,129},{129,257},{257,385},{3... | collective-permute-start | bytes 1966088 | tf_op jit(solution)/shard_map/ppermute | solution.py:264
  51.9 27.0 %collective-permute-start.3 = (bf16[4,40,2048]{2,1,0:T(8,128)(2,1)}, bf16[4,40,2048]{2,1,0:T(8,128)(2,1)S(1)}, u32[]{:S(2)}, u32[]{:S(2)}) collective-permute-start(bf16[4,40,2048]{2,1,0:T(8,128)(2,1)} %collective-permute-done.2.refs_6_), channel_id=1, source_target_pairs={{0,128},{128,256},{256,384},{384,0},{1,129},{129,257},{257,385},{3... | collective-permute-start | bytes 1966088 | tf_op jit(solution)/shard_map/ppermute | solution.py:264
  57.5 28.1 %collective-permute-start.4 = (bf16[4,40,2048]{2,1,0:T(8,128)(2,1)S(1)}, bf16[4,40,2048]{2,1,0:T(8,128)(2,1)S(1)}, u32[]{:S(2)}, u32[]{:S(2)}) collective-permute-start(bf16[4,40,2048]{2,1,0:T(8,128)(2,1)S(1)} %collective-permute-done.1.refs_3_), channel_id=1, source_target_pairs={{0,384},{128,0},{256,128},{384,256},{1,385},{129,1},{257,129},{385... | collective-permute-start | bytes 1966088 | tf_op jit(solution)/shard_map/ppermute | solution.py:264
  71.5 7.3 %copy-start.5 = (bf16[4,40,2048]{2,1,0:T(8,128)(2,1)}, bf16[4,40,2048]{2,1,0:T(8,128)(2,1)S(1)}, u32[]{:S(2)}) copy-start(bf16[4,40,2048]{2,1,0:T(8,128)(2,1)S(1)} %collective-permute-done.5.refs_7_) | copy-start | bytes 1966084
  85.6 0.9 copy-start
  103.0 1.1 copy-start.1
  141.2 5.5 %copy-start.6 = (s32[64,2]{0,1:T(2,128)S(1)}, s32[64,2]{0,1:T(2,128)}, u32[]{:S(2)}) copy-start(s32[64,2]{0,1:T(2,128)} %param.9) | copy-start | bytes 1540
  141.2 22.9 %all-to-all-start.3 = ((bf16[16,40,1024]{2,1,0:T(8,128)(2,1)}), bf16[16,40,1024]{2,1,0:T(8,128)(2,1)S(1)}, u32[]{:S(2)}, u32[]{:S(2)}) async-start(bf16[16,40,1024]{2,1,0:T(8,128)(2,1)} %shard_map.76), calls=%async_computation.3 | async-start | bytes 2621440 | tf_op jit(solution)/shard_map/all_to_all | solution.py:287
  164.1 0.8 copy-start.3
Sparse Core Ops, SparseCore 0:
  10.2 92.7 all-gather.2

commit v3 on v2

v3 whole, which is shorter than its diff:
```python
import functools

import jax
import jax.numpy as jnp
from jax import lax
from jax.experimental import pallas as pl
from jax.experimental.pallas import tpu as pltpu
from jax.sharding import Mesh
from jax.sharding import PartitionSpec as P

Y, C, X, Z = 4, 2, 4, 16
D, F, TOK = 4096, 1024, 64
SHARD = 512
MEMBERS = 8
CAP = 20
SLOTS = 2 * CAP
MAIN = 16
REST = SLOTS - 2 * MAIN
LEAD = MAIN + REST
SRC = Y * X
ROWS = SRC * SLOTS
ALL_SLOTS = X * SLOTS
FQ = F // Y
HALF = SHARD // 2
DEEP = 4
VMEM = 100 * 1024 * 1024 // 2


def slot_at(at):
    second = (at >= MAIN + REST // 2).astype(jnp.int32)
    slot = jnp.where(at < MAIN + REST // 2, at, jnp.where(at < LEAD, at - REST // 2, at - LEAD))
    return second, slot


def pack_kernel(place_ref, gate_ref, up_ref, *refs):
    out_ref = refs[Y]
    out_ref[:HALF, :FQ] = gate_ref[...]
    out_ref[:HALF, FQ:] = up_ref[...]
    for quarter in range(Y):
        out_ref[HALF:, quarter * 128 : (quarter + 1) * 128] = refs[quarter][...]


def restore(v):
    scale = (jnp.max(jnp.abs(v), axis=1, keepdims=True) + 1e-06) / 448.0
    scaled = v / scale
    x = jnp.abs(scaled)
    spacing = jnp.full_like(x, 2.0**-9)
    for shift, least in ((8, 2.0**2), (4, 2.0**-2), (2, 2.0**-4), (1, 2.0**-5)):
        big = x >= least
        x = jnp.where(big, x * 2.0**-shift, x)
        spacing = jnp.where(big, spacing * 2.0**shift, spacing)
    snapped = jnp.floor(x * 512.0 + 0.5) * spacing
    coded = jnp.where(scaled < 0.0, -snapped, snapped)
    return (coded * scale).astype(jnp.bfloat16)


def encode_kernel(count_ref, routes_ref, tokens_ref, first_ref, second_ref):
    place = lax.broadcasted_iota(jnp.int32, (ALL_SLOTS, TOK), 0)
    row = lax.broadcasted_iota(jnp.int32, (ALL_SLOTS, TOK), 1)
    column = (place * 1639) >> 16
    second, slot = slot_at(place - column * SLOTS)
    expert = 2 * column + second
    named = (routes_ref[0:1, :] == expert) | (routes_ref[1:2, :] == expert)
    named = named & (row < count_ref[0])
    earlier = lax.broadcasted_iota(jnp.int32, (TOK, TOK), 0) < lax.broadcasted_iota(jnp.int32, (TOK, TOK), 1)
    rank = jnp.dot(
        named.astype(jnp.float32).astype(jnp.bfloat16),
        earlier.astype(jnp.float32).astype(jnp.bfloat16),
        preferred_element_type=jnp.float32,
    )
    chosen = named & (rank.astype(jnp.int32) == slot)
    chosen = chosen.astype(jnp.float32).astype(jnp.bfloat16)

    def step(member, carry):
        for half, out_ref in enumerate((first_ref, second_ref)):
            start = pl.multiple_of(member * SHARD + half * HALF, HALF)
            values = tokens_ref[:, pl.ds(start, HALF)].astype(jnp.float32)
            restored = jnp.concatenate([restore(values[:, b * 128 : (b + 1) * 128]) for b in range(HALF // 128)], axis=1)
            rows = jnp.dot(chosen, restored, preferred_element_type=jnp.float32)
            out_ref[:, pl.ds(pl.multiple_of(member * HALF, HALF), HALF)] = rows.astype(jnp.bfloat16)
        return carry

    lax.fori_loop(0, MEMBERS, step, 0)


def shares_kernel(count_ref, routes_ref, numerators_ref, lead_ref, last_ref):
    share = numerators_ref[...].astype(jnp.float32) / 256.0
    earlier = lax.broadcasted_iota(jnp.int32, (TOK, TOK), 1) < lax.broadcasted_iota(jnp.int32, (TOK, TOK), 0)
    earlier = earlier.astype(jnp.float32).astype(jnp.bfloat16)
    for out_ref, start, length in ((lead_ref, 0, LEAD), (last_ref, LEAD, MAIN)):
        dims = (TOK, X * length)
        place = lax.broadcasted_iota(jnp.int32, dims, 1)
        column = sum((place >= i * length).astype(jnp.int32) for i in range(1, X))
        second, slot = slot_at(place - column * length + start)
        expert = 2 * column + second
        live = lax.broadcasted_iota(jnp.int32, dims, 0) < count_ref[0]
        by_first = (routes_ref[:, 0:1] == expert) & live
        by_second = (routes_ref[:, 1:2] == expert) & live
        named = (by_first | by_second).astype(jnp.float32).astype(jnp.bfloat16)
        rank = jnp.dot(earlier, named, preferred_element_type=jnp.float32)
        here = rank.astype(jnp.int32) == slot
        out = jnp.where(by_first & here, share[:, 0:1], 0.0) + jnp.where(by_second & here, share[:, 1:2], 0.0)
        out_ref[...] = out.astype(jnp.bfloat16)


def run_of(block, start, length):
    n = block.shape[-1]
    return block[:, start : start + length].astype(jnp.float32).reshape(-1, n).astype(jnp.bfloat16)


def mixed_rows(first, second):
    place = lax.broadcasted_iota(jnp.int32, first.shape, 0)
    return jnp.where((place & (REST - 1)) < REST // 2, first, second)


def sources(rows, length):
    return rows.reshape(-1, length, rows.shape[-1])


def swish(total):
    gate = total[:, :FQ]
    return gate / (1.0 + jnp.exp(-gate)) * total[:, FQ:]


def hidden_kernel(lead, place_ref, *refs):
    rows, weights_ref, out_ref, sums = refs[: 2 * Y], refs[2 * Y], refs[2 * Y + 1], refs[2 * Y + 2 :]
    steps = MEMBERS // DEEP
    step = pl.program_id(0)

    def add(parts, start):
        blocks = [ref[...] for ref in parts]
        if lead:
            mixed = [run_of(b, MAIN, REST) for b in blocks]
            groups = [[run_of(b, 0, MAIN) for b in blocks] + mixed, mixed]
        else:
            groups = [[run_of(b, LEAD, MAIN) for b in blocks]]
        for expert, (group, total) in enumerate(zip(groups, sums)):
            weights = jnp.concatenate([weights_ref[expert, m, 0] for m in range(DEEP)], axis=0)
            product = jnp.dot(jnp.concatenate(group, axis=0), weights, preferred_element_type=jnp.float32)
            total[...] = product if start else total[...] + product

    @pl.when(step == 0)
    def _():
        add(rows[0::2], True)

    @pl.when((step > 0) & (step < steps))
    def _():
        add(rows[0::2], False)

    @pl.when(step >= steps)
    def _():
        add(rows[1::2], False)

    @pl.when(step == 2 * steps - 1)
    def _():
        first = swish(sums[0][...])
        if lead:
            main = SRC * MAIN
            mixed = mixed_rows(first[main:], swish(sums[1][...]))
            joined = jnp.concatenate([sources(first[:main], MAIN), sources(mixed, REST)], axis=1)
        else:
            joined = sources(first, MAIN)
        joined = joined.astype(jnp.bfloat16)
        for offset in range(Y):
            source = lax.rem(place_ref[0] + offset, Y)
            block = joined[offset * X : (offset + 1) * X]
            for copy in range(Y):
                out_ref[copy, pl.ds(source * X, X)] = block


def down_kernel(lead, hidden_ref, weights_ref, out_ref, rows):
    main = SRC * MAIN

    @pl.when(pl.program_id(0) == 0)
    def _():
        for quarter in range(Y):
            block = hidden_ref[quarter]
            at = slice(quarter * FQ, (quarter + 1) * FQ)
            rows[:main, at] = run_of(block, 0, MAIN)
            if lead:
                rows[main:, at] = run_of(block, MAIN, REST)

    def result(expert, part):
        weights = jnp.concatenate(
            [
                jnp.concatenate([weights_ref[expert, m, half, :, q * 128 : (q + 1) * 128] for m in range(2)], axis=1)
                for q in range(Y)
                for half in range(C)
            ],
            axis=0,
        )
        return jnp.dot(part, weights, preferred_element_type=jnp.float32)

    first = result(0, rows[...])
    if lead:
        mixed = mixed_rows(first[main:], result(1, rows[main:]))
        first = jnp.concatenate([sources(first[:main], MAIN), sources(mixed, REST)], axis=1)
    else:
        first = sources(first, MAIN)
    out_ref[...] = first.astype(jnp.bfloat16)


def mix_kernel(lead_shares_ref, last_shares_ref, lead_ref, last_ref, out_ref):
    for quarter in range(Y):
        mixed = 0.0
        for shares_ref, ref in ((lead_shares_ref, lead_ref), (last_shares_ref, last_ref)):
            block = ref[quarter * X : (quarter + 1) * X]
            rows = block.reshape(-1, block.shape[-1])
            mixed += jnp.dot(shares_ref[...], rows, preferred_element_type=jnp.float32)
        mixed = mixed.astype(jnp.bfloat16)
        for member in range(MEMBERS):
            at = member * SHARD + quarter * 128
            out_ref[:, at : at + 128] = mixed[:, member * 128 : (member + 1) * 128]


SCALAR = pl.BlockSpec(memory_space=pltpu.SMEM)
WHOLE = pl.BlockSpec(memory_space=pltpu.VMEM)


def shape(dims):
    return jax.ShapeDtypeStruct(dims, jnp.bfloat16)


def params(**extra):
    return pltpu.CompilerParams(vmem_limit_bytes=VMEM, **extra)


def encode(counts, routes, tokens):
    return pl.pallas_call(
        encode_kernel,
        out_shape=[shape((ALL_SLOTS, D // 2))] * 2,
        in_specs=[SCALAR, WHOLE, WHOLE],
        out_specs=[WHOLE] * 2,
        compiler_params=params(),
        cost_estimate=pl.CostEstimate(flops=2 * ALL_SLOTS * TOK * D, bytes_accessed=2 * (TOK + ALL_SLOTS) * D, transcendentals=0),
    )(counts, routes.T, tokens)


def pack(place, w_gate, w_up, w_down):
    quarters = [pl.BlockSpec((128, 128), lambda i, p, q=q: (C * q + p[1], p[0])) for q in range(Y)]
    return pl.pallas_call(
        pack_kernel,
        out_shape=shape((HALF + 128, SHARD)),
        grid_spec=pltpu.PrefetchScalarGridSpec(
            num_scalar_prefetch=1,
            grid=(1,),
            in_specs=[pl.BlockSpec((HALF, FQ), lambda i, p: (p[1], p[0]))] * 2 + quarters,
            out_specs=pl.BlockSpec((HALF + 128, SHARD), lambda i, p: (0, 0)),
        ),
    )(place, w_gate, w_up, *[w_down] * Y)


def share_tables(counts, routes, numerators):
    return pl.pallas_call(
        shares_kernel,
        out_shape=[shape((TOK, X * LEAD)), shape((TOK, X * MAIN))],
        in_specs=[SCALAR, WHOLE, WHOLE],
        out_specs=[WHOLE] * 2,
    )(counts, routes, numerators)


def hidden_rows(lead, place, rows, weights):
    steps = MEMBERS // DEEP
    length = LEAD if lead else MAIN
    experts = 2 if lead else 1
    first = pl.BlockSpec((X, SLOTS, DEEP * HALF), lambda k: (0, 0, jnp.minimum(k, steps - 1)))
    second = pl.BlockSpec((X, SLOTS, DEEP * HALF), lambda k: (0, 0, jnp.maximum(k - steps, 0)))
    sums = [pltpu.VMEM((SRC * length, 2 * FQ), jnp.float32)]
    if lead:
        sums += [pltpu.VMEM((SRC * REST, 2 * FQ), jnp.float32)]
    return pl.pallas_call(
        functools.partial(hidden_kernel, lead),
        grid=(2 * steps,),
        out_shape=shape((Y, SRC, length, FQ)),
        in_specs=[
            SCALAR,
            *[first, second] * Y,
            pl.BlockSpec((experts, DEEP, 1, HALF, 2 * FQ), lambda k: (2 - experts, lax.rem(k, steps), k // steps, 0, 0)),
        ],
        out_specs=pl.BlockSpec((Y, SRC, length, FQ), lambda k: (0, 0, 0, 0)),
        scratch_shapes=sums,
        compiler_params=params(),
        cost_estimate=pl.CostEstimate(flops=2 * SRC * length * D * 2 * FQ, bytes_accessed=2 * ROWS * D + 4 * experts * D * FQ, transcendentals=0),
    )(place, *rows, weights)


def down_rows(lead, hidden, weights):
    length = LEAD if lead else MAIN
    experts = 2 if lead else 1
    return pl.pallas_call(
        functools.partial(down_kernel, lead),
        grid=(MEMBERS // 2,),
        out_shape=shape((SRC, length, MEMBERS * 128)),
        in_specs=[
            pl.BlockSpec((Y, SRC, length, FQ), lambda n: (0, 0, 0, 0)),
            pl.BlockSpec((experts, 2, C, 128, SHARD), lambda n: (2 - experts, n, 0, HALF // 128, 0)),
        ],
        out_specs=pl.BlockSpec((SRC, length, 256), lambda n: (0, 0, n)),
        scratch_shapes=[pltpu.VMEM((SRC * length, F), jnp.bfloat16)],
        compiler_params=params(),
        cost_estimate=pl.CostEstimate(flops=2 * SRC * length * F * F, bytes_accessed=4 * SRC * length * F + 2 * experts * F * F, transcendentals=0),
    )(hidden, weights)


def mix(shares, rows):
    return pl.pallas_call(
        mix_kernel,
        out_shape=shape((TOK, D)),
        in_specs=[WHOLE] * 4,
        out_specs=WHOLE,
        compiler_params=params(),
    )(*shares, *rows)


def shift(block, by):
    return lax.ppermute(block, "y", [(i, (i + by) % Y) for i in range(Y)])


def local(tokens, routes, numerators, counts, w_gate, w_up, w_down):
    place = jnp.stack([lax.axis_index("y"), lax.axis_index("c")]).astype(jnp.int32)
    weights = pack(place, w_gate, w_up, w_down)
    weights = lax.all_gather(weights, ("z", "c")).reshape(2, MEMBERS, C, HALF + 128, SHARD)
    shares = share_tables(counts, routes, numerators)
    first, second = encode(counts, routes, tokens)
    first = lax.all_to_all(first.reshape(X, SLOTS, D // 2), "x", 0, 0, tiled=True)
    second = lax.all_to_all(second.reshape(X, SLOTS, D // 2), "x", 0, 0, tiled=True)
    first_3, second_1 = shift(first, 1), shift(second, -1)
    second_3, first_1 = shift(second, 1), shift(first, -1)
    first_2, second_2 = shift(first_3, 1), shift(second_1, -1)
    rows = (first, second, first_1, second_1, first_2, second_2, first_3, second_3)
    results = []
    for lead in (True, False):
        hidden = hidden_rows(lead, place, rows, weights)
        hidden = lax.all_to_all(hidden, "y", 0, 0, tiled=True)
        results.append(lax.all_to_all(down_rows(lead, hidden, weights), ("y", "x"), 0, 0, tiled=True))
    return mix(shares, results)


def solution(mesh):
    grid = Mesh(mesh.devices.reshape(Y, C, X, Z), ("y", "c", "x", "z"))
    tokens = ("y", "c", "x", "z")
    group = ("x", "z")
    placed = (
        P(tokens, None),
        P(tokens, None),
        P(tokens, None),
        P(tokens),
        P(group, None),
        P(group, None),
        P(None, group),
    )
    return jax.shard_map(local, mesh=grid, in_specs=placed, out_specs=P(tokens, None), check_vma=False)
```

time: 175 us -> 178 us (1.017)
  blocking collectives: 33.6 us -> 12.3 us
  starting transfers between devices: 34.6 us -> 45.1 us
  Pallas kernels: 22.8 us -> 31.2 us
  waiting for transfers between devices: 60 us -> 65.9 us
    all_to_all x1 -> x0, blocking collectives: 21.3 us -> none  [local(): hidden = lax.all_to_all(hidden, 'y', 0, 0, tiled=True)]
    all_to_all x1 -> x4, starting transfers between devices: 4.8 us -> 15.5 us  [the longest x2 7.87 us: local(): lax.all_to_all(down_rows(lead, hidden, weights), ('y', 'x'), 0, 0, tiled=...]
    pallas_call x4 -> x7, Pallas kernels: 18.5 us -> 26.9 us  [the longest x2 12.4 us: hidden_rows(): pl.pallas_call(functools.partial(hidden_kernel, lead), grid=(2 * steps,),...]
    all_to_all x1 -> x4, waiting for transfers between devices: 15 us -> 21.6 us  [the longest x2 12.9 us: local(): lax.all_to_all(down_rows(lead, hidden, weights), ('y', 'x'), 0, 0, tiled=...]
    dynamic_slice x2 -> x0, local copies, waits for them, and re-layouts: 1.89 us -> none  [the longest x1 0.97 us: local(): up = lax.dynamic_slice(w_up, (c * HALF, y * FQ), (HALF, FQ))]
    unnamed x16 -> x22, local copies, waits for them, and re-layouts: 4.17 us -> 5.94 us
  transfers between devices with their start and end apart: 9 -> 12, of which waited for: 7 -> 10; matrix products, arithmetic and copies ran while one was open for 1% -> 1% of each run, Pallas kernels for 3% -> 13%
where the time goes in v3:
time: 178 us; the launch traced here: 175 us
  waiting for transfers between devices  65.9 us (37%)
  starting transfers between devices  45.1 us (25%)
  Pallas kernels  31.2 us (18%)
  between operations  14.2 us (8%)
  blocking collectives  12.3 us (7%)
  local copies, waits for them, and re-layouts  5.94 us (3%)
    ppermute x6, waiting for transfers between devices, shift(): return lax.ppermute(block, 'y', [(i, (i + by) % Y) for i in range(Y)])  26.5 us
    ppermute x6, starting transfers between devices, shift(): return lax.ppermute(block, 'y', [(i, (i + by) % Y) for i in range(Y)])  26.1 us
    all_gather x1, waiting for transfers between devices, local(): lax.all_gather(weights, ('z', 'c'))  15.7 us
    all_to_all x2, waiting for transfers between devices, local(): lax.all_to_all(down_rows(lead, hidden, weights), ('y', 'x'), 0, 0, tiled=...  12.9 us
    pallas_call x2, Pallas kernels, hidden_rows(): pl.pallas_call(functools.partial(hidden_kernel, lead), grid=(2 * steps,),...  12.4 us
    all_to_all x1, blocking collectives, local(): lax.all_to_all(first.reshape(X, SLOTS, D // 2), 'x', 0, 0, tiled=True)  12.3 us
    pallas_call x2, Pallas kernels, down_rows(): pl.pallas_call(functools.partial(down_kernel, lead), grid=(MEMBERS // 2,)...  9.22 us
    all_to_all x2, waiting for transfers between devices, local(): hidden = lax.all_to_all(hidden, 'y', 0, 0, tiled=True)  8.67 us
  transfers between devices with their start and end apart: 12, of which 10 were waited for; matrix products, arithmetic and copies ran while one was open for 1% of the time, Pallas kernels for 13%

profile of v3, /device:TPU:1, one launch (start us, length us, event | category | flops | bytes accessed | tf_op | source)
XLA Modules:
  0.0 175.2 jit_solution(5577015984910277755)
XLA Ops:
  6.5 0.0 all-gather.3.cloned.1.call-start
  6.5 0.6 pad_add_fusion.place_ref
  7.1 2.4 %shard_map.75 = bf16[384,512]{1,0:T(8,128)(2,1)} custom-call(s32[2]{0:T(128)} %pad_add_fusion.place_ref, bf16[512,1024]{1,0:T(8,128)(2,1)} %gate_ref.1, bf16[512,1024]{1,0:T(8,128)(2,1)} %up_ref.1, bf16[1024,512]{1,0:T(8,128)(2,1)} %refs_3_.1, bf16[1024,512]{1,0:T(8,128)(2,1)} %refs_3_.1, bf16[1024,512]{1,0:T(8,128)(2,1)} %refs_3_.1, bf16[1024,512]{1,0:T(8,128)(2,1)} %refs_3_.1), custom_call_target="tpu_custom_call" | custom-call | tf_op jit(solution)/shard_map/pallas_call | solution.py:241
  9.5 0.0 copy-start.5
  9.5 0.0 all-gather.3.cloned.1.call-update
  10.2 0.0 copy-start.1
  10.2 1.0 copy-done.1
  11.3 0.0 copy-start.6
  11.3 0.7 copy-done.6
  11.9 4.3 %shard_map.74 = (bf16[160,2048]{1,0:T(8,128)(2,1)S(1)}, bf16[160,2048]{1,0:T(8,128)(2,1)}) custom-call(s32[1]{0:T(128)S(6)} %copy.10.count_ref, s32[2,64]{1,0:T(2,128)S(1)} %bitcast.7, bf16[64,4096]{1,0:T(8,128)(2,1)S(1)} %copy-done.1), custom_call_target="tpu_custom_call" | custom-call | flops 83886080 | bytes 1835008 | tf_op jit(solution)/shard_map/pallas_call | solution.py:229
  16.2 12.3 %all_to_all.30.refs_0_ = bf16[4,40,2048]{2,1,0:T(8,128)(2,1)S(1)} all-to-all(bf16[4,40,2048]{2,1,0:T(8,128)(2,1)S(1)} %bitcast.6), channel_id=1, replica_groups=mesh['y'=4,'c'=2,'x'=4,'z'=16] {'x'}, dimensions={0} | all-to-all | bytes 1310720 | tf_op jit(solution)/shard_map/all_to_all | solution.py:325
  28.5 3.5 %all-to-all-start.1 = ((bf16[4,40,2048]{2,1,0:T(8,128)(2,1)}), bf16[4,40,2048]{2,1,0:T(8,128)(2,1)S(1)}, u32[]{:S(2)}, u32[]{:S(2)}) async-start(bf16[4,40,2048]{2,1,0:T(8,128)(2,1)} %bitcast.4), calls=%async_computation.1 | async-start | bytes 1310720 | tf_op jit(solution)/shard_map/all_to_all | solution.py:326
  32.0 5.5 %collective-permute-start.2 = (bf16[4,40,2048]{2,1,0:T(8,128)(2,1)S(1)}, bf16[4,40,2048]{2,1,0:T(8,128)(2,1)}, u32[]{:S(2)}, u32[]{:S(2)}) collective-permute-start(bf16[4,40,2048]{2,1,0:T(8,128)(2,1)S(1)} %all_to_all.30.refs_0_), channel_id=1, source_target_pairs={{0,128},{128,256},{256,384},{384,0},{1,129},{129,257},{257,385},{3... | collective-permute-start | bytes 1966088 | tf_op jit(solution)/shard_map/ppermute | solution.py:316
  37.5 2.1 %all-to-all-done.1.refs_1_ = bf16[4,40,2048]{2,1,0:T(8,128)(2,1)S(1)} async-done(((bf16[4,40,2048]{2,1,0:T(8,128)(2,1)}), bf16[4,40,2048]{2,1,0:T(8,128)(2,1)S(1)}, u32[]{:S(2)}, u32[]{:S(2)}) %all-to-all-start.1) | async-done | bytes 655392 | tf_op jit(solution)/shard_map/all_to_all | solution.py:326
  39.6 8.1 %collective-permute-start.1 = (bf16[4,40,2048]{2,1,0:T(8,128)(2,1)S(1)}, bf16[4,40,2048]{2,1,0:T(8,128)(2,1)S(1)}, u32[]{:S(2)}, u32[]{:S(2)}) collective-permute-start(bf16[4,40,2048]{2,1,0:T(8,128)(2,1)S(1)} %all-to-all-done.1.refs_1_), channel_id=1, source_target_pairs={{0,384},{128,0},{256,128},{384,256},{1,385},{129,1},{257,129},{385... | collective-permute-start | bytes 1966088 | tf_op jit(solution)/shard_map/ppermute | solution.py:316
  47.7 2.4 %collective-permute-start = (bf16[4,40,2048]{2,1,0:T(8,128)(2,1)S(1)}, bf16[4,40,2048]{2,1,0:T(8,128)(2,1)S(1)}, u32[]{:S(2)}, u32[]{:S(2)}) collective-permute-start(bf16[4,40,2048]{2,1,0:T(8,128)(2,1)S(1)} %all_to_all.30.refs_0_), channel_id=1, source_target_pairs={{0,384},{128,0},{256,128},{384,256},{1,385},{129,1},{257,129},{385... | collective-permute-start | bytes 1966088 | tf_op jit(solution)/shard_map/ppermute | solution.py:316
  50.1 2.9 %collective-permute-start.5 = (bf16[4,40,2048]{2,1,0:T(8,128)(2,1)S(1)}, bf16[4,40,2048]{2,1,0:T(8,128)(2,1)S(1)}, u32[]{:S(2)}, u32[]{:S(2)}) collective-permute-start(bf16[4,40,2048]{2,1,0:T(8,128)(2,1)S(1)} %all-to-all-done.1.refs_1_), channel_id=1, source_target_pairs={{0,128},{128,256},{256,384},{384,0},{1,129},{129,257},{257,385},{3... | collective-permute-start | bytes 1966088 | tf_op jit(solution)/shard_map/ppermute | solution.py:316
  53.0 0.0 collective-permute-done.2.refs_6_
  53.0 1.9 %collective-permute-start.3 = (bf16[4,40,2048]{2,1,0:T(8,128)(2,1)}, bf16[4,40,2048]{2,1,0:T(8,128)(2,1)S(1)}, u32[]{:S(2)}, u32[]{:S(2)}) collective-permute-start(bf16[4,40,2048]{2,1,0:T(8,128)(2,1)} %collective-permute-done.2.refs_6_), channel_id=1, source_target_pairs={{0,128},{128,256},{256,384},{384,0},{1,129},{129,257},{257,385},{3... | collective-permute-start | bytes 1966088 | tf_op jit(solution)/shard_map/ppermute | solution.py:316
  55.0 3.7 %collective-permute-done.1.refs_3_ = bf16[4,40,2048]{2,1,0:T(8,128)(2,1)S(1)} collective-permute-done((bf16[4,40,2048]{2,1,0:T(8,128)(2,1)S(1)}, bf16[4,40,2048]{2,1,0:T(8,128)(2,1)S(1)}, u32[]{:S(2)}, u32[]{:S(2)}) %collective-permute-start.1) | collective-permute-done | bytes 655392 | tf_op jit(solution)/shard_map/ppermute | solution.py:316
  58.7 5.3 %collective-permute-start.4 = (bf16[4,40,2048]{2,1,0:T(8,128)(2,1)S(1)}, bf16[4,40,2048]{2,1,0:T(8,128)(2,1)}, u32[]{:S(2)}, u32[]{:S(2)}) collective-permute-start(bf16[4,40,2048]{2,1,0:T(8,128)(2,1)S(1)} %collective-permute-done.1.refs_3_), channel_id=1, source_target_pairs={{0,384},{128,0},{256,128},{384,256},{1,385},{129,1},{257,129},{385... | collective-permute-start | bytes 1966088 | tf_op jit(solution)/shard_map/ppermute | solution.py:316
  64.0 8.7 %collective-permute-done.refs_2_ = bf16[4,40,2048]{2,1,0:T(8,128)(2,1)S(1)} collective-permute-done((bf16[4,40,2048]{2,1,0:T(8,128)(2,1)S(1)}, bf16[4,40,2048]{2,1,0:T(8,128)(2,1)S(1)}, u32[]{:S(2)}, u32[]{:S(2)}) %collective-permute-start) | collective-permute-done | bytes 655392 | tf_op jit(solution)/shard_map/ppermute | solution.py:316
  72.7 0.0 collective-permute-done.5.refs_7_
  72.7 0.0 copy-start.8
  72.8 7.2 %collective-permute-done.3.refs_4_ = bf16[4,40,2048]{2,1,0:T(8,128)(2,1)S(1)} collective-permute-done((bf16[4,40,2048]{2,1,0:T(8,128)(2,1)}, bf16[4,40,2048]{2,1,0:T(8,128)(2,1)S(1)}, u32[]{:S(2)}, u32[]{:S(2)}) %collective-permute-start.3) | collective-permute-done | bytes 655392 | tf_op jit(solution)/shard_map/ppermute | solution.py:316
  80.0 0.0 copy-done.8
  80.0 6.8 %collective-permute-done.4.refs_5_ = bf16[4,40,2048]{2,1,0:T(8,128)(2,1)} collective-permute-done((bf16[4,40,2048]{2,1,0:T(8,128)(2,1)S(1)}, bf16[4,40,2048]{2,1,0:T(8,128)(2,1)}, u32[]{:S(2)}, u32[]{:S(2)}) %collective-permute-start.4) | collective-permute-done | bytes 655392 | tf_op jit(solution)/shard_map/ppermute | solution.py:316
  86.8 15.7 %all-gather.3.cloned.1.call-done = bf16[12288,512]{1,0:T(8,128)(2,1)} async-done(((bf16[384,512]{1,0:T(8,128)(2,1)}), bf16[12288,512]{1,0:T(8,128)(2,1)}) %all-gather.3.cloned.1.call-update) | async-done | bytes 12582928 | tf_op jit(solution)/shard_map/all_gather | solution.py:322
  102.5 0.0 copy-start.4
  102.5 0.6 copy-done.4
  103.1 4.8 %shard_map.78 = bf16[4,16,16,256]{3,2,1,0:T(8,128)(2,1)S(1)} custom-call(s32[2]{0:T(128)S(1)} %copy-done.4, bf16[4,40,2048]{2,1,0:T(8,128)(2,1)S(1)} %all_to_all.30.refs_0_, bf16[4,40,2048]{2,1,0:T(8,128)(2,1)S(1)} %all-to-all-done.1.refs_1_, bf16[4,40,2048]{2,1,0:T(8,128)(2,1)S(1)} %collective-permute-done.refs_2_, ...), custom_call_target="tpu_custom_call" | custom-call | flops 1073741824 | bytes 9437184 | tf_op jit(solution)/shard_map/pallas_call | solution.py:271
  108.0 0.0 copy-start
  108.0 0.8 copy-done
  108.7 4.1 %all-to-all-start.4 = ((bf16[4,16,16,256]{3,2,1,0:T(8,128)(2,1)}), bf16[4,16,16,256]{3,2,1,0:T(8,128)(2,1)}, u32[]{:S(2)}, u32[]{:S(2)}) async-start(bf16[4,16,16,256]{3,2,1,0:T(8,128)(2,1)} %copy-done), calls=%async_computation.4 | async-start | bytes 1048576 | tf_op jit(solution)/shard_map/all_to_all | solution.py:334
  112.9 0.0 copy-done.5
  112.9 7.5 %shard_map.76 = bf16[4,16,24,256]{3,2,1,0:T(8,128)(2,1)} custom-call(s32[2]{0:T(128)S(1)} %copy-done.5, bf16[4,40,2048]{2,1,0:T(8,128)(2,1)S(1)} %all_to_all.30.refs_0_, bf16[4,40,2048]{2,1,0:T(8,128)(2,1)S(1)} %all-to-all-done.1.refs_1_, bf16[4,40,2048]{2,1,0:T(8,128)(2,1)S(1)} %collective-permute-done.refs_2_, ...), custom_call_target="tpu_custom_call" | custom-call | flops 1610612736 | bytes 13631488 | tf_op jit(solution)/shard_map/pallas_call | solution.py:271
  120.4 1.8 %all-to-all-done.4.hidden_ref = bf16[4,16,16,256]{3,2,1,0:T(8,128)(2,1)} async-done(((bf16[4,16,16,256]{3,2,1,0:T(8,128)(2,1)}), bf16[4,16,16,256]{3,2,1,0:T(8,128)(2,1)}, u32[]{:S(2)}, u32[]{:S(2)}) %all-to-all-start.4) | async-done | bytes 524320 | tf_op jit(solution)/shard_map/all_to_all | solution.py:334
  122.3 3.5 %all-to-all-start.2 = ((bf16[4,16,24,256]{3,2,1,0:T(8,128)(2,1)}), bf16[4,16,24,256]{3,2,1,0:T(8,128)(2,1)S(1)}, u32[]{:S(2)}, u32[]{:S(2)}) async-start(bf16[4,16,24,256]{3,2,1,0:T(8,128)(2,1)} %shard_map.76), calls=%async_computation.2 | async-start | bytes 1572864 | tf_op jit(solution)/shard_map/all_to_all | solution.py:334
  125.8 0.0 copy-start.7
  125.8 0.0 copy-start.9
  125.8 4.3 %shard_map.79 = bf16[16,16,1024]{2,1,0:T(8,128)(2,1)} custom-call(bf16[4,16,16,256]{3,2,1,0:T(8,128)(2,1)} %all-to-all-done.4.hidden_ref, bf16[2,8,2,384,512]{4,3,2,1,0:T(8,128)(2,1)} %bitcast.10), custom_call_target="tpu_custom_call" | custom-call | flops 536870912 | bytes 3145728 | tf_op jit(solution)/shard_map/pallas_call | solution.py:290
  130.1 6.8 %all-to-all-done.2.hidden_ref = bf16[4,16,24,256]{3,2,1,0:T(8,128)(2,1)S(1)} async-done(((bf16[4,16,24,256]{3,2,1,0:T(8,128)(2,1)}), bf16[4,16,24,256]{3,2,1,0:T(8,128)(2,1)S(1)}, u32[]{:S(2)}, u32[]{:S(2)}) %all-to-all-start.2) | async-done | bytes 786464 | tf_op jit(solution)/shard_map/all_to_all | solution.py:334
  136.9 4.3 %all-to-all-start.5 = ((bf16[16,16,1024]{2,1,0:T(8,128)(2,1)}), bf16[16,16,1024]{2,1,0:T(8,128)(2,1)S(1)}, u32[]{:S(2)}, u32[]{:S(2)}) async-start(bf16[16,16,1024]{2,1,0:T(8,128)(2,1)} %shard_map.79), calls=%async_computation.5 | async-start | bytes 1048576 | tf_op jit(solution)/shard_map/all_to_all | solution.py:335
  141.2 4.9 %shard_map.77 = bf16[16,24,1024]{2,1,0:T(8,128)(2,1)} custom-call(bf16[4,16,24,256]{3,2,1,0:T(8,128)(2,1)S(1)} %all-to-all-done.2.hidden_ref, bf16[2,8,2,384,512]{4,3,2,1,0:T(8,128)(2,1)} %bitcast.11), custom_call_target="tpu_custom_call" | custom-call | flops 805306368 | bytes 5767168 | tf_op jit(solution)/shard_map/pallas_call | solution.py:290
  146.1 4.4 %all-to-all-done.5.last_ref = bf16[16,16,1024]{2,1,0:T(8,128)(2,1)S(1)} async-done(((bf16[16,16,1024]{2,1,0:T(8,128)(2,1)}), bf16[16,16,1024]{2,1,0:T(8,128)(2,1)S(1)}, u32[]{:S(2)}, u32[]{:S(2)}) %all-to-all-start.5) | async-done | bytes 524320 | tf_op jit(solution)/shard_map/all_to_all | solution.py:335
  150.5 3.6 %all-to-all-start.3 = ((bf16[16,24,1024]{2,1,0:T(8,128)(2,1)}), bf16[16,24,1024]{2,1,0:T(8,128)(2,1)S(1)}, u32[]{:S(2)}, u32[]{:S(2)}) async-start(bf16[16,24,1024]{2,1,0:T(8,128)(2,1)} %shard_map.77), calls=%async_computation.3 | async-start | bytes 1572864 | tf_op jit(solution)/shard_map/all_to_all | solution.py:335
  154.1 0.0 copy-done.7
  154.2 0.7 copy.8.routes_ref
  154.9 0.0 copy-done.9
  154.9 0.7 copy.9.numerators_ref
  155.6 1.6 shard_map.73
  157.2 8.5 %all-to-all-done.3.lead_ref = bf16[16,24,1024]{2,1,0:T(8,128)(2,1)S(1)} async-done(((bf16[16,24,1024]{2,1,0:T(8,128)(2,1)}), bf16[16,24,1024]{2,1,0:T(8,128)(2,1)S(1)}, u32[]{:S(2)}, u32[]{:S(2)}) %all-to-all-start.3) | async-done | bytes 786464 | tf_op jit(solution)/shard_map/all_to_all | solution.py:335
  165.7 0.0 copy-start.2
  165.7 0.7 copy-done.2
  166.4 0.0 copy-start.3
  166.4 0.7 copy-done.3
  167.1 1.2 shard_map.80
Async XLA Ops:
  6.5 96.0 %all-gather.3.cloned.1.call-start = ((), (), s32[]{:S(2)}) async-start(), calls=%async_computation.6 | async-start | bytes 12976128 | tf_op jit(solution)/shard_map/all_gather | solution.py:322
  9.5 103.4 %copy-start.5 = (s32[2]{0:T(128)S(1)}, s32[2]{0:T(128)}, u32[]{:S(2)}) copy-start(s32[2]{0:T(128)} %pad_add_fusion.place_ref) | copy-start | bytes 28
  10.2 1.0 copy-start.1
  11.3 0.7 copy-start.6
  28.5 11.1 %all-to-all-start.1 = ((bf16[4,40,2048]{2,1,0:T(8,128)(2,1)}), bf16[4,40,2048]{2,1,0:T(8,128)(2,1)S(1)}, u32[]{:S(2)}, u32[]{:S(2)}) async-start(bf16[4,40,2048]{2,1,0:T(8,128)(2,1)} %bitcast.4), calls=%async_computation.1 | async-start | bytes 1310720 | tf_op jit(solution)/shard_map/all_to_all | solution.py:326
  32.0 21.0 %collective-permute-start.2 = (bf16[4,40,2048]{2,1,0:T(8,128)(2,1)S(1)}, bf16[4,40,2048]{2,1,0:T(8,128)(2,1)}, u32[]{:S(2)}, u32[]{:S(2)}) collective-permute-start(bf16[4,40,2048]{2,1,0:T(8,128)(2,1)S(1)} %all_to_all.30.refs_0_), channel_id=1, source_target_pairs={{0,128},{128,256},{256,384},{384,0},{1,129},{129,257},{257,385},{3... | collective-permute-start | bytes 1966088 | tf_op jit(solution)/shard_map/ppermute | solution.py:316
  39.6 19.1 %collective-permute-start.1 = (bf16[4,40,2048]{2,1,0:T(8,128)(2,1)S(1)}, bf16[4,40,2048]{2,1,0:T(8,128)(2,1)S(1)}, u32[]{:S(2)}, u32[]{:S(2)}) collective-permute-start(bf16[4,40,2048]{2,1,0:T(8,128)(2,1)S(1)} %all-to-all-done.1.refs_1_), channel_id=1, source_target_pairs={{0,384},{128,0},{256,128},{384,256},{1,385},{129,1},{257,129},{385... | collective-permute-start | bytes 1966088 | tf_op jit(solution)/shard_map/ppermute | solution.py:316
  47.7 25.0 %collective-permute-start = (bf16[4,40,2048]{2,1,0:T(8,128)(2,1)S(1)}, bf16[4,40,2048]{2,1,0:T(8,128)(2,1)S(1)}, u32[]{:S(2)}, u32[]{:S(2)}) collective-permute-start(bf16[4,40,2048]{2,1,0:T(8,128)(2,1)S(1)} %all_to_all.30.refs_0_), channel_id=1, source_target_pairs={{0,384},{128,0},{256,128},{384,256},{1,385},{129,1},{257,129},{385... | collective-permute-start | bytes 1966088 | tf_op jit(solution)/shard_map/ppermute | solution.py:316
  50.1 22.6 %collective-permute-start.5 = (bf16[4,40,2048]{2,1,0:T(8,128)(2,1)S(1)}, bf16[4,40,2048]{2,1,0:T(8,128)(2,1)S(1)}, u32[]{:S(2)}, u32[]{:S(2)}) collective-permute-start(bf16[4,40,2048]{2,1,0:T(8,128)(2,1)S(1)} %all-to-all-done.1.refs_1_), channel_id=1, source_target_pairs={{0,128},{128,256},{256,384},{384,0},{1,129},{129,257},{257,385},{3... | collective-permute-start | bytes 1966088 | tf_op jit(solution)/shard_map/ppermute | solution.py:316
  53.0 27.0 %collective-permute-start.3 = (bf16[4,40,2048]{2,1,0:T(8,128)(2,1)}, bf16[4,40,2048]{2,1,0:T(8,128)(2,1)S(1)}, u32[]{:S(2)}, u32[]{:S(2)}) collective-permute-start(bf16[4,40,2048]{2,1,0:T(8,128)(2,1)} %collective-permute-done.2.refs_6_), channel_id=1, source_target_pairs={{0,128},{128,256},{256,384},{384,0},{1,129},{129,257},{257,385},{3... | collective-permute-start | bytes 1966088 | tf_op jit(solution)/shard_map/ppermute | solution.py:316
  58.7 28.1 %collective-permute-start.4 = (bf16[4,40,2048]{2,1,0:T(8,128)(2,1)S(1)}, bf16[4,40,2048]{2,1,0:T(8,128)(2,1)}, u32[]{:S(2)}, u32[]{:S(2)}) collective-permute-start(bf16[4,40,2048]{2,1,0:T(8,128)(2,1)S(1)} %collective-permute-done.1.refs_3_), channel_id=1, source_target_pairs={{0,384},{128,0},{256,128},{384,256},{1,385},{129,1},{257,129},{385... | collective-permute-start | bytes 1966088 | tf_op jit(solution)/shard_map/ppermute | solution.py:316
  72.7 7.3 %copy-start.8 = (bf16[4,40,2048]{2,1,0:T(8,128)(2,1)}, bf16[4,40,2048]{2,1,0:T(8,128)(2,1)S(1)}, u32[]{:S(2)}) copy-start(bf16[4,40,2048]{2,1,0:T(8,128)(2,1)S(1)} %collective-permute-done.5.refs_7_) | copy-start | bytes 1966084
  102.5 0.6 copy-start.4
  108.0 0.8 copy-start
  108.7 13.5 %all-to-all-start.4 = ((bf16[4,16,16,256]{3,2,1,0:T(8,128)(2,1)}), bf16[4,16,16,256]{3,2,1,0:T(8,128)(2,1)}, u32[]{:S(2)}, u32[]{:S(2)}) async-start(bf16[4,16,16,256]{3,2,1,0:T(8,128)(2,1)} %copy-done), calls=%async_computation.4 | async-start | bytes 1048576 | tf_op jit(solution)/shard_map/all_to_all | solution.py:334
  122.3 14.7 %all-to-all-start.2 = ((bf16[4,16,24,256]{3,2,1,0:T(8,128)(2,1)}), bf16[4,16,24,256]{3,2,1,0:T(8,128)(2,1)S(1)}, u32[]{:S(2)}, u32[]{:S(2)}) async-start(bf16[4,16,24,256]{3,2,1,0:T(8,128)(2,1)} %shard_map.76), calls=%async_computation.2 | async-start | bytes 1572864 | tf_op jit(solution)/shard_map/all_to_all | solution.py:334
  125.8 28.4 %copy-start.7 = (s32[64,2]{0,1:T(2,128)S(1)}, s32[64,2]{0,1:T(2,128)}, u32[]{:S(2)}) copy-start(s32[64,2]{0,1:T(2,128)} %param.8) | copy-start | bytes 1540
  125.8 29.1 %copy-start.9 = (s32[64,2]{0,1:T(2,128)S(1)}, s32[64,2]{0,1:T(2,128)}, u32[]{:S(2)}) copy-start(s32[64,2]{0,1:T(2,128)} %param.9) | copy-start | bytes 1540
  136.9 13.6 %all-to-all-start.5 = ((bf16[16,16,1024]{2,1,0:T(8,128)(2,1)}), bf16[16,16,1024]{2,1,0:T(8,128)(2,1)S(1)}, u32[]{:S(2)}, u32[]{:S(2)}) async-start(bf16[16,16,1024]{2,1,0:T(8,128)(2,1)} %shard_map.79), calls=%async_computation.5 | async-start | bytes 1048576 | tf_op jit(solution)/shard_map/all_to_all | solution.py:335
  150.5 15.2 %all-to-all-start.3 = ((bf16[16,24,1024]{2,1,0:T(8,128)(2,1)}), bf16[16,24,1024]{2,1,0:T(8,128)(2,1)S(1)}, u32[]{:S(2)}, u32[]{:S(2)}) async-start(bf16[16,24,1024]{2,1,0:T(8,128)(2,1)} %shard_map.77), calls=%async_computation.3 | async-start | bytes 1572864 | tf_op jit(solution)/shard_map/all_to_all | solution.py:335
  165.7 0.7 copy-start.2
  166.4 0.7 copy-start.3
Sparse Core Ops, SparseCore 0:
  9.7 92.7 all-gather.2

commit v4 on v3

v4 whole, which is shorter than its diff:
```python
import jax
import jax.numpy as jnp
from jax import lax
from jax.experimental import pallas as pl
from jax.experimental.pallas import tpu as pltpu
from jax.sharding import Mesh
from jax.sharding import PartitionSpec as P

Y, C, X, Z = 4, 2, 4, 16
D, F, TOK = 4096, 1024, 64
SHARD = 512
MEMBERS = 8
CAP = 20
SLOTS = 2 * CAP
MAIN = 16
REST = SLOTS - 2 * MAIN
LEAD = MAIN + REST
SRC = Y * X
ROWS = SRC * SLOTS
ALL_SLOTS = X * SLOTS
FQ = F // Y
HALF = SHARD // 2
WIDE = 4


def slot_at(at):
    second = (at >= MAIN + REST // 2).astype(jnp.int32)
    slot = jnp.where(at < MAIN + REST // 2, at, jnp.where(at < LEAD, at - REST // 2, at - LEAD))
    return second, slot


def pack_kernel(gate_ref, up_ref, down_ref, out_ref, packed, sems):
    y, c = lax.axis_index("y"), lax.axis_index("c")
    rows = pl.ds(pl.multiple_of(c * HALF, HALF), HALF)
    columns = pl.ds(pl.multiple_of(y * FQ, FQ), FQ)
    copies = [
        pltpu.make_async_copy(gate_ref.at[rows, columns], packed.at[:HALF, :FQ], sems.at[0]),
        pltpu.make_async_copy(up_ref.at[rows, columns], packed.at[:HALF, FQ:], sems.at[1]),
    ]
    columns = pl.ds(pl.multiple_of(y * 128, 128), 128)
    for quarter in range(Y):
        rows = pl.ds(pl.multiple_of(quarter * FQ + c * 128, 128), 128)
        to = packed.at[HALF:, quarter * 128 : (quarter + 1) * 128]
        copies.append(pltpu.make_async_copy(down_ref.at[rows, columns], to, sems.at[2 + quarter]))
    for copy in copies:
        copy.start()
    for copy in copies:
        copy.wait()
    copy = pltpu.make_async_copy(packed, out_ref, sems.at[2 + Y])
    copy.start()
    copy.wait()


def restore(v):
    scale = (jnp.max(jnp.abs(v), axis=1, keepdims=True) + 1e-06) / 448.0
    scaled = v / scale
    x = jnp.abs(scaled)
    spacing = jnp.full_like(x, 2.0**-9)
    for shift, least in ((8, 2.0**2), (4, 2.0**-2), (2, 2.0**-4), (1, 2.0**-5)):
        big = x >= least
        x = jnp.where(big, x * 2.0**-shift, x)
        spacing = jnp.where(big, spacing * 2.0**shift, spacing)
    snapped = jnp.floor(x * 512.0 + 0.5) * spacing
    coded = jnp.where(scaled < 0.0, -snapped, snapped)
    return (coded * scale).astype(jnp.bfloat16)


def places(dims, axis):
    place = lax.broadcasted_iota(jnp.int32, dims, axis)
    column = (place * 1639) >> 16
    second, slot = slot_at(place - column * SLOTS)
    return 2 * column + second, slot


def earlier_rows(axis):
    first, second = (lax.broadcasted_iota(jnp.int32, (TOK, TOK), a) for a in (axis, 1 - axis))
    return (first < second).astype(jnp.float32).astype(jnp.bfloat16)


def encode_kernel(count_ref, columns_ref, tokens_ref, first_ref, second_ref):
    dims = (ALL_SLOTS, TOK)
    expert, slot = places(dims, 0)
    named = (columns_ref[0:1, :] == expert) | (columns_ref[1:2, :] == expert)
    named = named & (lax.broadcasted_iota(jnp.int32, dims, 1) < count_ref[0])
    one = named.astype(jnp.float32).astype(jnp.bfloat16)
    rank = jnp.dot(one, earlier_rows(0), preferred_element_type=jnp.float32)
    chosen = named & (rank.astype(jnp.int32) == slot)
    chosen = chosen.astype(jnp.float32).astype(jnp.bfloat16)

    def step(member, carry):
        for half, out_ref in enumerate((first_ref, second_ref)):
            start = pl.multiple_of(member * SHARD + half * HALF, HALF)
            values = tokens_ref[:, pl.ds(start, HALF)].astype(jnp.float32)
            restored = jnp.concatenate([restore(values[:, b * 128 : (b + 1) * 128]) for b in range(HALF // 128)], axis=1)
            rows = jnp.dot(chosen, restored, preferred_element_type=jnp.float32)
            out_ref[:, pl.ds(pl.multiple_of(member * HALF, HALF), HALF)] = rows.astype(jnp.bfloat16)
        return carry

    lax.fori_loop(0, MEMBERS, step, 0)


def mix_kernel(count_ref, routes_ref, numerators_ref, rows_ref, out_ref):
    dims = (TOK, ALL_SLOTS)
    expert, slot = places(dims, 1)
    live = lax.broadcasted_iota(jnp.int32, dims, 0) < count_ref[0]
    by_first = (routes_ref[:, 0:1] == expert) & live
    by_second = (routes_ref[:, 1:2] == expert) & live
    one = (by_first | by_second).astype(jnp.float32).astype(jnp.bfloat16)
    rank = jnp.dot(earlier_rows(1), one, preferred_element_type=jnp.float32)
    here = rank.astype(jnp.int32) == slot
    share = numerators_ref[...].astype(jnp.float32) / 256.0
    shares = jnp.where(by_first & here, share[:, 0:1], 0.0) + jnp.where(by_second & here, share[:, 1:2], 0.0)
    shares = shares.astype(jnp.bfloat16)
    for quarter in range(Y):
        rows = rows_ref[quarter * X : (quarter + 1) * X].reshape(ALL_SLOTS, MEMBERS * 128)
        mixed = jnp.dot(shares, rows, preferred_element_type=jnp.float32).astype(jnp.bfloat16)
        for member in range(MEMBERS):
            at = member * SHARD + quarter * 128
            out_ref[:, at : at + 128] = mixed[:, member * 128 : (member + 1) * 128]


def run_of(block, start, length):
    n = block.shape[-1]
    return block[:, start : start + length].astype(jnp.float32).reshape(-1, n).astype(jnp.bfloat16)


def mixed_rows(first, second):
    place = lax.broadcasted_iota(jnp.int32, first.shape, 0)
    return jnp.where((place & (REST - 1)) < REST // 2, first, second)


def sources(rows, length):
    return rows.reshape(-1, length, rows.shape[-1])


def swish(total):
    gate = total[:, :FQ]
    return gate / (1.0 + jnp.exp(-gate)) * total[:, FQ:]


def hidden_kernel(place_ref, *refs):
    rows, weights_ref, out_ref, sums = refs[: 2 * Y], refs[2 * Y], refs[2 * Y + 1], refs[2 * Y + 2 :]
    main = SRC * MAIN

    def add(parts, start):
        blocks = [ref[...] for ref in parts]
        mixed = [run_of(b, MAIN, REST) for b in blocks]
        for expert, total in enumerate(sums):
            group = [run_of(b, expert * LEAD, MAIN) for b in blocks] + mixed
            weights = weights_ref[expert, :, 0].reshape(MEMBERS * HALF, 2 * FQ)
            product = jnp.dot(jnp.concatenate(group, axis=0), weights, preferred_element_type=jnp.float32)
            total[...] = product if start else total[...] + product

    @pl.when(pl.program_id(0) == 0)
    def _():
        add(rows[0::2], True)

    @pl.when(pl.program_id(0) == 1)
    def _():
        add(rows[1::2], False)
        first, second = (swish(total[...]) for total in sums)
        mixed = mixed_rows(first[main:], second[main:])
        joined = [sources(first[:main], MAIN), sources(mixed, REST), sources(second[:main], MAIN)]
        joined = jnp.concatenate(joined, axis=1).astype(jnp.bfloat16)
        for offset in range(Y):
            source = lax.rem(place_ref[0] + offset, Y)
            block = joined[offset * X : (offset + 1) * X]
            for copy in range(Y):
                out_ref[copy, pl.ds(source * X, X)] = block


def down_kernel(hidden_ref, weights_ref, out_ref, *rows):
    main = SRC * MAIN

    @pl.when(pl.program_id(0) == 0)
    def _():
        for quarter in range(Y):
            block = hidden_ref[quarter]
            at = slice(quarter * FQ, (quarter + 1) * FQ)
            mixed = run_of(block, MAIN, REST)
            for expert in range(2):
                rows[expert][:main, at] = run_of(block, expert * LEAD, MAIN)
                rows[expert][main:, at] = mixed

    def result(expert):
        weights = jnp.concatenate(
            [
                jnp.concatenate([weights_ref[expert, m, half, :, q * 128 : (q + 1) * 128] for m in range(WIDE)], axis=1)
                for q in range(Y)
                for half in range(C)
            ],
            axis=0,
        )
        return jnp.dot(rows[expert][...], weights, preferred_element_type=jnp.float32)

    first, second = result(0), result(1)
    mixed = mixed_rows(first[main:], second[main:])
    joined = [sources(first[:main], MAIN), sources(mixed, REST), sources(second[:main], MAIN)]
    out_ref[...] = jnp.concatenate(joined, axis=1).astype(jnp.bfloat16)


SCALAR = pl.BlockSpec(memory_space=pltpu.SMEM)
WHOLE = pl.BlockSpec(memory_space=pltpu.VMEM)
ANY = pl.BlockSpec(memory_space=pl.ANY)


def shape(dims):
    return jax.ShapeDtypeStruct(dims, jnp.bfloat16)


def params(mebibytes):
    return pltpu.CompilerParams(vmem_limit_bytes=mebibytes << 20)


def encode(counts, routes, tokens):
    return pl.pallas_call(
        encode_kernel,
        out_shape=[shape((ALL_SLOTS, D // 2))] * 2,
        in_specs=[SCALAR, WHOLE, WHOLE],
        out_specs=[WHOLE] * 2,
        compiler_params=params(8),
        cost_estimate=pl.CostEstimate(flops=2 * ALL_SLOTS * TOK * D, bytes_accessed=2 * (TOK + ALL_SLOTS) * D, transcendentals=0),
    )(counts, routes.T, tokens)


def pack(w_gate, w_up, w_down):
    return pl.pallas_call(
        pack_kernel,
        out_shape=shape((HALF + 128, SHARD)),
        in_specs=[ANY] * 3,
        out_specs=ANY,
        scratch_shapes=[pltpu.VMEM((HALF + 128, SHARD), jnp.bfloat16), pltpu.SemaphoreType.DMA((3 + Y,))],
    )(w_gate, w_up, w_down)


def hidden_rows(place, rows, weights):
    return pl.pallas_call(
        hidden_kernel,
        grid=(2,),
        out_shape=shape((Y, SRC, SLOTS, FQ)),
        in_specs=[SCALAR, *[WHOLE] * (2 * Y), pl.BlockSpec((2, MEMBERS, 1, HALF, 2 * FQ), lambda k: (0, 0, k, 0, 0))],
        out_specs=pl.BlockSpec((Y, SRC, SLOTS, FQ), lambda k: (0, 0, 0, 0)),
        scratch_shapes=[pltpu.VMEM((SRC * (MAIN + REST), 2 * FQ), jnp.float32)] * 2,
        compiler_params=params(36),
        cost_estimate=pl.CostEstimate(flops=2 * ROWS * D * 2 * FQ, bytes_accessed=2 * ROWS * D + 8 * D * FQ, transcendentals=0),
    )(place, *rows, weights)


def down_rows(hidden, weights):
    return pl.pallas_call(
        down_kernel,
        grid=(MEMBERS // WIDE,),
        out_shape=shape((SRC, SLOTS, MEMBERS * 128)),
        in_specs=[WHOLE, pl.BlockSpec((2, WIDE, C, 128, SHARD), lambda n: (0, n, 0, HALF // 128, 0))],
        out_specs=pl.BlockSpec((SRC, SLOTS, WIDE * 128), lambda n: (0, 0, n)),
        scratch_shapes=[pltpu.VMEM((SRC * (MAIN + REST), F), jnp.bfloat16)] * 2,
        compiler_params=params(24),
        cost_estimate=pl.CostEstimate(flops=2 * ROWS * F * F, bytes_accessed=4 * ROWS * F + 4 * F * F, transcendentals=0),
    )(hidden, weights)


def mix(counts, routes, numerators, rows):
    return pl.pallas_call(
        mix_kernel,
        out_shape=shape((TOK, D)),
        in_specs=[SCALAR] + [WHOLE] * 3,
        out_specs=WHOLE,
        compiler_params=params(8),
    )(counts, routes, numerators, rows)


def shift(block, by):
    return lax.ppermute(block, "y", [(i, (i + by) % Y) for i in range(Y)])


def local(tokens, routes, numerators, counts, w_gate, w_up, w_down):
    place = lax.axis_index("y").astype(jnp.int32).reshape(1)
    weights = pack(w_gate, w_up, w_down)
    weights = lax.all_gather(weights, ("z", "c")).reshape(2, MEMBERS, C, HALF + 128, SHARD)
    first, second = encode(counts, routes, tokens)
    first = lax.all_to_all(first.reshape(X, SLOTS, D // 2), "x", 0, 0, tiled=True)
    second = lax.all_to_all(second.reshape(X, SLOTS, D // 2), "x", 0, 0, tiled=True)
    first_3, second_1 = shift(first, 1), shift(second, -1)
    second_3, first_1 = shift(second, 1), shift(first, -1)
    first_2, second_2 = shift(first_3, 1), shift(second_1, -1)
    rows = (first, second, first_1, second_1, first_2, second_2, first_3, second_3)
    hidden = lax.all_to_all(hidden_rows(place, rows, weights), "y", 0, 0, tiled=True)
    result = lax.all_to_all(down_rows(hidden, weights), ("y", "x"), 0, 0, tiled=True)
    return mix(counts, routes, numerators, result)


def solution(mesh):
    grid = Mesh(mesh.devices.reshape(Y, C, X, Z), ("y", "c", "x", "z"))
    tokens = ("y", "c", "x", "z")
    group = ("x", "z")
    placed = (
        P(tokens, None),
        P(tokens, None),
        P(tokens, None),
        P(tokens),
        P(group, None),
        P(group, None),
        P(None, group),
    )
    return jax.shard_map(local, mesh=grid, in_specs=placed, out_specs=P(tokens, None), check_vma=False)
```

time: 178 us -> 166 us (0.933)
  blocking collectives: 12.3 us -> 33.4 us
  Pallas kernels: 31.2 us -> 17.5 us
  starting transfers between devices: 45.1 us -> 34.5 us
  local copies, waits for them, and re-layouts: 5.94 us -> 0.21 us
    all_to_all x0 -> x1, blocking collectives: none -> 21.1 us  [local(): lax.all_to_all(hidden_rows(place, rows, weights), 'y', 0, 0, tiled=True)]
    pallas_call x7 -> x4, Pallas kernels: 26.9 us -> 13.2 us  [the longest x1 6.62 us: hidden_rows(): pl.pallas_call(hidden_kernel, grid=(2,), out_shape=shape((Y, SRC, SLOTS,...]
    all_to_all x4 -> x1, starting transfers between devices: 15.5 us -> 4.83 us  [local(): lax.all_to_all(down_rows(hidden, weights), ('y', 'x'), 0, 0, tiled=True)]
    unnamed x22 -> x10, local copies, waits for them, and re-layouts: 5.94 us -> 0.21 us
    all_to_all x4 -> x1, waiting for transfers between devices: 21.6 us -> 17.9 us  [local(): lax.all_to_all(down_rows(hidden, weights), ('y', 'x'), 0, 0, tiled=True)]
    all_gather x1, waiting for transfers between devices: 15.7 us -> 18.5 us  [local(): lax.all_gather(weights, ('z', 'c'))]
  transfers between devices with their start and end apart: 12 -> 9, of which waited for: 10 -> 7; matrix products, arithmetic and copies ran while one was open for 1% -> 0% of each run, Pallas kernels for 13% -> 3%
where the time goes in v4:
time: 166 us; the launch traced here: 165 us
  waiting for transfers between devices  64.8 us (39%)
  starting transfers between devices  34.5 us (21%)
  blocking collectives  33.4 us (20%)
  Pallas kernels  17.5 us (11%)
  between operations  14.2 us (9%)
    ppermute x6, waiting for transfers between devices, shift(): return lax.ppermute(block, 'y', [(i, (i + by) % Y) for i in range(Y)])  26.3 us
    ppermute x6, starting transfers between devices, shift(): return lax.ppermute(block, 'y', [(i, (i + by) % Y) for i in range(Y)])  26.2 us
    all_to_all x1, blocking collectives, local(): lax.all_to_all(hidden_rows(place, rows, weights), 'y', 0, 0, tiled=True)  21.1 us
    all_gather x1, waiting for transfers between devices, local(): lax.all_gather(weights, ('z', 'c'))  18.5 us
    all_to_all x1, waiting for transfers between devices, local(): lax.all_to_all(down_rows(hidden, weights), ('y', 'x'), 0, 0, tiled=True)  17.9 us
    all_to_all x1, blocking collectives, local(): lax.all_to_all(first.reshape(X, SLOTS, D // 2), 'x', 0, 0, tiled=True)  12.3 us
    pallas_call x1, Pallas kernels, hidden_rows(): pl.pallas_call(hidden_kernel, grid=(2,), out_shape=shape((Y, SRC, SLOTS,...  6.62 us
    all_to_all x1, starting transfers between devices, local(): lax.all_to_all(down_rows(hidden, weights), ('y', 'x'), 0, 0, tiled=True)  4.83 us
  transfers between devices with their start and end apart: 9, of which 7 were waited for; matrix products, arithmetic and copies ran while one was open for 0% of the time, Pallas kernels for 3%

profile of v4, /device:TPU:1, one launch (start us, length us, event | category | flops | bytes accessed | tf_op | source)
XLA Modules:
  0.0 164.5 jit_solution(5843627335211985328)
XLA Ops:
  6.5 0.0 copy-start.2
  6.5 0.0 copy-start.1
  6.5 0.0 all-gather.3.cloned.1.call-start
  6.5 1.8 %shard_map.74 = bf16[384,512]{1,0:T(8,128)(2,1)} custom-call(bf16[512,1024]{1,0:T(8,128)(2,1)} %gate_ref.1, bf16[512,1024]{1,0:T(8,128)(2,1)} %up_ref.1, bf16[1024,512]{1,0:T(8,128)(2,1)} %down_ref.1), custom_call_target="tpu_custom_call" | custom-call | tf_op jit(solution)/shard_map/pallas_call | solution.py:227
  8.4 0.0 all-gather.3.cloned.1.call-update
  9.1 0.0 copy-done.2
  9.1 0.0 copy-done.1
  9.1 4.3 %shard_map.73 = (bf16[160,2048]{1,0:T(8,128)(2,1)S(1)}, bf16[160,2048]{1,0:T(8,128)(2,1)}) custom-call(s32[1]{0:T(128)S(6)} %copy.10.count_ref, s32[2,64]{1,0:T(2,128)S(1)} %bitcast.8, bf16[64,4096]{1,0:T(8,128)(2,1)S(1)} %copy-done.1), custom_call_target="tpu_custom_call" | custom-call | flops 83886080 | bytes 1835008 | tf_op jit(solution)/shard_map/pallas_call | solution.py:216
  13.4 12.3 %all_to_all.20.refs_0_ = bf16[4,40,2048]{2,1,0:T(8,128)(2,1)S(1)} all-to-all(bf16[4,40,2048]{2,1,0:T(8,128)(2,1)S(1)} %bitcast.7), channel_id=1, replica_groups=mesh['y'=4,'c'=2,'x'=4,'z'=16] {'x'}, dimensions={0} | all-to-all | bytes 1310720 | tf_op jit(solution)/shard_map/all_to_all | solution.py:281
  25.7 3.5 %all-to-all-start.1 = ((bf16[4,40,2048]{2,1,0:T(8,128)(2,1)}), bf16[4,40,2048]{2,1,0:T(8,128)(2,1)S(1)}, u32[]{:S(2)}, u32[]{:S(2)}) async-start(bf16[4,40,2048]{2,1,0:T(8,128)(2,1)} %bitcast.3), calls=%async_computation.1 | async-start | bytes 1310720 | tf_op jit(solution)/shard_map/all_to_all | solution.py:282
  29.2 5.5 %collective-permute-start.2 = (bf16[4,40,2048]{2,1,0:T(8,128)(2,1)S(1)}, bf16[4,40,2048]{2,1,0:T(8,128)(2,1)S(1)}, u32[]{:S(2)}, u32[]{:S(2)}) collective-permute-start(bf16[4,40,2048]{2,1,0:T(8,128)(2,1)S(1)} %all_to_all.20.refs_0_), channel_id=1, source_target_pairs={{0,128},{128,256},{256,384},{384,0},{1,129},{129,257},{257,385},{3... | collective-permute-start | bytes 1966088 | tf_op jit(solution)/shard_map/ppermute | solution.py:273
  34.7 2.1 %all-to-all-done.1.refs_1_ = bf16[4,40,2048]{2,1,0:T(8,128)(2,1)S(1)} async-done(((bf16[4,40,2048]{2,1,0:T(8,128)(2,1)}), bf16[4,40,2048]{2,1,0:T(8,128)(2,1)S(1)}, u32[]{:S(2)}, u32[]{:S(2)}) %all-to-all-start.1) | async-done | bytes 655392 | tf_op jit(solution)/shard_map/all_to_all | solution.py:282
  36.8 8.1 %collective-permute-start.1 = (bf16[4,40,2048]{2,1,0:T(8,128)(2,1)S(1)}, bf16[4,40,2048]{2,1,0:T(8,128)(2,1)S(1)}, u32[]{:S(2)}, u32[]{:S(2)}) collective-permute-start(bf16[4,40,2048]{2,1,0:T(8,128)(2,1)S(1)} %all-to-all-done.1.refs_1_), channel_id=1, source_target_pairs={{0,384},{128,0},{256,128},{384,256},{1,385},{129,1},{257,129},{385... | collective-permute-start | bytes 1966088 | tf_op jit(solution)/shard_map/ppermute | solution.py:273
  44.8 2.4 %collective-permute-start = (bf16[4,40,2048]{2,1,0:T(8,128)(2,1)S(1)}, bf16[4,40,2048]{2,1,0:T(8,128)(2,1)S(1)}, u32[]{:S(2)}, u32[]{:S(2)}) collective-permute-start(bf16[4,40,2048]{2,1,0:T(8,128)(2,1)S(1)} %all_to_all.20.refs_0_), channel_id=1, source_target_pairs={{0,384},{128,0},{256,128},{384,256},{1,385},{129,1},{257,129},{385... | collective-permute-start | bytes 1966088 | tf_op jit(solution)/shard_map/ppermute | solution.py:273
  47.2 2.9 %collective-permute-start.5 = (bf16[4,40,2048]{2,1,0:T(8,128)(2,1)S(1)}, bf16[4,40,2048]{2,1,0:T(8,128)(2,1)}, u32[]{:S(2)}, u32[]{:S(2)}) collective-permute-start(bf16[4,40,2048]{2,1,0:T(8,128)(2,1)S(1)} %all-to-all-done.1.refs_1_), channel_id=1, source_target_pairs={{0,128},{128,256},{256,384},{384,0},{1,129},{129,257},{257,385},{3... | collective-permute-start | bytes 1966088 | tf_op jit(solution)/shard_map/ppermute | solution.py:273
  50.1 0.0 collective-permute-done.2.refs_6_
  50.1 1.9 %collective-permute-start.3 = (bf16[4,40,2048]{2,1,0:T(8,128)(2,1)S(1)}, bf16[4,40,2048]{2,1,0:T(8,128)(2,1)}, u32[]{:S(2)}, u32[]{:S(2)}) collective-permute-start(bf16[4,40,2048]{2,1,0:T(8,128)(2,1)S(1)} %collective-permute-done.2.refs_6_), channel_id=1, source_target_pairs={{0,128},{128,256},{256,384},{384,0},{1,129},{129,257},{257,385},{3... | collective-permute-start | bytes 1966088 | tf_op jit(solution)/shard_map/ppermute | solution.py:273
  52.1 3.7 %collective-permute-done.1.refs_3_ = bf16[4,40,2048]{2,1,0:T(8,128)(2,1)S(1)} collective-permute-done((bf16[4,40,2048]{2,1,0:T(8,128)(2,1)S(1)}, bf16[4,40,2048]{2,1,0:T(8,128)(2,1)S(1)}, u32[]{:S(2)}, u32[]{:S(2)}) %collective-permute-start.1) | collective-permute-done | bytes 655392 | tf_op jit(solution)/shard_map/ppermute | solution.py:273
  55.7 5.4 %collective-permute-start.4 = (bf16[4,40,2048]{2,1,0:T(8,128)(2,1)S(1)}, bf16[4,40,2048]{2,1,0:T(8,128)(2,1)}, u32[]{:S(2)}, u32[]{:S(2)}) collective-permute-start(bf16[4,40,2048]{2,1,0:T(8,128)(2,1)S(1)} %collective-permute-done.1.refs_3_), channel_id=1, source_target_pairs={{0,384},{128,0},{256,128},{384,256},{1,385},{129,1},{257,129},{385... | collective-permute-start | bytes 1966088 | tf_op jit(solution)/shard_map/ppermute | solution.py:273
  61.2 8.6 %collective-permute-done.refs_2_ = bf16[4,40,2048]{2,1,0:T(8,128)(2,1)S(1)} collective-permute-done((bf16[4,40,2048]{2,1,0:T(8,128)(2,1)S(1)}, bf16[4,40,2048]{2,1,0:T(8,128)(2,1)S(1)}, u32[]{:S(2)}, u32[]{:S(2)}) %collective-permute-start) | collective-permute-done | bytes 655392 | tf_op jit(solution)/shard_map/ppermute | solution.py:273
  69.8 0.0 collective-permute-done.5.refs_7_
  69.8 7.3 %collective-permute-done.3.refs_4_ = bf16[4,40,2048]{2,1,0:T(8,128)(2,1)} collective-permute-done((bf16[4,40,2048]{2,1,0:T(8,128)(2,1)S(1)}, bf16[4,40,2048]{2,1,0:T(8,128)(2,1)}, u32[]{:S(2)}, u32[]{:S(2)}) %collective-permute-start.3) | collective-permute-done | bytes 655392 | tf_op jit(solution)/shard_map/ppermute | solution.py:273
  77.1 6.7 %collective-permute-done.4.refs_5_ = bf16[4,40,2048]{2,1,0:T(8,128)(2,1)} collective-permute-done((bf16[4,40,2048]{2,1,0:T(8,128)(2,1)S(1)}, bf16[4,40,2048]{2,1,0:T(8,128)(2,1)}, u32[]{:S(2)}, u32[]{:S(2)}) %collective-permute-start.4) | collective-permute-done | bytes 655392 | tf_op jit(solution)/shard_map/ppermute | solution.py:273
  83.8 18.5 %all-gather.3.cloned.1.call-done = bf16[12288,512]{1,0:T(8,128)(2,1)} async-done(((bf16[384,512]{1,0:T(8,128)(2,1)}), bf16[12288,512]{1,0:T(8,128)(2,1)}) %all-gather.3.cloned.1.call-update) | async-done | bytes 12582928 | tf_op jit(solution)/shard_map/all_gather | solution.py:279
  102.3 0.0 copy-start
  102.3 6.6 %shard_map.75 = bf16[4,16,40,256]{3,2,1,0:T(8,128)(2,1)S(1)} custom-call(s32[1]{0:T(128)} %bitcast.place_ref, bf16[4,40,2048]{2,1,0:T(8,128)(2,1)S(1)} %all_to_all.20.refs_0_, bf16[4,40,2048]{2,1,0:T(8,128)(2,1)S(1)} %all-to-all-done.1.refs_1_, bf16[4,40,2048]{2,1,0:T(8,128)(2,1)S(1)} %collective-permute-done.refs_2_, ...), custom_call_target="tpu_custom_call" | custom-call | flops 2684354560 | bytes 13631488 | tf_op jit(solution)/shard_map/pallas_call | solution.py:237
  109.0 21.1 %all_to_all.21.hidden_ref = bf16[4,16,40,256]{3,2,1,0:T(8,128)(2,1)S(1)} all-to-all(bf16[4,16,40,256]{3,2,1,0:T(8,128)(2,1)S(1)} %shard_map.75), channel_id=1, replica_groups=mesh['y'=4,'c'=2,'x'=4,'z'=16] {'y'}, dimensions={0} | all-to-all | bytes 2621440 | tf_op jit(solution)/shard_map/all_to_all | solution.py:287
  130.1 0.0 copy-done
  130.1 3.4 %shard_map.76 = bf16[16,40,1024]{2,1,0:T(8,128)(2,1)} custom-call(bf16[4,16,40,256]{3,2,1,0:T(8,128)(2,1)S(1)} %all_to_all.21.hidden_ref, bf16[2,8,2,384,512]{4,3,2,1,0:T(8,128)(2,1)S(1)} %bitcast.6), custom_call_target="tpu_custom_call" | custom-call | flops 1342177280 | bytes 6815744 | tf_op jit(solution)/shard_map/pallas_call | solution.py:250
  133.4 0.0 copy-start.3
  133.4 4.8 %all-to-all-start.3 = ((bf16[16,40,1024]{2,1,0:T(8,128)(2,1)}), bf16[16,40,1024]{2,1,0:T(8,128)(2,1)S(1)}, u32[]{:S(2)}, u32[]{:S(2)}) async-start(bf16[16,40,1024]{2,1,0:T(8,128)(2,1)} %shard_map.76), calls=%async_computation.3 | async-start | bytes 2621440 | tf_op jit(solution)/shard_map/all_to_all | solution.py:288
  138.3 0.1 copy.8.routes_ref
  138.4 0.0 copy-done.3
  138.4 0.1 copy.9.numerators_ref
  138.5 17.9 %all-to-all-done.3.rows_ref = bf16[16,40,1024]{2,1,0:T(8,128)(2,1)S(1)} async-done(((bf16[16,40,1024]{2,1,0:T(8,128)(2,1)}), bf16[16,40,1024]{2,1,0:T(8,128)(2,1)S(1)}, u32[]{:S(2)}, u32[]{:S(2)}) %all-to-all-start.3) | async-done | bytes 1310752 | tf_op jit(solution)/shard_map/all_to_all | solution.py:288
  156.4 1.3 shard_map.77
Async XLA Ops:
  6.5 2.5 %copy-start.2 = (s32[64,2]{0,1:T(2,128)S(1)}, s32[64,2]{0,1:T(2,128)}, u32[]{:S(2)}) copy-start(s32[64,2]{0,1:T(2,128)} %param.8) | copy-start | bytes 1540
  6.5 2.5 %copy-start.1 = (bf16[64,4096]{1,0:T(8,128)(2,1)S(1)}, bf16[64,4096]{1,0:T(8,128)(2,1)}, u32[]{:S(2)}) copy-start(bf16[64,4096]{1,0:T(8,128)(2,1)} %tokens_ref.1) | copy-start | bytes 1572868
  6.5 95.8 %all-gather.3.cloned.1.call-start = ((), (), s32[]{:S(2)}) async-start(), calls=%async_computation.4 | async-start | bytes 12976128 | tf_op jit(solution)/shard_map/all_gather | solution.py:279
  25.7 11.1 %all-to-all-start.1 = ((bf16[4,40,2048]{2,1,0:T(8,128)(2,1)}), bf16[4,40,2048]{2,1,0:T(8,128)(2,1)S(1)}, u32[]{:S(2)}, u32[]{:S(2)}) async-start(bf16[4,40,2048]{2,1,0:T(8,128)(2,1)} %bitcast.3), calls=%async_computation.1 | async-start | bytes 1310720 | tf_op jit(solution)/shard_map/all_to_all | solution.py:282
  29.2 21.0 %collective-permute-start.2 = (bf16[4,40,2048]{2,1,0:T(8,128)(2,1)S(1)}, bf16[4,40,2048]{2,1,0:T(8,128)(2,1)S(1)}, u32[]{:S(2)}, u32[]{:S(2)}) collective-permute-start(bf16[4,40,2048]{2,1,0:T(8,128)(2,1)S(1)} %all_to_all.20.refs_0_), channel_id=1, source_target_pairs={{0,128},{128,256},{256,384},{384,0},{1,129},{129,257},{257,385},{3... | collective-permute-start | bytes 1966088 | tf_op jit(solution)/shard_map/ppermute | solution.py:273
  36.8 19.0 %collective-permute-start.1 = (bf16[4,40,2048]{2,1,0:T(8,128)(2,1)S(1)}, bf16[4,40,2048]{2,1,0:T(8,128)(2,1)S(1)}, u32[]{:S(2)}, u32[]{:S(2)}) collective-permute-start(bf16[4,40,2048]{2,1,0:T(8,128)(2,1)S(1)} %all-to-all-done.1.refs_1_), channel_id=1, source_target_pairs={{0,384},{128,0},{256,128},{384,256},{1,385},{129,1},{257,129},{385... | collective-permute-start | bytes 1966088 | tf_op jit(solution)/shard_map/ppermute | solution.py:273
  44.8 25.0 %collective-permute-start = (bf16[4,40,2048]{2,1,0:T(8,128)(2,1)S(1)}, bf16[4,40,2048]{2,1,0:T(8,128)(2,1)S(1)}, u32[]{:S(2)}, u32[]{:S(2)}) collective-permute-start(bf16[4,40,2048]{2,1,0:T(8,128)(2,1)S(1)} %all_to_all.20.refs_0_), channel_id=1, source_target_pairs={{0,384},{128,0},{256,128},{384,256},{1,385},{129,1},{257,129},{385... | collective-permute-start | bytes 1966088 | tf_op jit(solution)/shard_map/ppermute | solution.py:273
  47.2 22.5 %collective-permute-start.5 = (bf16[4,40,2048]{2,1,0:T(8,128)(2,1)S(1)}, bf16[4,40,2048]{2,1,0:T(8,128)(2,1)}, u32[]{:S(2)}, u32[]{:S(2)}) collective-permute-start(bf16[4,40,2048]{2,1,0:T(8,128)(2,1)S(1)} %all-to-all-done.1.refs_1_), channel_id=1, source_target_pairs={{0,128},{128,256},{256,384},{384,0},{1,129},{129,257},{257,385},{3... | collective-permute-start | bytes 1966088 | tf_op jit(solution)/shard_map/ppermute | solution.py:273
  50.1 27.0 %collective-permute-start.3 = (bf16[4,40,2048]{2,1,0:T(8,128)(2,1)S(1)}, bf16[4,40,2048]{2,1,0:T(8,128)(2,1)}, u32[]{:S(2)}, u32[]{:S(2)}) collective-permute-start(bf16[4,40,2048]{2,1,0:T(8,128)(2,1)S(1)} %collective-permute-done.2.refs_6_), channel_id=1, source_target_pairs={{0,128},{128,256},{256,384},{384,0},{1,129},{129,257},{257,385},{3... | collective-permute-start | bytes 1966088 | tf_op jit(solution)/shard_map/ppermute | solution.py:273
  55.7 28.1 %collective-permute-start.4 = (bf16[4,40,2048]{2,1,0:T(8,128)(2,1)S(1)}, bf16[4,40,2048]{2,1,0:T(8,128)(2,1)}, u32[]{:S(2)}, u32[]{:S(2)}) collective-permute-start(bf16[4,40,2048]{2,1,0:T(8,128)(2,1)S(1)} %collective-permute-done.1.refs_3_), channel_id=1, source_target_pairs={{0,384},{128,0},{256,128},{384,256},{1,385},{129,1},{257,129},{385... | collective-permute-start | bytes 1966088 | tf_op jit(solution)/shard_map/ppermute | solution.py:273
  102.3 27.8 %copy-start = (bf16[12288,512]{1,0:T(8,128)(2,1)S(1)}, bf16[12288,512]{1,0:T(8,128)(2,1)}, u32[]{:S(2)}) copy-start(bf16[12288,512]{1,0:T(8,128)(2,1)} %all-gather.3.cloned.1.call-done) | copy-start | bytes 37748740
  133.4 4.9 %copy-start.3 = (s32[64,2]{0,1:T(2,128)S(1)}, s32[64,2]{0,1:T(2,128)}, u32[]{:S(2)}) copy-start(s32[64,2]{0,1:T(2,128)} %param.9) | copy-start | bytes 1540
  133.4 22.9 %all-to-all-start.3 = ((bf16[16,40,1024]{2,1,0:T(8,128)(2,1)}), bf16[16,40,1024]{2,1,0:T(8,128)(2,1)S(1)}, u32[]{:S(2)}, u32[]{:S(2)}) async-start(bf16[16,40,1024]{2,1,0:T(8,128)(2,1)} %shard_map.76), calls=%async_computation.3 | async-start | bytes 2621440 | tf_op jit(solution)/shard_map/all_to_all | solution.py:288
Sparse Core Ops, SparseCore 0:
  9.5 92.7 all-gather.2

commit v5 on v4

--- a/solution.py
+++ b/solution.py
@@ -20,6 +20,7 @@
 ALL_SLOTS = X * SLOTS
 FQ = F // Y
 HALF = SHARD // 2
+DEEP = 4
 WIDE = 4
 
 
@@ -119,18 +120,32 @@
             out_ref[:, at : at + 128] = mixed[:, member * 128 : (member + 1) * 128]
 
 
-def run_of(block, start, length):
-    n = block.shape[-1]
-    return block[:, start : start + length].astype(jnp.float32).reshape(-1, n).astype(jnp.bfloat16)
-
-
-def mixed_rows(first, second):
-    place = lax.broadcasted_iota(jnp.int32, first.shape, 0)
-    return jnp.where((place & (REST - 1)) < REST // 2, first, second)
-
-
-def sources(rows, length):
-    return rows.reshape(-1, length, rows.shape[-1])
+def split_rows(block):
+    wide = block.astype(jnp.float32)
+    n = wide.shape[-1]
+    mixed = wide[:, MAIN:LEAD].reshape(-1, 2, REST, n)
+    even, odd = mixed[:, 0], mixed[:, 1]
+    low = lax.broadcasted_iota(jnp.int32, even.shape, 1) < REST // 2
+    rest = (jnp.where(low, even, swap_halves(odd)), jnp.where(low, swap_halves(even), odd))
+    return [
+        (wide[:, e * LEAD : e * LEAD + MAIN].reshape(-1, n).astype(jnp.bfloat16), rest[e].reshape(-1, n).astype(jnp.bfloat16))
+        for e in range(2)
+    ]
+
+
+def swap_halves(rows):
+    return jnp.concatenate([rows[:, REST // 2 :], rows[:, : REST // 2]], axis=1)
+
+
+def join_rows(first, second):
+    main = SRC * MAIN
+    n = first.shape[-1]
+    one, two = (rows[main:].reshape(-1, REST, n) for rows in (first, second))
+    low = lax.broadcasted_iota(jnp.int32, one.shape, 1) < REST // 2
+    even, odd = jnp.where(low, one, swap_halves(two)), jnp.where(low, swap_halves(one), two)
+    mixed = jnp.stack([even, odd], axis=1).reshape(SRC, REST, n)
+    runs = [rows[:main].reshape(SRC, MAIN, n) for rows in (first, second)]
+    return jnp.concatenate([runs[0], mixed, runs[1]], axis=1).astype(jnp.bfloat16)
 
 
 def swish(total):
@@ -139,34 +154,35 @@
 
 
 def hidden_kernel(place_ref, *refs):
-    rows, weights_ref, out_ref, sums = refs[: 2 * Y], refs[2 * Y], refs[2 * Y + 1], refs[2 * Y + 2 :]
-    main = SRC * MAIN
-
-    def add(parts, start):
-        blocks = [ref[...] for ref in parts]
-        mixed = [run_of(b, MAIN, REST) for b in blocks]
+    rows, weights_ref, out_ref, held, sems = refs[: 2 * Y], *refs[2 * Y : 2 * Y + 4]
+    sums = refs[2 * Y + 4 :]
+    groups = MEMBERS // DEEP
+    copies = [
+        pltpu.make_async_copy(
+            weights_ref.at[:, (i % groups) * DEEP : (i % groups + 1) * DEEP, i // groups, :HALF], held.at[i], sems.at[i]
+        )
+        for i in range(C * groups)
+    ]
+    copies[0].start()
+    copies[1].start()
+    for i, copy in enumerate(copies):
+        half, group = i // groups, i % groups
+        at = slice(group * DEEP * HALF, (group + 1) * DEEP * HALF)
+        blocks = [split_rows(ref[:, :, at]) for ref in rows[half::2]]
+        copy.wait()
+        if i + 2 < len(copies):
+            copies[i + 2].start()
         for expert, total in enumerate(sums):
-            group = [run_of(b, expert * LEAD, MAIN) for b in blocks] + mixed
-            weights = weights_ref[expert, :, 0].reshape(MEMBERS * HALF, 2 * FQ)
-            product = jnp.dot(jnp.concatenate(group, axis=0), weights, preferred_element_type=jnp.float32)
-            total[...] = product if start else total[...] + product
-
-    @pl.when(pl.program_id(0) == 0)
-    def _():
-        add(rows[0::2], True)
-
-    @pl.when(pl.program_id(0) == 1)
-    def _():
-        add(rows[1::2], False)
-        first, second = (swish(total[...]) for total in sums)
-        mixed = mixed_rows(first[main:], second[main:])
-        joined = [sources(first[:main], MAIN), sources(mixed, REST), sources(second[:main], MAIN)]
-        joined = jnp.concatenate(joined, axis=1).astype(jnp.bfloat16)
-        for offset in range(Y):
-            source = lax.rem(place_ref[0] + offset, Y)
-            block = joined[offset * X : (offset + 1) * X]
-            for copy in range(Y):
-                out_ref[copy, pl.ds(source * X, X)] = block
+            block = jnp.concatenate([b[expert][part] for part in range(2) for b in blocks], axis=0)
+            weights = held[i, expert].reshape(DEEP * HALF, 2 * FQ)
+            product = jnp.dot(block, weights, preferred_element_type=jnp.float32)
+            total[...] = product if i == 0 else total[...] + product
+    joined = join_rows(*(swish(total[...]) for total in sums))
+    for offset in range(Y):
+        source = lax.rem(place_ref[0] + offset, Y)
+        block = joined[offset * X : (offset + 1) * X]
+        for copy in range(Y):
+            out_ref[copy, pl.ds(source * X, X)] = block
 
 
 def down_kernel(hidden_ref, weights_ref, out_ref, *rows):
@@ -175,12 +191,10 @@
     @pl.when(pl.program_id(0) == 0)
     def _():
         for quarter in range(Y):
-            block = hidden_ref[quarter]
             at = slice(quarter * FQ, (quarter + 1) * FQ)
-            mixed = run_of(block, MAIN, REST)
-            for expert in range(2):
-                rows[expert][:main, at] = run_of(block, expert * LEAD, MAIN)
-                rows[expert][main:, at] = mixed
+            for ref, (run, rest) in zip(rows, split_rows(hidden_ref[quarter])):
+                ref[:main, at] = run
+                ref[main:, at] = rest
 
     def result(expert):
         weights = jnp.concatenate(
@@ -193,10 +207,7 @@
         )
         return jnp.dot(rows[expert][...], weights, preferred_element_type=jnp.float32)
 
-    first, second = result(0), result(1)
-    mixed = mixed_rows(first[main:], second[main:])
-    joined = [sources(first[:main], MAIN), sources(mixed, REST), sources(second[:main], MAIN)]
-    out_ref[...] = jnp.concatenate(joined, axis=1).astype(jnp.bfloat16)
+    out_ref[...] = join_rows(result(0), result(1))
 
 
 SCALAR = pl.BlockSpec(memory_space=pltpu.SMEM)
@@ -234,13 +245,17 @@
 
 
 def hidden_rows(place, rows, weights):
+    pieces = C * MEMBERS // DEEP
     return pl.pallas_call(
         hidden_kernel,
-        grid=(2,),
         out_shape=shape((Y, SRC, SLOTS, FQ)),
-        in_specs=[SCALAR, *[WHOLE] * (2 * Y), pl.BlockSpec((2, MEMBERS, 1, HALF, 2 * FQ), lambda k: (0, 0, k, 0, 0))],
-        out_specs=pl.BlockSpec((Y, SRC, SLOTS, FQ), lambda k: (0, 0, 0, 0)),
-        scratch_shapes=[pltpu.VMEM((SRC * (MAIN + REST), 2 * FQ), jnp.float32)] * 2,
+        in_specs=[SCALAR, *[WHOLE] * (2 * Y), ANY],
+        out_specs=WHOLE,
+        scratch_shapes=[
+            pltpu.VMEM((pieces, 2, DEEP, HALF, 2 * FQ), jnp.bfloat16),
+            pltpu.SemaphoreType.DMA((pieces,)),
+            *[pltpu.VMEM((SRC * SLOTS // 2, 2 * FQ), jnp.float32)] * 2,
+        ],
         compiler_params=params(36),
         cost_estimate=pl.CostEstimate(flops=2 * ROWS * D * 2 * FQ, bytes_accessed=2 * ROWS * D + 8 * D * FQ, transcendentals=0),
     )(place, *rows, weights)
@@ -253,7 +268,7 @@
         out_shape=shape((SRC, SLOTS, MEMBERS * 128)),
         in_specs=[WHOLE, pl.BlockSpec((2, WIDE, C, 128, SHARD), lambda n: (0, n, 0, HALF // 128, 0))],
         out_specs=pl.BlockSpec((SRC, SLOTS, WIDE * 128), lambda n: (0, 0, n)),
-        scratch_shapes=[pltpu.VMEM((SRC * (MAIN + REST), F), jnp.bfloat16)] * 2,
+        scratch_shapes=[pltpu.VMEM((SRC * SLOTS // 2, F), jnp.bfloat16)] * 2,
         compiler_params=params(24),
         cost_estimate=pl.CostEstimate(flops=2 * ROWS * F * F, bytes_accessed=4 * ROWS * F + 4 * F * F, transcendentals=0),
     )(hidden, weights)

time: 166 us -> 166 us (level)
  no operation moved by 1% of the time
where the time goes in v5:
time: 166 us; the launch traced here: 165 us
  waiting for transfers between devices  64.8 us (39%)
  starting transfers between devices  34.5 us (21%)
  blocking collectives  33.4 us (20%)
  Pallas kernels  17.6 us (11%)
  between operations  14.2 us (9%)
    ppermute x6, waiting for transfers between devices, shift(): return lax.ppermute(block, 'y', [(i, (i + by) % Y) for i in range(Y)])  26.3 us
    ppermute x6, starting transfers between devices, shift(): return lax.ppermute(block, 'y', [(i, (i + by) % Y) for i in range(Y)])  26.2 us
    all_to_all x1, blocking collectives, local(): lax.all_to_all(hidden_rows(place, rows, weights), 'y', 0, 0, tiled=True)  21.1 us
    all_gather x1, waiting for transfers between devices, local(): lax.all_gather(weights, ('z', 'c'))  18.5 us
    all_to_all x1, waiting for transfers between devices, local(): lax.all_to_all(down_rows(hidden, weights), ('y', 'x'), 0, 0, tiled=True)  17.9 us
    all_to_all x1, blocking collectives, local(): lax.all_to_all(first.reshape(X, SLOTS, D // 2), 'x', 0, 0, tiled=True)  12.3 us
    pallas_call x1, Pallas kernels, hidden_rows(): pl.pallas_call(hidden_kernel, out_shape=shape((Y, SRC, SLOTS, FQ)), in_sp...  7.06 us
    all_to_all x1, starting transfers between devices, local(): lax.all_to_all(down_rows(hidden, weights), ('y', 'x'), 0, 0, tiled=True)  4.81 us
  transfers between devices with their start and end apart: 9, of which 7 were waited for; matrix products, arithmetic and copies ran while one was open for 0% of the time, Pallas kernels for 3%

profile of v5, /device:TPU:1, one launch (start us, length us, event | category | flops | bytes accessed | tf_op | source)
XLA Modules:
  0.0 164.6 jit_solution(17760739932499791692)
XLA Ops:
  6.5 0.0 copy-start.2
  6.5 0.0 copy-start.1
  6.5 0.0 all-gather.3.cloned.1.call-start
  6.5 1.8 %shard_map.74 = bf16[384,512]{1,0:T(8,128)(2,1)} custom-call(bf16[512,1024]{1,0:T(8,128)(2,1)} %gate_ref.1, bf16[512,1024]{1,0:T(8,128)(2,1)} %up_ref.1, bf16[1024,512]{1,0:T(8,128)(2,1)} %down_ref.1), custom_call_target="tpu_custom_call" | custom-call | tf_op jit(solution)/shard_map/pallas_call | solution.py:238
  8.4 0.0 all-gather.3.cloned.1.call-update
  9.1 0.0 copy-done.2
  9.1 0.0 copy-done.1
  9.1 4.3 %shard_map.73 = (bf16[160,2048]{1,0:T(8,128)(2,1)S(1)}, bf16[160,2048]{1,0:T(8,128)(2,1)}) custom-call(s32[1]{0:T(128)S(6)} %copy.10.count_ref, s32[2,64]{1,0:T(2,128)S(1)} %bitcast.8, bf16[64,4096]{1,0:T(8,128)(2,1)S(1)} %copy-done.1), custom_call_target="tpu_custom_call" | custom-call | flops 83886080 | bytes 1835008 | tf_op jit(solution)/shard_map/pallas_call | solution.py:227
  13.4 12.3 %all_to_all.20.refs_0_ = bf16[4,40,2048]{2,1,0:T(8,128)(2,1)S(1)} all-to-all(bf16[4,40,2048]{2,1,0:T(8,128)(2,1)S(1)} %bitcast.7), channel_id=1, replica_groups=mesh['y'=4,'c'=2,'x'=4,'z'=16] {'x'}, dimensions={0} | all-to-all | bytes 1310720 | tf_op jit(solution)/shard_map/all_to_all | solution.py:296
  25.7 3.5 %all-to-all-start.1 = ((bf16[4,40,2048]{2,1,0:T(8,128)(2,1)}), bf16[4,40,2048]{2,1,0:T(8,128)(2,1)S(1)}, u32[]{:S(2)}, u32[]{:S(2)}) async-start(bf16[4,40,2048]{2,1,0:T(8,128)(2,1)} %bitcast.3), calls=%async_computation.1 | async-start | bytes 1310720 | tf_op jit(solution)/shard_map/all_to_all | solution.py:297
  29.2 5.5 %collective-permute-start.2 = (bf16[4,40,2048]{2,1,0:T(8,128)(2,1)S(1)}, bf16[4,40,2048]{2,1,0:T(8,128)(2,1)S(1)}, u32[]{:S(2)}, u32[]{:S(2)}) collective-permute-start(bf16[4,40,2048]{2,1,0:T(8,128)(2,1)S(1)} %all_to_all.20.refs_0_), channel_id=1, source_target_pairs={{0,128},{128,256},{256,384},{384,0},{1,129},{129,257},{257,385},{3... | collective-permute-start | bytes 1966088 | tf_op jit(solution)/shard_map/ppermute | solution.py:288
  34.7 2.1 %all-to-all-done.1.refs_1_ = bf16[4,40,2048]{2,1,0:T(8,128)(2,1)S(1)} async-done(((bf16[4,40,2048]{2,1,0:T(8,128)(2,1)}), bf16[4,40,2048]{2,1,0:T(8,128)(2,1)S(1)}, u32[]{:S(2)}, u32[]{:S(2)}) %all-to-all-start.1) | async-done | bytes 655392 | tf_op jit(solution)/shard_map/all_to_all | solution.py:297
  36.8 8.1 %collective-permute-start.1 = (bf16[4,40,2048]{2,1,0:T(8,128)(2,1)S(1)}, bf16[4,40,2048]{2,1,0:T(8,128)(2,1)S(1)}, u32[]{:S(2)}, u32[]{:S(2)}) collective-permute-start(bf16[4,40,2048]{2,1,0:T(8,128)(2,1)S(1)} %all-to-all-done.1.refs_1_), channel_id=1, source_target_pairs={{0,384},{128,0},{256,128},{384,256},{1,385},{129,1},{257,129},{385... | collective-permute-start | bytes 1966088 | tf_op jit(solution)/shard_map/ppermute | solution.py:288
  44.8 2.4 %collective-permute-start = (bf16[4,40,2048]{2,1,0:T(8,128)(2,1)S(1)}, bf16[4,40,2048]{2,1,0:T(8,128)(2,1)S(1)}, u32[]{:S(2)}, u32[]{:S(2)}) collective-permute-start(bf16[4,40,2048]{2,1,0:T(8,128)(2,1)S(1)} %all_to_all.20.refs_0_), channel_id=1, source_target_pairs={{0,384},{128,0},{256,128},{384,256},{1,385},{129,1},{257,129},{385... | collective-permute-start | bytes 1966088 | tf_op jit(solution)/shard_map/ppermute | solution.py:288
  47.2 2.9 %collective-permute-start.5 = (bf16[4,40,2048]{2,1,0:T(8,128)(2,1)S(1)}, bf16[4,40,2048]{2,1,0:T(8,128)(2,1)}, u32[]{:S(2)}, u32[]{:S(2)}) collective-permute-start(bf16[4,40,2048]{2,1,0:T(8,128)(2,1)S(1)} %all-to-all-done.1.refs_1_), channel_id=1, source_target_pairs={{0,128},{128,256},{256,384},{384,0},{1,129},{129,257},{257,385},{3... | collective-permute-start | bytes 1966088 | tf_op jit(solution)/shard_map/ppermute | solution.py:288
  50.1 0.0 collective-permute-done.2.refs_6_
  50.1 1.9 %collective-permute-start.3 = (bf16[4,40,2048]{2,1,0:T(8,128)(2,1)S(1)}, bf16[4,40,2048]{2,1,0:T(8,128)(2,1)}, u32[]{:S(2)}, u32[]{:S(2)}) collective-permute-start(bf16[4,40,2048]{2,1,0:T(8,128)(2,1)S(1)} %collective-permute-done.2.refs_6_), channel_id=1, source_target_pairs={{0,128},{128,256},{256,384},{384,0},{1,129},{129,257},{257,385},{3... | collective-permute-start | bytes 1966088 | tf_op jit(solution)/shard_map/ppermute | solution.py:288
  52.1 3.7 %collective-permute-done.1.refs_3_ = bf16[4,40,2048]{2,1,0:T(8,128)(2,1)S(1)} collective-permute-done((bf16[4,40,2048]{2,1,0:T(8,128)(2,1)S(1)}, bf16[4,40,2048]{2,1,0:T(8,128)(2,1)S(1)}, u32[]{:S(2)}, u32[]{:S(2)}) %collective-permute-start.1) | collective-permute-done | bytes 655392 | tf_op jit(solution)/shard_map/ppermute | solution.py:288
  55.7 5.4 %collective-permute-start.4 = (bf16[4,40,2048]{2,1,0:T(8,128)(2,1)S(1)}, bf16[4,40,2048]{2,1,0:T(8,128)(2,1)}, u32[]{:S(2)}, u32[]{:S(2)}) collective-permute-start(bf16[4,40,2048]{2,1,0:T(8,128)(2,1)S(1)} %collective-permute-done.1.refs_3_), channel_id=1, source_target_pairs={{0,384},{128,0},{256,128},{384,256},{1,385},{129,1},{257,129},{385... | collective-permute-start | bytes 1966088 | tf_op jit(solution)/shard_map/ppermute | solution.py:288
  61.2 8.6 %collective-permute-done.refs_2_ = bf16[4,40,2048]{2,1,0:T(8,128)(2,1)S(1)} collective-permute-done((bf16[4,40,2048]{2,1,0:T(8,128)(2,1)S(1)}, bf16[4,40,2048]{2,1,0:T(8,128)(2,1)S(1)}, u32[]{:S(2)}, u32[]{:S(2)}) %collective-permute-start) | collective-permute-done | bytes 655392 | tf_op jit(solution)/shard_map/ppermute | solution.py:288
  69.8 0.0 collective-permute-done.5.refs_7_
  69.8 7.3 %collective-permute-done.3.refs_4_ = bf16[4,40,2048]{2,1,0:T(8,128)(2,1)} collective-permute-done((bf16[4,40,2048]{2,1,0:T(8,128)(2,1)S(1)}, bf16[4,40,2048]{2,1,0:T(8,128)(2,1)}, u32[]{:S(2)}, u32[]{:S(2)}) %collective-permute-start.3) | collective-permute-done | bytes 655392 | tf_op jit(solution)/shard_map/ppermute | solution.py:288
  77.1 6.7 %collective-permute-done.4.refs_5_ = bf16[4,40,2048]{2,1,0:T(8,128)(2,1)} collective-permute-done((bf16[4,40,2048]{2,1,0:T(8,128)(2,1)S(1)}, bf16[4,40,2048]{2,1,0:T(8,128)(2,1)}, u32[]{:S(2)}, u32[]{:S(2)}) %collective-permute-start.4) | collective-permute-done | bytes 655392 | tf_op jit(solution)/shard_map/ppermute | solution.py:288
  83.8 18.5 %all-gather.3.cloned.1.call-done = bf16[12288,512]{1,0:T(8,128)(2,1)} async-done(((bf16[384,512]{1,0:T(8,128)(2,1)}), bf16[12288,512]{1,0:T(8,128)(2,1)}) %all-gather.3.cloned.1.call-update) | async-done | bytes 12582928 | tf_op jit(solution)/shard_map/all_gather | solution.py:294
  102.3 0.0 copy-start
  102.3 7.1 %shard_map.75 = bf16[4,16,40,256]{3,2,1,0:T(8,128)(2,1)S(1)} custom-call(s32[1]{0:T(128)} %bitcast.place_ref, bf16[4,40,2048]{2,1,0:T(8,128)(2,1)S(1)} %all_to_all.20.refs_0_, bf16[4,40,2048]{2,1,0:T(8,128)(2,1)S(1)} %all-to-all-done.1.refs_1_, bf16[4,40,2048]{2,1,0:T(8,128)(2,1)S(1)} %collective-permute-done.refs_2_, ...), custom_call_target="tpu_custom_call" | custom-call | flops 2684354560 | bytes 13631488 | tf_op jit(solution)/shard_map/pallas_call | solution.py:249
  109.4 21.1 %all_to_all.21.hidden_ref = bf16[4,16,40,256]{3,2,1,0:T(8,128)(2,1)S(1)} all-to-all(bf16[4,16,40,256]{3,2,1,0:T(8,128)(2,1)S(1)} %shard_map.75), channel_id=1, replica_groups=mesh['y'=4,'c'=2,'x'=4,'z'=16] {'y'}, dimensions={0} | all-to-all | bytes 2621440 | tf_op jit(solution)/shard_map/all_to_all | solution.py:302
  130.5 0.0 copy-done
  130.5 3.1 %shard_map.76 = bf16[16,40,1024]{2,1,0:T(8,128)(2,1)} custom-call(bf16[4,16,40,256]{3,2,1,0:T(8,128)(2,1)S(1)} %all_to_all.21.hidden_ref, bf16[2,8,2,384,512]{4,3,2,1,0:T(8,128)(2,1)S(1)} %bitcast.6), custom_call_target="tpu_custom_call" | custom-call | flops 1342177280 | bytes 6815744 | tf_op jit(solution)/shard_map/pallas_call | solution.py:265
  133.6 0.0 copy-start.3
  133.6 4.8 %all-to-all-start.3 = ((bf16[16,40,1024]{2,1,0:T(8,128)(2,1)}), bf16[16,40,1024]{2,1,0:T(8,128)(2,1)S(1)}, u32[]{:S(2)}, u32[]{:S(2)}) async-start(bf16[16,40,1024]{2,1,0:T(8,128)(2,1)} %shard_map.76), calls=%async_computation.3 | async-start | bytes 2621440 | tf_op jit(solution)/shard_map/all_to_all | solution.py:303
  138.4 0.1 copy.8.routes_ref
  138.5 0.0 copy-done.3
  138.5 0.1 copy.9.numerators_ref
  138.6 17.9 %all-to-all-done.3.rows_ref = bf16[16,40,1024]{2,1,0:T(8,128)(2,1)S(1)} async-done(((bf16[16,40,1024]{2,1,0:T(8,128)(2,1)}), bf16[16,40,1024]{2,1,0:T(8,128)(2,1)S(1)}, u32[]{:S(2)}, u32[]{:S(2)}) %all-to-all-start.3) | async-done | bytes 1310752 | tf_op jit(solution)/shard_map/all_to_all | solution.py:303
  156.5 1.3 shard_map.77
Async XLA Ops:
  6.5 2.5 %copy-start.2 = (s32[64,2]{0,1:T(2,128)S(1)}, s32[64,2]{0,1:T(2,128)}, u32[]{:S(2)}) copy-start(s32[64,2]{0,1:T(2,128)} %param.8) | copy-start | bytes 1540
  6.5 2.5 %copy-start.1 = (bf16[64,4096]{1,0:T(8,128)(2,1)S(1)}, bf16[64,4096]{1,0:T(8,128)(2,1)}, u32[]{:S(2)}) copy-start(bf16[64,4096]{1,0:T(8,128)(2,1)} %tokens_ref.1) | copy-start | bytes 1572868
  6.5 95.8 %all-gather.3.cloned.1.call-start = ((), (), s32[]{:S(2)}) async-start(), calls=%async_computation.4 | async-start | bytes 12976128 | tf_op jit(solution)/shard_map/all_gather | solution.py:294
  25.7 11.1 %all-to-all-start.1 = ((bf16[4,40,2048]{2,1,0:T(8,128)(2,1)}), bf16[4,40,2048]{2,1,0:T(8,128)(2,1)S(1)}, u32[]{:S(2)}, u32[]{:S(2)}) async-start(bf16[4,40,2048]{2,1,0:T(8,128)(2,1)} %bitcast.3), calls=%async_computation.1 | async-start | bytes 1310720 | tf_op jit(solution)/shard_map/all_to_all | solution.py:297
  29.2 21.0 %collective-permute-start.2 = (bf16[4,40,2048]{2,1,0:T(8,128)(2,1)S(1)}, bf16[4,40,2048]{2,1,0:T(8,128)(2,1)S(1)}, u32[]{:S(2)}, u32[]{:S(2)}) collective-permute-start(bf16[4,40,2048]{2,1,0:T(8,128)(2,1)S(1)} %all_to_all.20.refs_0_), channel_id=1, source_target_pairs={{0,128},{128,256},{256,384},{384,0},{1,129},{129,257},{257,385},{3... | collective-permute-start | bytes 1966088 | tf_op jit(solution)/shard_map/ppermute | solution.py:288
  36.8 19.0 %collective-permute-start.1 = (bf16[4,40,2048]{2,1,0:T(8,128)(2,1)S(1)}, bf16[4,40,2048]{2,1,0:T(8,128)(2,1)S(1)}, u32[]{:S(2)}, u32[]{:S(2)}) collective-permute-start(bf16[4,40,2048]{2,1,0:T(8,128)(2,1)S(1)} %all-to-all-done.1.refs_1_), channel_id=1, source_target_pairs={{0,384},{128,0},{256,128},{384,256},{1,385},{129,1},{257,129},{385... | collective-permute-start | bytes 1966088 | tf_op jit(solution)/shard_map/ppermute | solution.py:288
  44.8 25.0 %collective-permute-start = (bf16[4,40,2048]{2,1,0:T(8,128)(2,1)S(1)}, bf16[4,40,2048]{2,1,0:T(8,128)(2,1)S(1)}, u32[]{:S(2)}, u32[]{:S(2)}) collective-permute-start(bf16[4,40,2048]{2,1,0:T(8,128)(2,1)S(1)} %all_to_all.20.refs_0_), channel_id=1, source_target_pairs={{0,384},{128,0},{256,128},{384,256},{1,385},{129,1},{257,129},{385... | collective-permute-start | bytes 1966088 | tf_op jit(solution)/shard_map/ppermute | solution.py:288
  47.2 22.5 %collective-permute-start.5 = (bf16[4,40,2048]{2,1,0:T(8,128)(2,1)S(1)}, bf16[4,40,2048]{2,1,0:T(8,128)(2,1)}, u32[]{:S(2)}, u32[]{:S(2)}) collective-permute-start(bf16[4,40,2048]{2,1,0:T(8,128)(2,1)S(1)} %all-to-all-done.1.refs_1_), channel_id=1, source_target_pairs={{0,128},{128,256},{256,384},{384,0},{1,129},{129,257},{257,385},{3... | collective-permute-start | bytes 1966088 | tf_op jit(solution)/shard_map/ppermute | solution.py:288
  50.1 27.0 %collective-permute-start.3 = (bf16[4,40,2048]{2,1,0:T(8,128)(2,1)S(1)}, bf16[4,40,2048]{2,1,0:T(8,128)(2,1)}, u32[]{:S(2)}, u32[]{:S(2)}) collective-permute-start(bf16[4,40,2048]{2,1,0:T(8,128)(2,1)S(1)} %collective-permute-done.2.refs_6_), channel_id=1, source_target_pairs={{0,128},{128,256},{256,384},{384,0},{1,129},{129,257},{257,385},{3... | collective-permute-start | bytes 1966088 | tf_op jit(solution)/shard_map/ppermute | solution.py:288
  55.7 28.1 %collective-permute-start.4 = (bf16[4,40,2048]{2,1,0:T(8,128)(2,1)S(1)}, bf16[4,40,2048]{2,1,0:T(8,128)(2,1)}, u32[]{:S(2)}, u32[]{:S(2)}) collective-permute-start(bf16[4,40,2048]{2,1,0:T(8,128)(2,1)S(1)} %collective-permute-done.1.refs_3_), channel_id=1, source_target_pairs={{0,384},{128,0},{256,128},{384,256},{1,385},{129,1},{257,129},{385... | collective-permute-start | bytes 1966088 | tf_op jit(solution)/shard_map/ppermute | solution.py:288
  102.3 28.2 %copy-start = (bf16[12288,512]{1,0:T(8,128)(2,1)S(1)}, bf16[12288,512]{1,0:T(8,128)(2,1)}, u32[]{:S(2)}) copy-start(bf16[12288,512]{1,0:T(8,128)(2,1)} %all-gather.3.cloned.1.call-done) | copy-start | bytes 37748740
  133.6 4.9 %copy-start.3 = (s32[64,2]{0,1:T(2,128)S(1)}, s32[64,2]{0,1:T(2,128)}, u32[]{:S(2)}) copy-start(s32[64,2]{0,1:T(2,128)} %param.9) | copy-start | bytes 1540
  133.6 22.9 %all-to-all-start.3 = ((bf16[16,40,1024]{2,1,0:T(8,128)(2,1)}), bf16[16,40,1024]{2,1,0:T(8,128)(2,1)S(1)}, u32[]{:S(2)}, u32[]{:S(2)}) async-start(bf16[16,40,1024]{2,1,0:T(8,128)(2,1)} %shard_map.76), calls=%async_computation.3 | async-start | bytes 2621440 | tf_op jit(solution)/shard_map/all_to_all | solution.py:303
Sparse Core Ops, SparseCore 0:
  9.5 92.7 all-gather.2

commit v6 on v5

--- a/solution.py
+++ b/solution.py
@@ -154,8 +154,8 @@
 
 
 def hidden_kernel(place_ref, *refs):
-    rows, weights_ref, out_ref, held, sems = refs[: 2 * Y], *refs[2 * Y : 2 * Y + 4]
-    sums = refs[2 * Y + 4 :]
+    rows, weights_ref, out_ref, down_ref, held, sems = refs[: 2 * Y], *refs[2 * Y : 2 * Y + 5]
+    sums = refs[2 * Y + 5 :]
     groups = MEMBERS // DEEP
     copies = [
         pltpu.make_async_copy(
@@ -163,9 +163,10 @@
         )
         for i in range(C * groups)
     ]
+    copies.append(pltpu.make_async_copy(weights_ref.at[:, :, :, HALF:], down_ref, sems.at[C * groups]))
     copies[0].start()
     copies[1].start()
-    for i, copy in enumerate(copies):
+    for i, copy in enumerate(copies[:-1]):
         half, group = i // groups, i % groups
         at = slice(group * DEEP * HALF, (group + 1) * DEEP * HALF)
         blocks = [split_rows(ref[:, :, at]) for ref in rows[half::2]]
@@ -183,23 +184,21 @@
         block = joined[offset * X : (offset + 1) * X]
         for copy in range(Y):
             out_ref[copy, pl.ds(source * X, X)] = block
+    copies[-1].wait()
 
 
 def down_kernel(hidden_ref, weights_ref, out_ref, *rows):
     main = SRC * MAIN
-
-    @pl.when(pl.program_id(0) == 0)
-    def _():
-        for quarter in range(Y):
-            at = slice(quarter * FQ, (quarter + 1) * FQ)
-            for ref, (run, rest) in zip(rows, split_rows(hidden_ref[quarter])):
-                ref[:main, at] = run
-                ref[main:, at] = rest
-
-    def result(expert):
+    for quarter in range(Y):
+        at = slice(quarter * FQ, (quarter + 1) * FQ)
+        for ref, (run, rest) in zip(rows, split_rows(hidden_ref[quarter])):
+            ref[:main, at] = run
+            ref[main:, at] = rest
+
+    def result(expert, members):
         weights = jnp.concatenate(
             [
-                jnp.concatenate([weights_ref[expert, m, half, :, q * 128 : (q + 1) * 128] for m in range(WIDE)], axis=1)
+                jnp.concatenate([weights_ref[expert, m, half, :, q * 128 : (q + 1) * 128] for m in members], axis=1)
                 for q in range(Y)
                 for half in range(C)
             ],
@@ -207,7 +206,9 @@
         )
         return jnp.dot(rows[expert][...], weights, preferred_element_type=jnp.float32)
 
-    out_ref[...] = join_rows(result(0), result(1))
+    for start in range(0, MEMBERS, WIDE):
+        members = range(start, start + WIDE)
+        out_ref[:, :, start * 128 : (start + WIDE) * 128] = join_rows(result(0, members), result(1, members))
 
 
 SCALAR = pl.BlockSpec(memory_space=pltpu.SMEM)
@@ -248,12 +249,12 @@
     pieces = C * MEMBERS // DEEP
     return pl.pallas_call(
         hidden_kernel,
-        out_shape=shape((Y, SRC, SLOTS, FQ)),
+        out_shape=[shape((Y, SRC, SLOTS, FQ)), shape((2, MEMBERS, C, 128, SHARD))],
         in_specs=[SCALAR, *[WHOLE] * (2 * Y), ANY],
-        out_specs=WHOLE,
+        out_specs=[WHOLE] * 2,
         scratch_shapes=[
             pltpu.VMEM((pieces, 2, DEEP, HALF, 2 * FQ), jnp.bfloat16),
-            pltpu.SemaphoreType.DMA((pieces,)),
+            pltpu.SemaphoreType.DMA((pieces + 1,)),
             *[pltpu.VMEM((SRC * SLOTS // 2, 2 * FQ), jnp.float32)] * 2,
         ],
         compiler_params=params(36),
@@ -264,10 +265,9 @@
 def down_rows(hidden, weights):
     return pl.pallas_call(
         down_kernel,
-        grid=(MEMBERS // WIDE,),
         out_shape=shape((SRC, SLOTS, MEMBERS * 128)),
-        in_specs=[WHOLE, pl.BlockSpec((2, WIDE, C, 128, SHARD), lambda n: (0, n, 0, HALF // 128, 0))],
-        out_specs=pl.BlockSpec((SRC, SLOTS, WIDE * 128), lambda n: (0, 0, n)),
+        in_specs=[WHOLE] * 2,
+        out_specs=WHOLE,
         scratch_shapes=[pltpu.VMEM((SRC * SLOTS // 2, F), jnp.bfloat16)] * 2,
         compiler_params=params(24),
         cost_estimate=pl.CostEstimate(flops=2 * ROWS * F * F, bytes_accessed=4 * ROWS * F + 4 * F * F, transcendentals=0),
@@ -299,8 +299,9 @@
     second_3, first_1 = shift(second, 1), shift(first, -1)
     first_2, second_2 = shift(first_3, 1), shift(second_1, -1)
     rows = (first, second, first_1, second_1, first_2, second_2, first_3, second_3)
-    hidden = lax.all_to_all(hidden_rows(place, rows, weights), "y", 0, 0, tiled=True)
-    result = lax.all_to_all(down_rows(hidden, weights), ("y", "x"), 0, 0, tiled=True)
+    hidden, down = hidden_rows(place, rows, weights)
+    hidden = lax.all_to_all(hidden, "y", 0, 0, tiled=True)
+    result = lax.all_to_all(down_rows(hidden, down), ("y", "x"), 0, 0, tiled=True)
     return mix(counts, routes, numerators, result)
 
 

time: 166 us -> 166 us (level)
  no operation moved by 1% of the time
where the time goes in v6:
time: 166 us; the launch traced here: 164 us
  waiting for transfers between devices  64.8 us (39%)
  starting transfers between devices  34.5 us (21%)
  blocking collectives  33.4 us (20%)
  Pallas kernels  17.3 us (10%)
  between operations  14.2 us (9%)
    ppermute x6, waiting for transfers between devices, shift(): return lax.ppermute(block, 'y', [(i, (i + by) % Y) for i in range(Y)])  26.3 us
    ppermute x6, starting transfers between devices, shift(): return lax.ppermute(block, 'y', [(i, (i + by) % Y) for i in range(Y)])  26.2 us
    all_to_all x1, blocking collectives, local(): hidden = lax.all_to_all(hidden, 'y', 0, 0, tiled=True)  21.1 us
    all_gather x1, waiting for transfers between devices, local(): lax.all_gather(weights, ('z', 'c'))  18.5 us
    all_to_all x1, waiting for transfers between devices, local(): lax.all_to_all(down_rows(hidden, down), ('y', 'x'), 0, 0, tiled=True)  17.9 us
    all_to_all x1, blocking collectives, local(): lax.all_to_all(first.reshape(X, SLOTS, D // 2), 'x', 0, 0, tiled=True)  12.3 us
    pallas_call x1, Pallas kernels, hidden_rows(): pl.pallas_call(hidden_kernel, out_shape=[shape((Y, SRC, SLOTS, FQ)), shap...  7.22 us
    all_to_all x1, starting transfers between devices, local(): lax.all_to_all(down_rows(hidden, down), ('y', 'x'), 0, 0, tiled=True)  4.81 us
  transfers between devices with their start and end apart: 9, of which 7 were waited for; matrix products, arithmetic and copies ran while one was open for 0% of the time, Pallas kernels for 3%

profile of v6, /device:TPU:1, one launch (start us, length us, event | category | flops | bytes accessed | tf_op | source)
XLA Modules:
  0.0 164.4 jit_solution(3080845651891120556)
XLA Ops:
  6.5 0.0 copy-start.1
  6.5 0.0 copy-start
  6.5 0.0 all-gather.3.cloned.1.call-start
  6.5 1.8 %shard_map.74 = bf16[384,512]{1,0:T(8,128)(2,1)} custom-call(bf16[512,1024]{1,0:T(8,128)(2,1)} %gate_ref.1, bf16[512,1024]{1,0:T(8,128)(2,1)} %up_ref.1, bf16[1024,512]{1,0:T(8,128)(2,1)} %down_ref.1), custom_call_target="tpu_custom_call" | custom-call | tf_op jit(solution)/shard_map/pallas_call | solution.py:239
  8.4 0.0 all-gather.3.cloned.1.call-update
  9.1 0.0 copy-done.1
  9.1 0.0 copy-done
  9.1 4.3 %shard_map.73 = (bf16[160,2048]{1,0:T(8,128)(2,1)S(1)}, bf16[160,2048]{1,0:T(8,128)(2,1)}) custom-call(s32[1]{0:T(128)S(6)} %copy.10.count_ref, s32[2,64]{1,0:T(2,128)S(1)} %bitcast.6, bf16[64,4096]{1,0:T(8,128)(2,1)S(1)} %copy-done), custom_call_target="tpu_custom_call" | custom-call | flops 83886080 | bytes 1835008 | tf_op jit(solution)/shard_map/pallas_call | solution.py:228
  13.4 12.3 %all_to_all.20.refs_0_ = bf16[4,40,2048]{2,1,0:T(8,128)(2,1)S(1)} all-to-all(bf16[4,40,2048]{2,1,0:T(8,128)(2,1)S(1)} %bitcast.5), channel_id=1, replica_groups=mesh['y'=4,'c'=2,'x'=4,'z'=16] {'x'}, dimensions={0} | all-to-all | bytes 1310720 | tf_op jit(solution)/shard_map/all_to_all | solution.py:296
  25.7 3.5 %all-to-all-start.1 = ((bf16[4,40,2048]{2,1,0:T(8,128)(2,1)}), bf16[4,40,2048]{2,1,0:T(8,128)(2,1)S(1)}, u32[]{:S(2)}, u32[]{:S(2)}) async-start(bf16[4,40,2048]{2,1,0:T(8,128)(2,1)} %bitcast.3), calls=%async_computation.1 | async-start | bytes 1310720 | tf_op jit(solution)/shard_map/all_to_all | solution.py:297
  29.2 5.5 %collective-permute-start.2 = (bf16[4,40,2048]{2,1,0:T(8,128)(2,1)S(1)}, bf16[4,40,2048]{2,1,0:T(8,128)(2,1)S(1)}, u32[]{:S(2)}, u32[]{:S(2)}) collective-permute-start(bf16[4,40,2048]{2,1,0:T(8,128)(2,1)S(1)} %all_to_all.20.refs_0_), channel_id=1, source_target_pairs={{0,128},{128,256},{256,384},{384,0},{1,129},{129,257},{257,385},{3... | collective-permute-start | bytes 1966088 | tf_op jit(solution)/shard_map/ppermute | solution.py:288
  34.7 2.1 %all-to-all-done.1.refs_1_ = bf16[4,40,2048]{2,1,0:T(8,128)(2,1)S(1)} async-done(((bf16[4,40,2048]{2,1,0:T(8,128)(2,1)}), bf16[4,40,2048]{2,1,0:T(8,128)(2,1)S(1)}, u32[]{:S(2)}, u32[]{:S(2)}) %all-to-all-start.1) | async-done | bytes 655392 | tf_op jit(solution)/shard_map/all_to_all | solution.py:297
  36.8 8.1 %collective-permute-start.1 = (bf16[4,40,2048]{2,1,0:T(8,128)(2,1)S(1)}, bf16[4,40,2048]{2,1,0:T(8,128)(2,1)S(1)}, u32[]{:S(2)}, u32[]{:S(2)}) collective-permute-start(bf16[4,40,2048]{2,1,0:T(8,128)(2,1)S(1)} %all-to-all-done.1.refs_1_), channel_id=1, source_target_pairs={{0,384},{128,0},{256,128},{384,256},{1,385},{129,1},{257,129},{385... | collective-permute-start | bytes 1966088 | tf_op jit(solution)/shard_map/ppermute | solution.py:288
  44.8 2.4 %collective-permute-start = (bf16[4,40,2048]{2,1,0:T(8,128)(2,1)S(1)}, bf16[4,40,2048]{2,1,0:T(8,128)(2,1)S(1)}, u32[]{:S(2)}, u32[]{:S(2)}) collective-permute-start(bf16[4,40,2048]{2,1,0:T(8,128)(2,1)S(1)} %all_to_all.20.refs_0_), channel_id=1, source_target_pairs={{0,384},{128,0},{256,128},{384,256},{1,385},{129,1},{257,129},{385... | collective-permute-start | bytes 1966088 | tf_op jit(solution)/shard_map/ppermute | solution.py:288
  47.2 2.9 %collective-permute-start.5 = (bf16[4,40,2048]{2,1,0:T(8,128)(2,1)S(1)}, bf16[4,40,2048]{2,1,0:T(8,128)(2,1)}, u32[]{:S(2)}, u32[]{:S(2)}) collective-permute-start(bf16[4,40,2048]{2,1,0:T(8,128)(2,1)S(1)} %all-to-all-done.1.refs_1_), channel_id=1, source_target_pairs={{0,128},{128,256},{256,384},{384,0},{1,129},{129,257},{257,385},{3... | collective-permute-start | bytes 1966088 | tf_op jit(solution)/shard_map/ppermute | solution.py:288
  50.1 0.0 collective-permute-done.2.refs_6_
  50.1 1.9 %collective-permute-start.3 = (bf16[4,40,2048]{2,1,0:T(8,128)(2,1)S(1)}, bf16[4,40,2048]{2,1,0:T(8,128)(2,1)}, u32[]{:S(2)}, u32[]{:S(2)}) collective-permute-start(bf16[4,40,2048]{2,1,0:T(8,128)(2,1)S(1)} %collective-permute-done.2.refs_6_), channel_id=1, source_target_pairs={{0,128},{128,256},{256,384},{384,0},{1,129},{129,257},{257,385},{3... | collective-permute-start | bytes 1966088 | tf_op jit(solution)/shard_map/ppermute | solution.py:288
  52.1 3.7 %collective-permute-done.1.refs_3_ = bf16[4,40,2048]{2,1,0:T(8,128)(2,1)S(1)} collective-permute-done((bf16[4,40,2048]{2,1,0:T(8,128)(2,1)S(1)}, bf16[4,40,2048]{2,1,0:T(8,128)(2,1)S(1)}, u32[]{:S(2)}, u32[]{:S(2)}) %collective-permute-start.1) | collective-permute-done | bytes 655392 | tf_op jit(solution)/shard_map/ppermute | solution.py:288
  55.7 5.4 %collective-permute-start.4 = (bf16[4,40,2048]{2,1,0:T(8,128)(2,1)S(1)}, bf16[4,40,2048]{2,1,0:T(8,128)(2,1)}, u32[]{:S(2)}, u32[]{:S(2)}) collective-permute-start(bf16[4,40,2048]{2,1,0:T(8,128)(2,1)S(1)} %collective-permute-done.1.refs_3_), channel_id=1, source_target_pairs={{0,384},{128,0},{256,128},{384,256},{1,385},{129,1},{257,129},{385... | collective-permute-start | bytes 1966088 | tf_op jit(solution)/shard_map/ppermute | solution.py:288
  61.2 8.6 %collective-permute-done.refs_2_ = bf16[4,40,2048]{2,1,0:T(8,128)(2,1)S(1)} collective-permute-done((bf16[4,40,2048]{2,1,0:T(8,128)(2,1)S(1)}, bf16[4,40,2048]{2,1,0:T(8,128)(2,1)S(1)}, u32[]{:S(2)}, u32[]{:S(2)}) %collective-permute-start) | collective-permute-done | bytes 655392 | tf_op jit(solution)/shard_map/ppermute | solution.py:288
  69.8 0.0 collective-permute-done.5.refs_7_
  69.8 7.3 %collective-permute-done.3.refs_4_ = bf16[4,40,2048]{2,1,0:T(8,128)(2,1)} collective-permute-done((bf16[4,40,2048]{2,1,0:T(8,128)(2,1)S(1)}, bf16[4,40,2048]{2,1,0:T(8,128)(2,1)}, u32[]{:S(2)}, u32[]{:S(2)}) %collective-permute-start.3) | collective-permute-done | bytes 655392 | tf_op jit(solution)/shard_map/ppermute | solution.py:288
  77.1 6.7 %collective-permute-done.4.refs_5_ = bf16[4,40,2048]{2,1,0:T(8,128)(2,1)} collective-permute-done((bf16[4,40,2048]{2,1,0:T(8,128)(2,1)S(1)}, bf16[4,40,2048]{2,1,0:T(8,128)(2,1)}, u32[]{:S(2)}, u32[]{:S(2)}) %collective-permute-start.4) | collective-permute-done | bytes 655392 | tf_op jit(solution)/shard_map/ppermute | solution.py:288
  83.8 18.5 %all-gather.3.cloned.1.call-done = bf16[12288,512]{1,0:T(8,128)(2,1)} async-done(((bf16[384,512]{1,0:T(8,128)(2,1)}), bf16[12288,512]{1,0:T(8,128)(2,1)}) %all-gather.3.cloned.1.call-update) | async-done | bytes 12582928 | tf_op jit(solution)/shard_map/all_gather | solution.py:294
  102.3 7.2 %shard_map.75 = (bf16[4,16,40,256]{3,2,1,0:T(8,128)(2,1)S(1)}, bf16[2,8,2,128,512]{4,3,2,1,0:T(8,128)(2,1)S(1)}) custom-call(s32[1]{0:T(128)} %bitcast.place_ref, bf16[4,40,2048]{2,1,0:T(8,128)(2,1)S(1)} %all_to_all.20.refs_0_, bf16[4,40,2048]{2,1,0:T(8,128)(2,1)S(1)} %all-to-all-done.1.refs_1_, bf16[4,40,2048]{2,1,0:T(8,128)(2,1)S(1)} %collective-permute-done.refs_2_, ...), custom_call_target="tpu_custom_call" | custom-call | flops 2684354560 | bytes 13631488 | tf_op jit(solution)/shard_map/pallas_call | solution.py:250
  109.5 21.1 %all_to_all.21.hidden_ref = bf16[4,16,40,256]{3,2,1,0:T(8,128)(2,1)S(1)} all-to-all(bf16[4,16,40,256]{3,2,1,0:T(8,128)(2,1)S(1)} %get-tuple-element.11), channel_id=1, replica_groups=mesh['y'=4,'c'=2,'x'=4,'z'=16] {'y'}, dimensions={0} | all-to-all | bytes 2621440 | tf_op jit(solution)/shard_map/all_to_all | solution.py:303
  130.7 2.6 %shard_map.76 = bf16[16,40,1024]{2,1,0:T(8,128)(2,1)} custom-call(bf16[4,16,40,256]{3,2,1,0:T(8,128)(2,1)S(1)} %all_to_all.21.hidden_ref, bf16[2,8,2,128,512]{4,3,2,1,0:T(8,128)(2,1)S(1)} %get-tuple-element.12.weights_ref), custom_call_target="tpu_custom_call" | custom-call | flops 1342177280 | bytes 6815744 | tf_op jit(solution)/shard_map/pallas_call | solution.py:266
  133.3 0.0 copy-start.2
  133.3 4.8 %all-to-all-start.3 = ((bf16[16,40,1024]{2,1,0:T(8,128)(2,1)}), bf16[16,40,1024]{2,1,0:T(8,128)(2,1)S(1)}, u32[]{:S(2)}, u32[]{:S(2)}) async-start(bf16[16,40,1024]{2,1,0:T(8,128)(2,1)} %shard_map.76), calls=%async_computation.3 | async-start | bytes 2621440 | tf_op jit(solution)/shard_map/all_to_all | solution.py:304
  138.1 0.1 copy.8.routes_ref
  138.2 0.0 copy-done.2
  138.2 0.1 copy.9.numerators_ref
  138.3 17.9 %all-to-all-done.3.rows_ref = bf16[16,40,1024]{2,1,0:T(8,128)(2,1)S(1)} async-done(((bf16[16,40,1024]{2,1,0:T(8,128)(2,1)}), bf16[16,40,1024]{2,1,0:T(8,128)(2,1)S(1)}, u32[]{:S(2)}, u32[]{:S(2)}) %all-to-all-start.3) | async-done | bytes 1310752 | tf_op jit(solution)/shard_map/all_to_all | solution.py:304
  156.2 1.3 shard_map.77
Async XLA Ops:
  6.5 2.5 %copy-start.1 = (s32[64,2]{0,1:T(2,128)S(1)}, s32[64,2]{0,1:T(2,128)}, u32[]{:S(2)}) copy-start(s32[64,2]{0,1:T(2,128)} %param.8) | copy-start | bytes 1540
  6.5 2.5 %copy-start = (bf16[64,4096]{1,0:T(8,128)(2,1)S(1)}, bf16[64,4096]{1,0:T(8,128)(2,1)}, u32[]{:S(2)}) copy-start(bf16[64,4096]{1,0:T(8,128)(2,1)} %tokens_ref.1) | copy-start | bytes 1572868
  6.5 95.8 %all-gather.3.cloned.1.call-start = ((), (), s32[]{:S(2)}) async-start(), calls=%async_computation.4 | async-start | bytes 12976128 | tf_op jit(solution)/shard_map/all_gather | solution.py:294
  25.7 11.1 %all-to-all-start.1 = ((bf16[4,40,2048]{2,1,0:T(8,128)(2,1)}), bf16[4,40,2048]{2,1,0:T(8,128)(2,1)S(1)}, u32[]{:S(2)}, u32[]{:S(2)}) async-start(bf16[4,40,2048]{2,1,0:T(8,128)(2,1)} %bitcast.3), calls=%async_computation.1 | async-start | bytes 1310720 | tf_op jit(solution)/shard_map/all_to_all | solution.py:297
  29.2 21.0 %collective-permute-start.2 = (bf16[4,40,2048]{2,1,0:T(8,128)(2,1)S(1)}, bf16[4,40,2048]{2,1,0:T(8,128)(2,1)S(1)}, u32[]{:S(2)}, u32[]{:S(2)}) collective-permute-start(bf16[4,40,2048]{2,1,0:T(8,128)(2,1)S(1)} %all_to_all.20.refs_0_), channel_id=1, source_target_pairs={{0,128},{128,256},{256,384},{384,0},{1,129},{129,257},{257,385},{3... | collective-permute-start | bytes 1966088 | tf_op jit(solution)/shard_map/ppermute | solution.py:288
  36.8 19.0 %collective-permute-start.1 = (bf16[4,40,2048]{2,1,0:T(8,128)(2,1)S(1)}, bf16[4,40,2048]{2,1,0:T(8,128)(2,1)S(1)}, u32[]{:S(2)}, u32[]{:S(2)}) collective-permute-start(bf16[4,40,2048]{2,1,0:T(8,128)(2,1)S(1)} %all-to-all-done.1.refs_1_), channel_id=1, source_target_pairs={{0,384},{128,0},{256,128},{384,256},{1,385},{129,1},{257,129},{385... | collective-permute-start | bytes 1966088 | tf_op jit(solution)/shard_map/ppermute | solution.py:288
  44.8 25.0 %collective-permute-start = (bf16[4,40,2048]{2,1,0:T(8,128)(2,1)S(1)}, bf16[4,40,2048]{2,1,0:T(8,128)(2,1)S(1)}, u32[]{:S(2)}, u32[]{:S(2)}) collective-permute-start(bf16[4,40,2048]{2,1,0:T(8,128)(2,1)S(1)} %all_to_all.20.refs_0_), channel_id=1, source_target_pairs={{0,384},{128,0},{256,128},{384,256},{1,385},{129,1},{257,129},{385... | collective-permute-start | bytes 1966088 | tf_op jit(solution)/shard_map/ppermute | solution.py:288
  47.2 22.5 %collective-permute-start.5 = (bf16[4,40,2048]{2,1,0:T(8,128)(2,1)S(1)}, bf16[4,40,2048]{2,1,0:T(8,128)(2,1)}, u32[]{:S(2)}, u32[]{:S(2)}) collective-permute-start(bf16[4,40,2048]{2,1,0:T(8,128)(2,1)S(1)} %all-to-all-done.1.refs_1_), channel_id=1, source_target_pairs={{0,128},{128,256},{256,384},{384,0},{1,129},{129,257},{257,385},{3... | collective-permute-start | bytes 1966088 | tf_op jit(solution)/shard_map/ppermute | solution.py:288
  50.1 27.0 %collective-permute-start.3 = (bf16[4,40,2048]{2,1,0:T(8,128)(2,1)S(1)}, bf16[4,40,2048]{2,1,0:T(8,128)(2,1)}, u32[]{:S(2)}, u32[]{:S(2)}) collective-permute-start(bf16[4,40,2048]{2,1,0:T(8,128)(2,1)S(1)} %collective-permute-done.2.refs_6_), channel_id=1, source_target_pairs={{0,128},{128,256},{256,384},{384,0},{1,129},{129,257},{257,385},{3... | collective-permute-start | bytes 1966088 | tf_op jit(solution)/shard_map/ppermute | solution.py:288
  55.7 28.1 %collective-permute-start.4 = (bf16[4,40,2048]{2,1,0:T(8,128)(2,1)S(1)}, bf16[4,40,2048]{2,1,0:T(8,128)(2,1)}, u32[]{:S(2)}, u32[]{:S(2)}) collective-permute-start(bf16[4,40,2048]{2,1,0:T(8,128)(2,1)S(1)} %collective-permute-done.1.refs_3_), channel_id=1, source_target_pairs={{0,384},{128,0},{256,128},{384,256},{1,385},{129,1},{257,129},{385... | collective-permute-start | bytes 1966088 | tf_op jit(solution)/shard_map/ppermute | solution.py:288
  133.3 4.9 %copy-start.2 = (s32[64,2]{0,1:T(2,128)S(1)}, s32[64,2]{0,1:T(2,128)}, u32[]{:S(2)}) copy-start(s32[64,2]{0,1:T(2,128)} %param.9) | copy-start | bytes 1540
  133.3 22.9 %all-to-all-start.3 = ((bf16[16,40,1024]{2,1,0:T(8,128)(2,1)}), bf16[16,40,1024]{2,1,0:T(8,128)(2,1)S(1)}, u32[]{:S(2)}, u32[]{:S(2)}) async-start(bf16[16,40,1024]{2,1,0:T(8,128)(2,1)} %shard_map.76), calls=%async_computation.3 | async-start | bytes 2621440 | tf_op jit(solution)/shard_map/all_to_all | solution.py:304
Sparse Core Ops, SparseCore 0:
  9.5 92.7 all-gather.2

commit v7 on v5

--- a/solution.py
+++ b/solution.py
@@ -66,27 +66,25 @@
     return (coded * scale).astype(jnp.bfloat16)
 
 
-def places(dims, axis):
-    place = lax.broadcasted_iota(jnp.int32, dims, axis)
+def placements(count_ref, columns_ref):
+    dims = (ALL_SLOTS, TOK)
+    place = lax.broadcasted_iota(jnp.int32, dims, 0)
+    row = lax.broadcasted_iota(jnp.int32, dims, 1)
     column = (place * 1639) >> 16
     second, slot = slot_at(place - column * SLOTS)
-    return 2 * column + second, slot
-
-
-def earlier_rows(axis):
-    first, second = (lax.broadcasted_iota(jnp.int32, (TOK, TOK), a) for a in (axis, 1 - axis))
-    return (first < second).astype(jnp.float32).astype(jnp.bfloat16)
+    expert = 2 * column + second
+    live = row < count_ref[0]
+    by_first, by_second = ((columns_ref[i : i + 1, :] == expert) & live for i in range(2))
+    named = (by_first | by_second).astype(jnp.float32).astype(jnp.bfloat16)
+    earlier = (lax.broadcasted_iota(jnp.int32, (TOK, TOK), 0) < lax.broadcasted_iota(jnp.int32, (TOK, TOK), 1))
+    rank = jnp.dot(named, earlier.astype(jnp.float32).astype(jnp.bfloat16), preferred_element_type=jnp.float32)
+    here = rank.astype(jnp.int32) == slot
+    return by_first & here, by_second & here
 
 
 def encode_kernel(count_ref, columns_ref, tokens_ref, first_ref, second_ref):
-    dims = (ALL_SLOTS, TOK)
-    expert, slot = places(dims, 0)
-    named = (columns_ref[0:1, :] == expert) | (columns_ref[1:2, :] == expert)
-    named = named & (lax.broadcasted_iota(jnp.int32, dims, 1) < count_ref[0])
-    one = named.astype(jnp.float32).astype(jnp.bfloat16)
-    rank = jnp.dot(one, earlier_rows(0), preferred_element_type=jnp.float32)
-    chosen = named & (rank.astype(jnp.int32) == slot)
-    chosen = chosen.astype(jnp.float32).astype(jnp.bfloat16)
+    by_first, by_second = placements(count_ref, columns_ref)
+    chosen = (by_first | by_second).astype(jnp.float32).astype(jnp.bfloat16)
 
     def step(member, carry):
         for half, out_ref in enumerate((first_ref, second_ref)):
@@ -100,21 +98,15 @@
     lax.fori_loop(0, MEMBERS, step, 0)
 
 
-def mix_kernel(count_ref, routes_ref, numerators_ref, rows_ref, out_ref):
-    dims = (TOK, ALL_SLOTS)
-    expert, slot = places(dims, 1)
-    live = lax.broadcasted_iota(jnp.int32, dims, 0) < count_ref[0]
-    by_first = (routes_ref[:, 0:1] == expert) & live
-    by_second = (routes_ref[:, 1:2] == expert) & live
-    one = (by_first | by_second).astype(jnp.float32).astype(jnp.bfloat16)
-    rank = jnp.dot(earlier_rows(1), one, preferred_element_type=jnp.float32)
-    here = rank.astype(jnp.int32) == slot
+def mix_kernel(count_ref, columns_ref, numerators_ref, rows_ref, out_ref):
+    by_first, by_second = placements(count_ref, columns_ref)
     share = numerators_ref[...].astype(jnp.float32) / 256.0
-    shares = jnp.where(by_first & here, share[:, 0:1], 0.0) + jnp.where(by_second & here, share[:, 1:2], 0.0)
+    shares = jnp.where(by_first, share[0:1], 0.0) + jnp.where(by_second, share[1:2], 0.0)
     shares = shares.astype(jnp.bfloat16)
     for quarter in range(Y):
         rows = rows_ref[quarter * X : (quarter + 1) * X].reshape(ALL_SLOTS, MEMBERS * 128)
-        mixed = jnp.dot(shares, rows, preferred_element_type=jnp.float32).astype(jnp.bfloat16)
+        mixed = lax.dot_general(shares, rows, (((0,), (0,)), ((), ())), preferred_element_type=jnp.float32)
+        mixed = mixed.astype(jnp.bfloat16)
         for member in range(MEMBERS):
             at = member * SHARD + quarter * 128
             out_ref[:, at : at + 128] = mixed[:, member * 128 : (member + 1) * 128]
@@ -154,8 +146,8 @@
 
 
 def hidden_kernel(place_ref, *refs):
-    rows, weights_ref, out_ref, held, sems = refs[: 2 * Y], *refs[2 * Y : 2 * Y + 4]
-    sums = refs[2 * Y + 4 :]
+    rows, weights_ref, out_ref, held, here, sems, row_sems = refs[: 2 * Y], *refs[2 * Y : 2 * Y + 6]
+    sums = refs[2 * Y + 6 :]
     groups = MEMBERS // DEEP
     copies = [
         pltpu.make_async_copy(
@@ -163,12 +155,20 @@
         )
         for i in range(C * groups)
     ]
+    moves = [pltpu.make_async_copy(ref, here.at[i], row_sems.at[i]) for i, ref in enumerate(rows)]
+    for move in moves[0::2]:
+        move.start()
     copies[0].start()
+    for move in moves[1::2]:
+        move.start()
     copies[1].start()
     for i, copy in enumerate(copies):
         half, group = i // groups, i % groups
         at = slice(group * DEEP * HALF, (group + 1) * DEEP * HALF)
-        blocks = [split_rows(ref[:, :, at]) for ref in rows[half::2]]
+        if group == 0:
+            for move in moves[half::2]:
+                move.wait()
+        blocks = [split_rows(here[2 * offset + half, :, :, at]) for offset in range(Y)]
         copy.wait()
         if i + 2 < len(copies):
             copies[i + 2].start()
@@ -185,21 +185,25 @@
             out_ref[copy, pl.ds(source * X, X)] = block
 
 
-def down_kernel(hidden_ref, weights_ref, out_ref, *rows):
+def down_kernel(hidden_ref, weights_ref, out_ref, held, sems, *rows):
     main = SRC * MAIN
-
-    @pl.when(pl.program_id(0) == 0)
-    def _():
-        for quarter in range(Y):
-            at = slice(quarter * FQ, (quarter + 1) * FQ)
-            for ref, (run, rest) in zip(rows, split_rows(hidden_ref[quarter])):
-                ref[:main, at] = run
-                ref[main:, at] = rest
-
-    def result(expert):
+    starts = range(0, MEMBERS, WIDE)
+    copies = [
+        pltpu.make_async_copy(weights_ref.at[:, start : start + WIDE, :, HALF:], held.at[i], sems.at[i])
+        for i, start in enumerate(starts)
+    ]
+    for copy in copies:
+        copy.start()
+    for quarter in range(Y):
+        at = slice(quarter * FQ, (quarter + 1) * FQ)
+        for ref, (run, rest) in zip(rows, split_rows(hidden_ref[quarter])):
+            ref[:main, at] = run
+            ref[main:, at] = rest
+
+    def result(i, expert):
         weights = jnp.concatenate(
             [
-                jnp.concatenate([weights_ref[expert, m, half, :, q * 128 : (q + 1) * 128] for m in range(WIDE)], axis=1)
+                jnp.concatenate([held[i, expert, m, half, :, q * 128 : (q + 1) * 128] for m in range(WIDE)], axis=1)
                 for q in range(Y)
                 for half in range(C)
             ],
@@ -207,7 +211,9 @@
         )
         return jnp.dot(rows[expert][...], weights, preferred_element_type=jnp.float32)
 
-    out_ref[...] = join_rows(result(0), result(1))
+    for i, start in enumerate(starts):
+        copies[i].wait()
+        out_ref[:, :, start * 128 : (start + WIDE) * 128] = join_rows(result(i, 0), result(i, 1))
 
 
 SCALAR = pl.BlockSpec(memory_space=pltpu.SMEM)
@@ -249,11 +255,13 @@
     return pl.pallas_call(
         hidden_kernel,
         out_shape=shape((Y, SRC, SLOTS, FQ)),
-        in_specs=[SCALAR, *[WHOLE] * (2 * Y), ANY],
+        in_specs=[SCALAR, *[ANY] * (2 * Y), ANY],
         out_specs=WHOLE,
         scratch_shapes=[
             pltpu.VMEM((pieces, 2, DEEP, HALF, 2 * FQ), jnp.bfloat16),
+            pltpu.VMEM((2 * Y, X, SLOTS, D // 2), jnp.bfloat16),
             pltpu.SemaphoreType.DMA((pieces,)),
+            pltpu.SemaphoreType.DMA((2 * Y,)),
             *[pltpu.VMEM((SRC * SLOTS // 2, 2 * FQ), jnp.float32)] * 2,
         ],
         compiler_params=params(36),
@@ -262,14 +270,18 @@
 
 
 def down_rows(hidden, weights):
+    pieces = MEMBERS // WIDE
     return pl.pallas_call(
         down_kernel,
-        grid=(MEMBERS // WIDE,),
         out_shape=shape((SRC, SLOTS, MEMBERS * 128)),
-        in_specs=[WHOLE, pl.BlockSpec((2, WIDE, C, 128, SHARD), lambda n: (0, n, 0, HALF // 128, 0))],
-        out_specs=pl.BlockSpec((SRC, SLOTS, WIDE * 128), lambda n: (0, 0, n)),
-        scratch_shapes=[pltpu.VMEM((SRC * SLOTS // 2, F), jnp.bfloat16)] * 2,
-        compiler_params=params(24),
+        in_specs=[WHOLE, ANY],
+        out_specs=WHOLE,
+        scratch_shapes=[
+            pltpu.VMEM((pieces, 2, WIDE, C, 128, SHARD), jnp.bfloat16),
+            pltpu.SemaphoreType.DMA((pieces,)),
+            *[pltpu.VMEM((SRC * SLOTS // 2, F), jnp.bfloat16)] * 2,
+        ],
+        compiler_params=params(50),
         cost_estimate=pl.CostEstimate(flops=2 * ROWS * F * F, bytes_accessed=4 * ROWS * F + 4 * F * F, transcendentals=0),
     )(hidden, weights)
 
@@ -281,7 +293,7 @@
         in_specs=[SCALAR] + [WHOLE] * 3,
         out_specs=WHOLE,
         compiler_params=params(8),
-    )(counts, routes, numerators, rows)
+    )(counts, routes.T, numerators.T, rows)
 
 
 def shift(block, by):

time: 166 us -> 165 us (level)
  blocking collectives: 33.4 us -> 56.1 us
  waiting for transfers between devices: 64.8 us -> 46.9 us
  starting transfers between devices: 34.5 us -> 29.7 us
    all_to_all x0 -> x1, blocking collectives: none -> 22.7 us  [local(): lax.all_to_all(down_rows(hidden, weights), ('y', 'x'), 0, 0, tiled=True)]
    all_to_all x1 -> x0, waiting for transfers between devices: 17.9 us -> none  [local(): lax.all_to_all(down_rows(hidden, weights), ('y', 'x'), 0, 0, tiled=True)]
    all_to_all x1 -> x0, starting transfers between devices: 4.81 us -> none  [local(): lax.all_to_all(down_rows(hidden, weights), ('y', 'x'), 0, 0, tiled=True)]
  transfers between devices with their start and end apart: 9 -> 8, of which waited for: 7 -> 6; matrix products, arithmetic and copies ran while one was open for 0% -> 0% of each run, Pallas kernels for 3% -> 3%
where the time goes in v7:
time: 165 us; the launch traced here: 164 us
  blocking collectives  56.1 us (34%)
  waiting for transfers between devices  46.9 us (28%)
  starting transfers between devices  29.7 us (18%)
  Pallas kernels  16.9 us (10%)
  between operations  14.2 us (9%)
    ppermute x6, waiting for transfers between devices, shift(): return lax.ppermute(block, 'y', [(i, (i + by) % Y) for i in range(Y)])  26.3 us
    ppermute x6, starting transfers between devices, shift(): return lax.ppermute(block, 'y', [(i, (i + by) % Y) for i in range(Y)])  26.2 us
    all_to_all x1, blocking collectives, local(): lax.all_to_all(down_rows(hidden, weights), ('y', 'x'), 0, 0, tiled=True)  22.7 us
    all_to_all x1, blocking collectives, local(): lax.all_to_all(hidden_rows(place, rows, weights), 'y', 0, 0, tiled=True)  21.1 us
    all_gather x1, waiting for transfers between devices, local(): lax.all_gather(weights, ('z', 'c'))  18.4 us
    all_to_all x1, blocking collectives, local(): lax.all_to_all(first.reshape(X, SLOTS, D // 2), 'x', 0, 0, tiled=True)  12.3 us
    pallas_call x1, Pallas kernels, hidden_rows(): pl.pallas_call(hidden_kernel, out_shape=shape((Y, SRC, SLOTS, FQ)), in_sp...  6.1 us
    pallas_call x1, Pallas kernels, encode(): pl.pallas_call(encode_kernel, out_shape=[shape((ALL_SLOTS, D // 2))] * 2,...  4.31 us
  transfers between devices with their start and end apart: 8, of which 6 were waited for; matrix products, arithmetic and copies ran while one was open for 0% of the time, Pallas kernels for 3%

profile of v7, /device:TPU:1, one launch (start us, length us, event | category | flops | bytes accessed | tf_op | source)
XLA Modules:
  0.0 163.8 jit_solution(16148602866330591722)
XLA Ops:
  6.5 0.0 copy-start.1
  6.5 0.0 copy-start
  6.5 0.0 all-gather.3.cloned.1.call-start
  6.5 1.8 %shard_map.74 = bf16[384,512]{1,0:T(8,128)(2,1)} custom-call(bf16[512,1024]{1,0:T(8,128)(2,1)} %gate_ref.1, bf16[512,1024]{1,0:T(8,128)(2,1)} %up_ref.1, bf16[1024,512]{1,0:T(8,128)(2,1)} %down_ref.1), custom_call_target="tpu_custom_call" | custom-call | tf_op jit(solution)/shard_map/pallas_call | solution.py:244
  8.4 0.0 all-gather.3.cloned.1.call-update
  9.1 0.0 copy-done.1
  9.1 0.0 copy-done
  9.1 4.3 %shard_map.73 = (bf16[160,2048]{1,0:T(8,128)(2,1)S(1)}, bf16[160,2048]{1,0:T(8,128)(2,1)}) custom-call(s32[1]{0:T(128)S(6)} %copy.8.count_ref, s32[2,64]{1,0:T(2,128)S(1)} %bitcast.7, bf16[64,4096]{1,0:T(8,128)(2,1)S(1)} %copy-done), custom_call_target="tpu_custom_call" | custom-call | flops 83886080 | bytes 1835008 | tf_op jit(solution)/shard_map/pallas_call | solution.py:233
  13.4 12.3 %all_to_all.20.refs_0_ = bf16[4,40,2048]{2,1,0:T(8,128)(2,1)S(1)} all-to-all(bf16[4,40,2048]{2,1,0:T(8,128)(2,1)S(1)} %bitcast.6), channel_id=1, replica_groups=mesh['y'=4,'c'=2,'x'=4,'z'=16] {'x'}, dimensions={0} | all-to-all | bytes 1310720 | tf_op jit(solution)/shard_map/all_to_all | solution.py:308
  25.7 3.5 %all-to-all-start.1 = ((bf16[4,40,2048]{2,1,0:T(8,128)(2,1)}), bf16[4,40,2048]{2,1,0:T(8,128)(2,1)S(1)}, u32[]{:S(2)}, u32[]{:S(2)}) async-start(bf16[4,40,2048]{2,1,0:T(8,128)(2,1)} %bitcast.4), calls=%async_computation.1 | async-start | bytes 1310720 | tf_op jit(solution)/shard_map/all_to_all | solution.py:309
  29.2 5.5 %collective-permute-start.2 = (bf16[4,40,2048]{2,1,0:T(8,128)(2,1)S(1)}, bf16[4,40,2048]{2,1,0:T(8,128)(2,1)S(1)}, u32[]{:S(2)}, u32[]{:S(2)}) collective-permute-start(bf16[4,40,2048]{2,1,0:T(8,128)(2,1)S(1)} %all_to_all.20.refs_0_), channel_id=1, source_target_pairs={{0,128},{128,256},{256,384},{384,0},{1,129},{129,257},{257,385},{3... | collective-permute-start | bytes 1966088 | tf_op jit(solution)/shard_map/ppermute | solution.py:300
  34.7 2.1 %all-to-all-done.1.refs_1_ = bf16[4,40,2048]{2,1,0:T(8,128)(2,1)S(1)} async-done(((bf16[4,40,2048]{2,1,0:T(8,128)(2,1)}), bf16[4,40,2048]{2,1,0:T(8,128)(2,1)S(1)}, u32[]{:S(2)}, u32[]{:S(2)}) %all-to-all-start.1) | async-done | bytes 655392 | tf_op jit(solution)/shard_map/all_to_all | solution.py:309
  36.8 8.1 %collective-permute-start.1 = (bf16[4,40,2048]{2,1,0:T(8,128)(2,1)S(1)}, bf16[4,40,2048]{2,1,0:T(8,128)(2,1)S(1)}, u32[]{:S(2)}, u32[]{:S(2)}) collective-permute-start(bf16[4,40,2048]{2,1,0:T(8,128)(2,1)S(1)} %all-to-all-done.1.refs_1_), channel_id=1, source_target_pairs={{0,384},{128,0},{256,128},{384,256},{1,385},{129,1},{257,129},{385... | collective-permute-start | bytes 1966088 | tf_op jit(solution)/shard_map/ppermute | solution.py:300
  44.9 2.4 %collective-permute-start = (bf16[4,40,2048]{2,1,0:T(8,128)(2,1)S(1)}, bf16[4,40,2048]{2,1,0:T(8,128)(2,1)S(1)}, u32[]{:S(2)}, u32[]{:S(2)}) collective-permute-start(bf16[4,40,2048]{2,1,0:T(8,128)(2,1)S(1)} %all_to_all.20.refs_0_), channel_id=1, source_target_pairs={{0,384},{128,0},{256,128},{384,256},{1,385},{129,1},{257,129},{385... | collective-permute-start | bytes 1966088 | tf_op jit(solution)/shard_map/ppermute | solution.py:300
  47.3 2.9 %collective-permute-start.5 = (bf16[4,40,2048]{2,1,0:T(8,128)(2,1)S(1)}, bf16[4,40,2048]{2,1,0:T(8,128)(2,1)}, u32[]{:S(2)}, u32[]{:S(2)}) collective-permute-start(bf16[4,40,2048]{2,1,0:T(8,128)(2,1)S(1)} %all-to-all-done.1.refs_1_), channel_id=1, source_target_pairs={{0,128},{128,256},{256,384},{384,0},{1,129},{129,257},{257,385},{3... | collective-permute-start | bytes 1966088 | tf_op jit(solution)/shard_map/ppermute | solution.py:300
  50.2 0.0 collective-permute-done.2.refs_6_
  50.2 1.9 %collective-permute-start.3 = (bf16[4,40,2048]{2,1,0:T(8,128)(2,1)S(1)}, bf16[4,40,2048]{2,1,0:T(8,128)(2,1)}, u32[]{:S(2)}, u32[]{:S(2)}) collective-permute-start(bf16[4,40,2048]{2,1,0:T(8,128)(2,1)S(1)} %collective-permute-done.2.refs_6_), channel_id=1, source_target_pairs={{0,128},{128,256},{256,384},{384,0},{1,129},{129,257},{257,385},{3... | collective-permute-start | bytes 1966088 | tf_op jit(solution)/shard_map/ppermute | solution.py:300
  52.1 3.7 %collective-permute-done.1.refs_3_ = bf16[4,40,2048]{2,1,0:T(8,128)(2,1)S(1)} collective-permute-done((bf16[4,40,2048]{2,1,0:T(8,128)(2,1)S(1)}, bf16[4,40,2048]{2,1,0:T(8,128)(2,1)S(1)}, u32[]{:S(2)}, u32[]{:S(2)}) %collective-permute-start.1) | collective-permute-done | bytes 655392 | tf_op jit(solution)/shard_map/ppermute | solution.py:300
  55.8 5.4 %collective-permute-start.4 = (bf16[4,40,2048]{2,1,0:T(8,128)(2,1)S(1)}, bf16[4,40,2048]{2,1,0:T(8,128)(2,1)}, u32[]{:S(2)}, u32[]{:S(2)}) collective-permute-start(bf16[4,40,2048]{2,1,0:T(8,128)(2,1)S(1)} %collective-permute-done.1.refs_3_), channel_id=1, source_target_pairs={{0,384},{128,0},{256,128},{384,256},{1,385},{129,1},{257,129},{385... | collective-permute-start | bytes 1966088 | tf_op jit(solution)/shard_map/ppermute | solution.py:300
  61.2 8.6 %collective-permute-done.refs_2_ = bf16[4,40,2048]{2,1,0:T(8,128)(2,1)S(1)} collective-permute-done((bf16[4,40,2048]{2,1,0:T(8,128)(2,1)S(1)}, bf16[4,40,2048]{2,1,0:T(8,128)(2,1)S(1)}, u32[]{:S(2)}, u32[]{:S(2)}) %collective-permute-start) | collective-permute-done | bytes 655392 | tf_op jit(solution)/shard_map/ppermute | solution.py:300
  69.8 0.0 collective-permute-done.5.refs_7_
  69.8 7.3 %collective-permute-done.3.refs_4_ = bf16[4,40,2048]{2,1,0:T(8,128)(2,1)} collective-permute-done((bf16[4,40,2048]{2,1,0:T(8,128)(2,1)S(1)}, bf16[4,40,2048]{2,1,0:T(8,128)(2,1)}, u32[]{:S(2)}, u32[]{:S(2)}) %collective-permute-start.3) | collective-permute-done | bytes 655392 | tf_op jit(solution)/shard_map/ppermute | solution.py:300
  77.2 6.7 %collective-permute-done.4.refs_5_ = bf16[4,40,2048]{2,1,0:T(8,128)(2,1)} collective-permute-done((bf16[4,40,2048]{2,1,0:T(8,128)(2,1)S(1)}, bf16[4,40,2048]{2,1,0:T(8,128)(2,1)}, u32[]{:S(2)}, u32[]{:S(2)}) %collective-permute-start.4) | collective-permute-done | bytes 655392 | tf_op jit(solution)/shard_map/ppermute | solution.py:300
  83.9 18.4 %all-gather.3.cloned.1.call-done = bf16[12288,512]{1,0:T(8,128)(2,1)} async-done(((bf16[384,512]{1,0:T(8,128)(2,1)}), bf16[12288,512]{1,0:T(8,128)(2,1)}) %all-gather.3.cloned.1.call-update) | async-done | bytes 12582928 | tf_op jit(solution)/shard_map/all_gather | solution.py:306
  102.3 6.1 %shard_map.75 = bf16[4,16,40,256]{3,2,1,0:T(8,128)(2,1)S(1)} custom-call(s32[1]{0:T(128)} %bitcast.2.place_ref, bf16[4,40,2048]{2,1,0:T(8,128)(2,1)S(1)} %all_to_all.20.refs_0_, bf16[4,40,2048]{2,1,0:T(8,128)(2,1)S(1)} %all-to-all-done.1.refs_1_, bf16[4,40,2048]{2,1,0:T(8,128)(2,1)S(1)} %collective-permute-done.refs_2_, ...), custom_call_target="tpu_custom_call" | custom-call | flops 2684354560 | bytes 13631488 | tf_op jit(solution)/shard_map/pallas_call | solution.py:255
  108.4 21.1 %all_to_all.21.hidden_ref = bf16[4,16,40,256]{3,2,1,0:T(8,128)(2,1)S(1)} all-to-all(bf16[4,16,40,256]{3,2,1,0:T(8,128)(2,1)S(1)} %shard_map.75), channel_id=1, replica_groups=mesh['y'=4,'c'=2,'x'=4,'z'=16] {'y'}, dimensions={0} | all-to-all | bytes 2621440 | tf_op jit(solution)/shard_map/all_to_all | solution.py:314
  129.6 3.3 %shard_map.76 = bf16[16,40,1024]{2,1,0:T(8,128)(2,1)S(1)} custom-call(bf16[4,16,40,256]{3,2,1,0:T(8,128)(2,1)S(1)} %all_to_all.21.hidden_ref, bf16[2,8,2,384,512]{4,3,2,1,0:T(8,128)(2,1)} %bitcast.11), custom_call_target="tpu_custom_call" | custom-call | flops 1342177280 | bytes 6815744 | tf_op jit(solution)/shard_map/pallas_call | solution.py:274
  132.9 0.0 copy-start.2
  132.9 22.7 %all_to_all.22.rows_ref = bf16[16,40,1024]{2,1,0:T(8,128)(2,1)S(1)} all-to-all(bf16[16,40,1024]{2,1,0:T(8,128)(2,1)S(1)} %shard_map.76), channel_id=1, replica_groups=mesh['y'=4,'c'=2,'x'=4,'z'=16] {'y','x'}, dimensions={0} | all-to-all | bytes 2621440 | tf_op jit(solution)/shard_map/all_to_all | solution.py:315
  155.6 0.0 copy-done.2
  155.6 1.3 shard_map.77
Async XLA Ops:
  6.5 2.5 %copy-start.1 = (s32[64,2]{0,1:T(2,128)S(1)}, s32[64,2]{0,1:T(2,128)}, u32[]{:S(2)}) copy-start(s32[64,2]{0,1:T(2,128)} %param.8) | copy-start | bytes 1540
  6.5 2.5 %copy-start = (bf16[64,4096]{1,0:T(8,128)(2,1)S(1)}, bf16[64,4096]{1,0:T(8,128)(2,1)}, u32[]{:S(2)}) copy-start(bf16[64,4096]{1,0:T(8,128)(2,1)} %tokens_ref.1) | copy-start | bytes 1572868
  6.5 95.8 %all-gather.3.cloned.1.call-start = ((), (), s32[]{:S(2)}) async-start(), calls=%async_computation.4 | async-start | bytes 12976128 | tf_op jit(solution)/shard_map/all_gather | solution.py:306
  25.7 11.1 %all-to-all-start.1 = ((bf16[4,40,2048]{2,1,0:T(8,128)(2,1)}), bf16[4,40,2048]{2,1,0:T(8,128)(2,1)S(1)}, u32[]{:S(2)}, u32[]{:S(2)}) async-start(bf16[4,40,2048]{2,1,0:T(8,128)(2,1)} %bitcast.4), calls=%async_computation.1 | async-start | bytes 1310720 | tf_op jit(solution)/shard_map/all_to_all | solution.py:309
  29.2 21.0 %collective-permute-start.2 = (bf16[4,40,2048]{2,1,0:T(8,128)(2,1)S(1)}, bf16[4,40,2048]{2,1,0:T(8,128)(2,1)S(1)}, u32[]{:S(2)}, u32[]{:S(2)}) collective-permute-start(bf16[4,40,2048]{2,1,0:T(8,128)(2,1)S(1)} %all_to_all.20.refs_0_), channel_id=1, source_target_pairs={{0,128},{128,256},{256,384},{384,0},{1,129},{129,257},{257,385},{3... | collective-permute-start | bytes 1966088 | tf_op jit(solution)/shard_map/ppermute | solution.py:300
  36.8 19.0 %collective-permute-start.1 = (bf16[4,40,2048]{2,1,0:T(8,128)(2,1)S(1)}, bf16[4,40,2048]{2,1,0:T(8,128)(2,1)S(1)}, u32[]{:S(2)}, u32[]{:S(2)}) collective-permute-start(bf16[4,40,2048]{2,1,0:T(8,128)(2,1)S(1)} %all-to-all-done.1.refs_1_), channel_id=1, source_target_pairs={{0,384},{128,0},{256,128},{384,256},{1,385},{129,1},{257,129},{385... | collective-permute-start | bytes 1966088 | tf_op jit(solution)/shard_map/ppermute | solution.py:300
  44.9 25.0 %collective-permute-start = (bf16[4,40,2048]{2,1,0:T(8,128)(2,1)S(1)}, bf16[4,40,2048]{2,1,0:T(8,128)(2,1)S(1)}, u32[]{:S(2)}, u32[]{:S(2)}) collective-permute-start(bf16[4,40,2048]{2,1,0:T(8,128)(2,1)S(1)} %all_to_all.20.refs_0_), channel_id=1, source_target_pairs={{0,384},{128,0},{256,128},{384,256},{1,385},{129,1},{257,129},{385... | collective-permute-start | bytes 1966088 | tf_op jit(solution)/shard_map/ppermute | solution.py:300
  47.3 22.6 %collective-permute-start.5 = (bf16[4,40,2048]{2,1,0:T(8,128)(2,1)S(1)}, bf16[4,40,2048]{2,1,0:T(8,128)(2,1)}, u32[]{:S(2)}, u32[]{:S(2)}) collective-permute-start(bf16[4,40,2048]{2,1,0:T(8,128)(2,1)S(1)} %all-to-all-done.1.refs_1_), channel_id=1, source_target_pairs={{0,128},{128,256},{256,384},{384,0},{1,129},{129,257},{257,385},{3... | collective-permute-start | bytes 1966088 | tf_op jit(solution)/shard_map/ppermute | solution.py:300
  50.2 27.0 %collective-permute-start.3 = (bf16[4,40,2048]{2,1,0:T(8,128)(2,1)S(1)}, bf16[4,40,2048]{2,1,0:T(8,128)(2,1)}, u32[]{:S(2)}, u32[]{:S(2)}) collective-permute-start(bf16[4,40,2048]{2,1,0:T(8,128)(2,1)S(1)} %collective-permute-done.2.refs_6_), channel_id=1, source_target_pairs={{0,128},{128,256},{256,384},{384,0},{1,129},{129,257},{257,385},{3... | collective-permute-start | bytes 1966088 | tf_op jit(solution)/shard_map/ppermute | solution.py:300
  55.8 28.1 %collective-permute-start.4 = (bf16[4,40,2048]{2,1,0:T(8,128)(2,1)S(1)}, bf16[4,40,2048]{2,1,0:T(8,128)(2,1)}, u32[]{:S(2)}, u32[]{:S(2)}) collective-permute-start(bf16[4,40,2048]{2,1,0:T(8,128)(2,1)S(1)} %collective-permute-done.1.refs_3_), channel_id=1, source_target_pairs={{0,384},{128,0},{256,128},{384,256},{1,385},{129,1},{257,129},{385... | collective-permute-start | bytes 1966088 | tf_op jit(solution)/shard_map/ppermute | solution.py:300
  132.9 22.7 %copy-start.2 = (s32[64,2]{0,1:T(2,128)S(1)}, s32[64,2]{0,1:T(2,128)}, u32[]{:S(2)}) copy-start(s32[64,2]{0,1:T(2,128)} %param.9) | copy-start | bytes 1540
Sparse Core Ops, SparseCore 0:
  9.5 92.7 all-gather.2

commit v8 on v7

--- a/solution.py
+++ b/solution.py
@@ -104,7 +104,7 @@
     shares = jnp.where(by_first, share[0:1], 0.0) + jnp.where(by_second, share[1:2], 0.0)
     shares = shares.astype(jnp.bfloat16)
     for quarter in range(Y):
-        rows = rows_ref[quarter * X : (quarter + 1) * X].reshape(ALL_SLOTS, MEMBERS * 128)
+        rows = jnp.concatenate([rows_ref[x * Y + quarter] for x in range(X)], axis=0)
         mixed = lax.dot_general(shares, rows, (((0,), (0,)), ((), ())), preferred_element_type=jnp.float32)
         mixed = mixed.astype(jnp.bfloat16)
         for member in range(MEMBERS):
@@ -213,7 +213,10 @@
 
     for i, start in enumerate(starts):
         copies[i].wait()
-        out_ref[:, :, start * 128 : (start + WIDE) * 128] = join_rows(result(i, 0), result(i, 1))
+        joined = join_rows(result(i, 0), result(i, 1))
+        for x in range(X):
+            for y in range(Y):
+                out_ref[x * Y + y, :, start * 128 : (start + WIDE) * 128] = joined[y * X + x]
 
 
 SCALAR = pl.BlockSpec(memory_space=pltpu.SMEM)
@@ -312,7 +315,7 @@
     first_2, second_2 = shift(first_3, 1), shift(second_1, -1)
     rows = (first, second, first_1, second_1, first_2, second_2, first_3, second_3)
     hidden = lax.all_to_all(hidden_rows(place, rows, weights), "y", 0, 0, tiled=True)
-    result = lax.all_to_all(down_rows(hidden, weights), ("y", "x"), 0, 0, tiled=True)
+    result = lax.all_to_all(down_rows(hidden, weights), ("x", "y"), 0, 0, tiled=True)
     return mix(counts, routes, numerators, result)
 
 

time: 165 us -> 164 us (level)
  no operation moved by 1% of the time
where the time goes in v8:
time: 164 us; the launch traced here: 163 us
  blocking collectives  55.2 us (34%)
  waiting for transfers between devices  46.9 us (29%)
  starting transfers between devices  29.7 us (18%)
  Pallas kernels  16.9 us (10%)
  between operations  14.2 us (9%)
    ppermute x6, waiting for transfers between devices, shift(): return lax.ppermute(block, 'y', [(i, (i + by) % Y) for i in range(Y)])  26.3 us
    ppermute x6, starting transfers between devices, shift(): return lax.ppermute(block, 'y', [(i, (i + by) % Y) for i in range(Y)])  26.2 us
    all_to_all x1, blocking collectives, local(): lax.all_to_all(down_rows(hidden, weights), ('x', 'y'), 0, 0, tiled=True)  21.8 us
    all_to_all x1, blocking collectives, local(): lax.all_to_all(hidden_rows(place, rows, weights), 'y', 0, 0, tiled=True)  21.1 us
    all_gather x1, waiting for transfers between devices, local(): lax.all_gather(weights, ('z', 'c'))  18.4 us
    all_to_all x1, blocking collectives, local(): lax.all_to_all(first.reshape(X, SLOTS, D // 2), 'x', 0, 0, tiled=True)  12.3 us
    pallas_call x1, Pallas kernels, hidden_rows(): pl.pallas_call(hidden_kernel, out_shape=shape((Y, SRC, SLOTS, FQ)), in_sp...  6.1 us
    pallas_call x1, Pallas kernels, encode(): pl.pallas_call(encode_kernel, out_shape=[shape((ALL_SLOTS, D // 2))] * 2,...  4.31 us
  transfers between devices with their start and end apart: 8, of which 6 were waited for; matrix products, arithmetic and copies ran while one was open for 0% of the time, Pallas kernels for 3%

profile of v8, /device:TPU:1, one launch (start us, length us, event | category | flops | bytes accessed | tf_op | source)
XLA Modules:
  0.0 162.9 jit_solution(9744033584760615327)
XLA Ops:
  6.5 0.0 copy-start.1
  6.5 0.0 copy-start
  6.5 0.0 all-gather.3.cloned.1.call-start
  6.5 1.8 %shard_map.74 = bf16[384,512]{1,0:T(8,128)(2,1)} custom-call(bf16[512,1024]{1,0:T(8,128)(2,1)} %gate_ref.1, bf16[512,1024]{1,0:T(8,128)(2,1)} %up_ref.1, bf16[1024,512]{1,0:T(8,128)(2,1)} %down_ref.1), custom_call_target="tpu_custom_call" | custom-call | tf_op jit(solution)/shard_map/pallas_call | solution.py:247
  8.4 0.0 all-gather.3.cloned.1.call-update
  9.1 0.0 copy-done.1
  9.1 0.0 copy-done
  9.1 4.3 %shard_map.73 = (bf16[160,2048]{1,0:T(8,128)(2,1)S(1)}, bf16[160,2048]{1,0:T(8,128)(2,1)}) custom-call(s32[1]{0:T(128)S(6)} %copy.8.count_ref, s32[2,64]{1,0:T(2,128)S(1)} %bitcast.7, bf16[64,4096]{1,0:T(8,128)(2,1)S(1)} %copy-done), custom_call_target="tpu_custom_call" | custom-call | flops 83886080 | bytes 1835008 | tf_op jit(solution)/shard_map/pallas_call | solution.py:236
  13.4 12.3 %all_to_all.20.refs_0_ = bf16[4,40,2048]{2,1,0:T(8,128)(2,1)S(1)} all-to-all(bf16[4,40,2048]{2,1,0:T(8,128)(2,1)S(1)} %bitcast.6), channel_id=1, replica_groups=mesh['y'=4,'c'=2,'x'=4,'z'=16] {'x'}, dimensions={0} | all-to-all | bytes 1310720 | tf_op jit(solution)/shard_map/all_to_all | solution.py:311
  25.7 3.5 %all-to-all-start.1 = ((bf16[4,40,2048]{2,1,0:T(8,128)(2,1)}), bf16[4,40,2048]{2,1,0:T(8,128)(2,1)S(1)}, u32[]{:S(2)}, u32[]{:S(2)}) async-start(bf16[4,40,2048]{2,1,0:T(8,128)(2,1)} %bitcast.4), calls=%async_computation.1 | async-start | bytes 1310720 | tf_op jit(solution)/shard_map/all_to_all | solution.py:312
  29.2 5.5 %collective-permute-start.2 = (bf16[4,40,2048]{2,1,0:T(8,128)(2,1)S(1)}, bf16[4,40,2048]{2,1,0:T(8,128)(2,1)S(1)}, u32[]{:S(2)}, u32[]{:S(2)}) collective-permute-start(bf16[4,40,2048]{2,1,0:T(8,128)(2,1)S(1)} %all_to_all.20.refs_0_), channel_id=1, source_target_pairs={{0,128},{128,256},{256,384},{384,0},{1,129},{129,257},{257,385},{3... | collective-permute-start | bytes 1966088 | tf_op jit(solution)/shard_map/ppermute | solution.py:303
  34.7 2.1 %all-to-all-done.1.refs_1_ = bf16[4,40,2048]{2,1,0:T(8,128)(2,1)S(1)} async-done(((bf16[4,40,2048]{2,1,0:T(8,128)(2,1)}), bf16[4,40,2048]{2,1,0:T(8,128)(2,1)S(1)}, u32[]{:S(2)}, u32[]{:S(2)}) %all-to-all-start.1) | async-done | bytes 655392 | tf_op jit(solution)/shard_map/all_to_all | solution.py:312
  36.8 8.1 %collective-permute-start.1 = (bf16[4,40,2048]{2,1,0:T(8,128)(2,1)S(1)}, bf16[4,40,2048]{2,1,0:T(8,128)(2,1)S(1)}, u32[]{:S(2)}, u32[]{:S(2)}) collective-permute-start(bf16[4,40,2048]{2,1,0:T(8,128)(2,1)S(1)} %all-to-all-done.1.refs_1_), channel_id=1, source_target_pairs={{0,384},{128,0},{256,128},{384,256},{1,385},{129,1},{257,129},{385... | collective-permute-start | bytes 1966088 | tf_op jit(solution)/shard_map/ppermute | solution.py:303
  44.9 2.4 %collective-permute-start = (bf16[4,40,2048]{2,1,0:T(8,128)(2,1)S(1)}, bf16[4,40,2048]{2,1,0:T(8,128)(2,1)S(1)}, u32[]{:S(2)}, u32[]{:S(2)}) collective-permute-start(bf16[4,40,2048]{2,1,0:T(8,128)(2,1)S(1)} %all_to_all.20.refs_0_), channel_id=1, source_target_pairs={{0,384},{128,0},{256,128},{384,256},{1,385},{129,1},{257,129},{385... | collective-permute-start | bytes 1966088 | tf_op jit(solution)/shard_map/ppermute | solution.py:303
  47.3 2.9 %collective-permute-start.5 = (bf16[4,40,2048]{2,1,0:T(8,128)(2,1)S(1)}, bf16[4,40,2048]{2,1,0:T(8,128)(2,1)}, u32[]{:S(2)}, u32[]{:S(2)}) collective-permute-start(bf16[4,40,2048]{2,1,0:T(8,128)(2,1)S(1)} %all-to-all-done.1.refs_1_), channel_id=1, source_target_pairs={{0,128},{128,256},{256,384},{384,0},{1,129},{129,257},{257,385},{3... | collective-permute-start | bytes 1966088 | tf_op jit(solution)/shard_map/ppermute | solution.py:303
  50.2 0.0 collective-permute-done.2.refs_6_
  50.2 1.9 %collective-permute-start.3 = (bf16[4,40,2048]{2,1,0:T(8,128)(2,1)S(1)}, bf16[4,40,2048]{2,1,0:T(8,128)(2,1)}, u32[]{:S(2)}, u32[]{:S(2)}) collective-permute-start(bf16[4,40,2048]{2,1,0:T(8,128)(2,1)S(1)} %collective-permute-done.2.refs_6_), channel_id=1, source_target_pairs={{0,128},{128,256},{256,384},{384,0},{1,129},{129,257},{257,385},{3... | collective-permute-start | bytes 1966088 | tf_op jit(solution)/shard_map/ppermute | solution.py:303
  52.1 3.7 %collective-permute-done.1.refs_3_ = bf16[4,40,2048]{2,1,0:T(8,128)(2,1)S(1)} collective-permute-done((bf16[4,40,2048]{2,1,0:T(8,128)(2,1)S(1)}, bf16[4,40,2048]{2,1,0:T(8,128)(2,1)S(1)}, u32[]{:S(2)}, u32[]{:S(2)}) %collective-permute-start.1) | collective-permute-done | bytes 655392 | tf_op jit(solution)/shard_map/ppermute | solution.py:303
  55.8 5.4 %collective-permute-start.4 = (bf16[4,40,2048]{2,1,0:T(8,128)(2,1)S(1)}, bf16[4,40,2048]{2,1,0:T(8,128)(2,1)}, u32[]{:S(2)}, u32[]{:S(2)}) collective-permute-start(bf16[4,40,2048]{2,1,0:T(8,128)(2,1)S(1)} %collective-permute-done.1.refs_3_), channel_id=1, source_target_pairs={{0,384},{128,0},{256,128},{384,256},{1,385},{129,1},{257,129},{385... | collective-permute-start | bytes 1966088 | tf_op jit(solution)/shard_map/ppermute | solution.py:303
  61.2 8.6 %collective-permute-done.refs_2_ = bf16[4,40,2048]{2,1,0:T(8,128)(2,1)S(1)} collective-permute-done((bf16[4,40,2048]{2,1,0:T(8,128)(2,1)S(1)}, bf16[4,40,2048]{2,1,0:T(8,128)(2,1)S(1)}, u32[]{:S(2)}, u32[]{:S(2)}) %collective-permute-start) | collective-permute-done | bytes 655392 | tf_op jit(solution)/shard_map/ppermute | solution.py:303
  69.8 0.0 collective-permute-done.5.refs_7_
  69.8 7.3 %collective-permute-done.3.refs_4_ = bf16[4,40,2048]{2,1,0:T(8,128)(2,1)} collective-permute-done((bf16[4,40,2048]{2,1,0:T(8,128)(2,1)S(1)}, bf16[4,40,2048]{2,1,0:T(8,128)(2,1)}, u32[]{:S(2)}, u32[]{:S(2)}) %collective-permute-start.3) | collective-permute-done | bytes 655392 | tf_op jit(solution)/shard_map/ppermute | solution.py:303
  77.2 6.7 %collective-permute-done.4.refs_5_ = bf16[4,40,2048]{2,1,0:T(8,128)(2,1)} collective-permute-done((bf16[4,40,2048]{2,1,0:T(8,128)(2,1)S(1)}, bf16[4,40,2048]{2,1,0:T(8,128)(2,1)}, u32[]{:S(2)}, u32[]{:S(2)}) %collective-permute-start.4) | collective-permute-done | bytes 655392 | tf_op jit(solution)/shard_map/ppermute | solution.py:303
  83.9 18.4 %all-gather.3.cloned.1.call-done = bf16[12288,512]{1,0:T(8,128)(2,1)} async-done(((bf16[384,512]{1,0:T(8,128)(2,1)}), bf16[12288,512]{1,0:T(8,128)(2,1)}) %all-gather.3.cloned.1.call-update) | async-done | bytes 12582928 | tf_op jit(solution)/shard_map/all_gather | solution.py:309
  102.3 6.1 %shard_map.75 = bf16[4,16,40,256]{3,2,1,0:T(8,128)(2,1)S(1)} custom-call(s32[1]{0:T(128)} %bitcast.2.place_ref, bf16[4,40,2048]{2,1,0:T(8,128)(2,1)S(1)} %all_to_all.20.refs_0_, bf16[4,40,2048]{2,1,0:T(8,128)(2,1)S(1)} %all-to-all-done.1.refs_1_, bf16[4,40,2048]{2,1,0:T(8,128)(2,1)S(1)} %collective-permute-done.refs_2_, ...), custom_call_target="tpu_custom_call" | custom-call | flops 2684354560 | bytes 13631488 | tf_op jit(solution)/shard_map/pallas_call | solution.py:258
  108.4 21.1 %all_to_all.21.hidden_ref = bf16[4,16,40,256]{3,2,1,0:T(8,128)(2,1)S(1)} all-to-all(bf16[4,16,40,256]{3,2,1,0:T(8,128)(2,1)S(1)} %shard_map.75), channel_id=1, replica_groups=mesh['y'=4,'c'=2,'x'=4,'z'=16] {'y'}, dimensions={0} | all-to-all | bytes 2621440 | tf_op jit(solution)/shard_map/all_to_all | solution.py:317
  129.6 3.3 %shard_map.76 = bf16[16,40,1024]{2,1,0:T(8,128)(2,1)S(1)} custom-call(bf16[4,16,40,256]{3,2,1,0:T(8,128)(2,1)S(1)} %all_to_all.21.hidden_ref, bf16[2,8,2,384,512]{4,3,2,1,0:T(8,128)(2,1)} %bitcast.11), custom_call_target="tpu_custom_call" | custom-call | flops 1342177280 | bytes 6815744 | tf_op jit(solution)/shard_map/pallas_call | solution.py:277
  132.9 0.0 copy-start.2
  132.9 21.8 %all_to_all.22.rows_ref = bf16[16,40,1024]{2,1,0:T(8,128)(2,1)S(1)} all-to-all(bf16[16,40,1024]{2,1,0:T(8,128)(2,1)S(1)} %shard_map.76), channel_id=1, replica_groups=mesh['y'=4,'c'=2,'x'=4,'z'=16] {'x','y'}, dimensions={0} | all-to-all | bytes 2621440 | tf_op jit(solution)/shard_map/all_to_all | solution.py:318
  154.7 0.0 copy-done.2
  154.7 1.4 shard_map.77
Async XLA Ops:
  6.5 2.5 %copy-start.1 = (s32[64,2]{0,1:T(2,128)S(1)}, s32[64,2]{0,1:T(2,128)}, u32[]{:S(2)}) copy-start(s32[64,2]{0,1:T(2,128)} %param.8) | copy-start | bytes 1540
  6.5 2.5 %copy-start = (bf16[64,4096]{1,0:T(8,128)(2,1)S(1)}, bf16[64,4096]{1,0:T(8,128)(2,1)}, u32[]{:S(2)}) copy-start(bf16[64,4096]{1,0:T(8,128)(2,1)} %tokens_ref.1) | copy-start | bytes 1572868
  6.5 95.8 %all-gather.3.cloned.1.call-start = ((), (), s32[]{:S(2)}) async-start(), calls=%async_computation.4 | async-start | bytes 12976128 | tf_op jit(solution)/shard_map/all_gather | solution.py:309
  25.7 11.1 %all-to-all-start.1 = ((bf16[4,40,2048]{2,1,0:T(8,128)(2,1)}), bf16[4,40,2048]{2,1,0:T(8,128)(2,1)S(1)}, u32[]{:S(2)}, u32[]{:S(2)}) async-start(bf16[4,40,2048]{2,1,0:T(8,128)(2,1)} %bitcast.4), calls=%async_computation.1 | async-start | bytes 1310720 | tf_op jit(solution)/shard_map/all_to_all | solution.py:312
  29.2 21.0 %collective-permute-start.2 = (bf16[4,40,2048]{2,1,0:T(8,128)(2,1)S(1)}, bf16[4,40,2048]{2,1,0:T(8,128)(2,1)S(1)}, u32[]{:S(2)}, u32[]{:S(2)}) collective-permute-start(bf16[4,40,2048]{2,1,0:T(8,128)(2,1)S(1)} %all_to_all.20.refs_0_), channel_id=1, source_target_pairs={{0,128},{128,256},{256,384},{384,0},{1,129},{129,257},{257,385},{3... | collective-permute-start | bytes 1966088 | tf_op jit(solution)/shard_map/ppermute | solution.py:303
  36.8 19.0 %collective-permute-start.1 = (bf16[4,40,2048]{2,1,0:T(8,128)(2,1)S(1)}, bf16[4,40,2048]{2,1,0:T(8,128)(2,1)S(1)}, u32[]{:S(2)}, u32[]{:S(2)}) collective-permute-start(bf16[4,40,2048]{2,1,0:T(8,128)(2,1)S(1)} %all-to-all-done.1.refs_1_), channel_id=1, source_target_pairs={{0,384},{128,0},{256,128},{384,256},{1,385},{129,1},{257,129},{385... | collective-permute-start | bytes 1966088 | tf_op jit(solution)/shard_map/ppermute | solution.py:303
  44.9 25.0 %collective-permute-start = (bf16[4,40,2048]{2,1,0:T(8,128)(2,1)S(1)}, bf16[4,40,2048]{2,1,0:T(8,128)(2,1)S(1)}, u32[]{:S(2)}, u32[]{:S(2)}) collective-permute-start(bf16[4,40,2048]{2,1,0:T(8,128)(2,1)S(1)} %all_to_all.20.refs_0_), channel_id=1, source_target_pairs={{0,384},{128,0},{256,128},{384,256},{1,385},{129,1},{257,129},{385... | collective-permute-start | bytes 1966088 | tf_op jit(solution)/shard_map/ppermute | solution.py:303
  47.3 22.6 %collective-permute-start.5 = (bf16[4,40,2048]{2,1,0:T(8,128)(2,1)S(1)}, bf16[4,40,2048]{2,1,0:T(8,128)(2,1)}, u32[]{:S(2)}, u32[]{:S(2)}) collective-permute-start(bf16[4,40,2048]{2,1,0:T(8,128)(2,1)S(1)} %all-to-all-done.1.refs_1_), channel_id=1, source_target_pairs={{0,128},{128,256},{256,384},{384,0},{1,129},{129,257},{257,385},{3... | collective-permute-start | bytes 1966088 | tf_op jit(solution)/shard_map/ppermute | solution.py:303
  50.2 27.0 %collective-permute-start.3 = (bf16[4,40,2048]{2,1,0:T(8,128)(2,1)S(1)}, bf16[4,40,2048]{2,1,0:T(8,128)(2,1)}, u32[]{:S(2)}, u32[]{:S(2)}) collective-permute-start(bf16[4,40,2048]{2,1,0:T(8,128)(2,1)S(1)} %collective-permute-done.2.refs_6_), channel_id=1, source_target_pairs={{0,128},{128,256},{256,384},{384,0},{1,129},{129,257},{257,385},{3... | collective-permute-start | bytes 1966088 | tf_op jit(solution)/shard_map/ppermute | solution.py:303
  55.8 28.1 %collective-permute-start.4 = (bf16[4,40,2048]{2,1,0:T(8,128)(2,1)S(1)}, bf16[4,40,2048]{2,1,0:T(8,128)(2,1)}, u32[]{:S(2)}, u32[]{:S(2)}) collective-permute-start(bf16[4,40,2048]{2,1,0:T(8,128)(2,1)S(1)} %collective-permute-done.1.refs_3_), channel_id=1, source_target_pairs={{0,384},{128,0},{256,128},{384,256},{1,385},{129,1},{257,129},{385... | collective-permute-start | bytes 1966088 | tf_op jit(solution)/shard_map/ppermute | solution.py:303
  132.9 21.9 %copy-start.2 = (s32[64,2]{0,1:T(2,128)S(1)}, s32[64,2]{0,1:T(2,128)}, u32[]{:S(2)}) copy-start(s32[64,2]{0,1:T(2,128)} %param.9) | copy-start | bytes 1540
Sparse Core Ops, SparseCore 0:
  9.5 92.7 all-gather.2

commit v9 on v8

--- a/solution.py
+++ b/solution.py
@@ -20,8 +20,8 @@
 ALL_SLOTS = X * SLOTS
 FQ = F // Y
 HALF = SHARD // 2
-DEEP = 4
-WIDE = 4
+DEEP = 2
+WIDE = 2
 
 
 def slot_at(at):
@@ -156,12 +156,13 @@
         for i in range(C * groups)
     ]
     moves = [pltpu.make_async_copy(ref, here.at[i], row_sems.at[i]) for i, ref in enumerate(rows)]
+    copies[0].start()
     for move in moves[0::2]:
         move.start()
-    copies[0].start()
+    copies[1].start()
     for move in moves[1::2]:
         move.start()
-    copies[1].start()
+    copies[2].start()
     for i, copy in enumerate(copies):
         half, group = i // groups, i % groups
         at = slice(group * DEEP * HALF, (group + 1) * DEEP * HALF)
@@ -170,8 +171,8 @@
                 move.wait()
         blocks = [split_rows(here[2 * offset + half, :, :, at]) for offset in range(Y)]
         copy.wait()
-        if i + 2 < len(copies):
-            copies[i + 2].start()
+        if i + 3 < len(copies):
+            copies[i + 3].start()
         for expert, total in enumerate(sums):
             block = jnp.concatenate([b[expert][part] for part in range(2) for b in blocks], axis=0)
             weights = held[i, expert].reshape(DEEP * HALF, 2 * FQ)

time: 164 us -> 164 us (level)
  no operation moved by 1% of the time
where the time goes in v9:
time: 164 us; the launch traced here: 163 us
  blocking collectives  55.2 us (34%)
  waiting for transfers between devices  46.9 us (29%)
  starting transfers between devices  29.7 us (18%)
  Pallas kernels  16.6 us (10%)
  between operations  14.2 us (9%)
    ppermute x6, waiting for transfers between devices, shift(): return lax.ppermute(block, 'y', [(i, (i + by) % Y) for i in range(Y)])  26.3 us
    ppermute x6, starting transfers between devices, shift(): return lax.ppermute(block, 'y', [(i, (i + by) % Y) for i in range(Y)])  26.2 us
    all_to_all x1, blocking collectives, local(): lax.all_to_all(down_rows(hidden, weights), ('x', 'y'), 0, 0, tiled=True)  21.8 us
    all_to_all x1, blocking collectives, local(): lax.all_to_all(hidden_rows(place, rows, weights), 'y', 0, 0, tiled=True)  21.1 us
    all_gather x1, waiting for transfers between devices, local(): lax.all_gather(weights, ('z', 'c'))  18.4 us
    all_to_all x1, blocking collectives, local(): lax.all_to_all(first.reshape(X, SLOTS, D // 2), 'x', 0, 0, tiled=True)  12.3 us
    pallas_call x1, Pallas kernels, hidden_rows(): pl.pallas_call(hidden_kernel, out_shape=shape((Y, SRC, SLOTS, FQ)), in_sp...  5.76 us
    pallas_call x1, Pallas kernels, encode(): pl.pallas_call(encode_kernel, out_shape=[shape((ALL_SLOTS, D // 2))] * 2,...  4.31 us
  transfers between devices with their start and end apart: 8, of which 6 were waited for; matrix products, arithmetic and copies ran while one was open for 0% of the time, Pallas kernels for 3%

profile of v9, /device:TPU:1, one launch (start us, length us, event | category | flops | bytes accessed | tf_op | source)
XLA Modules:
  0.0 162.6 jit_solution(9872745491000458443)
XLA Ops:
  6.5 0.0 copy-start.1
  6.5 0.0 copy-start
  6.5 0.0 all-gather.3.cloned.1.call-start
  6.5 1.8 %shard_map.74 = bf16[384,512]{1,0:T(8,128)(2,1)} custom-call(bf16[512,1024]{1,0:T(8,128)(2,1)} %gate_ref.1, bf16[512,1024]{1,0:T(8,128)(2,1)} %up_ref.1, bf16[1024,512]{1,0:T(8,128)(2,1)} %down_ref.1), custom_call_target="tpu_custom_call" | custom-call | tf_op jit(solution)/shard_map/pallas_call | solution.py:248
  8.4 0.0 all-gather.3.cloned.1.call-update
  9.1 0.0 copy-done.1
  9.1 0.0 copy-done
  9.1 4.3 %shard_map.73 = (bf16[160,2048]{1,0:T(8,128)(2,1)S(1)}, bf16[160,2048]{1,0:T(8,128)(2,1)}) custom-call(s32[1]{0:T(128)S(6)} %copy.8.count_ref, s32[2,64]{1,0:T(2,128)S(1)} %bitcast.7, bf16[64,4096]{1,0:T(8,128)(2,1)S(1)} %copy-done), custom_call_target="tpu_custom_call" | custom-call | flops 83886080 | bytes 1835008 | tf_op jit(solution)/shard_map/pallas_call | solution.py:237
  13.4 12.3 %all_to_all.20.refs_0_ = bf16[4,40,2048]{2,1,0:T(8,128)(2,1)S(1)} all-to-all(bf16[4,40,2048]{2,1,0:T(8,128)(2,1)S(1)} %bitcast.6), channel_id=1, replica_groups=mesh['y'=4,'c'=2,'x'=4,'z'=16] {'x'}, dimensions={0} | all-to-all | bytes 1310720 | tf_op jit(solution)/shard_map/all_to_all | solution.py:312
  25.7 3.5 %all-to-all-start.1 = ((bf16[4,40,2048]{2,1,0:T(8,128)(2,1)}), bf16[4,40,2048]{2,1,0:T(8,128)(2,1)S(1)}, u32[]{:S(2)}, u32[]{:S(2)}) async-start(bf16[4,40,2048]{2,1,0:T(8,128)(2,1)} %bitcast.4), calls=%async_computation.1 | async-start | bytes 1310720 | tf_op jit(solution)/shard_map/all_to_all | solution.py:313
  29.2 5.5 %collective-permute-start.2 = (bf16[4,40,2048]{2,1,0:T(8,128)(2,1)S(1)}, bf16[4,40,2048]{2,1,0:T(8,128)(2,1)S(1)}, u32[]{:S(2)}, u32[]{:S(2)}) collective-permute-start(bf16[4,40,2048]{2,1,0:T(8,128)(2,1)S(1)} %all_to_all.20.refs_0_), channel_id=1, source_target_pairs={{0,128},{128,256},{256,384},{384,0},{1,129},{129,257},{257,385},{3... | collective-permute-start | bytes 1966088 | tf_op jit(solution)/shard_map/ppermute | solution.py:304
  34.7 2.1 %all-to-all-done.1.refs_1_ = bf16[4,40,2048]{2,1,0:T(8,128)(2,1)S(1)} async-done(((bf16[4,40,2048]{2,1,0:T(8,128)(2,1)}), bf16[4,40,2048]{2,1,0:T(8,128)(2,1)S(1)}, u32[]{:S(2)}, u32[]{:S(2)}) %all-to-all-start.1) | async-done | bytes 655392 | tf_op jit(solution)/shard_map/all_to_all | solution.py:313
  36.8 8.1 %collective-permute-start.1 = (bf16[4,40,2048]{2,1,0:T(8,128)(2,1)S(1)}, bf16[4,40,2048]{2,1,0:T(8,128)(2,1)S(1)}, u32[]{:S(2)}, u32[]{:S(2)}) collective-permute-start(bf16[4,40,2048]{2,1,0:T(8,128)(2,1)S(1)} %all-to-all-done.1.refs_1_), channel_id=1, source_target_pairs={{0,384},{128,0},{256,128},{384,256},{1,385},{129,1},{257,129},{385... | collective-permute-start | bytes 1966088 | tf_op jit(solution)/shard_map/ppermute | solution.py:304
  44.9 2.4 %collective-permute-start = (bf16[4,40,2048]{2,1,0:T(8,128)(2,1)S(1)}, bf16[4,40,2048]{2,1,0:T(8,128)(2,1)S(1)}, u32[]{:S(2)}, u32[]{:S(2)}) collective-permute-start(bf16[4,40,2048]{2,1,0:T(8,128)(2,1)S(1)} %all_to_all.20.refs_0_), channel_id=1, source_target_pairs={{0,384},{128,0},{256,128},{384,256},{1,385},{129,1},{257,129},{385... | collective-permute-start | bytes 1966088 | tf_op jit(solution)/shard_map/ppermute | solution.py:304
  47.3 2.9 %collective-permute-start.5 = (bf16[4,40,2048]{2,1,0:T(8,128)(2,1)S(1)}, bf16[4,40,2048]{2,1,0:T(8,128)(2,1)}, u32[]{:S(2)}, u32[]{:S(2)}) collective-permute-start(bf16[4,40,2048]{2,1,0:T(8,128)(2,1)S(1)} %all-to-all-done.1.refs_1_), channel_id=1, source_target_pairs={{0,128},{128,256},{256,384},{384,0},{1,129},{129,257},{257,385},{3... | collective-permute-start | bytes 1966088 | tf_op jit(solution)/shard_map/ppermute | solution.py:304
  50.2 0.0 collective-permute-done.2.refs_6_
  50.2 1.9 %collective-permute-start.3 = (bf16[4,40,2048]{2,1,0:T(8,128)(2,1)S(1)}, bf16[4,40,2048]{2,1,0:T(8,128)(2,1)}, u32[]{:S(2)}, u32[]{:S(2)}) collective-permute-start(bf16[4,40,2048]{2,1,0:T(8,128)(2,1)S(1)} %collective-permute-done.2.refs_6_), channel_id=1, source_target_pairs={{0,128},{128,256},{256,384},{384,0},{1,129},{129,257},{257,385},{3... | collective-permute-start | bytes 1966088 | tf_op jit(solution)/shard_map/ppermute | solution.py:304
  52.1 3.7 %collective-permute-done.1.refs_3_ = bf16[4,40,2048]{2,1,0:T(8,128)(2,1)S(1)} collective-permute-done((bf16[4,40,2048]{2,1,0:T(8,128)(2,1)S(1)}, bf16[4,40,2048]{2,1,0:T(8,128)(2,1)S(1)}, u32[]{:S(2)}, u32[]{:S(2)}) %collective-permute-start.1) | collective-permute-done | bytes 655392 | tf_op jit(solution)/shard_map/ppermute | solution.py:304
  55.8 5.4 %collective-permute-start.4 = (bf16[4,40,2048]{2,1,0:T(8,128)(2,1)S(1)}, bf16[4,40,2048]{2,1,0:T(8,128)(2,1)}, u32[]{:S(2)}, u32[]{:S(2)}) collective-permute-start(bf16[4,40,2048]{2,1,0:T(8,128)(2,1)S(1)} %collective-permute-done.1.refs_3_), channel_id=1, source_target_pairs={{0,384},{128,0},{256,128},{384,256},{1,385},{129,1},{257,129},{385... | collective-permute-start | bytes 1966088 | tf_op jit(solution)/shard_map/ppermute | solution.py:304
  61.2 8.6 %collective-permute-done.refs_2_ = bf16[4,40,2048]{2,1,0:T(8,128)(2,1)S(1)} collective-permute-done((bf16[4,40,2048]{2,1,0:T(8,128)(2,1)S(1)}, bf16[4,40,2048]{2,1,0:T(8,128)(2,1)S(1)}, u32[]{:S(2)}, u32[]{:S(2)}) %collective-permute-start) | collective-permute-done | bytes 655392 | tf_op jit(solution)/shard_map/ppermute | solution.py:304
  69.8 0.0 collective-permute-done.5.refs_7_
  69.8 7.3 %collective-permute-done.3.refs_4_ = bf16[4,40,2048]{2,1,0:T(8,128)(2,1)} collective-permute-done((bf16[4,40,2048]{2,1,0:T(8,128)(2,1)S(1)}, bf16[4,40,2048]{2,1,0:T(8,128)(2,1)}, u32[]{:S(2)}, u32[]{:S(2)}) %collective-permute-start.3) | collective-permute-done | bytes 655392 | tf_op jit(solution)/shard_map/ppermute | solution.py:304
  77.2 6.7 %collective-permute-done.4.refs_5_ = bf16[4,40,2048]{2,1,0:T(8,128)(2,1)} collective-permute-done((bf16[4,40,2048]{2,1,0:T(8,128)(2,1)S(1)}, bf16[4,40,2048]{2,1,0:T(8,128)(2,1)}, u32[]{:S(2)}, u32[]{:S(2)}) %collective-permute-start.4) | collective-permute-done | bytes 655392 | tf_op jit(solution)/shard_map/ppermute | solution.py:304
  83.9 18.4 %all-gather.3.cloned.1.call-done = bf16[12288,512]{1,0:T(8,128)(2,1)} async-done(((bf16[384,512]{1,0:T(8,128)(2,1)}), bf16[12288,512]{1,0:T(8,128)(2,1)}) %all-gather.3.cloned.1.call-update) | async-done | bytes 12582928 | tf_op jit(solution)/shard_map/all_gather | solution.py:310
  102.3 5.8 %shard_map.75 = bf16[4,16,40,256]{3,2,1,0:T(8,128)(2,1)S(1)} custom-call(s32[1]{0:T(128)} %bitcast.2.place_ref, bf16[4,40,2048]{2,1,0:T(8,128)(2,1)S(1)} %all_to_all.20.refs_0_, bf16[4,40,2048]{2,1,0:T(8,128)(2,1)S(1)} %all-to-all-done.1.refs_1_, bf16[4,40,2048]{2,1,0:T(8,128)(2,1)S(1)} %collective-permute-done.refs_2_, ...), custom_call_target="tpu_custom_call" | custom-call | flops 2684354560 | bytes 13631488 | tf_op jit(solution)/shard_map/pallas_call | solution.py:259
  108.1 21.1 %all_to_all.21.hidden_ref = bf16[4,16,40,256]{3,2,1,0:T(8,128)(2,1)S(1)} all-to-all(bf16[4,16,40,256]{3,2,1,0:T(8,128)(2,1)S(1)} %shard_map.75), channel_id=1, replica_groups=mesh['y'=4,'c'=2,'x'=4,'z'=16] {'y'}, dimensions={0} | all-to-all | bytes 2621440 | tf_op jit(solution)/shard_map/all_to_all | solution.py:318
  129.2 3.3 %shard_map.76 = bf16[16,40,1024]{2,1,0:T(8,128)(2,1)S(1)} custom-call(bf16[4,16,40,256]{3,2,1,0:T(8,128)(2,1)S(1)} %all_to_all.21.hidden_ref, bf16[2,8,2,384,512]{4,3,2,1,0:T(8,128)(2,1)} %bitcast.11), custom_call_target="tpu_custom_call" | custom-call | flops 1342177280 | bytes 6815744 | tf_op jit(solution)/shard_map/pallas_call | solution.py:278
  132.5 0.0 copy-start.2
  132.5 21.8 %all_to_all.22.rows_ref = bf16[16,40,1024]{2,1,0:T(8,128)(2,1)S(1)} all-to-all(bf16[16,40,1024]{2,1,0:T(8,128)(2,1)S(1)} %shard_map.76), channel_id=1, replica_groups=mesh['y'=4,'c'=2,'x'=4,'z'=16] {'x','y'}, dimensions={0} | all-to-all | bytes 2621440 | tf_op jit(solution)/shard_map/all_to_all | solution.py:319
  154.4 0.0 copy-done.2
  154.4 1.4 shard_map.77
Async XLA Ops:
  6.5 2.5 %copy-start.1 = (s32[64,2]{0,1:T(2,128)S(1)}, s32[64,2]{0,1:T(2,128)}, u32[]{:S(2)}) copy-start(s32[64,2]{0,1:T(2,128)} %param.8) | copy-start | bytes 1540
  6.5 2.5 %copy-start = (bf16[64,4096]{1,0:T(8,128)(2,1)S(1)}, bf16[64,4096]{1,0:T(8,128)(2,1)}, u32[]{:S(2)}) copy-start(bf16[64,4096]{1,0:T(8,128)(2,1)} %tokens_ref.1) | copy-start | bytes 1572868
  6.5 95.8 %all-gather.3.cloned.1.call-start = ((), (), s32[]{:S(2)}) async-start(), calls=%async_computation.4 | async-start | bytes 12976128 | tf_op jit(solution)/shard_map/all_gather | solution.py:310
  25.7 11.1 %all-to-all-start.1 = ((bf16[4,40,2048]{2,1,0:T(8,128)(2,1)}), bf16[4,40,2048]{2,1,0:T(8,128)(2,1)S(1)}, u32[]{:S(2)}, u32[]{:S(2)}) async-start(bf16[4,40,2048]{2,1,0:T(8,128)(2,1)} %bitcast.4), calls=%async_computation.1 | async-start | bytes 1310720 | tf_op jit(solution)/shard_map/all_to_all | solution.py:313
  29.2 21.0 %collective-permute-start.2 = (bf16[4,40,2048]{2,1,0:T(8,128)(2,1)S(1)}, bf16[4,40,2048]{2,1,0:T(8,128)(2,1)S(1)}, u32[]{:S(2)}, u32[]{:S(2)}) collective-permute-start(bf16[4,40,2048]{2,1,0:T(8,128)(2,1)S(1)} %all_to_all.20.refs_0_), channel_id=1, source_target_pairs={{0,128},{128,256},{256,384},{384,0},{1,129},{129,257},{257,385},{3... | collective-permute-start | bytes 1966088 | tf_op jit(solution)/shard_map/ppermute | solution.py:304
  36.8 19.0 %collective-permute-start.1 = (bf16[4,40,2048]{2,1,0:T(8,128)(2,1)S(1)}, bf16[4,40,2048]{2,1,0:T(8,128)(2,1)S(1)}, u32[]{:S(2)}, u32[]{:S(2)}) collective-permute-start(bf16[4,40,2048]{2,1,0:T(8,128)(2,1)S(1)} %all-to-all-done.1.refs_1_), channel_id=1, source_target_pairs={{0,384},{128,0},{256,128},{384,256},{1,385},{129,1},{257,129},{385... | collective-permute-start | bytes 1966088 | tf_op jit(solution)/shard_map/ppermute | solution.py:304
  44.9 25.0 %collective-permute-start = (bf16[4,40,2048]{2,1,0:T(8,128)(2,1)S(1)}, bf16[4,40,2048]{2,1,0:T(8,128)(2,1)S(1)}, u32[]{:S(2)}, u32[]{:S(2)}) collective-permute-start(bf16[4,40,2048]{2,1,0:T(8,128)(2,1)S(1)} %all_to_all.20.refs_0_), channel_id=1, source_target_pairs={{0,384},{128,0},{256,128},{384,256},{1,385},{129,1},{257,129},{385... | collective-permute-start | bytes 1966088 | tf_op jit(solution)/shard_map/ppermute | solution.py:304
  47.3 22.6 %collective-permute-start.5 = (bf16[4,40,2048]{2,1,0:T(8,128)(2,1)S(1)}, bf16[4,40,2048]{2,1,0:T(8,128)(2,1)}, u32[]{:S(2)}, u32[]{:S(2)}) collective-permute-start(bf16[4,40,2048]{2,1,0:T(8,128)(2,1)S(1)} %all-to-all-done.1.refs_1_), channel_id=1, source_target_pairs={{0,128},{128,256},{256,384},{384,0},{1,129},{129,257},{257,385},{3... | collective-permute-start | bytes 1966088 | tf_op jit(solution)/shard_map/ppermute | solution.py:304
  50.2 27.0 %collective-permute-start.3 = (bf16[4,40,2048]{2,1,0:T(8,128)(2,1)S(1)}, bf16[4,40,2048]{2,1,0:T(8,128)(2,1)}, u32[]{:S(2)}, u32[]{:S(2)}) collective-permute-start(bf16[4,40,2048]{2,1,0:T(8,128)(2,1)S(1)} %collective-permute-done.2.refs_6_), channel_id=1, source_target_pairs={{0,128},{128,256},{256,384},{384,0},{1,129},{129,257},{257,385},{3... | collective-permute-start | bytes 1966088 | tf_op jit(solution)/shard_map/ppermute | solution.py:304
  55.8 28.1 %collective-permute-start.4 = (bf16[4,40,2048]{2,1,0:T(8,128)(2,1)S(1)}, bf16[4,40,2048]{2,1,0:T(8,128)(2,1)}, u32[]{:S(2)}, u32[]{:S(2)}) collective-permute-start(bf16[4,40,2048]{2,1,0:T(8,128)(2,1)S(1)} %collective-permute-done.1.refs_3_), channel_id=1, source_target_pairs={{0,384},{128,0},{256,128},{384,256},{1,385},{129,1},{257,129},{385... | collective-permute-start | bytes 1966088 | tf_op jit(solution)/shard_map/ppermute | solution.py:304
  132.5 21.9 %copy-start.2 = (s32[64,2]{0,1:T(2,128)S(1)}, s32[64,2]{0,1:T(2,128)}, u32[]{:S(2)}) copy-start(s32[64,2]{0,1:T(2,128)} %param.9) | copy-start | bytes 1540
Sparse Core Ops, SparseCore 0:
  9.5 92.7 all-gather.2

commit v10 on v9

--- a/solution.py
+++ b/solution.py
@@ -181,12 +181,12 @@
     joined = join_rows(*(swish(total[...]) for total in sums))
     for offset in range(Y):
         source = lax.rem(place_ref[0] + offset, Y)
-        block = joined[offset * X : (offset + 1) * X]
-        for copy in range(Y):
-            out_ref[copy, pl.ds(source * X, X)] = block
-
-
-def down_kernel(hidden_ref, weights_ref, out_ref, held, sems, *rows):
+        out_ref[pl.ds(source * X, X)] = joined[offset * X : (offset + 1) * X]
+
+
+def down_kernel(place_ref, *refs):
+    hidden, weights_ref, out_ref, held, sems = refs[:Y], *refs[Y : Y + 4]
+    rows = refs[Y + 4 :]
     main = SRC * MAIN
     starts = range(0, MEMBERS, WIDE)
     copies = [
@@ -195,9 +195,9 @@
     ]
     for copy in copies:
         copy.start()
-    for quarter in range(Y):
-        at = slice(quarter * FQ, (quarter + 1) * FQ)
-        for ref, (run, rest) in zip(rows, split_rows(hidden_ref[quarter])):
+    for offset in range(Y):
+        at = pl.ds(pl.multiple_of(lax.rem(place_ref[0] + offset, Y) * FQ, FQ), FQ)
+        for ref, (run, rest) in zip(rows, split_rows(hidden[offset][...])):
             ref[:main, at] = run
             ref[main:, at] = rest
 
@@ -258,7 +258,7 @@
     pieces = C * MEMBERS // DEEP
     return pl.pallas_call(
         hidden_kernel,
-        out_shape=shape((Y, SRC, SLOTS, FQ)),
+        out_shape=shape((SRC, SLOTS, FQ)),
         in_specs=[SCALAR, *[ANY] * (2 * Y), ANY],
         out_specs=WHOLE,
         scratch_shapes=[
@@ -273,12 +273,12 @@
     )(place, *rows, weights)
 
 
-def down_rows(hidden, weights):
+def down_rows(place, hidden, weights):
     pieces = MEMBERS // WIDE
     return pl.pallas_call(
         down_kernel,
         out_shape=shape((SRC, SLOTS, MEMBERS * 128)),
-        in_specs=[WHOLE, ANY],
+        in_specs=[SCALAR, *[WHOLE] * Y, ANY],
         out_specs=WHOLE,
         scratch_shapes=[
             pltpu.VMEM((pieces, 2, WIDE, C, 128, SHARD), jnp.bfloat16),
@@ -287,7 +287,7 @@
         ],
         compiler_params=params(50),
         cost_estimate=pl.CostEstimate(flops=2 * ROWS * F * F, bytes_accessed=4 * ROWS * F + 4 * F * F, transcendentals=0),
-    )(hidden, weights)
+    )(place, *hidden, weights)
 
 
 def mix(counts, routes, numerators, rows):
@@ -315,8 +315,9 @@
     second_3, first_1 = shift(second, 1), shift(first, -1)
     first_2, second_2 = shift(first_3, 1), shift(second_1, -1)
     rows = (first, second, first_1, second_1, first_2, second_2, first_3, second_3)
-    hidden = lax.all_to_all(hidden_rows(place, rows, weights), "y", 0, 0, tiled=True)
-    result = lax.all_to_all(down_rows(hidden, weights), ("x", "y"), 0, 0, tiled=True)
+    own = hidden_rows(place, rows, weights)
+    hidden = (own, shift(own, -1), shift(own, 2), shift(own, 1))
+    result = lax.all_to_all(down_rows(place, hidden, weights), ("x", "y"), 0, 0, tiled=True)
     return mix(counts, routes, numerators, result)
 
 

time: 164 us -> 172 us (1.049)
  blocking collectives: 55.2 us -> 38.1 us
  waiting for transfers between devices: 46.9 us -> 57.8 us
  starting transfers between devices: 29.7 us -> 40.1 us
  local copies, waits for them, and re-layouts: 0.01 us -> 4.59 us
    all_to_all x2 -> x1, blocking collectives: 43 us -> 25.8 us  [local(): lax.all_to_all(down_rows(place, hidden, weights), ('x', 'y'), 0, 0, tiled...]
    ppermute x6 -> x9, waiting for transfers between devices: 26.3 us -> 37.3 us  [shift(): return lax.ppermute(block, 'y', [(i, (i + by) % Y) for i in range(Y)])]
    ppermute x6 -> x9, starting transfers between devices: 26.2 us -> 36.7 us  [shift(): return lax.ppermute(block, 'y', [(i, (i + by) % Y) for i in range(Y)])]
    unnamed x6 -> x8, local copies, waits for them, and re-layouts: 0.01 us -> 4.59 us
  transfers between devices with their start and end apart: 8 -> 11, of which waited for: 6 -> 9; matrix products, arithmetic and copies ran while one was open for 0% -> 0% of each run, Pallas kernels for 3% -> 3%
where the time goes in v10:
time: 172 us; the launch traced here: 171 us
  waiting for transfers between devices  57.8 us (34%)
  starting transfers between devices  40.1 us (23%)
  blocking collectives  38.1 us (22%)
  Pallas kernels  16.3 us (9%)
  between operations  14.2 us (8%)
  local copies, waits for them, and re-layouts  4.59 us (3%)
    ppermute x9, waiting for transfers between devices, shift(): return lax.ppermute(block, 'y', [(i, (i + by) % Y) for i in range(Y)])  37.3 us
    ppermute x9, starting transfers between devices, shift(): return lax.ppermute(block, 'y', [(i, (i + by) % Y) for i in range(Y)])  36.7 us
    all_to_all x1, blocking collectives, local(): lax.all_to_all(down_rows(place, hidden, weights), ('x', 'y'), 0, 0, tiled...  25.8 us
    all_gather x1, waiting for transfers between devices, local(): lax.all_gather(weights, ('z', 'c'))  18.4 us
    all_to_all x1, blocking collectives, local(): lax.all_to_all(first.reshape(X, SLOTS, D // 2), 'x', 0, 0, tiled=True)  12.3 us
    pallas_call x1, Pallas kernels, hidden_rows(): pl.pallas_call(hidden_kernel, out_shape=shape((SRC, SLOTS, FQ)), in_specs...  5.51 us
    unnamed x8, local copies, waits for them, and re-layouts  4.59 us
    pallas_call x1, Pallas kernels, encode(): pl.pallas_call(encode_kernel, out_shape=[shape((ALL_SLOTS, D // 2))] * 2,...  4.31 us
  transfers between devices with their start and end apart: 11, of which 9 were waited for; matrix products, arithmetic and copies ran while one was open for 0% of the time, Pallas kernels for 3%

profile of v10, /device:TPU:1, one launch (start us, length us, event | category | flops | bytes accessed | tf_op | source)
XLA Modules:
  0.0 171.2 jit_solution(4064301715860051045)
XLA Ops:
  6.5 0.0 copy-start.2
  6.5 0.0 copy-start.1
  6.5 0.0 all-gather.3.cloned.1.call-start
  6.5 1.8 %shard_map.74 = bf16[384,512]{1,0:T(8,128)(2,1)} custom-call(bf16[512,1024]{1,0:T(8,128)(2,1)} %gate_ref.1, bf16[512,1024]{1,0:T(8,128)(2,1)} %up_ref.1, bf16[1024,512]{1,0:T(8,128)(2,1)} %down_ref.1), custom_call_target="tpu_custom_call" | custom-call | tf_op jit(solution)/shard_map/pallas_call | solution.py:248
  8.4 0.0 all-gather.3.cloned.1.call-update
  9.1 0.0 copy-done.2
  9.1 0.0 copy-done.1
  9.1 4.3 %shard_map.73 = (bf16[160,2048]{1,0:T(8,128)(2,1)S(1)}, bf16[160,2048]{1,0:T(8,128)(2,1)}) custom-call(s32[1]{0:T(128)S(6)} %copy.8.count_ref, s32[2,64]{1,0:T(2,128)S(1)} %bitcast.9, bf16[64,4096]{1,0:T(8,128)(2,1)S(1)} %copy-done.1), custom_call_target="tpu_custom_call" | custom-call | flops 83886080 | bytes 1835008 | tf_op jit(solution)/shard_map/pallas_call | solution.py:237
  13.4 12.3 %all_to_all.15.refs_0_ = bf16[4,40,2048]{2,1,0:T(8,128)(2,1)S(1)} all-to-all(bf16[4,40,2048]{2,1,0:T(8,128)(2,1)S(1)} %bitcast.8), channel_id=1, replica_groups=mesh['y'=4,'c'=2,'x'=4,'z'=16] {'x'}, dimensions={0} | all-to-all | bytes 1310720 | tf_op jit(solution)/shard_map/all_to_all | solution.py:312
  25.7 3.5 %all-to-all-start.1 = ((bf16[4,40,2048]{2,1,0:T(8,128)(2,1)}), bf16[4,40,2048]{2,1,0:T(8,128)(2,1)S(1)}, u32[]{:S(2)}, u32[]{:S(2)}) async-start(bf16[4,40,2048]{2,1,0:T(8,128)(2,1)} %bitcast.4), calls=%async_computation.1 | async-start | bytes 1310720 | tf_op jit(solution)/shard_map/all_to_all | solution.py:313
  29.2 5.5 %collective-permute-start.2 = (bf16[4,40,2048]{2,1,0:T(8,128)(2,1)S(1)}, bf16[4,40,2048]{2,1,0:T(8,128)(2,1)S(1)}, u32[]{:S(2)}, u32[]{:S(2)}) collective-permute-start(bf16[4,40,2048]{2,1,0:T(8,128)(2,1)S(1)} %all_to_all.15.refs_0_), channel_id=1, source_target_pairs={{0,128},{128,256},{256,384},{384,0},{1,129},{129,257},{257,385},{3... | collective-permute-start | bytes 1966088 | tf_op jit(solution)/shard_map/ppermute | solution.py:304
  34.7 2.1 %all-to-all-done.1.refs_1_ = bf16[4,40,2048]{2,1,0:T(8,128)(2,1)S(1)} async-done(((bf16[4,40,2048]{2,1,0:T(8,128)(2,1)}), bf16[4,40,2048]{2,1,0:T(8,128)(2,1)S(1)}, u32[]{:S(2)}, u32[]{:S(2)}) %all-to-all-start.1) | async-done | bytes 655392 | tf_op jit(solution)/shard_map/all_to_all | solution.py:313
  36.8 8.1 %collective-permute-start.1 = (bf16[4,40,2048]{2,1,0:T(8,128)(2,1)S(1)}, bf16[4,40,2048]{2,1,0:T(8,128)(2,1)S(1)}, u32[]{:S(2)}, u32[]{:S(2)}) collective-permute-start(bf16[4,40,2048]{2,1,0:T(8,128)(2,1)S(1)} %all-to-all-done.1.refs_1_), channel_id=1, source_target_pairs={{0,384},{128,0},{256,128},{384,256},{1,385},{129,1},{257,129},{385... | collective-permute-start | bytes 1966088 | tf_op jit(solution)/shard_map/ppermute | solution.py:304
  44.9 2.4 %collective-permute-start = (bf16[4,40,2048]{2,1,0:T(8,128)(2,1)S(1)}, bf16[4,40,2048]{2,1,0:T(8,128)(2,1)S(1)}, u32[]{:S(2)}, u32[]{:S(2)}) collective-permute-start(bf16[4,40,2048]{2,1,0:T(8,128)(2,1)S(1)} %all_to_all.15.refs_0_), channel_id=1, source_target_pairs={{0,384},{128,0},{256,128},{384,256},{1,385},{129,1},{257,129},{385... | collective-permute-start | bytes 1966088 | tf_op jit(solution)/shard_map/ppermute | solution.py:304
  47.3 2.9 %collective-permute-start.5 = (bf16[4,40,2048]{2,1,0:T(8,128)(2,1)S(1)}, bf16[4,40,2048]{2,1,0:T(8,128)(2,1)}, u32[]{:S(2)}, u32[]{:S(2)}) collective-permute-start(bf16[4,40,2048]{2,1,0:T(8,128)(2,1)S(1)} %all-to-all-done.1.refs_1_), channel_id=1, source_target_pairs={{0,128},{128,256},{256,384},{384,0},{1,129},{129,257},{257,385},{3... | collective-permute-start | bytes 1966088 | tf_op jit(solution)/shard_map/ppermute | solution.py:304
  50.2 0.0 collective-permute-done.2.refs_6_
  50.2 1.9 %collective-permute-start.3 = (bf16[4,40,2048]{2,1,0:T(8,128)(2,1)S(1)}, bf16[4,40,2048]{2,1,0:T(8,128)(2,1)}, u32[]{:S(2)}, u32[]{:S(2)}) collective-permute-start(bf16[4,40,2048]{2,1,0:T(8,128)(2,1)S(1)} %collective-permute-done.2.refs_6_), channel_id=1, source_target_pairs={{0,128},{128,256},{256,384},{384,0},{1,129},{129,257},{257,385},{3... | collective-permute-start | bytes 1966088 | tf_op jit(solution)/shard_map/ppermute | solution.py:304
  52.1 3.7 %collective-permute-done.1.refs_3_ = bf16[4,40,2048]{2,1,0:T(8,128)(2,1)S(1)} collective-permute-done((bf16[4,40,2048]{2,1,0:T(8,128)(2,1)S(1)}, bf16[4,40,2048]{2,1,0:T(8,128)(2,1)S(1)}, u32[]{:S(2)}, u32[]{:S(2)}) %collective-permute-start.1) | collective-permute-done | bytes 655392 | tf_op jit(solution)/shard_map/ppermute | solution.py:304
  55.8 5.4 %collective-permute-start.4 = (bf16[4,40,2048]{2,1,0:T(8,128)(2,1)S(1)}, bf16[4,40,2048]{2,1,0:T(8,128)(2,1)}, u32[]{:S(2)}, u32[]{:S(2)}) collective-permute-start(bf16[4,40,2048]{2,1,0:T(8,128)(2,1)S(1)} %collective-permute-done.1.refs_3_), channel_id=1, source_target_pairs={{0,384},{128,0},{256,128},{384,256},{1,385},{129,1},{257,129},{385... | collective-permute-start | bytes 1966088 | tf_op jit(solution)/shard_map/ppermute | solution.py:304
  61.2 8.6 %collective-permute-done.refs_2_ = bf16[4,40,2048]{2,1,0:T(8,128)(2,1)S(1)} collective-permute-done((bf16[4,40,2048]{2,1,0:T(8,128)(2,1)S(1)}, bf16[4,40,2048]{2,1,0:T(8,128)(2,1)S(1)}, u32[]{:S(2)}, u32[]{:S(2)}) %collective-permute-start) | collective-permute-done | bytes 655392 | tf_op jit(solution)/shard_map/ppermute | solution.py:304
  69.8 0.0 collective-permute-done.5.refs_7_
  69.8 7.3 %collective-permute-done.3.refs_4_ = bf16[4,40,2048]{2,1,0:T(8,128)(2,1)} collective-permute-done((bf16[4,40,2048]{2,1,0:T(8,128)(2,1)S(1)}, bf16[4,40,2048]{2,1,0:T(8,128)(2,1)}, u32[]{:S(2)}, u32[]{:S(2)}) %collective-permute-start.3) | collective-permute-done | bytes 655392 | tf_op jit(solution)/shard_map/ppermute | solution.py:304
  77.2 6.7 %collective-permute-done.4.refs_5_ = bf16[4,40,2048]{2,1,0:T(8,128)(2,1)} collective-permute-done((bf16[4,40,2048]{2,1,0:T(8,128)(2,1)S(1)}, bf16[4,40,2048]{2,1,0:T(8,128)(2,1)}, u32[]{:S(2)}, u32[]{:S(2)}) %collective-permute-start.4) | collective-permute-done | bytes 655392 | tf_op jit(solution)/shard_map/ppermute | solution.py:304
  83.9 18.4 %all-gather.3.cloned.1.call-done = bf16[12288,512]{1,0:T(8,128)(2,1)} async-done(((bf16[384,512]{1,0:T(8,128)(2,1)}), bf16[12288,512]{1,0:T(8,128)(2,1)}) %all-gather.3.cloned.1.call-update) | async-done | bytes 12582928 | tf_op jit(solution)/shard_map/all_gather | solution.py:310
  102.3 0.0 copy-start
  102.3 4.6 %copy-done = bf16[12288,512]{1,0:T(8,128)(2,1)S(1)} copy-done((bf16[12288,512]{1,0:T(8,128)(2,1)S(1)}, bf16[12288,512]{1,0:T(8,128)(2,1)}, u32[]{:S(2)}) %copy-start) | copy-done | bytes 12582936
  106.9 5.5 %shard_map.75.refs_0_ = bf16[16,40,256]{2,1,0:T(8,128)(2,1)S(1)} custom-call(s32[1]{0:T(128)} %bitcast.2.place_ref, bf16[4,40,2048]{2,1,0:T(8,128)(2,1)S(1)} %all_to_all.15.refs_0_, bf16[4,40,2048]{2,1,0:T(8,128)(2,1)S(1)} %all-to-all-done.1.refs_1_, bf16[4,40,2048]{2,1,0:T(8,128)(2,1)S(1)} %collective-permute-done.refs_2_, ...), custom_call_target="tpu_custom_call" | custom-call | flops 2684354560 | bytes 13631488 | tf_op jit(solution)/shard_map/pallas_call | solution.py:259
  112.4 3.0 %collective-permute-start.8 = (bf16[16,40,256]{2,1,0:T(8,128)(2,1)S(1)}, bf16[16,40,256]{2,1,0:T(8,128)(2,1)S(1)}, u32[]{:S(2)}, u32[]{:S(2)}) collective-permute-start(bf16[16,40,256]{2,1,0:T(8,128)(2,1)S(1)} %shard_map.75.refs_0_), channel_id=1, source_target_pairs={{0,128},{128,256},{256,384},{384,0},{1,129},{129,257},{257,385},{3... | collective-permute-start | bytes 983048 | tf_op jit(solution)/shard_map/ppermute | solution.py:304
  115.4 4.4 %collective-permute-start.7 = (bf16[16,40,256]{2,1,0:T(8,128)(2,1)S(1)}, bf16[16,40,256]{2,1,0:T(8,128)(2,1)S(1)}, u32[]{:S(2)}, u32[]{:S(2)}) collective-permute-start(bf16[16,40,256]{2,1,0:T(8,128)(2,1)S(1)} %shard_map.75.refs_0_), channel_id=1, source_target_pairs={{0,256},{128,384},{256,0},{384,128},{1,257},{129,385},{257,1},{385... | collective-permute-start | bytes 983048 | tf_op jit(solution)/shard_map/ppermute | solution.py:304
  119.8 3.1 %collective-permute-start.6 = (bf16[16,40,256]{2,1,0:T(8,128)(2,1)S(1)}, bf16[16,40,256]{2,1,0:T(8,128)(2,1)S(1)}, u32[]{:S(2)}, u32[]{:S(2)}) collective-permute-start(bf16[16,40,256]{2,1,0:T(8,128)(2,1)S(1)} %shard_map.75.refs_0_), channel_id=1, source_target_pairs={{0,384},{128,0},{256,128},{384,256},{1,385},{129,1},{257,129},{385... | collective-permute-start | bytes 983048 | tf_op jit(solution)/shard_map/ppermute | solution.py:304
  122.8 1.7 %collective-permute-done.8.refs_3_ = bf16[16,40,256]{2,1,0:T(8,128)(2,1)S(1)} collective-permute-done((bf16[16,40,256]{2,1,0:T(8,128)(2,1)S(1)}, bf16[16,40,256]{2,1,0:T(8,128)(2,1)S(1)}, u32[]{:S(2)}, u32[]{:S(2)}) %collective-permute-start.8) | collective-permute-done | bytes 327712 | tf_op jit(solution)/shard_map/ppermute | solution.py:304
  124.6 7.9 %collective-permute-done.7.refs_2_ = bf16[16,40,256]{2,1,0:T(8,128)(2,1)S(1)} collective-permute-done((bf16[16,40,256]{2,1,0:T(8,128)(2,1)S(1)}, bf16[16,40,256]{2,1,0:T(8,128)(2,1)S(1)}, u32[]{:S(2)}, u32[]{:S(2)}) %collective-permute-start.7) | collective-permute-done | bytes 327712 | tf_op jit(solution)/shard_map/ppermute | solution.py:304
  132.4 1.4 collective-permute-done.6.refs_1_
  133.8 3.3 %shard_map.76 = bf16[16,40,1024]{2,1,0:T(8,128)(2,1)S(1)} custom-call(s32[1]{0:T(128)} %bitcast.2.place_ref, bf16[16,40,256]{2,1,0:T(8,128)(2,1)S(1)} %shard_map.75.refs_0_, bf16[16,40,256]{2,1,0:T(8,128)(2,1)S(1)} %collective-permute-done.6.refs_1_, bf16[16,40,256]{2,1,0:T(8,128)(2,1)S(1)} %collective-permute-done.7.refs_2_, ...), custom_call_target="tpu_custom_call" | custom-call | flops 1342177280 | bytes 6815744 | tf_op jit(solution)/shard_map/pallas_call | solution.py:278
  137.1 0.0 copy-start.3
  137.1 25.8 %all_to_all.16.rows_ref = bf16[16,40,1024]{2,1,0:T(8,128)(2,1)S(1)} all-to-all(bf16[16,40,1024]{2,1,0:T(8,128)(2,1)S(1)} %shard_map.76), channel_id=1, replica_groups=mesh['y'=4,'c'=2,'x'=4,'z'=16] {'x','y'}, dimensions={0} | all-to-all | bytes 2621440 | tf_op jit(solution)/shard_map/all_to_all | solution.py:320
  163.0 0.0 copy-done.3
  163.0 1.4 shard_map.77
Async XLA Ops:
  6.5 2.5 %copy-start.2 = (s32[64,2]{0,1:T(2,128)S(1)}, s32[64,2]{0,1:T(2,128)}, u32[]{:S(2)}) copy-start(s32[64,2]{0,1:T(2,128)} %param.8) | copy-start | bytes 1540
  6.5 2.5 %copy-start.1 = (bf16[64,4096]{1,0:T(8,128)(2,1)S(1)}, bf16[64,4096]{1,0:T(8,128)(2,1)}, u32[]{:S(2)}) copy-start(bf16[64,4096]{1,0:T(8,128)(2,1)} %tokens_ref.1) | copy-start | bytes 1572868
  6.5 95.8 %all-gather.3.cloned.1.call-start = ((), (), s32[]{:S(2)}) async-start(), calls=%async_computation.3 | async-start | bytes 12976128 | tf_op jit(solution)/shard_map/all_gather | solution.py:310
  25.7 11.1 %all-to-all-start.1 = ((bf16[4,40,2048]{2,1,0:T(8,128)(2,1)}), bf16[4,40,2048]{2,1,0:T(8,128)(2,1)S(1)}, u32[]{:S(2)}, u32[]{:S(2)}) async-start(bf16[4,40,2048]{2,1,0:T(8,128)(2,1)} %bitcast.4), calls=%async_computation.1 | async-start | bytes 1310720 | tf_op jit(solution)/shard_map/all_to_all | solution.py:313
  29.2 21.0 %collective-permute-start.2 = (bf16[4,40,2048]{2,1,0:T(8,128)(2,1)S(1)}, bf16[4,40,2048]{2,1,0:T(8,128)(2,1)S(1)}, u32[]{:S(2)}, u32[]{:S(2)}) collective-permute-start(bf16[4,40,2048]{2,1,0:T(8,128)(2,1)S(1)} %all_to_all.15.refs_0_), channel_id=1, source_target_pairs={{0,128},{128,256},{256,384},{384,0},{1,129},{129,257},{257,385},{3... | collective-permute-start | bytes 1966088 | tf_op jit(solution)/shard_map/ppermute | solution.py:304
  36.8 19.0 %collective-permute-start.1 = (bf16[4,40,2048]{2,1,0:T(8,128)(2,1)S(1)}, bf16[4,40,2048]{2,1,0:T(8,128)(2,1)S(1)}, u32[]{:S(2)}, u32[]{:S(2)}) collective-permute-start(bf16[4,40,2048]{2,1,0:T(8,128)(2,1)S(1)} %all-to-all-done.1.refs_1_), channel_id=1, source_target_pairs={{0,384},{128,0},{256,128},{384,256},{1,385},{129,1},{257,129},{385... | collective-permute-start | bytes 1966088 | tf_op jit(solution)/shard_map/ppermute | solution.py:304
  44.9 25.0 %collective-permute-start = (bf16[4,40,2048]{2,1,0:T(8,128)(2,1)S(1)}, bf16[4,40,2048]{2,1,0:T(8,128)(2,1)S(1)}, u32[]{:S(2)}, u32[]{:S(2)}) collective-permute-start(bf16[4,40,2048]{2,1,0:T(8,128)(2,1)S(1)} %all_to_all.15.refs_0_), channel_id=1, source_target_pairs={{0,384},{128,0},{256,128},{384,256},{1,385},{129,1},{257,129},{385... | collective-permute-start | bytes 1966088 | tf_op jit(solution)/shard_map/ppermute | solution.py:304
  47.3 22.6 %collective-permute-start.5 = (bf16[4,40,2048]{2,1,0:T(8,128)(2,1)S(1)}, bf16[4,40,2048]{2,1,0:T(8,128)(2,1)}, u32[]{:S(2)}, u32[]{:S(2)}) collective-permute-start(bf16[4,40,2048]{2,1,0:T(8,128)(2,1)S(1)} %all-to-all-done.1.refs_1_), channel_id=1, source_target_pairs={{0,128},{128,256},{256,384},{384,0},{1,129},{129,257},{257,385},{3... | collective-permute-start | bytes 1966088 | tf_op jit(solution)/shard_map/ppermute | solution.py:304
  50.2 27.0 %collective-permute-start.3 = (bf16[4,40,2048]{2,1,0:T(8,128)(2,1)S(1)}, bf16[4,40,2048]{2,1,0:T(8,128)(2,1)}, u32[]{:S(2)}, u32[]{:S(2)}) collective-permute-start(bf16[4,40,2048]{2,1,0:T(8,128)(2,1)S(1)} %collective-permute-done.2.refs_6_), channel_id=1, source_target_pairs={{0,128},{128,256},{256,384},{384,0},{1,129},{129,257},{257,385},{3... | collective-permute-start | bytes 1966088 | tf_op jit(solution)/shard_map/ppermute | solution.py:304
  55.8 28.1 %collective-permute-start.4 = (bf16[4,40,2048]{2,1,0:T(8,128)(2,1)S(1)}, bf16[4,40,2048]{2,1,0:T(8,128)(2,1)}, u32[]{:S(2)}, u32[]{:S(2)}) collective-permute-start(bf16[4,40,2048]{2,1,0:T(8,128)(2,1)S(1)} %collective-permute-done.1.refs_3_), channel_id=1, source_target_pairs={{0,384},{128,0},{256,128},{384,256},{1,385},{129,1},{257,129},{385... | collective-permute-start | bytes 1966088 | tf_op jit(solution)/shard_map/ppermute | solution.py:304
  102.3 4.6 %copy-start = (bf16[12288,512]{1,0:T(8,128)(2,1)S(1)}, bf16[12288,512]{1,0:T(8,128)(2,1)}, u32[]{:S(2)}) copy-start(bf16[12288,512]{1,0:T(8,128)(2,1)} %all-gather.3.cloned.1.call-done) | copy-start | bytes 37748740
  112.4 12.2 %collective-permute-start.8 = (bf16[16,40,256]{2,1,0:T(8,128)(2,1)S(1)}, bf16[16,40,256]{2,1,0:T(8,128)(2,1)S(1)}, u32[]{:S(2)}, u32[]{:S(2)}) collective-permute-start(bf16[16,40,256]{2,1,0:T(8,128)(2,1)S(1)} %shard_map.75.refs_0_), channel_id=1, source_target_pairs={{0,128},{128,256},{256,384},{384,0},{1,129},{129,257},{257,385},{3... | collective-permute-start | bytes 983048 | tf_op jit(solution)/shard_map/ppermute | solution.py:304
  115.4 17.0 %collective-permute-start.7 = (bf16[16,40,256]{2,1,0:T(8,128)(2,1)S(1)}, bf16[16,40,256]{2,1,0:T(8,128)(2,1)S(1)}, u32[]{:S(2)}, u32[]{:S(2)}) collective-permute-start(bf16[16,40,256]{2,1,0:T(8,128)(2,1)S(1)} %shard_map.75.refs_0_), channel_id=1, source_target_pairs={{0,256},{128,384},{256,0},{384,128},{1,257},{129,385},{257,1},{385... | collective-permute-start | bytes 983048 | tf_op jit(solution)/shard_map/ppermute | solution.py:304
  119.8 14.0 %collective-permute-start.6 = (bf16[16,40,256]{2,1,0:T(8,128)(2,1)S(1)}, bf16[16,40,256]{2,1,0:T(8,128)(2,1)S(1)}, u32[]{:S(2)}, u32[]{:S(2)}) collective-permute-start(bf16[16,40,256]{2,1,0:T(8,128)(2,1)S(1)} %shard_map.75.refs_0_), channel_id=1, source_target_pairs={{0,384},{128,0},{256,128},{384,256},{1,385},{129,1},{257,129},{385... | collective-permute-start | bytes 983048 | tf_op jit(solution)/shard_map/ppermute | solution.py:304
  137.1 25.8 %copy-start.3 = (s32[64,2]{0,1:T(2,128)S(1)}, s32[64,2]{0,1:T(2,128)}, u32[]{:S(2)}) copy-start(s32[64,2]{0,1:T(2,128)} %param.9) | copy-start | bytes 1540
Sparse Core Ops, SparseCore 0:
  9.5 92.7 all-gather.2

commit v11 on v9

--- a/solution.py
+++ b/solution.py
@@ -82,9 +82,12 @@
     return by_first & here, by_second & here
 
 
-def encode_kernel(count_ref, columns_ref, tokens_ref, first_ref, second_ref):
+def encode_kernel(count_ref, columns_ref, numerators_ref, tokens_ref, first_ref, second_ref, shares_ref):
     by_first, by_second = placements(count_ref, columns_ref)
     chosen = (by_first | by_second).astype(jnp.float32).astype(jnp.bfloat16)
+    share = numerators_ref[...].astype(jnp.float32) / 256.0
+    shares = jnp.where(by_first, share[0:1], 0.0) + jnp.where(by_second, share[1:2], 0.0)
+    shares_ref[...] = shares.astype(jnp.bfloat16)
 
     def step(member, carry):
         for half, out_ref in enumerate((first_ref, second_ref)):
@@ -98,11 +101,8 @@
     lax.fori_loop(0, MEMBERS, step, 0)
 
 
-def mix_kernel(count_ref, columns_ref, numerators_ref, rows_ref, out_ref):
-    by_first, by_second = placements(count_ref, columns_ref)
-    share = numerators_ref[...].astype(jnp.float32) / 256.0
-    shares = jnp.where(by_first, share[0:1], 0.0) + jnp.where(by_second, share[1:2], 0.0)
-    shares = shares.astype(jnp.bfloat16)
+def mix_kernel(shares_ref, rows_ref, out_ref):
+    shares = shares_ref[...]
     for quarter in range(Y):
         rows = jnp.concatenate([rows_ref[x * Y + quarter] for x in range(X)], axis=0)
         mixed = lax.dot_general(shares, rows, (((0,), (0,)), ((), ())), preferred_element_type=jnp.float32)
@@ -233,15 +233,15 @@
     return pltpu.CompilerParams(vmem_limit_bytes=mebibytes << 20)
 
 
-def encode(counts, routes, tokens):
+def encode(counts, routes, numerators, tokens):
     return pl.pallas_call(
         encode_kernel,
-        out_shape=[shape((ALL_SLOTS, D // 2))] * 2,
-        in_specs=[SCALAR, WHOLE, WHOLE],
-        out_specs=[WHOLE] * 2,
+        out_shape=[*[shape((ALL_SLOTS, D // 2))] * 2, shape((ALL_SLOTS, TOK))],
+        in_specs=[SCALAR, *[WHOLE] * 3],
+        out_specs=[WHOLE] * 3,
         compiler_params=params(8),
         cost_estimate=pl.CostEstimate(flops=2 * ALL_SLOTS * TOK * D, bytes_accessed=2 * (TOK + ALL_SLOTS) * D, transcendentals=0),
-    )(counts, routes.T, tokens)
+    )(counts, routes.T, numerators.T, tokens)
 
 
 def pack(w_gate, w_up, w_down):
@@ -290,14 +290,14 @@
     )(hidden, weights)
 
 
-def mix(counts, routes, numerators, rows):
+def mix(shares, rows):
     return pl.pallas_call(
         mix_kernel,
         out_shape=shape((TOK, D)),
-        in_specs=[SCALAR] + [WHOLE] * 3,
+        in_specs=[WHOLE] * 2,
         out_specs=WHOLE,
         compiler_params=params(8),
-    )(counts, routes.T, numerators.T, rows)
+    )(shares, rows)
 
 
 def shift(block, by):
@@ -308,7 +308,7 @@
     place = lax.axis_index("y").astype(jnp.int32).reshape(1)
     weights = pack(w_gate, w_up, w_down)
     weights = lax.all_gather(weights, ("z", "c")).reshape(2, MEMBERS, C, HALF + 128, SHARD)
-    first, second = encode(counts, routes, tokens)
+    first, second, shares = encode(counts, routes, numerators, tokens)
     first = lax.all_to_all(first.reshape(X, SLOTS, D // 2), "x", 0, 0, tiled=True)
     second = lax.all_to_all(second.reshape(X, SLOTS, D // 2), "x", 0, 0, tiled=True)
     first_3, second_1 = shift(first, 1), shift(second, -1)
@@ -317,7 +317,7 @@
     rows = (first, second, first_1, second_1, first_2, second_2, first_3, second_3)
     hidden = lax.all_to_all(hidden_rows(place, rows, weights), "y", 0, 0, tiled=True)
     result = lax.all_to_all(down_rows(hidden, weights), ("x", "y"), 0, 0, tiled=True)
-    return mix(counts, routes, numerators, result)
+    return mix(shares, result)
 
 
 def solution(mesh):

time: 164 us -> 163 us (level)
    ppermute x6, waiting for transfers between devices: 26.3 us -> 28.4 us  [shift(): return lax.ppermute(block, 'y', [(i, (i + by) % Y) for i in range(Y)])]
where the time goes in v11:
time: 163 us; the launch traced here: 162 us
  blocking collectives  55.2 us (34%)
  waiting for transfers between devices  46.9 us (29%)
  starting transfers between devices  29.7 us (18%)
  Pallas kernels  16.3 us (10%)
  between operations  14.2 us (9%)
    ppermute x6, waiting for transfers between devices, shift(): return lax.ppermute(block, 'y', [(i, (i + by) % Y) for i in range(Y)])  28.4 us
    ppermute x6, starting transfers between devices, shift(): return lax.ppermute(block, 'y', [(i, (i + by) % Y) for i in range(Y)])  26.2 us
    all_to_all x1, blocking collectives, local(): lax.all_to_all(down_rows(hidden, weights), ('x', 'y'), 0, 0, tiled=True)  21.8 us
    all_to_all x1, blocking collectives, local(): lax.all_to_all(hidden_rows(place, rows, weights), 'y', 0, 0, tiled=True)  21.1 us
    all_gather x1, waiting for transfers between devices, local(): lax.all_gather(weights, ('z', 'c'))  17.9 us
    all_to_all x1, blocking collectives, local(): lax.all_to_all(second.reshape(X, SLOTS, D // 2), 'x', 0, 0, tiled=True)  12.3 us
    pallas_call x1, Pallas kernels, hidden_rows(): pl.pallas_call(hidden_kernel, out_shape=shape((Y, SRC, SLOTS, FQ)), in_sp...  5.64 us
    pallas_call x1, Pallas kernels, encode(): pl.pallas_call(encode_kernel, out_shape=[*[shape((ALL_SLOTS, D // 2))] *...  4.31 us
  transfers between devices with their start and end apart: 8, of which 6 were waited for; matrix products, arithmetic and copies ran while one was open for 0% of the time, Pallas kernels for 3%

profile of v11, /device:TPU:1, one launch (start us, length us, event | category | flops | bytes accessed | tf_op | source)
XLA Modules:
  0.0 162.3 jit_solution(15418553678553003196)
XLA Ops:
  6.5 0.0 copy-start.2
  6.5 0.0 copy-start.1
  6.5 0.0 copy-start
  6.5 0.0 all-gather.3.cloned.1.call-start
  6.5 1.8 %shard_map.74 = bf16[384,512]{1,0:T(8,128)(2,1)} custom-call(bf16[512,1024]{1,0:T(8,128)(2,1)} %gate_ref.1, bf16[512,1024]{1,0:T(8,128)(2,1)} %up_ref.1, bf16[1024,512]{1,0:T(8,128)(2,1)} %down_ref.1), custom_call_target="tpu_custom_call" | custom-call | tf_op jit(solution)/shard_map/pallas_call | solution.py:248
  8.4 0.0 all-gather.3.cloned.1.call-update
  9.1 0.0 copy-done.2
  9.1 0.0 copy-done.1
  9.1 0.0 copy-done
  9.1 4.3 %shard_map.73 = (bf16[160,2048]{1,0:T(8,128)(2,1)}, bf16[160,2048]{1,0:T(8,128)(2,1)S(1)}, bf16[160,64]{1,0:T(8,128)(2,1)S(1)}) custom-call(s32[1]{0:T(128)S(6)} %copy.8.count_ref, s32[2,64]{1,0:T(2,128)S(1)} %bitcast.7, s32[2,64]{1,0:T(2,128)S(1)} %bitcast.8, bf16[64,4096]{1,0:T(8,128)(2,1)S(1)} %copy-done), custom_call_target="tpu_custom_call" | custom-call | flops 83886080 | bytes 1835008 | tf_op jit(solution)/shard_map/pallas_call | solution.py:237
  13.4 12.3 %all_to_all.20.refs_1_ = bf16[4,40,2048]{2,1,0:T(8,128)(2,1)S(1)} all-to-all(bf16[4,40,2048]{2,1,0:T(8,128)(2,1)S(1)} %bitcast.6), channel_id=1, replica_groups=mesh['y'=4,'c'=2,'x'=4,'z'=16] {'x'}, dimensions={0} | all-to-all | bytes 1310720 | tf_op jit(solution)/shard_map/all_to_all | solution.py:313
  25.7 3.5 %all-to-all-start = ((bf16[4,40,2048]{2,1,0:T(8,128)(2,1)}), bf16[4,40,2048]{2,1,0:T(8,128)(2,1)S(1)}, u32[]{:S(2)}, u32[]{:S(2)}) async-start(bf16[4,40,2048]{2,1,0:T(8,128)(2,1)} %bitcast.3), calls=%async_computation | async-start | bytes 1310720 | tf_op jit(solution)/shard_map/all_to_all | solution.py:312
  29.2 7.0 %collective-permute-start.1 = (bf16[4,40,2048]{2,1,0:T(8,128)(2,1)S(1)}, bf16[4,40,2048]{2,1,0:T(8,128)(2,1)S(1)}, u32[]{:S(2)}, u32[]{:S(2)}) collective-permute-start(bf16[4,40,2048]{2,1,0:T(8,128)(2,1)S(1)} %all_to_all.20.refs_1_), channel_id=1, source_target_pairs={{0,384},{128,0},{256,128},{384,256},{1,385},{129,1},{257,129},{385... | collective-permute-start | bytes 1966088 | tf_op jit(solution)/shard_map/ppermute | solution.py:304
  36.2 0.6 all-to-all-done.refs_0_
  36.8 6.7 %collective-permute-start.2 = (bf16[4,40,2048]{2,1,0:T(8,128)(2,1)S(1)}, bf16[4,40,2048]{2,1,0:T(8,128)(2,1)S(1)}, u32[]{:S(2)}, u32[]{:S(2)}) collective-permute-start(bf16[4,40,2048]{2,1,0:T(8,128)(2,1)S(1)} %all-to-all-done.refs_0_), channel_id=1, source_target_pairs={{0,128},{128,256},{256,384},{384,0},{1,129},{129,257},{257,385},{3... | collective-permute-start | bytes 1966088 | tf_op jit(solution)/shard_map/ppermute | solution.py:304
  43.5 3.2 %collective-permute-start.5 = (bf16[4,40,2048]{2,1,0:T(8,128)(2,1)S(1)}, bf16[4,40,2048]{2,1,0:T(8,128)(2,1)S(1)}, u32[]{:S(2)}, u32[]{:S(2)}) collective-permute-start(bf16[4,40,2048]{2,1,0:T(8,128)(2,1)S(1)} %all_to_all.20.refs_1_), channel_id=1, source_target_pairs={{0,128},{128,256},{256,384},{384,0},{1,129},{129,257},{257,385},{3... | collective-permute-start | bytes 1966088 | tf_op jit(solution)/shard_map/ppermute | solution.py:304
  46.7 3.3 %collective-permute-start = (bf16[4,40,2048]{2,1,0:T(8,128)(2,1)S(1)}, bf16[4,40,2048]{2,1,0:T(8,128)(2,1)}, u32[]{:S(2)}, u32[]{:S(2)}) collective-permute-start(bf16[4,40,2048]{2,1,0:T(8,128)(2,1)S(1)} %all-to-all-done.refs_0_), channel_id=1, source_target_pairs={{0,384},{128,0},{256,128},{384,256},{1,385},{129,1},{257,129},{385... | collective-permute-start | bytes 1966088 | tf_op jit(solution)/shard_map/ppermute | solution.py:304
  50.0 0.0 collective-permute-done.1.refs_3_
  50.0 3.7 %collective-permute-start.4 = (bf16[4,40,2048]{2,1,0:T(8,128)(2,1)S(1)}, bf16[4,40,2048]{2,1,0:T(8,128)(2,1)}, u32[]{:S(2)}, u32[]{:S(2)}) collective-permute-start(bf16[4,40,2048]{2,1,0:T(8,128)(2,1)S(1)} %collective-permute-done.1.refs_3_), channel_id=1, source_target_pairs={{0,384},{128,0},{256,128},{384,256},{1,385},{129,1},{257,129},{385... | collective-permute-start | bytes 1966088 | tf_op jit(solution)/shard_map/ppermute | solution.py:304
  53.7 2.6 %collective-permute-done.2.refs_6_ = bf16[4,40,2048]{2,1,0:T(8,128)(2,1)S(1)} collective-permute-done((bf16[4,40,2048]{2,1,0:T(8,128)(2,1)S(1)}, bf16[4,40,2048]{2,1,0:T(8,128)(2,1)S(1)}, u32[]{:S(2)}, u32[]{:S(2)}) %collective-permute-start.2) | collective-permute-done | bytes 655392 | tf_op jit(solution)/shard_map/ppermute | solution.py:304
  56.3 2.3 %collective-permute-start.3 = (bf16[4,40,2048]{2,1,0:T(8,128)(2,1)S(1)}, bf16[4,40,2048]{2,1,0:T(8,128)(2,1)}, u32[]{:S(2)}, u32[]{:S(2)}) collective-permute-start(bf16[4,40,2048]{2,1,0:T(8,128)(2,1)S(1)} %collective-permute-done.2.refs_6_), channel_id=1, source_target_pairs={{0,128},{128,256},{256,384},{384,0},{1,129},{129,257},{257,385},{3... | collective-permute-start | bytes 1966088 | tf_op jit(solution)/shard_map/ppermute | solution.py:304
  58.7 11.7 %collective-permute-done.5.refs_7_ = bf16[4,40,2048]{2,1,0:T(8,128)(2,1)S(1)} collective-permute-done((bf16[4,40,2048]{2,1,0:T(8,128)(2,1)S(1)}, bf16[4,40,2048]{2,1,0:T(8,128)(2,1)S(1)}, u32[]{:S(2)}, u32[]{:S(2)}) %collective-permute-start.5) | collective-permute-done | bytes 655392 | tf_op jit(solution)/shard_map/ppermute | solution.py:304
  70.3 0.0 collective-permute-done.refs_2_
  70.3 5.0 %collective-permute-done.4.refs_5_ = bf16[4,40,2048]{2,1,0:T(8,128)(2,1)} collective-permute-done((bf16[4,40,2048]{2,1,0:T(8,128)(2,1)S(1)}, bf16[4,40,2048]{2,1,0:T(8,128)(2,1)}, u32[]{:S(2)}, u32[]{:S(2)}) %collective-permute-start.4) | collective-permute-done | bytes 655392 | tf_op jit(solution)/shard_map/ppermute | solution.py:304
  75.3 9.1 %collective-permute-done.3.refs_4_ = bf16[4,40,2048]{2,1,0:T(8,128)(2,1)} collective-permute-done((bf16[4,40,2048]{2,1,0:T(8,128)(2,1)S(1)}, bf16[4,40,2048]{2,1,0:T(8,128)(2,1)}, u32[]{:S(2)}, u32[]{:S(2)}) %collective-permute-start.3) | collective-permute-done | bytes 655392 | tf_op jit(solution)/shard_map/ppermute | solution.py:304
  84.4 17.9 %all-gather.3.cloned.1.call-done = bf16[12288,512]{1,0:T(8,128)(2,1)} async-done(((bf16[384,512]{1,0:T(8,128)(2,1)}), bf16[12288,512]{1,0:T(8,128)(2,1)}) %all-gather.3.cloned.1.call-update) | async-done | bytes 12582928 | tf_op jit(solution)/shard_map/all_gather | solution.py:310
  102.3 5.6 %shard_map.75 = bf16[4,16,40,256]{3,2,1,0:T(8,128)(2,1)S(1)} custom-call(s32[1]{0:T(128)} %bitcast.2.place_ref, bf16[4,40,2048]{2,1,0:T(8,128)(2,1)S(1)} %all-to-all-done.refs_0_, bf16[4,40,2048]{2,1,0:T(8,128)(2,1)S(1)} %all_to_all.20.refs_1_, bf16[4,40,2048]{2,1,0:T(8,128)(2,1)} %collective-permute-done.refs_2_, ...), custom_call_target="tpu_custom_call" | custom-call | flops 2684354560 | bytes 13631488 | tf_op jit(solution)/shard_map/pallas_call | solution.py:259
  108.0 21.1 %all_to_all.21.hidden_ref = bf16[4,16,40,256]{3,2,1,0:T(8,128)(2,1)S(1)} all-to-all(bf16[4,16,40,256]{3,2,1,0:T(8,128)(2,1)S(1)} %shard_map.75), channel_id=1, replica_groups=mesh['y'=4,'c'=2,'x'=4,'z'=16] {'y'}, dimensions={0} | all-to-all | bytes 2621440 | tf_op jit(solution)/shard_map/all_to_all | solution.py:318
  129.1 3.3 %shard_map.76 = bf16[16,40,1024]{2,1,0:T(8,128)(2,1)S(1)} custom-call(bf16[4,16,40,256]{3,2,1,0:T(8,128)(2,1)S(1)} %all_to_all.21.hidden_ref, bf16[2,8,2,384,512]{4,3,2,1,0:T(8,128)(2,1)} %bitcast.10), custom_call_target="tpu_custom_call" | custom-call | flops 1342177280 | bytes 6815744 | tf_op jit(solution)/shard_map/pallas_call | solution.py:278
  132.4 21.8 %all_to_all.22.rows_ref = bf16[16,40,1024]{2,1,0:T(8,128)(2,1)S(1)} all-to-all(bf16[16,40,1024]{2,1,0:T(8,128)(2,1)S(1)} %shard_map.76), channel_id=1, replica_groups=mesh['y'=4,'c'=2,'x'=4,'z'=16] {'x','y'}, dimensions={0} | all-to-all | bytes 2621440 | tf_op jit(solution)/shard_map/all_to_all | solution.py:319
  154.2 1.2 shard_map.77
Async XLA Ops:
  6.5 2.5 %copy-start.2 = (s32[64,2]{0,1:T(2,128)S(1)}, s32[64,2]{0,1:T(2,128)}, u32[]{:S(2)}) copy-start(s32[64,2]{0,1:T(2,128)} %param.9) | copy-start | bytes 1540
  6.5 2.5 %copy-start.1 = (s32[64,2]{0,1:T(2,128)S(1)}, s32[64,2]{0,1:T(2,128)}, u32[]{:S(2)}) copy-start(s32[64,2]{0,1:T(2,128)} %param.8) | copy-start | bytes 1540
  6.5 2.6 %copy-start = (bf16[64,4096]{1,0:T(8,128)(2,1)S(1)}, bf16[64,4096]{1,0:T(8,128)(2,1)}, u32[]{:S(2)}) copy-start(bf16[64,4096]{1,0:T(8,128)(2,1)} %tokens_ref.1) | copy-start | bytes 1572868
  6.5 95.8 %all-gather.3.cloned.1.call-start = ((), (), s32[]{:S(2)}) async-start(), calls=%async_computation.4 | async-start | bytes 12976128 | tf_op jit(solution)/shard_map/all_gather | solution.py:310
  25.7 11.1 %all-to-all-start = ((bf16[4,40,2048]{2,1,0:T(8,128)(2,1)}), bf16[4,40,2048]{2,1,0:T(8,128)(2,1)S(1)}, u32[]{:S(2)}, u32[]{:S(2)}) async-start(bf16[4,40,2048]{2,1,0:T(8,128)(2,1)} %bitcast.3), calls=%async_computation | async-start | bytes 1310720 | tf_op jit(solution)/shard_map/all_to_all | solution.py:312
  29.2 20.8 %collective-permute-start.1 = (bf16[4,40,2048]{2,1,0:T(8,128)(2,1)S(1)}, bf16[4,40,2048]{2,1,0:T(8,128)(2,1)S(1)}, u32[]{:S(2)}, u32[]{:S(2)}) collective-permute-start(bf16[4,40,2048]{2,1,0:T(8,128)(2,1)S(1)} %all_to_all.20.refs_1_), channel_id=1, source_target_pairs={{0,384},{128,0},{256,128},{384,256},{1,385},{129,1},{257,129},{385... | collective-permute-start | bytes 1966088 | tf_op jit(solution)/shard_map/ppermute | solution.py:304
  36.8 19.6 %collective-permute-start.2 = (bf16[4,40,2048]{2,1,0:T(8,128)(2,1)S(1)}, bf16[4,40,2048]{2,1,0:T(8,128)(2,1)S(1)}, u32[]{:S(2)}, u32[]{:S(2)}) collective-permute-start(bf16[4,40,2048]{2,1,0:T(8,128)(2,1)S(1)} %all-to-all-done.refs_0_), channel_id=1, source_target_pairs={{0,128},{128,256},{256,384},{384,0},{1,129},{129,257},{257,385},{3... | collective-permute-start | bytes 1966088 | tf_op jit(solution)/shard_map/ppermute | solution.py:304
  43.5 26.9 %collective-permute-start.5 = (bf16[4,40,2048]{2,1,0:T(8,128)(2,1)S(1)}, bf16[4,40,2048]{2,1,0:T(8,128)(2,1)S(1)}, u32[]{:S(2)}, u32[]{:S(2)}) collective-permute-start(bf16[4,40,2048]{2,1,0:T(8,128)(2,1)S(1)} %all_to_all.20.refs_1_), channel_id=1, source_target_pairs={{0,128},{128,256},{256,384},{384,0},{1,129},{129,257},{257,385},{3... | collective-permute-start | bytes 1966088 | tf_op jit(solution)/shard_map/ppermute | solution.py:304
  46.7 23.6 %collective-permute-start = (bf16[4,40,2048]{2,1,0:T(8,128)(2,1)S(1)}, bf16[4,40,2048]{2,1,0:T(8,128)(2,1)}, u32[]{:S(2)}, u32[]{:S(2)}) collective-permute-start(bf16[4,40,2048]{2,1,0:T(8,128)(2,1)S(1)} %all-to-all-done.refs_0_), channel_id=1, source_target_pairs={{0,384},{128,0},{256,128},{384,256},{1,385},{129,1},{257,129},{385... | collective-permute-start | bytes 1966088 | tf_op jit(solution)/shard_map/ppermute | solution.py:304
  50.0 25.4 %collective-permute-start.4 = (bf16[4,40,2048]{2,1,0:T(8,128)(2,1)S(1)}, bf16[4,40,2048]{2,1,0:T(8,128)(2,1)}, u32[]{:S(2)}, u32[]{:S(2)}) collective-permute-start(bf16[4,40,2048]{2,1,0:T(8,128)(2,1)S(1)} %collective-permute-done.1.refs_3_), channel_id=1, source_target_pairs={{0,384},{128,0},{256,128},{384,256},{1,385},{129,1},{257,129},{385... | collective-permute-start | bytes 1966088 | tf_op jit(solution)/shard_map/ppermute | solution.py:304
  56.3 28.1 %collective-permute-start.3 = (bf16[4,40,2048]{2,1,0:T(8,128)(2,1)S(1)}, bf16[4,40,2048]{2,1,0:T(8,128)(2,1)}, u32[]{:S(2)}, u32[]{:S(2)}) collective-permute-start(bf16[4,40,2048]{2,1,0:T(8,128)(2,1)S(1)} %collective-permute-done.2.refs_6_), channel_id=1, source_target_pairs={{0,128},{128,256},{256,384},{384,0},{1,129},{129,257},{257,385},{3... | collective-permute-start | bytes 1966088 | tf_op jit(solution)/shard_map/ppermute | solution.py:304
Sparse Core Ops, SparseCore 0:
  9.5 92.7 all-gather.2

commit v12 on v11

--- a/solution.py
+++ b/solution.py
@@ -178,16 +178,18 @@
             weights = held[i, expert].reshape(DEEP * HALF, 2 * FQ)
             product = jnp.dot(block, weights, preferred_element_type=jnp.float32)
             total[...] = product if i == 0 else total[...] + product
-    joined = join_rows(*(swish(total[...]) for total in sums))
-    for offset in range(Y):
-        source = lax.rem(place_ref[0] + offset, Y)
-        block = joined[offset * X : (offset + 1) * X]
-        for copy in range(Y):
-            out_ref[copy, pl.ds(source * X, X)] = block
-
-
-def down_kernel(hidden_ref, weights_ref, out_ref, held, sems, *rows):
-    main = SRC * MAIN
+    for expert, total in enumerate(sums):
+        hidden = swish(total[...]).astype(jnp.bfloat16)
+        for start, length in ((0, X * MAIN), (SRC * MAIN, X * REST // 2)):
+            for offset in range(Y):
+                source = lax.rem(place_ref[0] + offset, Y)
+                to = pl.ds(pl.multiple_of(start + source * length, length), length)
+                block = hidden[start + offset * length : start + (offset + 1) * length]
+                for copy in range(Y):
+                    out_ref[copy, expert, to] = block
+
+
+def down_kernel(hidden_ref, weights_ref, out_ref, held, sems):
     starts = range(0, MEMBERS, WIDE)
     copies = [
         pltpu.make_async_copy(weights_ref.at[:, start : start + WIDE, :, HALF:], held.at[i], sems.at[i])
@@ -195,11 +197,7 @@
     ]
     for copy in copies:
         copy.start()
-    for quarter in range(Y):
-        at = slice(quarter * FQ, (quarter + 1) * FQ)
-        for ref, (run, rest) in zip(rows, split_rows(hidden_ref[quarter])):
-            ref[:main, at] = run
-            ref[main:, at] = rest
+    rows = [jnp.concatenate([hidden_ref[q, expert] for q in range(Y)], axis=1) for expert in range(2)]
 
     def result(i, expert):
         weights = jnp.concatenate(
@@ -210,7 +208,7 @@
             ],
             axis=0,
         )
-        return jnp.dot(rows[expert][...], weights, preferred_element_type=jnp.float32)
+        return jnp.dot(rows[expert], weights, preferred_element_type=jnp.float32)
 
     for i, start in enumerate(starts):
         copies[i].wait()
@@ -258,7 +256,7 @@
     pieces = C * MEMBERS // DEEP
     return pl.pallas_call(
         hidden_kernel,
-        out_shape=shape((Y, SRC, SLOTS, FQ)),
+        out_shape=shape((Y, 2, ROWS // 2, FQ)),
         in_specs=[SCALAR, *[ANY] * (2 * Y), ANY],
         out_specs=WHOLE,
         scratch_shapes=[
@@ -283,7 +281,6 @@
         scratch_shapes=[
             pltpu.VMEM((pieces, 2, WIDE, C, 128, SHARD), jnp.bfloat16),
             pltpu.SemaphoreType.DMA((pieces,)),
-            *[pltpu.VMEM((SRC * SLOTS // 2, F), jnp.bfloat16)] * 2,
         ],
         compiler_params=params(50),
         cost_estimate=pl.CostEstimate(flops=2 * ROWS * F * F, bytes_accessed=4 * ROWS * F + 4 * F * F, transcendentals=0),

time: 163 us -> 163 us (level)
  no operation moved by 1% of the time
where the time goes in v12:
time: 163 us; the launch traced here: 162 us
  blocking collectives  55.2 us (34%)
  waiting for transfers between devices  46.9 us (29%)
  starting transfers between devices  29.7 us (18%)
  Pallas kernels  16.3 us (10%)
  between operations  14.2 us (9%)
    ppermute x6, waiting for transfers between devices, shift(): return lax.ppermute(block, 'y', [(i, (i + by) % Y) for i in range(Y)])  28.4 us
    ppermute x6, starting transfers between devices, shift(): return lax.ppermute(block, 'y', [(i, (i + by) % Y) for i in range(Y)])  26.2 us
    all_to_all x1, blocking collectives, local(): lax.all_to_all(down_rows(hidden, weights), ('x', 'y'), 0, 0, tiled=True)  21.8 us
    all_to_all x1, blocking collectives, local(): lax.all_to_all(hidden_rows(place, rows, weights), 'y', 0, 0, tiled=True)  21.1 us
    all_gather x1, waiting for transfers between devices, local(): lax.all_gather(weights, ('z', 'c'))  17.9 us
    all_to_all x1, blocking collectives, local(): lax.all_to_all(second.reshape(X, SLOTS, D // 2), 'x', 0, 0, tiled=True)  12.3 us
    pallas_call x1, Pallas kernels, hidden_rows(): pl.pallas_call(hidden_kernel, out_shape=shape((Y, 2, ROWS // 2, FQ)), in_...  5.63 us
    pallas_call x1, Pallas kernels, encode(): pl.pallas_call(encode_kernel, out_shape=[*[shape((ALL_SLOTS, D // 2))] *...  4.31 us
  transfers between devices with their start and end apart: 8, of which 6 were waited for; matrix products, arithmetic and copies ran while one was open for 0% of the time, Pallas kernels for 3%

profile of v12, /device:TPU:1, one launch (start us, length us, event | category | flops | bytes accessed | tf_op | source)
XLA Modules:
  0.0 162.3 jit_solution(9812734591141046143)
XLA Ops:
  6.5 0.0 copy-start.2
  6.5 0.0 copy-start.1
  6.5 0.0 copy-start
  6.5 0.0 all-gather.3.cloned.1.call-start
  6.5 1.8 %shard_map.74 = bf16[384,512]{1,0:T(8,128)(2,1)} custom-call(bf16[512,1024]{1,0:T(8,128)(2,1)} %gate_ref.1, bf16[512,1024]{1,0:T(8,128)(2,1)} %up_ref.1, bf16[1024,512]{1,0:T(8,128)(2,1)} %down_ref.1), custom_call_target="tpu_custom_call" | custom-call | tf_op jit(solution)/shard_map/pallas_call | solution.py:246
  8.4 0.0 all-gather.3.cloned.1.call-update
  9.1 0.0 copy-done.2
  9.1 0.0 copy-done.1
  9.1 0.0 copy-done
  9.1 4.3 %shard_map.73 = (bf16[160,2048]{1,0:T(8,128)(2,1)}, bf16[160,2048]{1,0:T(8,128)(2,1)S(1)}, bf16[160,64]{1,0:T(8,128)(2,1)S(1)}) custom-call(s32[1]{0:T(128)S(6)} %copy.8.count_ref, s32[2,64]{1,0:T(2,128)S(1)} %bitcast.7, s32[2,64]{1,0:T(2,128)S(1)} %bitcast.8, bf16[64,4096]{1,0:T(8,128)(2,1)S(1)} %copy-done), custom_call_target="tpu_custom_call" | custom-call | flops 83886080 | bytes 1835008 | tf_op jit(solution)/shard_map/pallas_call | solution.py:235
  13.4 12.3 %all_to_all.20.refs_1_ = bf16[4,40,2048]{2,1,0:T(8,128)(2,1)S(1)} all-to-all(bf16[4,40,2048]{2,1,0:T(8,128)(2,1)S(1)} %bitcast.6), channel_id=1, replica_groups=mesh['y'=4,'c'=2,'x'=4,'z'=16] {'x'}, dimensions={0} | all-to-all | bytes 1310720 | tf_op jit(solution)/shard_map/all_to_all | solution.py:310
  25.7 3.5 %all-to-all-start = ((bf16[4,40,2048]{2,1,0:T(8,128)(2,1)}), bf16[4,40,2048]{2,1,0:T(8,128)(2,1)S(1)}, u32[]{:S(2)}, u32[]{:S(2)}) async-start(bf16[4,40,2048]{2,1,0:T(8,128)(2,1)} %bitcast.3), calls=%async_computation | async-start | bytes 1310720 | tf_op jit(solution)/shard_map/all_to_all | solution.py:309
  29.2 7.0 %collective-permute-start.1 = (bf16[4,40,2048]{2,1,0:T(8,128)(2,1)S(1)}, bf16[4,40,2048]{2,1,0:T(8,128)(2,1)S(1)}, u32[]{:S(2)}, u32[]{:S(2)}) collective-permute-start(bf16[4,40,2048]{2,1,0:T(8,128)(2,1)S(1)} %all_to_all.20.refs_1_), channel_id=1, source_target_pairs={{0,384},{128,0},{256,128},{384,256},{1,385},{129,1},{257,129},{385... | collective-permute-start | bytes 1966088 | tf_op jit(solution)/shard_map/ppermute | solution.py:301
  36.2 0.6 all-to-all-done.refs_0_
  36.8 6.7 %collective-permute-start.2 = (bf16[4,40,2048]{2,1,0:T(8,128)(2,1)S(1)}, bf16[4,40,2048]{2,1,0:T(8,128)(2,1)S(1)}, u32[]{:S(2)}, u32[]{:S(2)}) collective-permute-start(bf16[4,40,2048]{2,1,0:T(8,128)(2,1)S(1)} %all-to-all-done.refs_0_), channel_id=1, source_target_pairs={{0,128},{128,256},{256,384},{384,0},{1,129},{129,257},{257,385},{3... | collective-permute-start | bytes 1966088 | tf_op jit(solution)/shard_map/ppermute | solution.py:301
  43.5 3.2 %collective-permute-start.5 = (bf16[4,40,2048]{2,1,0:T(8,128)(2,1)S(1)}, bf16[4,40,2048]{2,1,0:T(8,128)(2,1)S(1)}, u32[]{:S(2)}, u32[]{:S(2)}) collective-permute-start(bf16[4,40,2048]{2,1,0:T(8,128)(2,1)S(1)} %all_to_all.20.refs_1_), channel_id=1, source_target_pairs={{0,128},{128,256},{256,384},{384,0},{1,129},{129,257},{257,385},{3... | collective-permute-start | bytes 1966088 | tf_op jit(solution)/shard_map/ppermute | solution.py:301
  46.7 3.3 %collective-permute-start = (bf16[4,40,2048]{2,1,0:T(8,128)(2,1)S(1)}, bf16[4,40,2048]{2,1,0:T(8,128)(2,1)}, u32[]{:S(2)}, u32[]{:S(2)}) collective-permute-start(bf16[4,40,2048]{2,1,0:T(8,128)(2,1)S(1)} %all-to-all-done.refs_0_), channel_id=1, source_target_pairs={{0,384},{128,0},{256,128},{384,256},{1,385},{129,1},{257,129},{385... | collective-permute-start | bytes 1966088 | tf_op jit(solution)/shard_map/ppermute | solution.py:301
  50.0 0.0 collective-permute-done.1.refs_3_
  50.0 3.7 %collective-permute-start.4 = (bf16[4,40,2048]{2,1,0:T(8,128)(2,1)S(1)}, bf16[4,40,2048]{2,1,0:T(8,128)(2,1)}, u32[]{:S(2)}, u32[]{:S(2)}) collective-permute-start(bf16[4,40,2048]{2,1,0:T(8,128)(2,1)S(1)} %collective-permute-done.1.refs_3_), channel_id=1, source_target_pairs={{0,384},{128,0},{256,128},{384,256},{1,385},{129,1},{257,129},{385... | collective-permute-start | bytes 1966088 | tf_op jit(solution)/shard_map/ppermute | solution.py:301
  53.7 2.6 %collective-permute-done.2.refs_6_ = bf16[4,40,2048]{2,1,0:T(8,128)(2,1)S(1)} collective-permute-done((bf16[4,40,2048]{2,1,0:T(8,128)(2,1)S(1)}, bf16[4,40,2048]{2,1,0:T(8,128)(2,1)S(1)}, u32[]{:S(2)}, u32[]{:S(2)}) %collective-permute-start.2) | collective-permute-done | bytes 655392 | tf_op jit(solution)/shard_map/ppermute | solution.py:301
  56.3 2.3 %collective-permute-start.3 = (bf16[4,40,2048]{2,1,0:T(8,128)(2,1)S(1)}, bf16[4,40,2048]{2,1,0:T(8,128)(2,1)}, u32[]{:S(2)}, u32[]{:S(2)}) collective-permute-start(bf16[4,40,2048]{2,1,0:T(8,128)(2,1)S(1)} %collective-permute-done.2.refs_6_), channel_id=1, source_target_pairs={{0,128},{128,256},{256,384},{384,0},{1,129},{129,257},{257,385},{3... | collective-permute-start | bytes 1966088 | tf_op jit(solution)/shard_map/ppermute | solution.py:301
  58.7 11.7 %collective-permute-done.5.refs_7_ = bf16[4,40,2048]{2,1,0:T(8,128)(2,1)S(1)} collective-permute-done((bf16[4,40,2048]{2,1,0:T(8,128)(2,1)S(1)}, bf16[4,40,2048]{2,1,0:T(8,128)(2,1)S(1)}, u32[]{:S(2)}, u32[]{:S(2)}) %collective-permute-start.5) | collective-permute-done | bytes 655392 | tf_op jit(solution)/shard_map/ppermute | solution.py:301
  70.3 0.0 collective-permute-done.refs_2_
  70.3 5.0 %collective-permute-done.4.refs_5_ = bf16[4,40,2048]{2,1,0:T(8,128)(2,1)} collective-permute-done((bf16[4,40,2048]{2,1,0:T(8,128)(2,1)S(1)}, bf16[4,40,2048]{2,1,0:T(8,128)(2,1)}, u32[]{:S(2)}, u32[]{:S(2)}) %collective-permute-start.4) | collective-permute-done | bytes 655392 | tf_op jit(solution)/shard_map/ppermute | solution.py:301
  75.3 9.1 %collective-permute-done.3.refs_4_ = bf16[4,40,2048]{2,1,0:T(8,128)(2,1)} collective-permute-done((bf16[4,40,2048]{2,1,0:T(8,128)(2,1)S(1)}, bf16[4,40,2048]{2,1,0:T(8,128)(2,1)}, u32[]{:S(2)}, u32[]{:S(2)}) %collective-permute-start.3) | collective-permute-done | bytes 655392 | tf_op jit(solution)/shard_map/ppermute | solution.py:301
  84.4 17.9 %all-gather.3.cloned.1.call-done = bf16[12288,512]{1,0:T(8,128)(2,1)} async-done(((bf16[384,512]{1,0:T(8,128)(2,1)}), bf16[12288,512]{1,0:T(8,128)(2,1)}) %all-gather.3.cloned.1.call-update) | async-done | bytes 12582928 | tf_op jit(solution)/shard_map/all_gather | solution.py:307
  102.3 5.6 %shard_map.75 = bf16[4,2,320,256]{3,2,1,0:T(8,128)(2,1)S(1)} custom-call(s32[1]{0:T(128)} %bitcast.2.place_ref, bf16[4,40,2048]{2,1,0:T(8,128)(2,1)S(1)} %all-to-all-done.refs_0_, bf16[4,40,2048]{2,1,0:T(8,128)(2,1)S(1)} %all_to_all.20.refs_1_, bf16[4,40,2048]{2,1,0:T(8,128)(2,1)} %collective-permute-done.refs_2_, ...), custom_call_target="tpu_custom_call" | custom-call | flops 2684354560 | bytes 13631488 | tf_op jit(solution)/shard_map/pallas_call | solution.py:257
  108.0 21.1 %all_to_all.21.hidden_ref = bf16[4,2,320,256]{3,2,1,0:T(8,128)(2,1)S(1)} all-to-all(bf16[4,2,320,256]{3,2,1,0:T(8,128)(2,1)S(1)} %shard_map.75), channel_id=1, replica_groups=mesh['y'=4,'c'=2,'x'=4,'z'=16] {'y'}, dimensions={0} | all-to-all | bytes 2621440 | tf_op jit(solution)/shard_map/all_to_all | solution.py:315
  129.1 3.3 %shard_map.76 = bf16[16,40,1024]{2,1,0:T(8,128)(2,1)S(1)} custom-call(bf16[4,2,320,256]{3,2,1,0:T(8,128)(2,1)S(1)} %all_to_all.21.hidden_ref, bf16[2,8,2,384,512]{4,3,2,1,0:T(8,128)(2,1)} %bitcast.10), custom_call_target="tpu_custom_call" | custom-call | flops 1342177280 | bytes 6815744 | tf_op jit(solution)/shard_map/pallas_call | solution.py:276
  132.4 21.8 %all_to_all.22.rows_ref = bf16[16,40,1024]{2,1,0:T(8,128)(2,1)S(1)} all-to-all(bf16[16,40,1024]{2,1,0:T(8,128)(2,1)S(1)} %shard_map.76), channel_id=1, replica_groups=mesh['y'=4,'c'=2,'x'=4,'z'=16] {'x','y'}, dimensions={0} | all-to-all | bytes 2621440 | tf_op jit(solution)/shard_map/all_to_all | solution.py:316
  154.2 1.2 shard_map.77
Async XLA Ops:
  6.5 2.5 %copy-start.2 = (s32[64,2]{0,1:T(2,128)S(1)}, s32[64,2]{0,1:T(2,128)}, u32[]{:S(2)}) copy-start(s32[64,2]{0,1:T(2,128)} %param.9) | copy-start | bytes 1540
  6.5 2.5 %copy-start.1 = (s32[64,2]{0,1:T(2,128)S(1)}, s32[64,2]{0,1:T(2,128)}, u32[]{:S(2)}) copy-start(s32[64,2]{0,1:T(2,128)} %param.8) | copy-start | bytes 1540
  6.5 2.6 %copy-start = (bf16[64,4096]{1,0:T(8,128)(2,1)S(1)}, bf16[64,4096]{1,0:T(8,128)(2,1)}, u32[]{:S(2)}) copy-start(bf16[64,4096]{1,0:T(8,128)(2,1)} %tokens_ref.1) | copy-start | bytes 1572868
  6.5 95.8 %all-gather.3.cloned.1.call-start = ((), (), s32[]{:S(2)}) async-start(), calls=%async_computation.4 | async-start | bytes 12976128 | tf_op jit(solution)/shard_map/all_gather | solution.py:307
  25.7 11.1 %all-to-all-start = ((bf16[4,40,2048]{2,1,0:T(8,128)(2,1)}), bf16[4,40,2048]{2,1,0:T(8,128)(2,1)S(1)}, u32[]{:S(2)}, u32[]{:S(2)}) async-start(bf16[4,40,2048]{2,1,0:T(8,128)(2,1)} %bitcast.3), calls=%async_computation | async-start | bytes 1310720 | tf_op jit(solution)/shard_map/all_to_all | solution.py:309
  29.2 20.8 %collective-permute-start.1 = (bf16[4,40,2048]{2,1,0:T(8,128)(2,1)S(1)}, bf16[4,40,2048]{2,1,0:T(8,128)(2,1)S(1)}, u32[]{:S(2)}, u32[]{:S(2)}) collective-permute-start(bf16[4,40,2048]{2,1,0:T(8,128)(2,1)S(1)} %all_to_all.20.refs_1_), channel_id=1, source_target_pairs={{0,384},{128,0},{256,128},{384,256},{1,385},{129,1},{257,129},{385... | collective-permute-start | bytes 1966088 | tf_op jit(solution)/shard_map/ppermute | solution.py:301
  36.8 19.6 %collective-permute-start.2 = (bf16[4,40,2048]{2,1,0:T(8,128)(2,1)S(1)}, bf16[4,40,2048]{2,1,0:T(8,128)(2,1)S(1)}, u32[]{:S(2)}, u32[]{:S(2)}) collective-permute-start(bf16[4,40,2048]{2,1,0:T(8,128)(2,1)S(1)} %all-to-all-done.refs_0_), channel_id=1, source_target_pairs={{0,128},{128,256},{256,384},{384,0},{1,129},{129,257},{257,385},{3... | collective-permute-start | bytes 1966088 | tf_op jit(solution)/shard_map/ppermute | solution.py:301
  43.5 26.9 %collective-permute-start.5 = (bf16[4,40,2048]{2,1,0:T(8,128)(2,1)S(1)}, bf16[4,40,2048]{2,1,0:T(8,128)(2,1)S(1)}, u32[]{:S(2)}, u32[]{:S(2)}) collective-permute-start(bf16[4,40,2048]{2,1,0:T(8,128)(2,1)S(1)} %all_to_all.20.refs_1_), channel_id=1, source_target_pairs={{0,128},{128,256},{256,384},{384,0},{1,129},{129,257},{257,385},{3... | collective-permute-start | bytes 1966088 | tf_op jit(solution)/shard_map/ppermute | solution.py:301
  46.7 23.6 %collective-permute-start = (bf16[4,40,2048]{2,1,0:T(8,128)(2,1)S(1)}, bf16[4,40,2048]{2,1,0:T(8,128)(2,1)}, u32[]{:S(2)}, u32[]{:S(2)}) collective-permute-start(bf16[4,40,2048]{2,1,0:T(8,128)(2,1)S(1)} %all-to-all-done.refs_0_), channel_id=1, source_target_pairs={{0,384},{128,0},{256,128},{384,256},{1,385},{129,1},{257,129},{385... | collective-permute-start | bytes 1966088 | tf_op jit(solution)/shard_map/ppermute | solution.py:301
  50.0 25.4 %collective-permute-start.4 = (bf16[4,40,2048]{2,1,0:T(8,128)(2,1)S(1)}, bf16[4,40,2048]{2,1,0:T(8,128)(2,1)}, u32[]{:S(2)}, u32[]{:S(2)}) collective-permute-start(bf16[4,40,2048]{2,1,0:T(8,128)(2,1)S(1)} %collective-permute-done.1.refs_3_), channel_id=1, source_target_pairs={{0,384},{128,0},{256,128},{384,256},{1,385},{129,1},{257,129},{385... | collective-permute-start | bytes 1966088 | tf_op jit(solution)/shard_map/ppermute | solution.py:301
  56.3 28.1 %collective-permute-start.3 = (bf16[4,40,2048]{2,1,0:T(8,128)(2,1)S(1)}, bf16[4,40,2048]{2,1,0:T(8,128)(2,1)}, u32[]{:S(2)}, u32[]{:S(2)}) collective-permute-start(bf16[4,40,2048]{2,1,0:T(8,128)(2,1)S(1)} %collective-permute-done.2.refs_6_), channel_id=1, source_target_pairs={{0,128},{128,256},{256,384},{384,0},{1,129},{129,257},{257,385},{3... | collective-permute-start | bytes 1966088 | tf_op jit(solution)/shard_map/ppermute | solution.py:301
Sparse Core Ops, SparseCore 0:
  9.5 92.7 all-gather.2

commit v13 on v12

--- a/solution.py
+++ b/solution.py
@@ -101,15 +101,23 @@
     lax.fori_loop(0, MEMBERS, step, 0)
 
 
-def mix_kernel(shares_ref, rows_ref, out_ref):
+def mix_kernel(shares_ref, rows_ref, out_ref, held, sems):
     shares = shares_ref[...]
-    for quarter in range(Y):
-        rows = jnp.concatenate([rows_ref[x * Y + quarter] for x in range(X)], axis=0)
-        mixed = lax.dot_general(shares, rows, (((0,), (0,)), ((), ())), preferred_element_type=jnp.float32)
-        mixed = mixed.astype(jnp.bfloat16)
-        for member in range(MEMBERS):
-            at = member * SHARD + quarter * 128
-            out_ref[:, at : at + 128] = mixed[:, member * 128 : (member + 1) * 128]
+    copies = []
+    for i, start in enumerate(range(0, MEMBERS, WIDE)):
+        for quarter in range(Y):
+            rows = [rows_ref[x * Y + quarter, :, start * 128 : (start + WIDE) * 128] for x in range(X)]
+            rows = jnp.concatenate(rows, axis=0)
+            mixed = lax.dot_general(shares, rows, (((0,), (0,)), ((), ())), preferred_element_type=jnp.float32)
+            mixed = mixed.astype(jnp.bfloat16)
+            for m in range(WIDE):
+                at = (start + m) * SHARD + quarter * 128
+                held[:, at : at + 128] = mixed[:, m * 128 : (m + 1) * 128]
+        done = slice(start * SHARD, (start + WIDE) * SHARD)
+        copies.append(pltpu.make_async_copy(held.at[:, done], out_ref.at[:, done], sems.at[i]))
+        copies[-1].start()
+    for copy in copies:
+        copy.wait()
 
 
 def split_rows(block):
@@ -292,7 +300,8 @@
         mix_kernel,
         out_shape=shape((TOK, D)),
         in_specs=[WHOLE] * 2,
-        out_specs=WHOLE,
+        out_specs=ANY,
+        scratch_shapes=[pltpu.VMEM((TOK, D), jnp.bfloat16), pltpu.SemaphoreType.DMA((MEMBERS // WIDE,))],
         compiler_params=params(8),
     )(shares, rows)
 

time: 163 us -> 163 us (level)
  no operation moved by 1% of the time
where the time goes in v13:
time: 163 us; the launch traced here: 162 us
  blocking collectives  55.2 us (34%)
  waiting for transfers between devices  46.9 us (29%)
  starting transfers between devices  29.7 us (18%)
  Pallas kernels  16.2 us (10%)
  between operations  14.2 us (9%)
    ppermute x6, waiting for transfers between devices, shift(): return lax.ppermute(block, 'y', [(i, (i + by) % Y) for i in range(Y)])  28.4 us
    ppermute x6, starting transfers between devices, shift(): return lax.ppermute(block, 'y', [(i, (i + by) % Y) for i in range(Y)])  26.2 us
    all_to_all x1, blocking collectives, local(): lax.all_to_all(down_rows(hidden, weights), ('x', 'y'), 0, 0, tiled=True)  21.8 us
    all_to_all x1, blocking collectives, local(): lax.all_to_all(hidden_rows(place, rows, weights), 'y', 0, 0, tiled=True)  21.1 us
    all_gather x1, waiting for transfers between devices, local(): lax.all_gather(weights, ('z', 'c'))  17.9 us
    all_to_all x1, blocking collectives, local(): lax.all_to_all(second.reshape(X, SLOTS, D // 2), 'x', 0, 0, tiled=True)  12.3 us
    pallas_call x1, Pallas kernels, hidden_rows(): pl.pallas_call(hidden_kernel, out_shape=shape((Y, 2, ROWS // 2, FQ)), in_...  5.63 us
    pallas_call x1, Pallas kernels, encode(): pl.pallas_call(encode_kernel, out_shape=[*[shape((ALL_SLOTS, D // 2))] *...  4.31 us
  transfers between devices with their start and end apart: 8, of which 6 were waited for; matrix products, arithmetic and copies ran while one was open for 0% of the time, Pallas kernels for 3%

profile of v13, /device:TPU:1, one launch (start us, length us, event | category | flops | bytes accessed | tf_op | source)
XLA Modules:
  0.0 162.2 jit_solution(5622957746060628057)
XLA Ops:
  6.5 0.0 copy-start.2
  6.5 0.0 copy-start.1
  6.5 0.0 copy-start
  6.5 0.0 all-gather.3.cloned.1.call-start
  6.5 1.8 %shard_map.74 = bf16[384,512]{1,0:T(8,128)(2,1)} custom-call(bf16[512,1024]{1,0:T(8,128)(2,1)} %gate_ref.1, bf16[512,1024]{1,0:T(8,128)(2,1)} %up_ref.1, bf16[1024,512]{1,0:T(8,128)(2,1)} %down_ref.1), custom_call_target="tpu_custom_call" | custom-call | tf_op jit(solution)/shard_map/pallas_call | solution.py:254
  8.4 0.0 all-gather.3.cloned.1.call-update
  9.1 0.0 copy-done.2
  9.1 0.0 copy-done.1
  9.1 0.0 copy-done
  9.1 4.3 %shard_map.73 = (bf16[160,2048]{1,0:T(8,128)(2,1)}, bf16[160,2048]{1,0:T(8,128)(2,1)S(1)}, bf16[160,64]{1,0:T(8,128)(2,1)S(1)}) custom-call(s32[1]{0:T(128)S(6)} %copy.8.count_ref, s32[2,64]{1,0:T(2,128)S(1)} %bitcast.7, s32[2,64]{1,0:T(2,128)S(1)} %bitcast.8, bf16[64,4096]{1,0:T(8,128)(2,1)S(1)} %copy-done), custom_call_target="tpu_custom_call" | custom-call | flops 83886080 | bytes 1835008 | tf_op jit(solution)/shard_map/pallas_call | solution.py:243
  13.4 12.3 %all_to_all.20.refs_1_ = bf16[4,40,2048]{2,1,0:T(8,128)(2,1)S(1)} all-to-all(bf16[4,40,2048]{2,1,0:T(8,128)(2,1)S(1)} %bitcast.6), channel_id=1, replica_groups=mesh['y'=4,'c'=2,'x'=4,'z'=16] {'x'}, dimensions={0} | all-to-all | bytes 1310720 | tf_op jit(solution)/shard_map/all_to_all | solution.py:319
  25.7 3.5 %all-to-all-start = ((bf16[4,40,2048]{2,1,0:T(8,128)(2,1)}), bf16[4,40,2048]{2,1,0:T(8,128)(2,1)S(1)}, u32[]{:S(2)}, u32[]{:S(2)}) async-start(bf16[4,40,2048]{2,1,0:T(8,128)(2,1)} %bitcast.3), calls=%async_computation | async-start | bytes 1310720 | tf_op jit(solution)/shard_map/all_to_all | solution.py:318
  29.2 7.0 %collective-permute-start.1 = (bf16[4,40,2048]{2,1,0:T(8,128)(2,1)S(1)}, bf16[4,40,2048]{2,1,0:T(8,128)(2,1)S(1)}, u32[]{:S(2)}, u32[]{:S(2)}) collective-permute-start(bf16[4,40,2048]{2,1,0:T(8,128)(2,1)S(1)} %all_to_all.20.refs_1_), channel_id=1, source_target_pairs={{0,384},{128,0},{256,128},{384,256},{1,385},{129,1},{257,129},{385... | collective-permute-start | bytes 1966088 | tf_op jit(solution)/shard_map/ppermute | solution.py:310
  36.2 0.6 all-to-all-done.refs_0_
  36.8 6.7 %collective-permute-start.2 = (bf16[4,40,2048]{2,1,0:T(8,128)(2,1)S(1)}, bf16[4,40,2048]{2,1,0:T(8,128)(2,1)S(1)}, u32[]{:S(2)}, u32[]{:S(2)}) collective-permute-start(bf16[4,40,2048]{2,1,0:T(8,128)(2,1)S(1)} %all-to-all-done.refs_0_), channel_id=1, source_target_pairs={{0,128},{128,256},{256,384},{384,0},{1,129},{129,257},{257,385},{3... | collective-permute-start | bytes 1966088 | tf_op jit(solution)/shard_map/ppermute | solution.py:310
  43.5 3.2 %collective-permute-start.5 = (bf16[4,40,2048]{2,1,0:T(8,128)(2,1)S(1)}, bf16[4,40,2048]{2,1,0:T(8,128)(2,1)S(1)}, u32[]{:S(2)}, u32[]{:S(2)}) collective-permute-start(bf16[4,40,2048]{2,1,0:T(8,128)(2,1)S(1)} %all_to_all.20.refs_1_), channel_id=1, source_target_pairs={{0,128},{128,256},{256,384},{384,0},{1,129},{129,257},{257,385},{3... | collective-permute-start | bytes 1966088 | tf_op jit(solution)/shard_map/ppermute | solution.py:310
  46.7 3.3 %collective-permute-start = (bf16[4,40,2048]{2,1,0:T(8,128)(2,1)S(1)}, bf16[4,40,2048]{2,1,0:T(8,128)(2,1)}, u32[]{:S(2)}, u32[]{:S(2)}) collective-permute-start(bf16[4,40,2048]{2,1,0:T(8,128)(2,1)S(1)} %all-to-all-done.refs_0_), channel_id=1, source_target_pairs={{0,384},{128,0},{256,128},{384,256},{1,385},{129,1},{257,129},{385... | collective-permute-start | bytes 1966088 | tf_op jit(solution)/shard_map/ppermute | solution.py:310
  50.0 0.0 collective-permute-done.1.refs_3_
  50.0 3.7 %collective-permute-start.4 = (bf16[4,40,2048]{2,1,0:T(8,128)(2,1)S(1)}, bf16[4,40,2048]{2,1,0:T(8,128)(2,1)}, u32[]{:S(2)}, u32[]{:S(2)}) collective-permute-start(bf16[4,40,2048]{2,1,0:T(8,128)(2,1)S(1)} %collective-permute-done.1.refs_3_), channel_id=1, source_target_pairs={{0,384},{128,0},{256,128},{384,256},{1,385},{129,1},{257,129},{385... | collective-permute-start | bytes 1966088 | tf_op jit(solution)/shard_map/ppermute | solution.py:310
  53.7 2.6 %collective-permute-done.2.refs_6_ = bf16[4,40,2048]{2,1,0:T(8,128)(2,1)S(1)} collective-permute-done((bf16[4,40,2048]{2,1,0:T(8,128)(2,1)S(1)}, bf16[4,40,2048]{2,1,0:T(8,128)(2,1)S(1)}, u32[]{:S(2)}, u32[]{:S(2)}) %collective-permute-start.2) | collective-permute-done | bytes 655392 | tf_op jit(solution)/shard_map/ppermute | solution.py:310
  56.3 2.3 %collective-permute-start.3 = (bf16[4,40,2048]{2,1,0:T(8,128)(2,1)S(1)}, bf16[4,40,2048]{2,1,0:T(8,128)(2,1)}, u32[]{:S(2)}, u32[]{:S(2)}) collective-permute-start(bf16[4,40,2048]{2,1,0:T(8,128)(2,1)S(1)} %collective-permute-done.2.refs_6_), channel_id=1, source_target_pairs={{0,128},{128,256},{256,384},{384,0},{1,129},{129,257},{257,385},{3... | collective-permute-start | bytes 1966088 | tf_op jit(solution)/shard_map/ppermute | solution.py:310
  58.7 11.7 %collective-permute-done.5.refs_7_ = bf16[4,40,2048]{2,1,0:T(8,128)(2,1)S(1)} collective-permute-done((bf16[4,40,2048]{2,1,0:T(8,128)(2,1)S(1)}, bf16[4,40,2048]{2,1,0:T(8,128)(2,1)S(1)}, u32[]{:S(2)}, u32[]{:S(2)}) %collective-permute-start.5) | collective-permute-done | bytes 655392 | tf_op jit(solution)/shard_map/ppermute | solution.py:310
  70.3 0.0 collective-permute-done.refs_2_
  70.3 5.0 %collective-permute-done.4.refs_5_ = bf16[4,40,2048]{2,1,0:T(8,128)(2,1)} collective-permute-done((bf16[4,40,2048]{2,1,0:T(8,128)(2,1)S(1)}, bf16[4,40,2048]{2,1,0:T(8,128)(2,1)}, u32[]{:S(2)}, u32[]{:S(2)}) %collective-permute-start.4) | collective-permute-done | bytes 655392 | tf_op jit(solution)/shard_map/ppermute | solution.py:310
  75.3 9.1 %collective-permute-done.3.refs_4_ = bf16[4,40,2048]{2,1,0:T(8,128)(2,1)} collective-permute-done((bf16[4,40,2048]{2,1,0:T(8,128)(2,1)S(1)}, bf16[4,40,2048]{2,1,0:T(8,128)(2,1)}, u32[]{:S(2)}, u32[]{:S(2)}) %collective-permute-start.3) | collective-permute-done | bytes 655392 | tf_op jit(solution)/shard_map/ppermute | solution.py:310
  84.4 17.9 %all-gather.3.cloned.1.call-done = bf16[12288,512]{1,0:T(8,128)(2,1)} async-done(((bf16[384,512]{1,0:T(8,128)(2,1)}), bf16[12288,512]{1,0:T(8,128)(2,1)}) %all-gather.3.cloned.1.call-update) | async-done | bytes 12582928 | tf_op jit(solution)/shard_map/all_gather | solution.py:316
  102.3 5.6 %shard_map.75 = bf16[4,2,320,256]{3,2,1,0:T(8,128)(2,1)S(1)} custom-call(s32[1]{0:T(128)} %bitcast.2.place_ref, bf16[4,40,2048]{2,1,0:T(8,128)(2,1)S(1)} %all-to-all-done.refs_0_, bf16[4,40,2048]{2,1,0:T(8,128)(2,1)S(1)} %all_to_all.20.refs_1_, bf16[4,40,2048]{2,1,0:T(8,128)(2,1)} %collective-permute-done.refs_2_, ...), custom_call_target="tpu_custom_call" | custom-call | flops 2684354560 | bytes 13631488 | tf_op jit(solution)/shard_map/pallas_call | solution.py:265
  108.0 21.1 %all_to_all.21.hidden_ref = bf16[4,2,320,256]{3,2,1,0:T(8,128)(2,1)S(1)} all-to-all(bf16[4,2,320,256]{3,2,1,0:T(8,128)(2,1)S(1)} %shard_map.75), channel_id=1, replica_groups=mesh['y'=4,'c'=2,'x'=4,'z'=16] {'y'}, dimensions={0} | all-to-all | bytes 2621440 | tf_op jit(solution)/shard_map/all_to_all | solution.py:324
  129.1 3.3 %shard_map.76 = bf16[16,40,1024]{2,1,0:T(8,128)(2,1)S(1)} custom-call(bf16[4,2,320,256]{3,2,1,0:T(8,128)(2,1)S(1)} %all_to_all.21.hidden_ref, bf16[2,8,2,384,512]{4,3,2,1,0:T(8,128)(2,1)} %bitcast.10), custom_call_target="tpu_custom_call" | custom-call | flops 1342177280 | bytes 6815744 | tf_op jit(solution)/shard_map/pallas_call | solution.py:284
  132.4 21.8 %all_to_all.22.rows_ref = bf16[16,40,1024]{2,1,0:T(8,128)(2,1)S(1)} all-to-all(bf16[16,40,1024]{2,1,0:T(8,128)(2,1)S(1)} %shard_map.76), channel_id=1, replica_groups=mesh['y'=4,'c'=2,'x'=4,'z'=16] {'x','y'}, dimensions={0} | all-to-all | bytes 2621440 | tf_op jit(solution)/shard_map/all_to_all | solution.py:325
  154.2 1.1 shard_map.77
Async XLA Ops:
  6.5 2.5 %copy-start.2 = (s32[64,2]{0,1:T(2,128)S(1)}, s32[64,2]{0,1:T(2,128)}, u32[]{:S(2)}) copy-start(s32[64,2]{0,1:T(2,128)} %param.9) | copy-start | bytes 1540
  6.5 2.5 %copy-start.1 = (s32[64,2]{0,1:T(2,128)S(1)}, s32[64,2]{0,1:T(2,128)}, u32[]{:S(2)}) copy-start(s32[64,2]{0,1:T(2,128)} %param.8) | copy-start | bytes 1540
  6.5 2.6 %copy-start = (bf16[64,4096]{1,0:T(8,128)(2,1)S(1)}, bf16[64,4096]{1,0:T(8,128)(2,1)}, u32[]{:S(2)}) copy-start(bf16[64,4096]{1,0:T(8,128)(2,1)} %tokens_ref.1) | copy-start | bytes 1572868
  6.5 95.8 %all-gather.3.cloned.1.call-start = ((), (), s32[]{:S(2)}) async-start(), calls=%async_computation.4 | async-start | bytes 12976128 | tf_op jit(solution)/shard_map/all_gather | solution.py:316
  25.7 11.1 %all-to-all-start = ((bf16[4,40,2048]{2,1,0:T(8,128)(2,1)}), bf16[4,40,2048]{2,1,0:T(8,128)(2,1)S(1)}, u32[]{:S(2)}, u32[]{:S(2)}) async-start(bf16[4,40,2048]{2,1,0:T(8,128)(2,1)} %bitcast.3), calls=%async_computation | async-start | bytes 1310720 | tf_op jit(solution)/shard_map/all_to_all | solution.py:318
  29.2 20.8 %collective-permute-start.1 = (bf16[4,40,2048]{2,1,0:T(8,128)(2,1)S(1)}, bf16[4,40,2048]{2,1,0:T(8,128)(2,1)S(1)}, u32[]{:S(2)}, u32[]{:S(2)}) collective-permute-start(bf16[4,40,2048]{2,1,0:T(8,128)(2,1)S(1)} %all_to_all.20.refs_1_), channel_id=1, source_target_pairs={{0,384},{128,0},{256,128},{384,256},{1,385},{129,1},{257,129},{385... | collective-permute-start | bytes 1966088 | tf_op jit(solution)/shard_map/ppermute | solution.py:310
  36.8 19.6 %collective-permute-start.2 = (bf16[4,40,2048]{2,1,0:T(8,128)(2,1)S(1)}, bf16[4,40,2048]{2,1,0:T(8,128)(2,1)S(1)}, u32[]{:S(2)}, u32[]{:S(2)}) collective-permute-start(bf16[4,40,2048]{2,1,0:T(8,128)(2,1)S(1)} %all-to-all-done.refs_0_), channel_id=1, source_target_pairs={{0,128},{128,256},{256,384},{384,0},{1,129},{129,257},{257,385},{3... | collective-permute-start | bytes 1966088 | tf_op jit(solution)/shard_map/ppermute | solution.py:310
  43.5 26.9 %collective-permute-start.5 = (bf16[4,40,2048]{2,1,0:T(8,128)(2,1)S(1)}, bf16[4,40,2048]{2,1,0:T(8,128)(2,1)S(1)}, u32[]{:S(2)}, u32[]{:S(2)}) collective-permute-start(bf16[4,40,2048]{2,1,0:T(8,128)(2,1)S(1)} %all_to_all.20.refs_1_), channel_id=1, source_target_pairs={{0,128},{128,256},{256,384},{384,0},{1,129},{129,257},{257,385},{3... | collective-permute-start | bytes 1966088 | tf_op jit(solution)/shard_map/ppermute | solution.py:310
  46.7 23.6 %collective-permute-start = (bf16[4,40,2048]{2,1,0:T(8,128)(2,1)S(1)}, bf16[4,40,2048]{2,1,0:T(8,128)(2,1)}, u32[]{:S(2)}, u32[]{:S(2)}) collective-permute-start(bf16[4,40,2048]{2,1,0:T(8,128)(2,1)S(1)} %all-to-all-done.refs_0_), channel_id=1, source_target_pairs={{0,384},{128,0},{256,128},{384,256},{1,385},{129,1},{257,129},{385... | collective-permute-start | bytes 1966088 | tf_op jit(solution)/shard_map/ppermute | solution.py:310
  50.0 25.4 %collective-permute-start.4 = (bf16[4,40,2048]{2,1,0:T(8,128)(2,1)S(1)}, bf16[4,40,2048]{2,1,0:T(8,128)(2,1)}, u32[]{:S(2)}, u32[]{:S(2)}) collective-permute-start(bf16[4,40,2048]{2,1,0:T(8,128)(2,1)S(1)} %collective-permute-done.1.refs_3_), channel_id=1, source_target_pairs={{0,384},{128,0},{256,128},{384,256},{1,385},{129,1},{257,129},{385... | collective-permute-start | bytes 1966088 | tf_op jit(solution)/shard_map/ppermute | solution.py:310
  56.3 28.1 %collective-permute-start.3 = (bf16[4,40,2048]{2,1,0:T(8,128)(2,1)S(1)}, bf16[4,40,2048]{2,1,0:T(8,128)(2,1)}, u32[]{:S(2)}, u32[]{:S(2)}) collective-permute-start(bf16[4,40,2048]{2,1,0:T(8,128)(2,1)S(1)} %collective-permute-done.2.refs_6_), channel_id=1, source_target_pairs={{0,128},{128,256},{256,384},{384,0},{1,129},{129,257},{257,385},{3... | collective-permute-start | bytes 1966088 | tf_op jit(solution)/shard_map/ppermute | solution.py:310
Sparse Core Ops, SparseCore 0:
  9.5 92.7 all-gather.2

commit v14 on v13

--- a/solution.py
+++ b/solution.py
@@ -154,8 +154,8 @@
 
 
 def hidden_kernel(place_ref, *refs):
-    rows, weights_ref, out_ref, held, here, sems, row_sems = refs[: 2 * Y], *refs[2 * Y : 2 * Y + 6]
-    sums = refs[2 * Y + 6 :]
+    rows, weights_ref, out_ref, down_ref, held, here, sems, row_sems = refs[: 2 * Y], *refs[2 * Y : 2 * Y + 7]
+    sums = refs[2 * Y + 7 :]
     groups = MEMBERS // DEEP
     copies = [
         pltpu.make_async_copy(
@@ -181,6 +181,9 @@
         copy.wait()
         if i + 3 < len(copies):
             copies[i + 3].start()
+        elif i + 3 == len(copies):
+            down_copy = pltpu.make_async_copy(weights_ref.at[:, :WIDE, :, HALF:], down_ref, sems.at[len(copies)])
+            down_copy.start()
         for expert, total in enumerate(sums):
             block = jnp.concatenate([b[expert][part] for part in range(2) for b in blocks], axis=0)
             weights = held[i, expert].reshape(DEEP * HALF, 2 * FQ)
@@ -195,22 +198,24 @@
                 block = hidden[start + offset * length : start + (offset + 1) * length]
                 for copy in range(Y):
                     out_ref[copy, expert, to] = block
-
-
-def down_kernel(hidden_ref, weights_ref, out_ref, held, sems):
+    down_copy.wait()
+
+
+def down_kernel(hidden_ref, piece_ref, weights_ref, out_ref, held, sems):
     starts = range(0, MEMBERS, WIDE)
     copies = [
         pltpu.make_async_copy(weights_ref.at[:, start : start + WIDE, :, HALF:], held.at[i], sems.at[i])
-        for i, start in enumerate(starts)
+        for i, start in enumerate(starts[1:])
     ]
     for copy in copies:
         copy.start()
     rows = [jnp.concatenate([hidden_ref[q, expert] for q in range(Y)], axis=1) for expert in range(2)]
 
     def result(i, expert):
+        piece = held.at[i - 1] if i else piece_ref
         weights = jnp.concatenate(
             [
-                jnp.concatenate([held[i, expert, m, half, :, q * 128 : (q + 1) * 128] for m in range(WIDE)], axis=1)
+                jnp.concatenate([piece[expert, m, half, :, q * 128 : (q + 1) * 128] for m in range(WIDE)], axis=1)
                 for q in range(Y)
                 for half in range(C)
             ],
@@ -219,7 +224,8 @@
         return jnp.dot(rows[expert], weights, preferred_element_type=jnp.float32)
 
     for i, start in enumerate(starts):
-        copies[i].wait()
+        if i:
+            copies[i - 1].wait()
         joined = join_rows(result(i, 0), result(i, 1))
         for x in range(X):
             for y in range(Y):
@@ -264,13 +270,13 @@
     pieces = C * MEMBERS // DEEP
     return pl.pallas_call(
         hidden_kernel,
-        out_shape=shape((Y, 2, ROWS // 2, FQ)),
+        out_shape=[shape((Y, 2, ROWS // 2, FQ)), shape((2, WIDE, C, 128, SHARD))],
         in_specs=[SCALAR, *[ANY] * (2 * Y), ANY],
-        out_specs=WHOLE,
+        out_specs=[WHOLE] * 2,
         scratch_shapes=[
             pltpu.VMEM((pieces, 2, DEEP, HALF, 2 * FQ), jnp.bfloat16),
             pltpu.VMEM((2 * Y, X, SLOTS, D // 2), jnp.bfloat16),
-            pltpu.SemaphoreType.DMA((pieces,)),
+            pltpu.SemaphoreType.DMA((pieces + 1,)),
             pltpu.SemaphoreType.DMA((2 * Y,)),
             *[pltpu.VMEM((SRC * SLOTS // 2, 2 * FQ), jnp.float32)] * 2,
         ],
@@ -279,12 +285,12 @@
     )(place, *rows, weights)
 
 
-def down_rows(hidden, weights):
-    pieces = MEMBERS // WIDE
+def down_rows(hidden, piece, weights):
+    pieces = MEMBERS // WIDE - 1
     return pl.pallas_call(
         down_kernel,
         out_shape=shape((SRC, SLOTS, MEMBERS * 128)),
-        in_specs=[WHOLE, ANY],
+        in_specs=[WHOLE, WHOLE, ANY],
         out_specs=WHOLE,
         scratch_shapes=[
             pltpu.VMEM((pieces, 2, WIDE, C, 128, SHARD), jnp.bfloat16),
@@ -292,7 +298,7 @@
         ],
         compiler_params=params(50),
         cost_estimate=pl.CostEstimate(flops=2 * ROWS * F * F, bytes_accessed=4 * ROWS * F + 4 * F * F, transcendentals=0),
-    )(hidden, weights)
+    )(hidden, piece, weights)
 
 
 def mix(shares, rows):
@@ -321,8 +327,9 @@
     second_3, first_1 = shift(second, 1), shift(first, -1)
     first_2, second_2 = shift(first_3, 1), shift(second_1, -1)
     rows = (first, second, first_1, second_1, first_2, second_2, first_3, second_3)
-    hidden = lax.all_to_all(hidden_rows(place, rows, weights), "y", 0, 0, tiled=True)
-    result = lax.all_to_all(down_rows(hidden, weights), ("x", "y"), 0, 0, tiled=True)
+    hidden, piece = hidden_rows(place, rows, weights)
+    hidden = lax.all_to_all(hidden, "y", 0, 0, tiled=True)
+    result = lax.all_to_all(down_rows(hidden, piece, weights), ("x", "y"), 0, 0, tiled=True)
     return mix(shares, result)
 
 

time: 163 us -> 163 us (level)
  no operation moved by 1% of the time
where the time goes in v14:
time: 163 us; the launch traced here: 162 us
  blocking collectives  55.2 us (34%)
  waiting for transfers between devices  46.9 us (29%)
  starting transfers between devices  29.7 us (18%)
  Pallas kernels  15.7 us (10%)
  between operations  14.2 us (9%)
    ppermute x6, waiting for transfers between devices, shift(): return lax.ppermute(block, 'y', [(i, (i + by) % Y) for i in range(Y)])  28.4 us
    ppermute x6, starting transfers between devices, shift(): return lax.ppermute(block, 'y', [(i, (i + by) % Y) for i in range(Y)])  26.2 us
    all_to_all x1, blocking collectives, local(): lax.all_to_all(down_rows(hidden, piece, weights), ('x', 'y'), 0, 0, tiled...  21.8 us
    all_to_all x1, blocking collectives, local(): hidden = lax.all_to_all(hidden, 'y', 0, 0, tiled=True)  21.1 us
    all_gather x1, waiting for transfers between devices, local(): lax.all_gather(weights, ('z', 'c'))  17.9 us
    all_to_all x1, blocking collectives, local(): lax.all_to_all(second.reshape(X, SLOTS, D // 2), 'x', 0, 0, tiled=True)  12.3 us
    pallas_call x1, Pallas kernels, hidden_rows(): pl.pallas_call(hidden_kernel, out_shape=[shape((Y, 2, ROWS // 2, FQ)), sh...  5.64 us
    pallas_call x1, Pallas kernels, encode(): pl.pallas_call(encode_kernel, out_shape=[*[shape((ALL_SLOTS, D // 2))] *...  4.31 us
  transfers between devices with their start and end apart: 8, of which 6 were waited for; matrix products, arithmetic and copies ran while one was open for 0% of the time, Pallas kernels for 3%

profile of v14, /device:TPU:1, one launch (start us, length us, event | category | flops | bytes accessed | tf_op | source)
XLA Modules:
  0.0 161.7 jit_solution(6711838777263324869)
XLA Ops:
  6.5 0.0 copy-start.2
  6.5 0.0 copy-start.1
  6.5 0.0 copy-start
  6.5 0.0 all-gather.3.cloned.1.call-start
  6.5 1.8 %shard_map.74 = bf16[384,512]{1,0:T(8,128)(2,1)} custom-call(bf16[512,1024]{1,0:T(8,128)(2,1)} %gate_ref.1, bf16[512,1024]{1,0:T(8,128)(2,1)} %up_ref.1, bf16[1024,512]{1,0:T(8,128)(2,1)} %down_ref.1), custom_call_target="tpu_custom_call" | custom-call | tf_op jit(solution)/shard_map/pallas_call | solution.py:260
  8.4 0.0 all-gather.3.cloned.1.call-update
  9.1 0.0 copy-done.2
  9.1 0.0 copy-done.1
  9.1 0.0 copy-done
  9.1 4.3 %shard_map.73 = (bf16[160,2048]{1,0:T(8,128)(2,1)}, bf16[160,2048]{1,0:T(8,128)(2,1)S(1)}, bf16[160,64]{1,0:T(8,128)(2,1)S(1)}) custom-call(s32[1]{0:T(128)S(6)} %copy.8.count_ref, s32[2,64]{1,0:T(2,128)S(1)} %bitcast.7, s32[2,64]{1,0:T(2,128)S(1)} %bitcast.8, bf16[64,4096]{1,0:T(8,128)(2,1)S(1)} %copy-done), custom_call_target="tpu_custom_call" | custom-call | flops 83886080 | bytes 1835008 | tf_op jit(solution)/shard_map/pallas_call | solution.py:249
  13.4 12.3 %all_to_all.20.refs_1_ = bf16[4,40,2048]{2,1,0:T(8,128)(2,1)S(1)} all-to-all(bf16[4,40,2048]{2,1,0:T(8,128)(2,1)S(1)} %bitcast.6), channel_id=1, replica_groups=mesh['y'=4,'c'=2,'x'=4,'z'=16] {'x'}, dimensions={0} | all-to-all | bytes 1310720 | tf_op jit(solution)/shard_map/all_to_all | solution.py:325
  25.7 3.5 %all-to-all-start = ((bf16[4,40,2048]{2,1,0:T(8,128)(2,1)}), bf16[4,40,2048]{2,1,0:T(8,128)(2,1)S(1)}, u32[]{:S(2)}, u32[]{:S(2)}) async-start(bf16[4,40,2048]{2,1,0:T(8,128)(2,1)} %bitcast.3), calls=%async_computation | async-start | bytes 1310720 | tf_op jit(solution)/shard_map/all_to_all | solution.py:324
  29.2 7.0 %collective-permute-start.1 = (bf16[4,40,2048]{2,1,0:T(8,128)(2,1)S(1)}, bf16[4,40,2048]{2,1,0:T(8,128)(2,1)S(1)}, u32[]{:S(2)}, u32[]{:S(2)}) collective-permute-start(bf16[4,40,2048]{2,1,0:T(8,128)(2,1)S(1)} %all_to_all.20.refs_1_), channel_id=1, source_target_pairs={{0,384},{128,0},{256,128},{384,256},{1,385},{129,1},{257,129},{385... | collective-permute-start | bytes 1966088 | tf_op jit(solution)/shard_map/ppermute | solution.py:316
  36.2 0.6 all-to-all-done.refs_0_
  36.8 6.7 %collective-permute-start.2 = (bf16[4,40,2048]{2,1,0:T(8,128)(2,1)S(1)}, bf16[4,40,2048]{2,1,0:T(8,128)(2,1)S(1)}, u32[]{:S(2)}, u32[]{:S(2)}) collective-permute-start(bf16[4,40,2048]{2,1,0:T(8,128)(2,1)S(1)} %all-to-all-done.refs_0_), channel_id=1, source_target_pairs={{0,128},{128,256},{256,384},{384,0},{1,129},{129,257},{257,385},{3... | collective-permute-start | bytes 1966088 | tf_op jit(solution)/shard_map/ppermute | solution.py:316
  43.5 3.2 %collective-permute-start.5 = (bf16[4,40,2048]{2,1,0:T(8,128)(2,1)S(1)}, bf16[4,40,2048]{2,1,0:T(8,128)(2,1)S(1)}, u32[]{:S(2)}, u32[]{:S(2)}) collective-permute-start(bf16[4,40,2048]{2,1,0:T(8,128)(2,1)S(1)} %all_to_all.20.refs_1_), channel_id=1, source_target_pairs={{0,128},{128,256},{256,384},{384,0},{1,129},{129,257},{257,385},{3... | collective-permute-start | bytes 1966088 | tf_op jit(solution)/shard_map/ppermute | solution.py:316
  46.7 3.3 %collective-permute-start = (bf16[4,40,2048]{2,1,0:T(8,128)(2,1)S(1)}, bf16[4,40,2048]{2,1,0:T(8,128)(2,1)}, u32[]{:S(2)}, u32[]{:S(2)}) collective-permute-start(bf16[4,40,2048]{2,1,0:T(8,128)(2,1)S(1)} %all-to-all-done.refs_0_), channel_id=1, source_target_pairs={{0,384},{128,0},{256,128},{384,256},{1,385},{129,1},{257,129},{385... | collective-permute-start | bytes 1966088 | tf_op jit(solution)/shard_map/ppermute | solution.py:316
  50.0 0.0 collective-permute-done.1.refs_3_
  50.0 3.7 %collective-permute-start.4 = (bf16[4,40,2048]{2,1,0:T(8,128)(2,1)S(1)}, bf16[4,40,2048]{2,1,0:T(8,128)(2,1)}, u32[]{:S(2)}, u32[]{:S(2)}) collective-permute-start(bf16[4,40,2048]{2,1,0:T(8,128)(2,1)S(1)} %collective-permute-done.1.refs_3_), channel_id=1, source_target_pairs={{0,384},{128,0},{256,128},{384,256},{1,385},{129,1},{257,129},{385... | collective-permute-start | bytes 1966088 | tf_op jit(solution)/shard_map/ppermute | solution.py:316
  53.7 2.6 %collective-permute-done.2.refs_6_ = bf16[4,40,2048]{2,1,0:T(8,128)(2,1)S(1)} collective-permute-done((bf16[4,40,2048]{2,1,0:T(8,128)(2,1)S(1)}, bf16[4,40,2048]{2,1,0:T(8,128)(2,1)S(1)}, u32[]{:S(2)}, u32[]{:S(2)}) %collective-permute-start.2) | collective-permute-done | bytes 655392 | tf_op jit(solution)/shard_map/ppermute | solution.py:316
  56.3 2.3 %collective-permute-start.3 = (bf16[4,40,2048]{2,1,0:T(8,128)(2,1)S(1)}, bf16[4,40,2048]{2,1,0:T(8,128)(2,1)}, u32[]{:S(2)}, u32[]{:S(2)}) collective-permute-start(bf16[4,40,2048]{2,1,0:T(8,128)(2,1)S(1)} %collective-permute-done.2.refs_6_), channel_id=1, source_target_pairs={{0,128},{128,256},{256,384},{384,0},{1,129},{129,257},{257,385},{3... | collective-permute-start | bytes 1966088 | tf_op jit(solution)/shard_map/ppermute | solution.py:316
  58.6 11.7 %collective-permute-done.5.refs_7_ = bf16[4,40,2048]{2,1,0:T(8,128)(2,1)S(1)} collective-permute-done((bf16[4,40,2048]{2,1,0:T(8,128)(2,1)S(1)}, bf16[4,40,2048]{2,1,0:T(8,128)(2,1)S(1)}, u32[]{:S(2)}, u32[]{:S(2)}) %collective-permute-start.5) | collective-permute-done | bytes 655392 | tf_op jit(solution)/shard_map/ppermute | solution.py:316
  70.3 0.0 collective-permute-done.refs_2_
  70.3 5.0 %collective-permute-done.4.refs_5_ = bf16[4,40,2048]{2,1,0:T(8,128)(2,1)} collective-permute-done((bf16[4,40,2048]{2,1,0:T(8,128)(2,1)S(1)}, bf16[4,40,2048]{2,1,0:T(8,128)(2,1)}, u32[]{:S(2)}, u32[]{:S(2)}) %collective-permute-start.4) | collective-permute-done | bytes 655392 | tf_op jit(solution)/shard_map/ppermute | solution.py:316
  75.3 9.1 %collective-permute-done.3.refs_4_ = bf16[4,40,2048]{2,1,0:T(8,128)(2,1)} collective-permute-done((bf16[4,40,2048]{2,1,0:T(8,128)(2,1)S(1)}, bf16[4,40,2048]{2,1,0:T(8,128)(2,1)}, u32[]{:S(2)}, u32[]{:S(2)}) %collective-permute-start.3) | collective-permute-done | bytes 655392 | tf_op jit(solution)/shard_map/ppermute | solution.py:316
  84.4 17.9 %all-gather.3.cloned.1.call-done = bf16[12288,512]{1,0:T(8,128)(2,1)} async-done(((bf16[384,512]{1,0:T(8,128)(2,1)}), bf16[12288,512]{1,0:T(8,128)(2,1)}) %all-gather.3.cloned.1.call-update) | async-done | bytes 12582928 | tf_op jit(solution)/shard_map/all_gather | solution.py:322
  102.3 5.6 %shard_map.75 = (bf16[4,2,320,256]{3,2,1,0:T(8,128)(2,1)S(1)}, bf16[2,2,2,128,512]{4,3,2,1,0:T(8,128)(2,1)S(1)}) custom-call(s32[1]{0:T(128)} %bitcast.2.place_ref, bf16[4,40,2048]{2,1,0:T(8,128)(2,1)S(1)} %all-to-all-done.refs_0_, bf16[4,40,2048]{2,1,0:T(8,128)(2,1)S(1)} %all_to_all.20.refs_1_, bf16[4,40,2048]{2,1,0:T(8,128)(2,1)} %collective-permute-done.refs_2_, ...), custom_call_target="tpu_custom_call" | custom-call | flops 2684354560 | bytes 13631488 | tf_op jit(solution)/shard_map/pallas_call | solution.py:271
  108.0 21.1 %all_to_all.21.hidden_ref = bf16[4,2,320,256]{3,2,1,0:T(8,128)(2,1)S(1)} all-to-all(bf16[4,2,320,256]{3,2,1,0:T(8,128)(2,1)S(1)} %get-tuple-element.13), channel_id=1, replica_groups=mesh['y'=4,'c'=2,'x'=4,'z'=16] {'y'}, dimensions={0} | all-to-all | bytes 2621440 | tf_op jit(solution)/shard_map/all_to_all | solution.py:331
  129.1 2.8 %shard_map.76 = bf16[16,40,1024]{2,1,0:T(8,128)(2,1)S(1)} custom-call(bf16[4,2,320,256]{3,2,1,0:T(8,128)(2,1)S(1)} %all_to_all.21.hidden_ref, bf16[2,2,2,128,512]{4,3,2,1,0:T(8,128)(2,1)S(1)} %get-tuple-element.14.piece_ref, bf16[2,8,2,384,512]{4,3,2,1,0:T(8,128)(2,1)} %bitcast.10), custom_call_target="tpu_custom_call" | custom-call | flops 1342177280 | bytes 6815744 | tf_op jit(solution)/shard_map/pallas_call | solution.py:290
  131.9 21.8 %all_to_all.22.rows_ref = bf16[16,40,1024]{2,1,0:T(8,128)(2,1)S(1)} all-to-all(bf16[16,40,1024]{2,1,0:T(8,128)(2,1)S(1)} %shard_map.76), channel_id=1, replica_groups=mesh['y'=4,'c'=2,'x'=4,'z'=16] {'x','y'}, dimensions={0} | all-to-all | bytes 2621440 | tf_op jit(solution)/shard_map/all_to_all | solution.py:332
  153.7 1.1 shard_map.77
Async XLA Ops:
  6.5 2.5 %copy-start.2 = (s32[64,2]{0,1:T(2,128)S(1)}, s32[64,2]{0,1:T(2,128)}, u32[]{:S(2)}) copy-start(s32[64,2]{0,1:T(2,128)} %param.9) | copy-start | bytes 1540
  6.5 2.5 %copy-start.1 = (s32[64,2]{0,1:T(2,128)S(1)}, s32[64,2]{0,1:T(2,128)}, u32[]{:S(2)}) copy-start(s32[64,2]{0,1:T(2,128)} %param.8) | copy-start | bytes 1540
  6.5 2.6 %copy-start = (bf16[64,4096]{1,0:T(8,128)(2,1)S(1)}, bf16[64,4096]{1,0:T(8,128)(2,1)}, u32[]{:S(2)}) copy-start(bf16[64,4096]{1,0:T(8,128)(2,1)} %tokens_ref.1) | copy-start | bytes 1572868
  6.5 95.8 %all-gather.3.cloned.1.call-start = ((), (), s32[]{:S(2)}) async-start(), calls=%async_computation.4 | async-start | bytes 12976128 | tf_op jit(solution)/shard_map/all_gather | solution.py:322
  25.7 11.1 %all-to-all-start = ((bf16[4,40,2048]{2,1,0:T(8,128)(2,1)}), bf16[4,40,2048]{2,1,0:T(8,128)(2,1)S(1)}, u32[]{:S(2)}, u32[]{:S(2)}) async-start(bf16[4,40,2048]{2,1,0:T(8,128)(2,1)} %bitcast.3), calls=%async_computation | async-start | bytes 1310720 | tf_op jit(solution)/shard_map/all_to_all | solution.py:324
  29.2 20.8 %collective-permute-start.1 = (bf16[4,40,2048]{2,1,0:T(8,128)(2,1)S(1)}, bf16[4,40,2048]{2,1,0:T(8,128)(2,1)S(1)}, u32[]{:S(2)}, u32[]{:S(2)}) collective-permute-start(bf16[4,40,2048]{2,1,0:T(8,128)(2,1)S(1)} %all_to_all.20.refs_1_), channel_id=1, source_target_pairs={{0,384},{128,0},{256,128},{384,256},{1,385},{129,1},{257,129},{385... | collective-permute-start | bytes 1966088 | tf_op jit(solution)/shard_map/ppermute | solution.py:316
  36.8 19.6 %collective-permute-start.2 = (bf16[4,40,2048]{2,1,0:T(8,128)(2,1)S(1)}, bf16[4,40,2048]{2,1,0:T(8,128)(2,1)S(1)}, u32[]{:S(2)}, u32[]{:S(2)}) collective-permute-start(bf16[4,40,2048]{2,1,0:T(8,128)(2,1)S(1)} %all-to-all-done.refs_0_), channel_id=1, source_target_pairs={{0,128},{128,256},{256,384},{384,0},{1,129},{129,257},{257,385},{3... | collective-permute-start | bytes 1966088 | tf_op jit(solution)/shard_map/ppermute | solution.py:316
  43.5 26.9 %collective-permute-start.5 = (bf16[4,40,2048]{2,1,0:T(8,128)(2,1)S(1)}, bf16[4,40,2048]{2,1,0:T(8,128)(2,1)S(1)}, u32[]{:S(2)}, u32[]{:S(2)}) collective-permute-start(bf16[4,40,2048]{2,1,0:T(8,128)(2,1)S(1)} %all_to_all.20.refs_1_), channel_id=1, source_target_pairs={{0,128},{128,256},{256,384},{384,0},{1,129},{129,257},{257,385},{3... | collective-permute-start | bytes 1966088 | tf_op jit(solution)/shard_map/ppermute | solution.py:316
  46.7 23.6 %collective-permute-start = (bf16[4,40,2048]{2,1,0:T(8,128)(2,1)S(1)}, bf16[4,40,2048]{2,1,0:T(8,128)(2,1)}, u32[]{:S(2)}, u32[]{:S(2)}) collective-permute-start(bf16[4,40,2048]{2,1,0:T(8,128)(2,1)S(1)} %all-to-all-done.refs_0_), channel_id=1, source_target_pairs={{0,384},{128,0},{256,128},{384,256},{1,385},{129,1},{257,129},{385... | collective-permute-start | bytes 1966088 | tf_op jit(solution)/shard_map/ppermute | solution.py:316
  50.0 25.4 %collective-permute-start.4 = (bf16[4,40,2048]{2,1,0:T(8,128)(2,1)S(1)}, bf16[4,40,2048]{2,1,0:T(8,128)(2,1)}, u32[]{:S(2)}, u32[]{:S(2)}) collective-permute-start(bf16[4,40,2048]{2,1,0:T(8,128)(2,1)S(1)} %collective-permute-done.1.refs_3_), channel_id=1, source_target_pairs={{0,384},{128,0},{256,128},{384,256},{1,385},{129,1},{257,129},{385... | collective-permute-start | bytes 1966088 | tf_op jit(solution)/shard_map/ppermute | solution.py:316
  56.3 28.1 %collective-permute-start.3 = (bf16[4,40,2048]{2,1,0:T(8,128)(2,1)S(1)}, bf16[4,40,2048]{2,1,0:T(8,128)(2,1)}, u32[]{:S(2)}, u32[]{:S(2)}) collective-permute-start(bf16[4,40,2048]{2,1,0:T(8,128)(2,1)S(1)} %collective-permute-done.2.refs_6_), channel_id=1, source_target_pairs={{0,128},{128,256},{256,384},{384,0},{1,129},{129,257},{257,385},{3... | collective-permute-start | bytes 1966088 | tf_op jit(solution)/shard_map/ppermute | solution.py:316
Sparse Core Ops, SparseCore 0:
  9.5 92.7 all-gather.2

commit v15 on v14

--- a/solution.py
+++ b/solution.py
@@ -21,7 +21,7 @@
 FQ = F // Y
 HALF = SHARD // 2
 DEEP = 2
-WIDE = 2
+WIDE = 4
 
 
 def slot_at(at):

time: 163 us -> 164 us (level)
  no operation moved by 1% of the time
where the time goes in v15:
time: 164 us; the launch traced here: 163 us
  blocking collectives  55.2 us (34%)
  waiting for transfers between devices  46.9 us (29%)
  starting transfers between devices  29.7 us (18%)
  Pallas kernels  17.2 us (10%)
  between operations  14.2 us (9%)
    ppermute x6, waiting for transfers between devices, shift(): return lax.ppermute(block, 'y', [(i, (i + by) % Y) for i in range(Y)])  28.4 us
    ppermute x6, starting transfers between devices, shift(): return lax.ppermute(block, 'y', [(i, (i + by) % Y) for i in range(Y)])  26.2 us
    all_to_all x1, blocking collectives, local(): lax.all_to_all(down_rows(hidden, piece, weights), ('x', 'y'), 0, 0, tiled...  21.8 us
    all_to_all x1, blocking collectives, local(): hidden = lax.all_to_all(hidden, 'y', 0, 0, tiled=True)  21.1 us
    all_gather x1, waiting for transfers between devices, local(): lax.all_gather(weights, ('z', 'c'))  17.9 us
    all_to_all x1, blocking collectives, local(): lax.all_to_all(second.reshape(X, SLOTS, D // 2), 'x', 0, 0, tiled=True)  12.3 us
    pallas_call x1, Pallas kernels, hidden_rows(): pl.pallas_call(hidden_kernel, out_shape=[shape((Y, 2, ROWS // 2, FQ)), sh...  5.93 us
    pallas_call x1, Pallas kernels, encode(): pl.pallas_call(encode_kernel, out_shape=[*[shape((ALL_SLOTS, D // 2))] *...  4.3 us
  transfers between devices with their start and end apart: 8, of which 6 were waited for; matrix products, arithmetic and copies ran while one was open for 0% of the time, Pallas kernels for 3%

profile of v15, /device:TPU:1, one launch (start us, length us, event | category | flops | bytes accessed | tf_op | source)
XLA Modules:
  0.0 163.3 jit_solution(13765735097781681834)
XLA Ops:
  6.5 0.0 copy-start.3
  6.5 0.0 copy-start.2
  6.5 0.0 copy-start.1
  6.5 0.0 all-gather.3.cloned.1.call-start
  6.5 1.8 %shard_map.74 = bf16[384,512]{1,0:T(8,128)(2,1)} custom-call(bf16[512,1024]{1,0:T(8,128)(2,1)} %gate_ref.1, bf16[512,1024]{1,0:T(8,128)(2,1)} %up_ref.1, bf16[1024,512]{1,0:T(8,128)(2,1)} %down_ref.1), custom_call_target="tpu_custom_call" | custom-call | tf_op jit(solution)/shard_map/pallas_call | solution.py:260
  8.4 0.0 all-gather.3.cloned.1.call-update
  9.1 0.0 copy-done.3
  9.1 0.0 copy-done.2
  9.1 0.0 copy-done.1
  9.1 4.3 %shard_map.73 = (bf16[160,2048]{1,0:T(8,128)(2,1)}, bf16[160,2048]{1,0:T(8,128)(2,1)S(1)}, bf16[160,64]{1,0:T(8,128)(2,1)S(1)}) custom-call(s32[1]{0:T(128)S(6)} %copy.8.count_ref, s32[2,64]{1,0:T(2,128)S(1)} %bitcast.7, s32[2,64]{1,0:T(2,128)S(1)} %bitcast.8, bf16[64,4096]{1,0:T(8,128)(2,1)S(1)} %copy-done.1), custom_call_target="tpu_custom_call" | custom-call | flops 83886080 | bytes 1835008 | tf_op jit(solution)/shard_map/pallas_call | solution.py:249
  13.4 12.3 %all_to_all.20.refs_1_ = bf16[4,40,2048]{2,1,0:T(8,128)(2,1)S(1)} all-to-all(bf16[4,40,2048]{2,1,0:T(8,128)(2,1)S(1)} %bitcast.6), channel_id=1, replica_groups=mesh['y'=4,'c'=2,'x'=4,'z'=16] {'x'}, dimensions={0} | all-to-all | bytes 1310720 | tf_op jit(solution)/shard_map/all_to_all | solution.py:325
  25.7 3.5 %all-to-all-start = ((bf16[4,40,2048]{2,1,0:T(8,128)(2,1)}), bf16[4,40,2048]{2,1,0:T(8,128)(2,1)S(1)}, u32[]{:S(2)}, u32[]{:S(2)}) async-start(bf16[4,40,2048]{2,1,0:T(8,128)(2,1)} %bitcast.3), calls=%async_computation | async-start | bytes 1310720 | tf_op jit(solution)/shard_map/all_to_all | solution.py:324
  29.2 7.0 %collective-permute-start.1 = (bf16[4,40,2048]{2,1,0:T(8,128)(2,1)S(1)}, bf16[4,40,2048]{2,1,0:T(8,128)(2,1)S(1)}, u32[]{:S(2)}, u32[]{:S(2)}) collective-permute-start(bf16[4,40,2048]{2,1,0:T(8,128)(2,1)S(1)} %all_to_all.20.refs_1_), channel_id=1, source_target_pairs={{0,384},{128,0},{256,128},{384,256},{1,385},{129,1},{257,129},{385... | collective-permute-start | bytes 1966088 | tf_op jit(solution)/shard_map/ppermute | solution.py:316
  36.2 0.6 all-to-all-done.refs_0_
  36.8 6.7 %collective-permute-start.2 = (bf16[4,40,2048]{2,1,0:T(8,128)(2,1)S(1)}, bf16[4,40,2048]{2,1,0:T(8,128)(2,1)S(1)}, u32[]{:S(2)}, u32[]{:S(2)}) collective-permute-start(bf16[4,40,2048]{2,1,0:T(8,128)(2,1)S(1)} %all-to-all-done.refs_0_), channel_id=1, source_target_pairs={{0,128},{128,256},{256,384},{384,0},{1,129},{129,257},{257,385},{3... | collective-permute-start | bytes 1966088 | tf_op jit(solution)/shard_map/ppermute | solution.py:316
  43.5 3.2 %collective-permute-start.5 = (bf16[4,40,2048]{2,1,0:T(8,128)(2,1)S(1)}, bf16[4,40,2048]{2,1,0:T(8,128)(2,1)S(1)}, u32[]{:S(2)}, u32[]{:S(2)}) collective-permute-start(bf16[4,40,2048]{2,1,0:T(8,128)(2,1)S(1)} %all_to_all.20.refs_1_), channel_id=1, source_target_pairs={{0,128},{128,256},{256,384},{384,0},{1,129},{129,257},{257,385},{3... | collective-permute-start | bytes 1966088 | tf_op jit(solution)/shard_map/ppermute | solution.py:316
  46.7 3.3 %collective-permute-start = (bf16[4,40,2048]{2,1,0:T(8,128)(2,1)S(1)}, bf16[4,40,2048]{2,1,0:T(8,128)(2,1)}, u32[]{:S(2)}, u32[]{:S(2)}) collective-permute-start(bf16[4,40,2048]{2,1,0:T(8,128)(2,1)S(1)} %all-to-all-done.refs_0_), channel_id=1, source_target_pairs={{0,384},{128,0},{256,128},{384,256},{1,385},{129,1},{257,129},{385... | collective-permute-start | bytes 1966088 | tf_op jit(solution)/shard_map/ppermute | solution.py:316
  50.0 0.0 collective-permute-done.1.refs_3_
  50.0 3.7 %collective-permute-start.4 = (bf16[4,40,2048]{2,1,0:T(8,128)(2,1)S(1)}, bf16[4,40,2048]{2,1,0:T(8,128)(2,1)}, u32[]{:S(2)}, u32[]{:S(2)}) collective-permute-start(bf16[4,40,2048]{2,1,0:T(8,128)(2,1)S(1)} %collective-permute-done.1.refs_3_), channel_id=1, source_target_pairs={{0,384},{128,0},{256,128},{384,256},{1,385},{129,1},{257,129},{385... | collective-permute-start | bytes 1966088 | tf_op jit(solution)/shard_map/ppermute | solution.py:316
  53.7 2.6 %collective-permute-done.2.refs_6_ = bf16[4,40,2048]{2,1,0:T(8,128)(2,1)S(1)} collective-permute-done((bf16[4,40,2048]{2,1,0:T(8,128)(2,1)S(1)}, bf16[4,40,2048]{2,1,0:T(8,128)(2,1)S(1)}, u32[]{:S(2)}, u32[]{:S(2)}) %collective-permute-start.2) | collective-permute-done | bytes 655392 | tf_op jit(solution)/shard_map/ppermute | solution.py:316
  56.3 2.3 %collective-permute-start.3 = (bf16[4,40,2048]{2,1,0:T(8,128)(2,1)S(1)}, bf16[4,40,2048]{2,1,0:T(8,128)(2,1)}, u32[]{:S(2)}, u32[]{:S(2)}) collective-permute-start(bf16[4,40,2048]{2,1,0:T(8,128)(2,1)S(1)} %collective-permute-done.2.refs_6_), channel_id=1, source_target_pairs={{0,128},{128,256},{256,384},{384,0},{1,129},{129,257},{257,385},{3... | collective-permute-start | bytes 1966088 | tf_op jit(solution)/shard_map/ppermute | solution.py:316
  58.6 11.7 %collective-permute-done.5.refs_7_ = bf16[4,40,2048]{2,1,0:T(8,128)(2,1)S(1)} collective-permute-done((bf16[4,40,2048]{2,1,0:T(8,128)(2,1)S(1)}, bf16[4,40,2048]{2,1,0:T(8,128)(2,1)S(1)}, u32[]{:S(2)}, u32[]{:S(2)}) %collective-permute-start.5) | collective-permute-done | bytes 655392 | tf_op jit(solution)/shard_map/ppermute | solution.py:316
  70.3 0.0 collective-permute-done.refs_2_
  70.3 5.0 %collective-permute-done.4.refs_5_ = bf16[4,40,2048]{2,1,0:T(8,128)(2,1)} collective-permute-done((bf16[4,40,2048]{2,1,0:T(8,128)(2,1)S(1)}, bf16[4,40,2048]{2,1,0:T(8,128)(2,1)}, u32[]{:S(2)}, u32[]{:S(2)}) %collective-permute-start.4) | collective-permute-done | bytes 655392 | tf_op jit(solution)/shard_map/ppermute | solution.py:316
  75.4 9.1 %collective-permute-done.3.refs_4_ = bf16[4,40,2048]{2,1,0:T(8,128)(2,1)} collective-permute-done((bf16[4,40,2048]{2,1,0:T(8,128)(2,1)S(1)}, bf16[4,40,2048]{2,1,0:T(8,128)(2,1)}, u32[]{:S(2)}, u32[]{:S(2)}) %collective-permute-start.3) | collective-permute-done | bytes 655392 | tf_op jit(solution)/shard_map/ppermute | solution.py:316
  84.4 17.9 %all-gather.3.cloned.1.call-done = bf16[12288,512]{1,0:T(8,128)(2,1)} async-done(((bf16[384,512]{1,0:T(8,128)(2,1)}), bf16[12288,512]{1,0:T(8,128)(2,1)}) %all-gather.3.cloned.1.call-update) | async-done | bytes 12582928 | tf_op jit(solution)/shard_map/all_gather | solution.py:322
  102.3 5.9 %shard_map.75 = (bf16[4,2,320,256]{3,2,1,0:T(8,128)(2,1)S(1)}, bf16[2,4,2,128,512]{4,3,2,1,0:T(8,128)(2,1)S(1)}) custom-call(s32[1]{0:T(128)} %bitcast.2.place_ref, bf16[4,40,2048]{2,1,0:T(8,128)(2,1)S(1)} %all-to-all-done.refs_0_, bf16[4,40,2048]{2,1,0:T(8,128)(2,1)S(1)} %all_to_all.20.refs_1_, bf16[4,40,2048]{2,1,0:T(8,128)(2,1)} %collective-permute-done.refs_2_, ...), custom_call_target="tpu_custom_call" | custom-call | flops 2684354560 | bytes 13631488 | tf_op jit(solution)/shard_map/pallas_call | solution.py:271
  108.3 0.0 copy-start
  108.3 21.1 %all_to_all.21.hidden_ref = bf16[4,2,320,256]{3,2,1,0:T(8,128)(2,1)S(1)} all-to-all(bf16[4,2,320,256]{3,2,1,0:T(8,128)(2,1)S(1)} %get-tuple-element.13), channel_id=1, replica_groups=mesh['y'=4,'c'=2,'x'=4,'z'=16] {'y'}, dimensions={0} | all-to-all | bytes 2621440 | tf_op jit(solution)/shard_map/all_to_all | solution.py:331
  129.4 0.0 copy-done
  129.4 4.0 %shard_map.76 = bf16[16,40,1024]{2,1,0:T(8,128)(2,1)S(1)} custom-call(bf16[4,2,320,256]{3,2,1,0:T(8,128)(2,1)S(1)} %all_to_all.21.hidden_ref, bf16[2,4,2,128,512]{4,3,2,1,0:T(8,128)(2,1)} %copy-done, bf16[2,8,2,384,512]{4,3,2,1,0:T(8,128)(2,1)} %bitcast.10), custom_call_target="tpu_custom_call" | custom-call | flops 1342177280 | bytes 6815744 | tf_op jit(solution)/shard_map/pallas_call | solution.py:290
  133.5 21.8 %all_to_all.22.rows_ref = bf16[16,40,1024]{2,1,0:T(8,128)(2,1)S(1)} all-to-all(bf16[16,40,1024]{2,1,0:T(8,128)(2,1)S(1)} %shard_map.76), channel_id=1, replica_groups=mesh['y'=4,'c'=2,'x'=4,'z'=16] {'x','y'}, dimensions={0} | all-to-all | bytes 2621440 | tf_op jit(solution)/shard_map/all_to_all | solution.py:332
  155.3 1.1 shard_map.77
Async XLA Ops:
  6.5 2.5 %copy-start.3 = (s32[64,2]{0,1:T(2,128)S(1)}, s32[64,2]{0,1:T(2,128)}, u32[]{:S(2)}) copy-start(s32[64,2]{0,1:T(2,128)} %param.9) | copy-start | bytes 1540
  6.5 2.5 %copy-start.2 = (s32[64,2]{0,1:T(2,128)S(1)}, s32[64,2]{0,1:T(2,128)}, u32[]{:S(2)}) copy-start(s32[64,2]{0,1:T(2,128)} %param.8) | copy-start | bytes 1540
  6.5 2.6 %copy-start.1 = (bf16[64,4096]{1,0:T(8,128)(2,1)S(1)}, bf16[64,4096]{1,0:T(8,128)(2,1)}, u32[]{:S(2)}) copy-start(bf16[64,4096]{1,0:T(8,128)(2,1)} %tokens_ref.1) | copy-start | bytes 1572868
  6.5 95.8 %all-gather.3.cloned.1.call-start = ((), (), s32[]{:S(2)}) async-start(), calls=%async_computation.4 | async-start | bytes 12976128 | tf_op jit(solution)/shard_map/all_gather | solution.py:322
  25.7 11.1 %all-to-all-start = ((bf16[4,40,2048]{2,1,0:T(8,128)(2,1)}), bf16[4,40,2048]{2,1,0:T(8,128)(2,1)S(1)}, u32[]{:S(2)}, u32[]{:S(2)}) async-start(bf16[4,40,2048]{2,1,0:T(8,128)(2,1)} %bitcast.3), calls=%async_computation | async-start | bytes 1310720 | tf_op jit(solution)/shard_map/all_to_all | solution.py:324
  29.2 20.8 %collective-permute-start.1 = (bf16[4,40,2048]{2,1,0:T(8,128)(2,1)S(1)}, bf16[4,40,2048]{2,1,0:T(8,128)(2,1)S(1)}, u32[]{:S(2)}, u32[]{:S(2)}) collective-permute-start(bf16[4,40,2048]{2,1,0:T(8,128)(2,1)S(1)} %all_to_all.20.refs_1_), channel_id=1, source_target_pairs={{0,384},{128,0},{256,128},{384,256},{1,385},{129,1},{257,129},{385... | collective-permute-start | bytes 1966088 | tf_op jit(solution)/shard_map/ppermute | solution.py:316
  36.8 19.6 %collective-permute-start.2 = (bf16[4,40,2048]{2,1,0:T(8,128)(2,1)S(1)}, bf16[4,40,2048]{2,1,0:T(8,128)(2,1)S(1)}, u32[]{:S(2)}, u32[]{:S(2)}) collective-permute-start(bf16[4,40,2048]{2,1,0:T(8,128)(2,1)S(1)} %all-to-all-done.refs_0_), channel_id=1, source_target_pairs={{0,128},{128,256},{256,384},{384,0},{1,129},{129,257},{257,385},{3... | collective-permute-start | bytes 1966088 | tf_op jit(solution)/shard_map/ppermute | solution.py:316
  43.5 26.9 %collective-permute-start.5 = (bf16[4,40,2048]{2,1,0:T(8,128)(2,1)S(1)}, bf16[4,40,2048]{2,1,0:T(8,128)(2,1)S(1)}, u32[]{:S(2)}, u32[]{:S(2)}) collective-permute-start(bf16[4,40,2048]{2,1,0:T(8,128)(2,1)S(1)} %all_to_all.20.refs_1_), channel_id=1, source_target_pairs={{0,128},{128,256},{256,384},{384,0},{1,129},{129,257},{257,385},{3... | collective-permute-start | bytes 1966088 | tf_op jit(solution)/shard_map/ppermute | solution.py:316
  46.7 23.6 %collective-permute-start = (bf16[4,40,2048]{2,1,0:T(8,128)(2,1)S(1)}, bf16[4,40,2048]{2,1,0:T(8,128)(2,1)}, u32[]{:S(2)}, u32[]{:S(2)}) collective-permute-start(bf16[4,40,2048]{2,1,0:T(8,128)(2,1)S(1)} %all-to-all-done.refs_0_), channel_id=1, source_target_pairs={{0,384},{128,0},{256,128},{384,256},{1,385},{129,1},{257,129},{385... | collective-permute-start | bytes 1966088 | tf_op jit(solution)/shard_map/ppermute | solution.py:316
  50.0 25.4 %collective-permute-start.4 = (bf16[4,40,2048]{2,1,0:T(8,128)(2,1)S(1)}, bf16[4,40,2048]{2,1,0:T(8,128)(2,1)}, u32[]{:S(2)}, u32[]{:S(2)}) collective-permute-start(bf16[4,40,2048]{2,1,0:T(8,128)(2,1)S(1)} %collective-permute-done.1.refs_3_), channel_id=1, source_target_pairs={{0,384},{128,0},{256,128},{384,256},{1,385},{129,1},{257,129},{385... | collective-permute-start | bytes 1966088 | tf_op jit(solution)/shard_map/ppermute | solution.py:316
  56.3 28.1 %collective-permute-start.3 = (bf16[4,40,2048]{2,1,0:T(8,128)(2,1)S(1)}, bf16[4,40,2048]{2,1,0:T(8,128)(2,1)}, u32[]{:S(2)}, u32[]{:S(2)}) collective-permute-start(bf16[4,40,2048]{2,1,0:T(8,128)(2,1)S(1)} %collective-permute-done.2.refs_6_), channel_id=1, source_target_pairs={{0,128},{128,256},{256,384},{384,0},{1,129},{129,257},{257,385},{3... | collective-permute-start | bytes 1966088 | tf_op jit(solution)/shard_map/ppermute | solution.py:316
  108.3 21.1 %copy-start = (bf16[2,4,2,128,512]{4,3,2,1,0:T(8,128)(2,1)}, bf16[2,4,2,128,512]{4,3,2,1,0:T(8,128)(2,1)S(1)}, u32[]{:S(2)}) copy-start(bf16[2,4,2,128,512]{4,3,2,1,0:T(8,128)(2,1)S(1)} %get-tuple-element.14.piece_ref) | copy-start | bytes 6291460
Sparse Core Ops, SparseCore 0:
  9.5 92.7 all-gather.2
